TPU v7x, 32 devices: a whole 2x2x4 slice. The times are simulated.
32 devices in a mesh: gx: 4 (over x, core), gy: 2 (over y), gz: 4 (over z).
Axes of the slice: x: 2, y: 2, z: 4, core: 2. Of those that a mesh axis runs over, the one named last changes fastest.
Arguments:
- intensity: float32 [32, 16, 512], P('gx', 'gy', 'gz'), may hold values from -6 to 6
- cotangent: float32 [32, 16, 512], P('gx', 'gy', 'gz'), may hold values from -6 to 6
- departure_cells: int32 [2, 2, 3, 32, 16, 512], P(None, None, None, 'gx', 'gy', 'gz'), may hold values from -2 to 2
- departure_fracs: float32 [2, 2, 3, 32, 16, 512], P(None, None, None, 'gx', 'gy', 'gz'), may hold values from 0 to 1
Outputs:
- intensity_adjoint: float32 [32, 16, 512], P('gx', 'gy', 'gz')
- velocity_adjoint: float32 [3, 32, 16, 512], P(None, 'gx', 'gy', 'gz')
All inputs are finite; a program needn't handle non-finite values.
Results may differ from a plain program's by a relative error of at most 0.00002.
Values sent between devices are 32-bit elements; how exact they have to be, the bound alone decides.
No kernel may reach another device: no remote copies, remote signals or barrier semaphores. Data moves between devices by JAX's collectives and lax.ppermute only.
A program may use at most 128 MiB of HBM per device.

v0:
```python
import functools

import jax
import jax.numpy as jnp
from jax import lax
from jax.experimental import pallas as pl
from jax.experimental.pallas import tpu as pltpu
from jax.sharding import PartitionSpec as P

LO = 3
HI = 4
ROWS = 4
SHIFTS = 8
LANES = 128
F32 = jnp.float32


def lane_of(rows):
    return lax.broadcasted_iota(jnp.int32, (rows, LANES), 1)


def group_of(rows):
    return ((lane_of(rows) + LO) & (LANES - 1)) >> 3


def low_lanes(rows):
    return (lane_of(rows) & 7) < HI


def cubic_weights(t):
    t2 = t * t
    t3 = t2 * t
    return (
        0.5 * (2.0 * t2 - t3 - t),
        0.5 * (3.0 * t3 - 5.0 * t2 + 2.0),
        0.5 * (4.0 * t2 - 3.0 * t3 + t),
        0.5 * (t3 - t2),
    )


def cubic_slopes(t):
    t2 = t * t
    return (
        0.5 * (4.0 * t - 3.0 * t2 - 1.0),
        0.5 * (9.0 * t2 - 10.0 * t),
        0.5 * (8.0 * t - 9.0 * t2 + 1.0),
        0.5 * (3.0 * t2 - 2.0 * t),
    )


def write_tables(cells, fracs, step, section, weights, slopes=None):
    def plane(x, carry):
        for c in range(3):
            k = cells[step, section, c, x]
            t = fracs[step, section, c, x]
            hits = {s: k == s for s in range(-2, 3)}
            for ref, taps in ((weights, cubic_weights), (slopes, cubic_slopes)):
                if ref is None:
                    continue
                values = taps(t)
                for j in range(SHIFTS):
                    entry = jnp.zeros_like(t)
                    for a in range(4):
                        s = j - 3 - (a - 1)
                        if -2 <= s <= 2:
                            entry = jnp.where(hits[s], values[a], entry)
                    ref[c, j, x] = entry
        return carry

    lax.fori_loop(0, cells.shape[3], plane, 0)


def shift_planes(extended, rim, shifted):
    planes, rows, _ = extended.shape
    lane = lane_of(rows)
    for X in range(planes):
        core = extended[X]
        ends = pltpu.roll(rim, (-8 * X) % LANES, 1)
        for j in range(SHIFTS):
            d = j - LO
            if d == 0:
                shifted[j, X] = core
            else:
                wraps = lane >= LANES + d if d < 0 else lane < d
                shifted[j, X] = pltpu.roll(jnp.where(wraps, ends, core), (-d) % LANES, 1)


def interpolate(shifted, weights, slopes, nx, ny, emit):
    def plane(x, carry):
        tz = [weights[2, j, x] for j in range(SHIFTS)]
        sz = None if slopes is None else [slopes[2, j, x] for j in range(SHIFTS)]

        def row(sy, sums):
            ty = weights[1, sy, x]
            a = b = c = None
            for sx in range(SHIFTS):
                window = [shifted[j, x + sx, pl.ds(sy + 1, ny), :] for j in range(SHIFTS)]
                column = total([tz[j] * window[j] for j in range(SHIFTS)])
                tx = weights[0, sx, x]
                a = plus(a, tx * column)
                if slopes is not None:
                    b = plus(b, slopes[0, sx, x] * column)
                    c = plus(c, tx * total([sz[j] * window[j] for j in range(SHIFTS)]))
            if slopes is None:
                return (sums[0] + ty * a,)
            return (sums[0] + ty * b, sums[1] + slopes[1, sy, x] * a, sums[2] + ty * c)

        zero = jnp.zeros((ny, LANES), F32)
        sums = lax.fori_loop(0, SHIFTS, row, (zero,) * (1 if slopes is None else 3))
        emit(x, sums)
        return carry

    lax.fori_loop(0, nx, plane, 0)


def total(terms):
    while len(terms) > 1:
        terms = [terms[i] + terms[i + 1] for i in range(0, len(terms), 2)]
    return terms[0]


def plus(a, b):
    return b if a is None else a + b


def deposit(sources, weights, scaled, piles):
    channels, nx, ny, _ = sources.shape
    planes = piles.shape[2]
    piles[...] = jnp.zeros(piles.shape, F32)

    def row(sy, carry):
        for x in range(nx):
            ty = weights[1, sy, x]
            for c in range(channels):
                scaled[c, x] = sources[c, x] * ty
        for X in range(planes):
            sums = [[None] * SHIFTS for _ in range(channels)]
            for x in range(max(0, X - SHIFTS + 1), min(nx - 1, X) + 1):
                tx = weights[0, X - x, x]
                parts = [scaled[c, x] * tx for c in range(channels)]
                for j in range(SHIFTS):
                    tz = weights[2, j, x]
                    for c in range(channels):
                        sums[c][j] = plus(sums[c][j], parts[c] * tz)
            for c in range(channels):
                for j in range(SHIFTS):
                    piles[c, j, X, pl.ds(sy + 1, ny), :] += sums[c][j]
        return carry

    lax.fori_loop(0, SHIFTS, row, 0)


def settle(piles, out, base=None):
    channels, _, planes, rows, _ = piles.shape
    lane = lane_of(rows)
    group = group_of(rows)
    for c in range(channels):
        rim = jnp.zeros((rows, LANES), F32)
        for X in range(planes):
            core = piles[c, LO, X]
            ends = jnp.zeros((rows, LANES), F32)
            for j in range(SHIFTS):
                d = j - LO
                if d == 0:
                    continue
                moved = pltpu.roll(piles[c, j, X], d % LANES, 1)
                wraps = lane >= LANES + d if d < 0 else lane < d
                core = core + jnp.where(wraps, 0.0, moved)
                ends = ends + jnp.where(wraps, moved, 0.0)
            out[c, X] = core if base is None else core + base[c, X]
            rim = jnp.where(group == X, pltpu.roll(ends, (8 * X) % LANES, 1), rim)
        out[c, planes] = rim if base is None else rim + base[c, planes]


def pack_rim(extended):
    planes, rows, _ = extended.shape
    group = group_of(rows)
    rim = jnp.zeros((rows, LANES), F32)
    for X in range(planes):
        rim = jnp.where(group == X, pltpu.roll(extended[X], (8 * X) % LANES, 1), rim)
    return rim


def unpack_rim(rim, X):
    lane = lane_of(rim.shape[0])
    return jnp.where((lane < HI) | (lane >= LANES - LO), pltpu.roll(rim, (-8 * X) % LANES, 1), 0.0)


def fold_rows(message, ny):
    if ny == 2 * ROWS:
        return pltpu.roll(message, ROWS, 0)
    below, above = message[:ROWS], message[ROWS:]
    if ny == ROWS:
        return below + above
    return jnp.concatenate([above, jnp.zeros((ny - 2 * ROWS, LANES), F32), below], axis=0)


def put_edges(out, at, plane, ny):
    if ny == 2 * ROWS:
        out[at] = plane
    else:
        out[at, 0:ROWS] = plane[0:ROWS]
        out[at, ROWS : 2 * ROWS] = plane[ny - ROWS : ny]


def put_rims(out, at, plane, ny):
    out[at, 0:ROWS] = plane[0:ROWS]
    out[at, ROWS : 2 * ROWS] = plane[ROWS + ny : 2 * ROWS + ny]


def split_deposits(piled, outs, at, nx, ny):
    to_y, to_left, to_right, to_left_y, to_right_y, own = outs
    at_y, at_left, at_right, at_own = at
    planes = nx + LO + HI
    core = slice(ROWS, ROWS + ny)
    for i, X in enumerate(list(range(LO, LO + nx)) + [planes]):
        own[at_own + i] = piled[X, core]
        put_rims(to_y, at_y + i, piled[X], ny)
    for i, X in enumerate(list(range(LO)) + [planes]):
        to_left[at_left + i] = piled[X, core]
        put_rims(to_left_y, at_left + i, piled[X], ny)
    for i, X in enumerate(list(range(LO + nx, planes)) + [planes]):
        to_right[at_right + i] = piled[X, core]
        put_rims(to_right_y, at_right + i, piled[X], ny)


def join_deposits(ins, at, nx, ny, put):
    from_y, from_right, from_left, from_right_y, from_left_y, own = ins
    at_y, at_left, at_right, at_own = at

    def right(i):
        return from_right[at_left + i] + fold_rows(from_right_y[at_left + i], ny)

    def left(i):
        return from_left[at_right + i] + fold_rows(from_left_y[at_right + i], ny)

    for x in range(nx):
        plane = own[at_own + x] + fold_rows(from_y[at_y + x], ny)
        if x >= nx - LO:
            plane = plane + right(x - (nx - LO))
        if x < HI:
            plane = plane + left(x)
        put(x, plane)
    group = group_of(ny)
    rim = own[at_own + nx] + fold_rows(from_y[at_y + nx], ny)
    turn = 8 * nx
    high = pltpu.roll(right(LO), turn % LANES, 1)
    low = pltpu.roll(left(HI), (-turn) % LANES, 1)
    rim = rim + jnp.where((group >= nx) & (group < nx + LO), high, 0.0)
    return rim + jnp.where((group >= LO) & (group < LO + HI), low, 0.0)


def join_halo(field, ins, extended, nx, ny):
    from_y, from_right, from_left, from_right_y, from_left_y = ins

    def place(X, core, edges):
        extended[X, 0:ROWS] = edges[ROWS : 2 * ROWS]
        extended[X, ROWS : ROWS + ny] = core
        extended[X, ROWS + ny : 2 * ROWS + ny] = edges[0:ROWS]

    for x in range(nx):
        place(LO + x, field[x], from_y[x])
    for i in range(HI):
        place(LO + nx + i, from_right[i], from_right_y[i])
    for i in range(LO):
        place(i, from_left[i], from_left_y[i])


def split_halo(field, outs, nx, ny):
    to_y, to_left, to_right, to_left_y, to_right_y = outs
    for x in range(nx):
        put_edges(to_y, x, field[x], ny)
    for i in range(HI):
        to_left[i] = field[i]
        put_edges(to_left_y, i, field[i], ny)
    for i in range(LO):
        to_right[i] = field[nx - LO + i]
        put_edges(to_right_y, i, field[nx - LO + i], ny)


def first_kernel(nx, ny, intensity, cotangent, cells, fracs, to_y, to_l, to_r, to_ly, to_ry, own, weights, scaled, piles, piled):
    write_tables(cells, fracs, 1, 1, weights)
    deposit(cotangent, weights, scaled, piles)
    settle(piles, piled)
    split_halo(intensity, (to_y, to_l, to_r, to_ly, to_ry), nx, ny)
    split_deposits(piled.at[0], (to_y, to_l, to_r, to_ly, to_ry, own), (nx, HI, LO, 0), nx, ny)


def first_join_kernel(nx, ny, intensity, from_y, from_r, from_l, from_ry, from_ly, own, extended, part, rims):
    rows = ny + 2 * ROWS
    join_halo(intensity, (from_y, from_r, from_l, from_ry, from_ly), extended, nx, ny)
    rims[0:rows] = pack_rim(extended)

    def put(x, plane):
        part[x] = plane

    rims[rows : rows + ny] = join_deposits((from_y, from_r, from_l, from_ry, from_ly, own), (nx, HI, LO, 0), nx, ny, put)


def middle_kernel(nx, ny, extended, rims_l, rims_r, part, cells, fracs, image, to_y, to_l, to_r, to_ly, to_ry, shifted, adjoint, weights):
    rows = ny + 2 * ROWS
    rim = jnp.where(low_lanes(rows), rims_r[0:rows], rims_l[0:rows])
    shift_planes(extended, rim, shifted)
    write_tables(cells, fracs, 0, 1, weights)

    def emit(x, sums):
        image[x] = sums[0]

    interpolate(shifted, weights, None, nx, ny, emit)
    split_halo(image, (to_y, to_l, to_r, to_ly, to_ry), nx, ny)
    back = jnp.where(low_lanes(ny), rims_l[rows : rows + ny], rims_r[rows : rows + ny])
    for x in range(nx):
        adjoint[0, x] = part[x] + unpack_rim(back, LO + x)


def early_kernel(nx, ny, shifted, adjoint, cells, fracs, grad, piled, weights, slopes, scaled, piles):
    write_tables(cells, fracs, 0, 1, weights, slopes)

    def emit(x, sums):
        for c in range(3):
            grad[c, x] = adjoint[0, x] * sums[c]

    interpolate(shifted, weights, slopes, nx, ny, emit)
    deposit(adjoint, weights, scaled, piles)
    settle(piles, piled)


def early_spread_kernel(nx, ny, grad, cells, fracs, piled, weights, scaled, piles):
    write_tables(cells, fracs, 0, 0, weights)
    deposit(grad, weights, scaled, piles)
    settle(piles, piled)


def second_join_kernel(nx, ny, image, from_y, from_r, from_l, from_ry, from_ly, extended, rims):
    join_halo(image, (from_y, from_r, from_l, from_ry, from_ly), extended, nx, ny)
    rims[...] = pack_rim(extended)


def late_kernel(
    nx, ny, extended, rims_l, rims_r, cotangent, cells, fracs, piled_adjoint, piled_early,
    to_y, to_l, to_r, to_ly, to_ry, own,
    shifted, weights, slopes, grad, scaled, piles, piled,
):
    rows = ny + 2 * ROWS
    shift_planes(extended, jnp.where(low_lanes(rows), rims_r[...], rims_l[...]), shifted)
    write_tables(cells, fracs, 1, 1, weights, slopes)

    def emit(x, sums):
        for c in range(3):
            grad[c, x] = cotangent[0, x] * sums[c]

    interpolate(shifted, weights, slopes, nx, ny, emit)
    write_tables(cells, fracs, 1, 0, weights)
    deposit(grad, weights, scaled, piles)
    settle(piles, piled, piled_early)
    outs = (to_y, to_l, to_r, to_ly, to_ry, own)
    for c in range(4):
        source = piled_adjoint.at[0] if c == 0 else piled.at[c - 1]
        at = (c * (nx + 1), c * (LO + 1), c * (HI + 1), c * (nx + 1))
        split_deposits(source, outs, at, nx, ny)


def last_join_kernel(nx, ny, from_y, from_r, from_l, from_ry, from_ly, own, part, rims):
    ins = (from_y, from_r, from_l, from_ry, from_ly, own)
    for c in range(4):

        def put(x, plane, c=c):
            part[c, x] = plane

        at = (c * (nx + 1), c * (LO + 1), c * (HI + 1), c * (nx + 1))
        rims[c * ny : (c + 1) * ny] = join_deposits(ins, at, nx, ny, put)


def last_kernel(nx, ny, part, rims_l, rims_r, intensity_adjoint, velocity_adjoint):
    low = low_lanes(ny)
    for c in range(4):
        rows = slice(c * ny, (c + 1) * ny)
        back = jnp.where(low, rims_l[rows], rims_r[rows])
        for x in range(nx):
            plane = part[c, x] + unpack_rim(back, LO + x)
            if c == 0:
                intensity_adjoint[x] = plane
            else:
                velocity_adjoint[c - 1, x] = plane


def call(kernel, args, outs, scratch, flops):
    def struct(shape):
        return jax.ShapeDtypeStruct(shape, F32)

    in_vmem = pl.BlockSpec(memory_space=pltpu.VMEM)
    moved = 4 * sum(a.size for a in args)
    return pl.pallas_call(
        kernel,
        out_shape=[struct(s) for s in outs],
        in_specs=[in_vmem] * len(args),
        out_specs=[in_vmem] * len(outs),
        scratch_shapes=[pltpu.VMEM(s, F32) for s in scratch],
        compiler_params=pltpu.CompilerParams(vmem_limit_bytes=24 * 1024 * 1024),
        cost_estimate=pl.CostEstimate(flops=flops, bytes_accessed=moved, transcendentals=0),
    )(*args)


def send(message, moves):
    axes = tuple(axis for axis, _ in moves)
    sizes = [lax.axis_size(axis) for axis in axes]
    if len(axes) == 1:
        pairs = [(i, (i + moves[0][1]) % sizes[0]) for i in range(sizes[0])]
        return lax.ppermute(message, axes[0], pairs)
    pairs = [
        (i * sizes[1] + j, (i + moves[0][1]) % sizes[0] * sizes[1] + (j + moves[1][1]) % sizes[1])
        for i in range(sizes[0])
        for j in range(sizes[1])
    ]
    return lax.ppermute(message, axes, pairs)


def send_y(message, *moves):
    if lax.axis_size("gy") == 2:
        return send(message, moves + (("gy", 1),))
    down = send(message[:, :ROWS], moves + (("gy", -1),))
    up = send(message[:, ROWS:], moves + (("gy", 1),))
    return jnp.concatenate([down, up], axis=1)


def send_sides(to_y, to_l, to_r, to_ly, to_ry):
    left, right = ("gx", -1), ("gx", 1)
    return (
        send_y(to_y),
        send(to_l, (left,)),
        send(to_r, (right,)),
        send_y(to_ly, left),
        send_y(to_ry, right),
    )


def send_z(rims):
    return send(rims, (("gz", 1),)), send(rims, (("gz", -1),))


def body(intensity, cotangent, cells, fracs):
    nx, ny, nz = intensity.shape
    rows = ny + 2 * ROWS
    planes = nx + LO + HI
    table = (3, SHIFTS, nx, ny, nz)
    bound = functools.partial
    ring = 2 * ROWS

    def pile(channels):
        return [(channels, nx, ny, nz), (channels, SHIFTS, planes, rows, nz)]

    def piled(channels):
        return (channels, planes + 1, rows, nz)

    cotangent = cotangent[None]
    unit = nx * ny * nz * 512

    y_planes, l_planes, r_planes = nx, HI, LO
    *outs, own = call(
        bound(first_kernel, nx, ny),
        (intensity, cotangent, cells, fracs),
        [
            (2 * nx + 1, ring, nz),
            (HI + LO + 1, ny, nz),
            (LO + HI + 1, ny, nz),
            (HI + LO + 1, ring, nz),
            (LO + HI + 1, ring, nz),
            (nx + 1, ny, nz),
        ],
        [table] + pile(1) + [piled(1)],
        2 * unit,
    )
    sides = send_sides(*outs)
    extended, part, rims = call(
        bound(first_join_kernel, nx, ny),
        (intensity,) + sides + (own,),
        [(planes, rows, nz), (nx, ny, nz), (rows + ny, nz)],
        [],
        unit // 16,
    )
    rims_l, rims_r = send_z(rims)
    image, *outs, shifted, adjoint = call(
        bound(middle_kernel, nx, ny),
        (extended, rims_l, rims_r, part, cells, fracs),
        [
            (nx, ny, nz),
            (nx, ring, nz),
            (HI, ny, nz),
            (LO, ny, nz),
            (HI, ring, nz),
            (LO, ring, nz),
            (SHIFTS, planes, rows, nz),
            (1, nx, ny, nz),
        ],
        [table],
        2 * unit,
    )
    sides = send_sides(*outs)
    grad, piled_adjoint = call(
        bound(early_kernel, nx, ny),
        (shifted, adjoint, cells, fracs),
        [(3, nx, ny, nz), piled(1)],
        [table, table] + pile(1),
        7 * unit,
    )
    extended, rims = call(
        bound(second_join_kernel, nx, ny),
        (image,) + sides,
        [(planes, rows, nz), (rows, nz)],
        [],
        unit // 16,
    )
    rims_l, rims_r = send_z(rims)
    (piled_early,) = call(
        bound(early_spread_kernel, nx, ny),
        (grad, cells, fracs),
        [piled(3)],
        [table] + pile(3),
        6 * unit,
    )
    *outs, own = call(
        bound(late_kernel, nx, ny),
        (extended, rims_l, rims_r, cotangent, cells, fracs, piled_adjoint, piled_early),
        [
            (4 * (nx + 1), ring, nz),
            (4 * (LO + 1), ny, nz),
            (4 * (HI + 1), ny, nz),
            (4 * (LO + 1), ring, nz),
            (4 * (HI + 1), ring, nz),
            (4 * (nx + 1), ny, nz),
        ],
        [(SHIFTS, planes, rows, nz), table, table, (3, nx, ny, nz)] + pile(3) + [piled(3)],
        11 * unit,
    )
    sides = send_sides(*outs)
    part, rims = call(
        bound(last_join_kernel, nx, ny),
        sides + (own,),
        [(4, nx, ny, nz), (4 * ny, nz)],
        [],
        unit // 16,
    )
    rims_l, rims_r = send_z(rims)
    return tuple(
        call(
            bound(last_kernel, nx, ny),
            (part, rims_l, rims_r),
            [(nx, ny, nz), (3, nx, ny, nz)],
            [],
            unit // 16,
        )
    )


def solution(mesh):
    in_specs = (
        P("gx", "gy", "gz"),
        P("gx", "gy", "gz"),
        P(None, None, None, "gx", "gy", "gz"),
        P(None, None, None, "gx", "gy", "gz"),
    )
    out_specs = (P("gx", "gy", "gz"), P(None, "gx", "gy", "gz"))
    return jax.shard_map(body, mesh=mesh, in_specs=in_specs, out_specs=out_specs, check_vma=False)
```

profile of v0, /device:TPU:0, one launch (start us, length us, event | category | flops | bytes accessed | tf_op | source)
XLA Modules:
  0.0 74.5 jit_solution(5686295413066697836)
XLA Ops:
  4.1 2.3 %shard_map.59 = (f32[17,8,128]{2,1,0:T(8,128)S(1)}, f32[8,8,128]{2,1,0:T(8,128)S(1)}, f32[8,8,128]{2,1,0:T(8,128)S(1)}, f32[8,8,128]{2,1,0:T(8,128)S(1)}, f32[8,...) custom-call(f32[8,8,128]{2,1,0:T(8,128)S(1)} %copy-done.4, f32[1,8,8,128]{3,2,1,0:T(8,128)S(1)} %bitcast.1, ...), custom_call_target="tpu_custom_call" | custom-call | flops 8388608 | bytes 851968 | tf_op jit(solution)/shard_map/pallas_call | solution.py:393
  6.5 3.0 %collective-permute-start = (f32[17,8,128]{2,1,0:T(8,128)S(1)}, f32[17,8,128]{2,1,0:T(8,128)S(1)}, u32[]{:S(2)}, u32[]{:S(2)}) collective-permute-start(f32[17,8,128]{2,1,0:T(8,128)S(1)} %get-tuple-element.31), channel_id=1, source_target_pairs={{0,4},{4,0},{1,5},{5,1},{2,6},{6,2},{3,7},{7,3},{8,12},{12,8},{9,1... | collective-permute-start | bytes 208904 | tf_op jit(solution)/shard_map/ppermute | solution.py:409
  10.1 1.7 %collective-permute-start.3 = (f32[8,8,128]{2,1,0:T(8,128)S(1)}, f32[8,8,128]{2,1,0:T(8,128)S(1)}, u32[]{:S(2)}, u32[]{:S(2)}) collective-permute-start(f32[8,8,128]{2,1,0:T(8,128)S(1)} %get-tuple-element.34), channel_id=1, source_target_pairs={{0,28},{4,24},{8,4},{12,0},{16,12},{20,8},{24,20},{28,16},{1,29},{... | collective-permute-start | bytes 98312 | tf_op jit(solution)/shard_map/ppermute | solution.py:415
  11.9 1.6 %collective-permute-done.2.from_l = f32[8,8,128]{2,1,0:T(8,128)S(1)} collective-permute-done((f32[8,8,128]{2,1,0:T(8,128)S(1)}, f32[8,8,128]{2,1,0:T(8,128)S(1)}, u32[]{:S(2)}, u32[]{:S(2)}) %collective-permute-start.2) | collective-permute-done | bytes 32800 | tf_op jit(solution)/shard_map/ppermute | solution.py:409
  13.5 2.6 %collective-permute-done.4.from_ly = f32[8,8,128]{2,1,0:T(8,128)S(1)} collective-permute-done((f32[8,8,128]{2,1,0:T(8,128)S(1)}, f32[8,8,128]{2,1,0:T(8,128)S(1)}, u32[]{:S(2)}, u32[]{:S(2)}) %collective-permute-start.4) | collective-permute-done | bytes 32800 | tf_op jit(solution)/shard_map/ppermute | solution.py:415
  16.2 1.6 %collective-permute-start.5 = (f32[24,128]{1,0:T(8,128)S(1)}, f32[24,128]{1,0:T(8,128)S(1)}, u32[]{:S(2)}, u32[]{:S(2)}) collective-permute-start(f32[24,128]{1,0:T(8,128)S(1)} %get-tuple-element.38), channel_id=1, source_target_pairs={{0,1},{1,2},{2,3},{3,0},{4,5},{5,6},{6,7},{7,4},{8,9},{9,10},{10,1... | collective-permute-start | bytes 36872 | tf_op jit(solution)/shard_map/ppermute | solution.py:409
  17.8 2.2 %collective-permute-start.6 = (f32[24,128]{1,0:T(8,128)S(1)}, f32[24,128]{1,0:T(8,128)S(1)}, u32[]{:S(2)}, u32[]{:S(2)}) collective-permute-start(f32[24,128]{1,0:T(8,128)S(1)} %get-tuple-element.38), channel_id=1, source_target_pairs={{0,3},{1,0},{2,1},{3,2},{4,7},{5,4},{6,5},{7,6},{8,11},{9,8},{10,9... | collective-permute-start | bytes 36872 | tf_op jit(solution)/shard_map/ppermute | solution.py:409
  20.0 1.7 %collective-permute-done.5.rims_l = f32[24,128]{1,0:T(8,128)S(1)} collective-permute-done((f32[24,128]{1,0:T(8,128)S(1)}, f32[24,128]{1,0:T(8,128)S(1)}, u32[]{:S(2)}, u32[]{:S(2)}) %collective-permute-start.5) | collective-permute-done | bytes 12320 | tf_op jit(solution)/shard_map/ppermute | solution.py:409
  21.7 3.1 %shard_map.61 = (f32[8,8,128]{2,1,0:T(8,128)S(1)}, f32[8,8,128]{2,1,0:T(8,128)S(1)}, f32[4,8,128]{2,1,0:T(8,128)S(1)}, f32[3,8,128]{2,1,0:T(8,128)S(1)}, f32[4,8...) custom-call(f32[15,16,128]{2,1,0:T(8,128)S(1)} %get-tuple-element.37, ...), custom_call_target="tpu_custom_call" | custom-call | flops 8388608 | bytes 966656 | tf_op jit(solution)/shard_map/pallas_call | solution.py:393
  24.8 1.5 %collective-permute-start.7 = (f32[8,8,128]{2,1,0:T(8,128)S(1)}, f32[8,8,128]{2,1,0:T(8,128)S(1)}, u32[]{:S(2)}, u32[]{:S(2)}) collective-permute-start(f32[8,8,128]{2,1,0:T(8,128)S(1)} %get-tuple-element.41), channel_id=1, source_target_pairs={{0,4},{4,0},{1,5},{5,1},{2,6},{6,2},{3,7},{7,3},{8,12},{12,8},{9,1... | collective-permute-start | bytes 98312 | tf_op jit(solution)/shard_map/ppermute | solution.py:409
  26.3 1.2 %collective-permute-start.8 = (f32[4,8,128]{2,1,0:T(8,128)S(1)}, f32[4,8,128]{2,1,0:T(8,128)S(1)}, u32[]{:S(2)}, u32[]{:S(2)}) collective-permute-start(f32[4,8,128]{2,1,0:T(8,128)S(1)} %get-tuple-element.42), channel_id=1, source_target_pairs={{0,24},{8,0},{16,8},{24,16},{1,25},{9,1},{17,9},{25,17},{2,26},{10... | collective-permute-start | bytes 49160 | tf_op jit(solution)/shard_map/ppermute | solution.py:409
  28.1 1.6 %collective-permute-start.9 = (f32[3,8,128]{2,1,0:T(8,128)S(1)}, f32[3,8,128]{2,1,0:T(8,128)S(1)}, u32[]{:S(2)}, u32[]{:S(2)}) collective-permute-start(f32[3,8,128]{2,1,0:T(8,128)S(1)} %get-tuple-element.43), channel_id=1, source_target_pairs={{0,8},{8,16},{16,24},{24,0},{1,9},{9,17},{17,25},{25,1},{2,10},{10... | collective-permute-start | bytes 36872 | tf_op jit(solution)/shard_map/ppermute | solution.py:409
  29.7 1.9 %collective-permute-done.11.from_ly = f32[3,8,128]{2,1,0:T(8,128)S(1)} collective-permute-done((f32[3,8,128]{2,1,0:T(8,128)S(1)}, f32[3,8,128]{2,1,0:T(8,128)S(1)}, u32[]{:S(2)}, u32[]{:S(2)}) %collective-permute-start.11) | collective-permute-done | bytes 12320 | tf_op jit(solution)/shard_map/ppermute | solution.py:415
  31.7 1.4 %collective-permute-start.12 = (f32[16,128]{1,0:T(8,128)S(1)}, f32[16,128]{1,0:T(8,128)S(1)}, u32[]{:S(2)}, u32[]{:S(2)}) collective-permute-start(f32[16,128]{1,0:T(8,128)S(1)} %get-tuple-element.47), channel_id=1, source_target_pairs={{0,1},{1,2},{2,3},{3,0},{4,5},{5,6},{6,7},{7,4},{8,9},{9,10},{10,1... | collective-permute-start | bytes 24584 | tf_op jit(solution)/shard_map/ppermute | solution.py:409
  33.1 2.5 %collective-permute-start.13 = (f32[16,128]{1,0:T(8,128)S(1)}, f32[16,128]{1,0:T(8,128)S(1)}, u32[]{:S(2)}, u32[]{:S(2)}) collective-permute-start(f32[16,128]{1,0:T(8,128)S(1)} %get-tuple-element.47), channel_id=1, source_target_pairs={{0,3},{1,0},{2,1},{3,2},{4,7},{5,4},{6,5},{7,6},{8,11},{9,8},{10,9... | collective-permute-start | bytes 24584 | tf_op jit(solution)/shard_map/ppermute | solution.py:409
  35.7 5.4 %shard_map.63 = (f32[3,8,8,128]{3,2,1,0:T(8,128)S(1)}, f32[1,16,16,128]{3,2,1,0:T(8,128)S(1)}) custom-call(f32[8,15,16,128]{3,2,1,0:T(8,128)S(1)} %get-tuple-element.48.shifted, f32[1,8,8,128]{3,2,1,0:T(8,128)S(1)} %get-tuple-element.49.adjoint, s32[2,2,3,8,8,128]{5,4,3,2,1,0:T(8,128)S(1)} %copy-done.1, f32[2,2,3,8,8,128]{5,4,3,2,1,0:T(8,128)S(1)} %copy-done.3), custom_call_target="tpu_custom_call" | custom-call | flops 29360128 | bytes 1802240 | tf_op jit(solution)/shard_map/pallas_call | solution.py:393
  41.1 7.1 %shard_map.64.piled_early = f32[3,16,16,128]{3,2,1,0:T(8,128)S(1)} custom-call(f32[3,8,8,128]{3,2,1,0:T(8,128)S(1)} %get-tuple-element.51.grad, s32[2,2,3,8,8,128]{5,4,3,2,1,0:T(8,128)S(1)} %copy-done.1, f32[2,2,3,8,8,128]{5,4,3,2,1,0:T(8,128)S(1)} %copy-done.3), custom_call_target="tpu_custom_call" | custom-call | flops 25165824 | bytes 884736 | tf_op jit(solution)/shard_map/pallas_call | solution.py:393
  48.3 11.4 %shard_map.65 = (f32[36,8,128]{2,1,0:T(8,128)S(1)}, f32[16,8,128]{2,1,0:T(8,128)S(1)}, f32[20,8,128]{2,1,0:T(8,128)S(1)}, f32[16,8,128]{2,1,0:T(8,128)S(1)}, f32...) custom-call(f32[15,16,128]{2,1,0:T(8,128)S(1)} %get-tuple-element.46.extended, ...), custom_call_target="tpu_custom_call" | custom-call | flops 46137344 | bytes 1482752 | tf_op jit(solution)/shard_map/pallas_call | solution.py:393
  59.6 1.4 %collective-permute-start.14 = (f32[36,8,128]{2,1,0:T(8,128)S(1)}, f32[36,8,128]{2,1,0:T(8,128)S(1)}, u32[]{:S(2)}, u32[]{:S(2)}) collective-permute-start(f32[36,8,128]{2,1,0:T(8,128)S(1)} %get-tuple-element.52), channel_id=1, source_target_pairs={{0,4},{4,0},{1,5},{5,1},{2,6},{6,2},{3,7},{7,3},{8,12},{12,8},{9,1... | collective-permute-start | bytes 442376 | tf_op jit(solution)/shard_map/ppermute | solution.py:409
  61.0 1.6 %collective-permute-start.18 = (f32[20,8,128]{2,1,0:T(8,128)S(1)}, f32[20,8,128]{2,1,0:T(8,128)S(1)}, u32[]{:S(2)}, u32[]{:S(2)}) collective-permute-start(f32[20,8,128]{2,1,0:T(8,128)S(1)} %get-tuple-element.56), channel_id=1, source_target_pairs={{0,12},{4,8},{8,20},{12,16},{16,28},{20,24},{24,4},{28,0},{1,13},{... | collective-permute-start | bytes 245768 | tf_op jit(solution)/shard_map/ppermute | solution.py:415
  62.9 1.5 %collective-permute-start.17 = (f32[16,8,128]{2,1,0:T(8,128)S(1)}, f32[16,8,128]{2,1,0:T(8,128)S(1)}, u32[]{:S(2)}, u32[]{:S(2)}) collective-permute-start(f32[16,8,128]{2,1,0:T(8,128)S(1)} %get-tuple-element.55), channel_id=1, source_target_pairs={{0,28},{4,24},{8,4},{12,0},{16,12},{20,8},{24,20},{28,16},{1,29},{... | collective-permute-start | bytes 196616 | tf_op jit(solution)/shard_map/ppermute | solution.py:415
  65.2 2.9 %collective-permute-done.17.from_ry = f32[16,8,128]{2,1,0:T(8,128)S(1)} collective-permute-done((f32[16,8,128]{2,1,0:T(8,128)S(1)}, f32[16,8,128]{2,1,0:T(8,128)S(1)}, u32[]{:S(2)}, u32[]{:S(2)}) %collective-permute-start.17) | collective-permute-done | bytes 65568 | tf_op jit(solution)/shard_map/ppermute | solution.py:415
  68.2 3.8 %collective-permute-start.20 = (f32[32,128]{1,0:T(8,128)S(1)}, f32[32,128]{1,0:T(8,128)S(1)}, u32[]{:S(2)}, u32[]{:S(2)}) collective-permute-start(f32[32,128]{1,0:T(8,128)S(1)} %get-tuple-element.59), channel_id=1, source_target_pairs={{0,3},{1,0},{2,1},{3,2},{4,7},{5,4},{6,5},{7,6},{8,11},{9,8},{10,9... | collective-permute-start | bytes 49160 | tf_op jit(solution)/shard_map/ppermute | solution.py:409
  72.0 1.7 %collective-permute-done.19.rims_l = f32[32,128]{1,0:T(8,128)S(1)} collective-permute-done((f32[32,128]{1,0:T(8,128)S(1)}, f32[32,128]{1,0:T(8,128)S(1)}, u32[]{:S(2)}, u32[]{:S(2)}) %collective-permute-start.19) | collective-permute-done | bytes 16416 | tf_op jit(solution)/shard_map/ppermute | solution.py:409
  (41 shorter events, 7.1 us)
Async XLA Ops:
  4.1 17.6 %copy-start.1 = (s32[2,2,3,8,8,128]{5,4,3,2,1,0:T(8,128)S(1)}, s32[2,2,3,8,8,128]{5,4,3,2,1,0:T(8,128)}, u32[]{:S(2)}) copy-start(s32[2,2,3,8,8,128]{5,4,3,2,1,0:T(8,128)} %cells.9) | copy-start | bytes 1179652
  4.1 17.6 %copy-start.3 = (f32[2,2,3,8,8,128]{5,4,3,2,1,0:T(8,128)S(1)}, f32[2,2,3,8,8,128]{5,4,3,2,1,0:T(8,128)}, u32[]{:S(2)}) copy-start(f32[2,2,3,8,8,128]{5,4,3,2,1,0:T(8,128)} %fracs.9) | copy-start | bytes 1179652
  6.5 9.6 %collective-permute-start = (f32[17,8,128]{2,1,0:T(8,128)S(1)}, f32[17,8,128]{2,1,0:T(8,128)S(1)}, u32[]{:S(2)}, u32[]{:S(2)}) collective-permute-start(f32[17,8,128]{2,1,0:T(8,128)S(1)} %get-tuple-element.31), channel_id=1, source_target_pairs={{0,4},{4,0},{1,5},{5,1},{2,6},{6,2},{3,7},{7,3},{8,12},{12,8},{9,1... | collective-permute-start | bytes 208904 | tf_op jit(solution)/shard_map/ppermute | solution.py:409
  9.5 2.4 %collective-permute-start.1 = (f32[8,8,128]{2,1,0:T(8,128)S(1)}, f32[8,8,128]{2,1,0:T(8,128)S(1)}, u32[]{:S(2)}, u32[]{:S(2)}) collective-permute-start(f32[8,8,128]{2,1,0:T(8,128)S(1)} %get-tuple-element.32), channel_id=1, source_target_pairs={{0,24},{8,0},{16,8},{24,16},{1,25},{9,1},{17,9},{25,17},{2,26},{10... | collective-permute-start | bytes 98312 | tf_op jit(solution)/shard_map/ppermute | solution.py:409
  10.1 3.3 %collective-permute-start.2 = (f32[8,8,128]{2,1,0:T(8,128)S(1)}, f32[8,8,128]{2,1,0:T(8,128)S(1)}, u32[]{:S(2)}, u32[]{:S(2)}) collective-permute-start(f32[8,8,128]{2,1,0:T(8,128)S(1)} %get-tuple-element.33), channel_id=1, source_target_pairs={{0,8},{8,16},{16,24},{24,0},{1,9},{9,17},{17,25},{25,1},{2,10},{10... | collective-permute-start | bytes 98312 | tf_op jit(solution)/shard_map/ppermute | solution.py:409
  10.1 3.3 %collective-permute-start.3 = (f32[8,8,128]{2,1,0:T(8,128)S(1)}, f32[8,8,128]{2,1,0:T(8,128)S(1)}, u32[]{:S(2)}, u32[]{:S(2)}) collective-permute-start(f32[8,8,128]{2,1,0:T(8,128)S(1)} %get-tuple-element.34), channel_id=1, source_target_pairs={{0,28},{4,24},{8,4},{12,0},{16,12},{20,8},{24,20},{28,16},{1,29},{... | collective-permute-start | bytes 98312 | tf_op jit(solution)/shard_map/ppermute | solution.py:415
  11.8 4.2 %collective-permute-start.4 = (f32[8,8,128]{2,1,0:T(8,128)S(1)}, f32[8,8,128]{2,1,0:T(8,128)S(1)}, u32[]{:S(2)}, u32[]{:S(2)}) collective-permute-start(f32[8,8,128]{2,1,0:T(8,128)S(1)} %get-tuple-element.35), channel_id=1, source_target_pairs={{0,12},{4,8},{8,20},{12,16},{16,28},{20,24},{24,4},{28,0},{1,13},{... | collective-permute-start | bytes 98312 | tf_op jit(solution)/shard_map/ppermute | solution.py:415
  16.2 5.6 %collective-permute-start.5 = (f32[24,128]{1,0:T(8,128)S(1)}, f32[24,128]{1,0:T(8,128)S(1)}, u32[]{:S(2)}, u32[]{:S(2)}) collective-permute-start(f32[24,128]{1,0:T(8,128)S(1)} %get-tuple-element.38), channel_id=1, source_target_pairs={{0,1},{1,2},{2,3},{3,0},{4,5},{5,6},{6,7},{7,4},{8,9},{9,10},{10,1... | collective-permute-start | bytes 36872 | tf_op jit(solution)/shard_map/ppermute | solution.py:409
  17.8 4.0 %collective-permute-start.6 = (f32[24,128]{1,0:T(8,128)S(1)}, f32[24,128]{1,0:T(8,128)S(1)}, u32[]{:S(2)}, u32[]{:S(2)}) collective-permute-start(f32[24,128]{1,0:T(8,128)S(1)} %get-tuple-element.38), channel_id=1, source_target_pairs={{0,3},{1,0},{2,1},{3,2},{4,7},{5,4},{6,5},{7,6},{8,11},{9,8},{10,9... | collective-permute-start | bytes 36872 | tf_op jit(solution)/shard_map/ppermute | solution.py:409
  24.8 6.8 %collective-permute-start.7 = (f32[8,8,128]{2,1,0:T(8,128)S(1)}, f32[8,8,128]{2,1,0:T(8,128)S(1)}, u32[]{:S(2)}, u32[]{:S(2)}) collective-permute-start(f32[8,8,128]{2,1,0:T(8,128)S(1)} %get-tuple-element.41), channel_id=1, source_target_pairs={{0,4},{4,0},{1,5},{5,1},{2,6},{6,2},{3,7},{7,3},{8,12},{12,8},{9,1... | collective-permute-start | bytes 98312 | tf_op jit(solution)/shard_map/ppermute | solution.py:409
  26.3 5.3 %collective-permute-start.10 = (f32[4,8,128]{2,1,0:T(8,128)S(1)}, f32[4,8,128]{2,1,0:T(8,128)S(1)}, u32[]{:S(2)}, u32[]{:S(2)}) collective-permute-start(f32[4,8,128]{2,1,0:T(8,128)S(1)} %get-tuple-element.44), channel_id=1, source_target_pairs={{0,28},{4,24},{8,4},{12,0},{16,12},{20,8},{24,20},{28,16},{1,29},{... | collective-permute-start | bytes 49160 | tf_op jit(solution)/shard_map/ppermute | solution.py:415
  26.3 5.3 %collective-permute-start.8 = (f32[4,8,128]{2,1,0:T(8,128)S(1)}, f32[4,8,128]{2,1,0:T(8,128)S(1)}, u32[]{:S(2)}, u32[]{:S(2)}) collective-permute-start(f32[4,8,128]{2,1,0:T(8,128)S(1)} %get-tuple-element.42), channel_id=1, source_target_pairs={{0,24},{8,0},{16,8},{24,16},{1,25},{9,1},{17,9},{25,17},{2,26},{10... | collective-permute-start | bytes 49160 | tf_op jit(solution)/shard_map/ppermute | solution.py:409
  27.5 4.0 %collective-permute-start.11 = (f32[3,8,128]{2,1,0:T(8,128)S(1)}, f32[3,8,128]{2,1,0:T(8,128)S(1)}, u32[]{:S(2)}, u32[]{:S(2)}) collective-permute-start(f32[3,8,128]{2,1,0:T(8,128)S(1)} %get-tuple-element.45), channel_id=1, source_target_pairs={{0,12},{4,8},{8,20},{12,16},{16,28},{20,24},{24,4},{28,0},{1,13},{... | collective-permute-start | bytes 36872 | tf_op jit(solution)/shard_map/ppermute | solution.py:415
  28.1 3.5 %collective-permute-start.9 = (f32[3,8,128]{2,1,0:T(8,128)S(1)}, f32[3,8,128]{2,1,0:T(8,128)S(1)}, u32[]{:S(2)}, u32[]{:S(2)}) collective-permute-start(f32[3,8,128]{2,1,0:T(8,128)S(1)} %get-tuple-element.43), channel_id=1, source_target_pairs={{0,8},{8,16},{16,24},{24,0},{1,9},{9,17},{17,25},{25,1},{2,10},{10... | collective-permute-start | bytes 36872 | tf_op jit(solution)/shard_map/ppermute | solution.py:409
  31.7 16.5 %collective-permute-start.12 = (f32[16,128]{1,0:T(8,128)S(1)}, f32[16,128]{1,0:T(8,128)S(1)}, u32[]{:S(2)}, u32[]{:S(2)}) collective-permute-start(f32[16,128]{1,0:T(8,128)S(1)} %get-tuple-element.47), channel_id=1, source_target_pairs={{0,1},{1,2},{2,3},{3,0},{4,5},{5,6},{6,7},{7,4},{8,9},{9,10},{10,1... | collective-permute-start | bytes 24584 | tf_op jit(solution)/shard_map/ppermute | solution.py:409
  33.1 15.1 %collective-permute-start.13 = (f32[16,128]{1,0:T(8,128)S(1)}, f32[16,128]{1,0:T(8,128)S(1)}, u32[]{:S(2)}, u32[]{:S(2)}) collective-permute-start(f32[16,128]{1,0:T(8,128)S(1)} %get-tuple-element.47), channel_id=1, source_target_pairs={{0,3},{1,0},{2,1},{3,2},{4,7},{5,4},{6,5},{7,6},{8,11},{9,8},{10,9... | collective-permute-start | bytes 24584 | tf_op jit(solution)/shard_map/ppermute | solution.py:409
  41.1 7.2 %copy-start.6 = (f32[8,8,128]{2,1,0:T(8,128)S(1)}, f32[8,8,128]{2,1,0:T(8,128)}, u32[]{:S(2)}) copy-start(f32[8,8,128]{2,1,0:T(8,128)} %param.5) | copy-start | bytes 98308
  59.6 8.4 %collective-permute-start.14 = (f32[36,8,128]{2,1,0:T(8,128)S(1)}, f32[36,8,128]{2,1,0:T(8,128)S(1)}, u32[]{:S(2)}, u32[]{:S(2)}) collective-permute-start(f32[36,8,128]{2,1,0:T(8,128)S(1)} %get-tuple-element.52), channel_id=1, source_target_pairs={{0,4},{4,0},{1,5},{5,1},{2,6},{6,2},{3,7},{7,3},{8,12},{12,8},{9,1... | collective-permute-start | bytes 442376 | tf_op jit(solution)/shard_map/ppermute | solution.py:409
  61.0 7.0 %collective-permute-start.16 = (f32[20,8,128]{2,1,0:T(8,128)S(1)}, f32[20,8,128]{2,1,0:T(8,128)S(1)}, u32[]{:S(2)}, u32[]{:S(2)}) collective-permute-start(f32[20,8,128]{2,1,0:T(8,128)S(1)} %get-tuple-element.54), channel_id=1, source_target_pairs={{0,8},{8,16},{16,24},{24,0},{1,9},{9,17},{17,25},{25,1},{2,10},{10... | collective-permute-start | bytes 245768 | tf_op jit(solution)/shard_map/ppermute | solution.py:409
  61.0 7.0 %collective-permute-start.18 = (f32[20,8,128]{2,1,0:T(8,128)S(1)}, f32[20,8,128]{2,1,0:T(8,128)S(1)}, u32[]{:S(2)}, u32[]{:S(2)}) collective-permute-start(f32[20,8,128]{2,1,0:T(8,128)S(1)} %get-tuple-element.56), channel_id=1, source_target_pairs={{0,12},{4,8},{8,20},{12,16},{16,28},{20,24},{24,4},{28,0},{1,13},{... | collective-permute-start | bytes 245768 | tf_op jit(solution)/shard_map/ppermute | solution.py:415
  62.6 2.6 %collective-permute-start.15 = (f32[16,8,128]{2,1,0:T(8,128)S(1)}, f32[16,8,128]{2,1,0:T(8,128)S(1)}, u32[]{:S(2)}, u32[]{:S(2)}) collective-permute-start(f32[16,8,128]{2,1,0:T(8,128)S(1)} %get-tuple-element.53), channel_id=1, source_target_pairs={{0,24},{8,0},{16,8},{24,16},{1,25},{9,1},{17,9},{25,17},{2,26},{10... | collective-permute-start | bytes 196616 | tf_op jit(solution)/shard_map/ppermute | solution.py:409
  62.9 5.1 %collective-permute-start.17 = (f32[16,8,128]{2,1,0:T(8,128)S(1)}, f32[16,8,128]{2,1,0:T(8,128)S(1)}, u32[]{:S(2)}, u32[]{:S(2)}) collective-permute-start(f32[16,8,128]{2,1,0:T(8,128)S(1)} %get-tuple-element.55), channel_id=1, source_target_pairs={{0,28},{4,24},{8,4},{12,0},{16,12},{20,8},{24,20},{28,16},{1,29},{... | collective-permute-start | bytes 196616 | tf_op jit(solution)/shard_map/ppermute | solution.py:415
  68.2 5.6 %collective-permute-start.19 = (f32[32,128]{1,0:T(8,128)S(1)}, f32[32,128]{1,0:T(8,128)S(1)}, u32[]{:S(2)}, u32[]{:S(2)}) collective-permute-start(f32[32,128]{1,0:T(8,128)S(1)} %get-tuple-element.59), channel_id=1, source_target_pairs={{0,1},{1,2},{2,3},{3,0},{4,5},{5,6},{6,7},{7,4},{8,9},{9,10},{10,1... | collective-permute-start | bytes 49160 | tf_op jit(solution)/shard_map/ppermute | solution.py:409
  68.2 5.5 %collective-permute-start.20 = (f32[32,128]{1,0:T(8,128)S(1)}, f32[32,128]{1,0:T(8,128)S(1)}, u32[]{:S(2)}, u32[]{:S(2)}) collective-permute-start(f32[32,128]{1,0:T(8,128)S(1)} %get-tuple-element.59), channel_id=1, source_target_pairs={{0,3},{1,0},{2,1},{3,2},{4,7},{5,4},{6,5},{7,6},{8,11},{9,8},{10,9... | collective-permute-start | bytes 49160 | tf_op jit(solution)/shard_map/ppermute | solution.py:409
  (4 other events, 3.5 us)
where the time goes:
time: 74.8 us; the launch traced here: 74.5 us
  Pallas kernels  30.4 us (41%)
  starting transfers between devices  26.6 us (36%)
  waiting for transfers between devices  13.3 us (18%)
  local copies, waits for them, and re-layouts  3.51 us (5%)
    pallas_call x9, Pallas kernels, call(): pl.pallas_call(kernel, out_shape=[struct(s) for s in outs], in_specs=[in_...  30.4 us
    ppermute x15, starting transfers between devices, send(): return lax.ppermute(message, axes[0], pairs)  21.3 us
    ppermute x6, waiting for transfers between devices, send(): return lax.ppermute(message, axes, pairs)  7.35 us
    ppermute x15, waiting for transfers between devices, send(): return lax.ppermute(message, axes[0], pairs)  5.9 us
    ppermute x6, starting transfers between devices, send(): return lax.ppermute(message, axes, pairs)  5.32 us
    unnamed x14, local copies, waits for them, and re-layouts  3.51 us
  transfers between devices with their start and end apart: 21, of which 7 were waited for; matrix products, arithmetic and copies ran while one was open for 0% of the time, Pallas kernels for 17%

commit v1 on v0

v1 whole, which is shorter than its diff:
```python
import functools

import jax
import jax.numpy as jnp
from jax import lax
from jax.experimental import pallas as pl
from jax.experimental.pallas import tpu as pltpu
from jax.sharding import PartitionSpec as P

LO = 3
HI = 4
ROWS = 4
SHIFTS = 8
LANES = 128
PILES = 4
F32 = jnp.float32


def lane_of(rows):
    return lax.broadcasted_iota(jnp.int32, (rows, LANES), 1)


def group_of(rows):
    return ((lane_of(rows) + LO) & (LANES - 1)) >> 3


def low_lanes(rows):
    return (lane_of(rows) & 7) < HI


def cubic_weights(t):
    t2 = t * t
    t3 = t2 * t
    return (
        0.5 * (2.0 * t2 - t3 - t),
        0.5 * (3.0 * t3 - 5.0 * t2 + 2.0),
        0.5 * (4.0 * t2 - 3.0 * t3 + t),
        0.5 * (t3 - t2),
    )


def cubic_slopes(t):
    t2 = t * t
    return (
        0.5 * (4.0 * t - 3.0 * t2 - 1.0),
        0.5 * (9.0 * t2 - 10.0 * t),
        0.5 * (8.0 * t - 9.0 * t2 + 1.0),
        0.5 * (3.0 * t2 - 2.0 * t),
    )


def write_tables(cells, fracs, weights, slopes=None):
    def plane(x, carry):
        for c in range(3):
            k = cells[c, x]
            t = fracs[c, x]
            hits = {s: k == s for s in range(-2, 3)}
            for ref, taps in ((weights, cubic_weights), (slopes, cubic_slopes)):
                if ref is None:
                    continue
                values = taps(t)
                for j in range(SHIFTS):
                    entry = jnp.zeros_like(t)
                    for a in range(4):
                        s = j - 3 - (a - 1)
                        if -2 <= s <= 2:
                            entry = jnp.where(hits[s], values[a], entry)
                    ref[c, j, x] = entry
        return carry

    lax.fori_loop(0, cells.shape[1], plane, 0)


def shift_planes(extended, rim, shifted):
    planes, rows, _ = extended.shape
    lane = lane_of(rows)
    for X in range(planes):
        core = extended[X]
        ends = pltpu.roll(rim, (-8 * X) % LANES, 1)
        for j in range(SHIFTS):
            d = j - LO
            if d == 0:
                shifted[j, X] = core
            else:
                wraps = lane >= LANES + d if d < 0 else lane < d
                shifted[j, X] = pltpu.roll(jnp.where(wraps, ends, core), (-d) % LANES, 1)


def interpolate(shifted, weights, slopes, nx, ny, emit):
    def plane(x, carry):
        tz = [weights[2, j, x] for j in range(SHIFTS)]
        sz = None if slopes is None else [slopes[2, j, x] for j in range(SHIFTS)]

        def row(sy, sums):
            ty = weights[1, sy, x]
            a = b = c = None
            for sx in range(SHIFTS):
                window = [shifted[j, x + sx, pl.ds(sy + 1, ny), :] for j in range(SHIFTS)]
                column = total([tz[j] * window[j] for j in range(SHIFTS)])
                tx = weights[0, sx, x]
                a = plus(a, tx * column)
                if slopes is not None:
                    b = plus(b, slopes[0, sx, x] * column)
                    c = plus(c, tx * total([sz[j] * window[j] for j in range(SHIFTS)]))
            if slopes is None:
                return (sums[0] + ty * a,)
            return (sums[0] + ty * b, sums[1] + slopes[1, sy, x] * a, sums[2] + ty * c)

        zero = jnp.zeros((ny, LANES), F32)
        sums = lax.fori_loop(0, SHIFTS, row, (zero,) * (1 if slopes is None else 3))
        emit(x, sums)
        return carry

    lax.fori_loop(0, nx, plane, 0)


def total(terms):
    while len(terms) > 1:
        terms = [terms[i] + terms[i + 1] for i in range(0, len(terms), 2)]
    return terms[0]


def plus(a, b):
    return b if a is None else a + b


def deposit(sources, weights, scaled, piles):
    channels, nx, ny, _ = sources.shape
    planes = nx + LO + HI
    for pile in piles:
        pile[...] = jnp.zeros(pile.shape, F32)

    def scale(sy, carry):
        for x in range(nx):
            ty = weights[1, sy, x]
            for c in range(channels):
                scaled[c, sy, x] = sources[c, x] * ty
        return carry

    lax.fori_loop(0, SHIFTS, scale, 0)

    def row(sy, carry):
        for X in range(planes):
            sums = [[None] * SHIFTS for _ in range(channels)]
            for x in range(max(0, X - SHIFTS + 1), min(nx - 1, X) + 1):
                tx = weights[0, X - x, x]
                parts = [scaled[c, sy, x] * tx for c in range(channels)]
                for j in range(SHIFTS):
                    tz = weights[2, j, x]
                    for c in range(channels):
                        sums[c][j] = plus(sums[c][j], parts[c] * tz)
            for c in range(channels):
                for j in range(SHIFTS):
                    piles[X % PILES][c, j, X // PILES, pl.ds(sy + 1, ny), :] += sums[c][j]
        return carry

    lax.fori_loop(0, SHIFTS, row, 0)


def settle(piles, out, rims, base=None, base_rims=None):
    channels, planes, rows, _ = out.shape
    lane = lane_of(rows)
    group = group_of(rows)
    for c in range(channels):
        rim = jnp.zeros((rows, LANES), F32)
        for X in range(planes):
            pile = piles[X % PILES]
            core = pile[c, LO, X // PILES]
            ends = jnp.zeros((rows, LANES), F32)
            for j in range(SHIFTS):
                d = j - LO
                if d == 0:
                    continue
                moved = pltpu.roll(pile[c, j, X // PILES], d % LANES, 1)
                wraps = lane >= LANES + d if d < 0 else lane < d
                core = core + jnp.where(wraps, 0.0, moved)
                ends = ends + jnp.where(wraps, moved, 0.0)
            out[c, X] = core if base is None else core + base[c, X]
            rim = jnp.where(group == X, pltpu.roll(ends, (8 * X) % LANES, 1), rim)
        rims[c] = rim if base_rims is None else rim + base_rims[c]


def pack_rim(extended):
    planes, rows, _ = extended.shape
    group = group_of(rows)
    rim = jnp.zeros((rows, LANES), F32)
    for X in range(planes):
        rim = jnp.where(group == X, pltpu.roll(extended[X], (8 * X) % LANES, 1), rim)
    return rim


def unpack_rim(rim, X):
    lane = lane_of(rim.shape[0])
    return jnp.where((lane < HI) | (lane >= LANES - LO), pltpu.roll(rim, (-8 * X) % LANES, 1), 0.0)


def fold_rows(message, ny):
    if ny == 2 * ROWS:
        return pltpu.roll(message, ROWS, 0)
    below, above = message[:ROWS], message[ROWS:]
    if ny == ROWS:
        return below + above
    return jnp.concatenate([above, jnp.zeros((ny - 2 * ROWS, LANES), F32), below], axis=0)


def put_edges(out, at, plane, ny):
    if ny == 2 * ROWS:
        out[at] = plane
    else:
        out[at, 0:ROWS] = plane[0:ROWS]
        out[at, ROWS : 2 * ROWS] = plane[ny - ROWS : ny]


def put_rims(out, at, plane, ny):
    out[at, 0:ROWS] = plane[0:ROWS]
    out[at, ROWS : 2 * ROWS] = plane[ROWS + ny : 2 * ROWS + ny]


def place_edges(extended, X, core, edges, ny):
    extended[X, 0:ROWS] = edges[ROWS : 2 * ROWS]
    extended[X, ROWS : ROWS + ny] = core
    extended[X, ROWS + ny : 2 * ROWS + ny] = edges[0:ROWS]


def fill_planes(extended, middle, from_right, from_left, nx):
    rows = middle.shape[1]
    for x in range(nx):
        extended[LO + x] = middle[x]
    for i in range(HI):
        extended[LO + nx + i] = from_right[i * rows : (i + 1) * rows]
    for i in range(LO):
        extended[i] = from_left[i * rows : (i + 1) * rows]


def edge_planes(middle, to_left, to_right, nx):
    rows = middle.shape[1]
    for i in range(HI):
        to_left[i * rows : (i + 1) * rows] = middle[i]
    for i in range(LO):
        to_right[i * rows : (i + 1) * rows] = middle[nx - LO + i]


def first_kernel(
    nx, ny, intensity, cotangent, cells, fracs,
    image, to_y, own,
    cells_here, fracs_here, cotangent_here, sems, weights, scaled, piled, rims, *piles,
):
    copies = [
        pltpu.make_async_copy(source, target, sems.at[i])
        for i, (source, target) in enumerate(
            (
                (cells.at[1, 1], cells_here),
                (fracs.at[1, 1], fracs_here),
                (cotangent, cotangent_here),
                (intensity, image),
            )
        )
    ]
    for copy in copies:
        copy.start()
    for copy in copies:
        copy.wait()
    write_tables(cells_here, fracs_here, weights)
    deposit(cotangent_here, weights, scaled, piles)
    settle(piles, piled, rims)
    planes = nx + LO + HI
    for x in range(nx):
        put_edges(to_y, x, image[x], ny)
    for X in range(planes + 1):
        plane = piled[0, X] if X < planes else rims[0]
        put_rims(to_y, nx + X, plane, ny)
        own[X] = plane[ROWS : ROWS + ny]


def first_y_kernel(nx, ny, image, own, from_y, middle, part, to_left, to_right):
    planes = nx + LO + HI
    rows = ny + 2 * ROWS
    for x in range(nx):
        place_edges(middle, x, image[x], from_y[x], ny)
    for X in range(planes + 1):
        part[X] = own[X] + fold_rows(from_y[nx + X], ny)
    edge_planes(middle, to_left, to_right, nx)
    for i, X in enumerate(list(range(LO)) + [planes]):
        to_left[HI * rows + i * ny : HI * rows + (i + 1) * ny] = part[X]
    for i, X in enumerate(list(range(LO + nx, planes)) + [planes]):
        to_right[LO * rows + i * ny : LO * rows + (i + 1) * ny] = part[X]


def first_x_kernel(nx, ny, middle, part, from_right, from_left, extended, folded, rims):
    rows = ny + 2 * ROWS
    fill_planes(extended, middle, from_right, from_left, nx)
    rims[0:rows] = pack_rim(extended)

    def right(i):
        return from_right[HI * rows + i * ny : HI * rows + (i + 1) * ny]

    def left(i):
        return from_left[LO * rows + i * ny : LO * rows + (i + 1) * ny]

    for x in range(nx):
        plane = part[LO + x]
        if x >= nx - LO:
            plane = plane + right(x - (nx - LO))
        if x < HI:
            plane = plane + left(x)
        folded[x] = plane
    group = group_of(ny)
    turn = 8 * nx
    high = pltpu.roll(right(LO), turn % LANES, 1)
    low = pltpu.roll(left(HI), (-turn) % LANES, 1)
    rim = part[nx + LO + HI]
    rim = rim + jnp.where((group >= nx) & (group < nx + LO), high, 0.0)
    rims[rows : rows + ny] = rim + jnp.where((group >= LO) & (group < LO + HI), low, 0.0)


def middle_kernel(nx, ny, extended, rims_l, rims_r, folded, cells, fracs, image, to_y, shifted, adjoint, weights):
    rows = ny + 2 * ROWS
    rim = jnp.where(low_lanes(rows), rims_r[0:rows], rims_l[0:rows])
    shift_planes(extended, rim, shifted)
    write_tables(cells.at[0, 1], fracs.at[0, 1], weights)

    def emit(x, sums):
        image[x] = sums[0]

    interpolate(shifted, weights, None, nx, ny, emit)
    for x in range(nx):
        put_edges(to_y, x, image[x], ny)
    back = jnp.where(low_lanes(ny), rims_l[rows : rows + ny], rims_r[rows : rows + ny])
    for x in range(nx):
        adjoint[0, x] = folded[x] + unpack_rim(back, LO + x)


def adjoint_kernel(nx, ny, adjoint, cells, fracs, piled, rims, weights, scaled, *piles):
    write_tables(cells.at[0, 1], fracs.at[0, 1], weights)
    deposit(adjoint, weights, scaled, piles)
    settle(piles, piled, rims)


def early_grad_kernel(nx, ny, shifted, adjoint, cells, fracs, grad, weights, slopes):
    write_tables(cells.at[0, 1], fracs.at[0, 1], weights, slopes)

    def emit(x, sums):
        for c in range(3):
            grad[c, x] = adjoint[0, x] * sums[c]

    interpolate(shifted, weights, slopes, nx, ny, emit)


def early_spread_kernel(nx, ny, grad, cells, fracs, piled, rims, weights, scaled, *piles):
    write_tables(cells.at[0, 0], fracs.at[0, 0], weights)
    deposit(grad, weights, scaled, piles)
    settle(piles, piled, rims)


def second_y_kernel(nx, ny, image, from_y, earlier, middle, to_left, to_right):
    for x in range(nx):
        place_edges(middle, x, image[x], from_y[x], ny)
    edge_planes(middle, to_left, to_right, nx)


def second_x_kernel(nx, ny, middle, from_right, from_left, earlier, extended, rims):
    fill_planes(extended, middle, from_right, from_left, nx)
    rims[...] = pack_rim(extended)


def late_kernel(
    nx, ny, extended, rims_l, rims_r, cotangent, cells, fracs, early, early_rims, adjoint_rims,
    piled, rims,
    shifted, weights, slopes, grad, scaled, rims_here, *piles,
):
    rows = ny + 2 * ROWS
    shift_planes(extended, jnp.where(low_lanes(rows), rims_r[...], rims_l[...]), shifted)
    write_tables(cells.at[1, 1], fracs.at[1, 1], weights, slopes)

    def emit(x, sums):
        for c in range(3):
            grad[c, x] = cotangent[0, x] * sums[c]

    interpolate(shifted, weights, slopes, nx, ny, emit)
    write_tables(cells.at[1, 0], fracs.at[1, 0], weights)
    deposit(grad, weights, scaled, piles)
    settle(piles, piled, rims_here, early, early_rims)
    for c in range(3):
        rims[c * rows : (c + 1) * rows] = rims_here[c]
    rims[3 * rows : 4 * rows] = adjoint_rims[0]


def last_z_kernel(nx, ny, velocity, adjoint, rims_l, rims_r, to_left, to_right, own):
    rows = ny + 2 * ROWS
    low = low_lanes(rows)
    for c in range(4):
        back = jnp.where(low, rims_l[c * rows : (c + 1) * rows], rims_r[c * rows : (c + 1) * rows])
        for X in range(nx + LO + HI):
            plane = (velocity[c, X] if c < 3 else adjoint[0, X]) + unpack_rim(back, X)
            if X < LO:
                i = c * LO + X
                to_left[i * rows : (i + 1) * rows] = plane
            elif X < LO + nx:
                own[c * nx + X - LO] = plane
            else:
                i = c * HI + X - LO - nx
                to_right[i * rows : (i + 1) * rows] = plane


def last_x_kernel(nx, ny, own, from_right, from_left, to_y, part):
    rows = ny + 2 * ROWS
    for c in range(4):
        for x in range(nx):
            plane = own[c * nx + x]
            if x >= nx - LO:
                i = c * LO + x - (nx - LO)
                plane = plane + from_right[i * rows : (i + 1) * rows]
            if x < HI:
                i = c * HI + x
                plane = plane + from_left[i * rows : (i + 1) * rows]
            put_rims(to_y, c * nx + x, plane, ny)
            part[c * nx + x] = plane[ROWS : ROWS + ny]


def last_y_kernel(nx, ny, part, from_y, intensity_adjoint, velocity_adjoint):
    for c in range(4):
        for x in range(nx):
            plane = part[c * nx + x] + fold_rows(from_y[c * nx + x], ny)
            if c == 3:
                intensity_adjoint[x] = plane
            else:
                velocity_adjoint[c, x] = plane


def call(kernel, args, outs, scratch, flops, spaces=None):
    def struct(shape):
        return jax.ShapeDtypeStruct(shape, F32)

    in_vmem = pl.BlockSpec(memory_space=pltpu.VMEM)
    in_specs = [in_vmem] * len(args)
    for i, space in (spaces or {}).items():
        in_specs[i] = pl.BlockSpec(memory_space=space)
    moved = 4 * sum(a.size for a in args)
    return pl.pallas_call(
        kernel,
        out_shape=[struct(s) for s in outs],
        in_specs=in_specs,
        out_specs=[in_vmem] * len(outs),
        scratch_shapes=[pltpu.VMEM(s, F32) if isinstance(s, tuple) else s for s in scratch],
        compiler_params=pltpu.CompilerParams(vmem_limit_bytes=24 * 1024 * 1024),
        cost_estimate=pl.CostEstimate(flops=flops, bytes_accessed=moved, transcendentals=0),
    )(*args)


def send(message, axis, move):
    size = lax.axis_size(axis)
    return lax.ppermute(message, axis, [(i, (i + move) % size) for i in range(size)])


def send_y(message):
    if lax.axis_size("gy") == 2:
        return send(message, "gy", 1)
    down = send(message[:, :ROWS], "gy", -1)
    up = send(message[:, ROWS:], "gy", 1)
    return jnp.concatenate([down, up], axis=1)


def send_x(to_left, to_right):
    return send(to_left, "gx", -1), send(to_right, "gx", 1)


def send_z(rims):
    return send(rims, "gz", 1), send(rims, "gz", -1)


def body(intensity, cotangent, cells, fracs):
    nx, ny, nz = intensity.shape
    rows = ny + 2 * ROWS
    planes = nx + LO + HI
    ring = 2 * ROWS
    table = (3, SHIFTS, nx, ny, nz)
    cotangent = cotangent[None]
    unit = nx * ny * nz * 512

    def run(kernel, *rest, **more):
        return call(functools.partial(kernel, nx, ny), *rest, **more)

    def piles(channels):
        return [(channels, SHIFTS, -(-planes // PILES), rows, nz)] * PILES

    def scaled(channels):
        return (channels, SHIFTS, nx, ny, nz)

    def piled(channels):
        return [(channels, planes, rows, nz), (channels, rows, nz)]

    part = (3, nx, ny, nz)
    image, to_y, own = run(
        first_kernel,
        (intensity, cotangent, cells, fracs),
        [(nx, ny, nz), (nx + planes + 1, ring, nz), (planes + 1, ny, nz)],
        [
            pltpu.VMEM(part, jnp.int32),
            part,
            (1, nx, ny, nz),
            pltpu.SemaphoreType.DMA((4,)),
            table,
            scaled(1),
        ]
        + piled(1)
        + piles(1),
        2 * unit,
        spaces=dict.fromkeys(range(4), pltpu.HBM),
    )
    middle, part, *to_x = run(
        first_y_kernel,
        (image, own, send_y(to_y)),
        [
            (nx, rows, nz),
            (planes + 1, ny, nz),
            (HI * rows + (LO + 1) * ny, nz),
            (LO * rows + (HI + 1) * ny, nz),
        ],
        [],
        unit // 32,
    )
    extended, folded, rims = run(
        first_x_kernel,
        (middle, part) + send_x(*to_x),
        [(planes, rows, nz), (nx, ny, nz), (rows + ny, nz)],
        [],
        unit // 32,
    )
    image, to_y, shifted, adjoint = run(
        middle_kernel,
        (extended,) + send_z(rims) + (folded, cells, fracs),
        [(nx, ny, nz), (nx, ring, nz), (SHIFTS, planes, rows, nz), (1, nx, ny, nz)],
        [table],
        2 * unit,
    )

    from_y = send_y(to_y)
    piled_adjoint, adjoint_rims = run(
        adjoint_kernel,
        (adjoint, cells, fracs),
        piled(1),
        [table, scaled(1)] + piles(1),
        2 * unit,
    )
    middle, *to_x = run(
        second_y_kernel,
        (image, from_y, piled_adjoint),
        [(nx, rows, nz), (HI * rows, nz), (LO * rows, nz)],
        [],
        unit // 32,
        spaces={2: pl.ANY},
    )
    from_right, from_left = send_x(*to_x)
    (grad,) = run(
        early_grad_kernel,
        (shifted, adjoint, cells, fracs),
        [(3, nx, ny, nz)],
        [table, table],
        5 * unit,
    )
    extended, rims = run(
        second_x_kernel,
        (middle, from_right, from_left, grad),
        [(planes, rows, nz), (rows, nz)],
        [],
        unit // 32,
        spaces={3: pl.ANY},
    )
    rims_l, rims_r = send_z(rims)
    early, early_rims = run(
        early_spread_kernel,
        (grad, cells, fracs),
        piled(3),
        [table, scaled(3)] + piles(3),
        6 * unit,
    )

    velocity, rims = run(
        late_kernel,
        (extended, rims_l, rims_r, cotangent, cells, fracs, early, early_rims, adjoint_rims),
        [(3, planes, rows, nz), (4 * rows, nz)],
        [(SHIFTS, planes, rows, nz), table, table, (3, nx, ny, nz), scaled(3), (3, rows, nz)] + piles(3),
        11 * unit,
    )
    *to_x, own = run(
        last_z_kernel,
        (velocity, piled_adjoint) + send_z(rims),
        [(4 * LO * rows, nz), (4 * HI * rows, nz), (4 * nx, rows, nz)],
        [],
        unit // 32,
    )
    to_y, part = run(
        last_x_kernel,
        (own,) + send_x(*to_x),
        [(4 * nx, ring, nz), (4 * nx, ny, nz)],
        [],
        unit // 32,
    )
    return tuple(
        run(
            last_y_kernel,
            (part, send_y(to_y)),
            [(nx, ny, nz), (3, nx, ny, nz)],
            [],
            unit // 32,
        )
    )


def solution(mesh):
    in_specs = (
        P("gx", "gy", "gz"),
        P("gx", "gy", "gz"),
        P(None, None, None, "gx", "gy", "gz"),
        P(None, None, None, "gx", "gy", "gz"),
    )
    out_specs = (P("gx", "gy", "gz"), P(None, "gx", "gy", "gz"))
    return jax.shard_map(body, mesh=mesh, in_specs=in_specs, out_specs=out_specs, check_vma=False)
```

time: 74.8 us -> 79 us (1.056)
  waiting for transfers between devices: 13.3 us -> 24.7 us
  starting transfers between devices: 26.6 us -> 17.2 us
  Pallas kernels: 30.4 us -> 32.5 us
    ppermute x21 -> x15, waiting for transfers between devices: 13.3 us -> 24.7 us  [send(): lax.ppermute(message, axis, [(i, (i + move) % size) for i in range(size)])]
    ppermute x21 -> x15, starting transfers between devices: 26.6 us -> 17.2 us  [send(): lax.ppermute(message, axis, [(i, (i + move) % size) for i in range(size)])]
    pallas_call x9 -> x13, Pallas kernels: 30.4 us -> 32.5 us  [call(): pl.pallas_call(kernel, out_shape=[struct(s) for s in outs], in_specs=in_s...]
  transfers between devices with their start and end apart: 21 -> 15, of which waited for: 7 -> 9; matrix products, arithmetic and copies ran while one was open for 0% -> 0% of each run, Pallas kernels for 17% -> 17%
where the time goes in v1:
time: 79 us; the launch traced here: 78.7 us
  Pallas kernels  32.5 us (41%)
  waiting for transfers between devices  24.7 us (31%)
  starting transfers between devices  17.2 us (22%)
  local copies, waits for them, and re-layouts  3.52 us (4%)
  between operations  0.79 us (1%)
    pallas_call x13, Pallas kernels, call(): pl.pallas_call(kernel, out_shape=[struct(s) for s in outs], in_specs=in_s...  32.5 us
    ppermute x15, waiting for transfers between devices, send(): lax.ppermute(message, axis, [(i, (i + move) % size) for i in range(size)])  24.7 us
    ppermute x15, starting transfers between devices, send(): lax.ppermute(message, axis, [(i, (i + move) % size) for i in range(size)])  17.2 us
    unnamed x14, local copies, waits for them, and re-layouts  3.52 us
  transfers between devices with their start and end apart: 15, of which 9 were waited for; matrix products, arithmetic and copies ran while one was open for 0% of the time, Pallas kernels for 17%

profile of v1, /device:TPU:0, one launch (start us, length us, event | category | flops | bytes accessed | tf_op | source)
XLA Modules:
  0.0 78.7 jit_solution(12923669287006802884)
XLA Ops:
  0.6 1.0 %copy-done = s32[2,2,3,8,8,128]{5,4,3,2,1,0:T(8,128)S(1)} copy-done((s32[2,2,3,8,8,128]{5,4,3,2,1,0:T(8,128)S(1)}, s32[2,2,3,8,8,128]{5,4,3,2,1,0:T(8,128)}, u32[]{:S(2)}) %copy-start) | copy-done | bytes 393240
  1.6 1.0 %copy-done.2 = f32[2,2,3,8,8,128]{5,4,3,2,1,0:T(8,128)S(1)} copy-done((f32[2,2,3,8,8,128]{5,4,3,2,1,0:T(8,128)S(1)}, f32[2,2,3,8,8,128]{5,4,3,2,1,0:T(8,128)}, u32[]{:S(2)}) %copy-start.2) | copy-done | bytes 393240
  2.6 0.8 copy-done.4
  4.1 2.8 %shard_map.59 = (f32[8,8,128]{2,1,0:T(8,128)S(1)}, f32[24,8,128]{2,1,0:T(8,128)S(1)}, f32[16,8,128]{2,1,0:T(8,128)S(1)}) custom-call(f32[8,8,128]{2,1,0:T(8,128)S(1)} %copy-done.6, f32[1,8,8,128]{3,2,1,0:T(8,128)S(1)} %bitcast.1, s32[2,2,3,8,8,128]{5,4,3,2,1,0:T(8,128)S(1)} %copy-done, f32[2,2,3,8,8,128]{5,4,3,2,1,0:T(8,128)S(1)} %copy-done.2), custom_call_target="tpu_custom_call" | custom-call | flops 8388608 | bytes 851968 | tf_op jit(solution)/shard_map/pallas_call | solution.py:439
  7.0 3.0 %collective-permute-start = (f32[24,8,128]{2,1,0:T(8,128)S(1)}, f32[24,8,128]{2,1,0:T(8,128)S(1)}, u32[]{:S(2)}, u32[]{:S(2)}) collective-permute-start(f32[24,8,128]{2,1,0:T(8,128)S(1)} %get-tuple-element.34), channel_id=1, source_target_pairs={{0,4},{4,0},{1,5},{5,1},{2,6},{6,2},{3,7},{7,3},{8,12},{12,8},{9,1... | collective-permute-start | bytes 294920 | tf_op jit(solution)/shard_map/ppermute | solution.py:452
  10.0 2.8 %collective-permute-done.from_y = f32[24,8,128]{2,1,0:T(8,128)S(1)} collective-permute-done((f32[24,8,128]{2,1,0:T(8,128)S(1)}, f32[24,8,128]{2,1,0:T(8,128)S(1)}, u32[]{:S(2)}, u32[]{:S(2)}) %collective-permute-start) | collective-permute-done | bytes 98336 | tf_op jit(solution)/shard_map/ppermute | solution.py:452
  13.4 3.4 %collective-permute-done.2.from_left = f32[88,128]{1,0:T(8,128)S(1)} collective-permute-done((f32[88,128]{1,0:T(8,128)S(1)}, f32[88,128]{1,0:T(8,128)S(1)}, u32[]{:S(2)}, u32[]{:S(2)}) %collective-permute-start.2) | collective-permute-done | bytes 45088 | tf_op jit(solution)/shard_map/ppermute | solution.py:452
  16.9 4.0 %collective-permute-start.4 = (f32[24,128]{1,0:T(8,128)S(1)}, f32[24,128]{1,0:T(8,128)S(1)}, u32[]{:S(2)}, u32[]{:S(2)}) collective-permute-start(f32[24,128]{1,0:T(8,128)S(1)} %get-tuple-element.40), channel_id=1, source_target_pairs={{0,3},{1,0},{2,1},{3,2},{4,7},{5,4},{6,5},{7,6},{8,11},{9,8},{10,9... | collective-permute-start | bytes 36872 | tf_op jit(solution)/shard_map/ppermute | solution.py:452
  20.9 1.4 %collective-permute-done.4.rims_r = f32[24,128]{1,0:T(8,128)S(1)} collective-permute-done((f32[24,128]{1,0:T(8,128)S(1)}, f32[24,128]{1,0:T(8,128)S(1)}, u32[]{:S(2)}, u32[]{:S(2)}) %collective-permute-start.4) | collective-permute-done | bytes 12320 | tf_op jit(solution)/shard_map/ppermute | solution.py:452
  22.3 4.1 %collective-permute-done.3.rims_l = f32[24,128]{1,0:T(8,128)S(1)} collective-permute-done((f32[24,128]{1,0:T(8,128)S(1)}, f32[24,128]{1,0:T(8,128)S(1)}, u32[]{:S(2)}, u32[]{:S(2)}) %collective-permute-start.3) | collective-permute-done | bytes 12320 | tf_op jit(solution)/shard_map/ppermute | solution.py:452
  26.4 3.1 %shard_map.62 = (f32[8,8,128]{2,1,0:T(8,128)S(1)}, f32[8,8,128]{2,1,0:T(8,128)S(1)}, f32[8,15,16,128]{3,2,1,0:T(8,128)S(1)}, f32[1,8,8,128]{3,2,1,0:T(8,128)S(1)}) custom-call(f32[15,16,128]{2,1,0:T(8,128)S(1)} %get-tuple-element.39.extended, f32[24,128]{1,0:T(8,128)S(1)} %collective-permute-done.3.rims_l, f32[24,128]{1,0:T(8,128)S(1)} %collective-permute-done.4.rims_r, ...), custom_call_target="tpu_custom_call" | custom-call | flops 8388608 | bytes 966656 | tf_op jit(solution)/shard_map/pallas_call | solution.py:439
  29.5 1.5 %collective-permute-start.5 = (f32[8,8,128]{2,1,0:T(8,128)S(1)}, f32[8,8,128]{2,1,0:T(8,128)S(1)}, u32[]{:S(2)}, u32[]{:S(2)}) collective-permute-start(f32[8,8,128]{2,1,0:T(8,128)S(1)} %get-tuple-element.43), channel_id=1, source_target_pairs={{0,4},{4,0},{1,5},{5,1},{2,6},{6,2},{3,7},{7,3},{8,12},{12,8},{9,1... | collective-permute-start | bytes 98312 | tf_op jit(solution)/shard_map/ppermute | solution.py:452
  31.0 2.4 %shard_map.63 = (f32[1,15,16,128]{3,2,1,0:T(8,128)S(1)}, f32[1,16,128]{2,1,0:T(8,128)S(1)}) custom-call(f32[1,8,8,128]{3,2,1,0:T(8,128)S(1)} %get-tuple-element.44.adjoint, s32[2,2,3,8,8,128]{5,4,3,2,1,0:T(8,128)S(1)} %copy-done.1, f32[2,2,3,8,8,128]{5,4,3,2,1,0:T(8,128)S(1)} %copy-done.3), custom_call_target="tpu_custom_call" | custom-call | flops 8388608 | bytes 819200 | tf_op jit(solution)/shard_map/pallas_call | solution.py:439
  34.1 3.3 %shard_map.65.earlier.grad = f32[3,8,8,128]{3,2,1,0:T(8,128)S(1)} custom-call(f32[8,15,16,128]{3,2,1,0:T(8,128)S(1)} %get-tuple-element.49.shifted, f32[1,8,8,128]{3,2,1,0:T(8,128)S(1)} %get-tuple-element.44.adjoint, s32[2,2,3,8,8,128]{5,4,3,2,1,0:T(8,128)S(1)} %copy-done.1, f32[2,2,3,8,8,128]{5,4,3,2,1,0:T(8,128)S(1)} %copy-done.3), custom_call_target="tpu_custom_call" | custom-call | flops 20971520 | bytes 1802240 | tf_op jit(solution)/shard_map/pallas_call | solution.py:439
  37.6 2.0 %collective-permute-start.8 = (f32[16,128]{1,0:T(8,128)S(1)}, f32[16,128]{1,0:T(8,128)S(1)}, u32[]{:S(2)}, u32[]{:S(2)}) collective-permute-start(f32[16,128]{1,0:T(8,128)S(1)} %get-tuple-element.51), channel_id=1, source_target_pairs={{0,1},{1,2},{2,3},{3,0},{4,5},{5,6},{6,7},{7,4},{8,9},{9,10},{10,1... | collective-permute-start | bytes 24584 | tf_op jit(solution)/shard_map/ppermute | solution.py:452
  39.6 7.8 %shard_map.67 = (f32[3,15,16,128]{3,2,1,0:T(8,128)S(1)}, f32[3,16,128]{2,1,0:T(8,128)S(1)}) custom-call(f32[3,8,8,128]{3,2,1,0:T(8,128)S(1)} %shard_map.65.earlier.grad, s32[2,2,3,8,8,128]{5,4,3,2,1,0:T(8,128)S(1)} %copy-done.1, f32[2,2,3,8,8,128]{5,4,3,2,1,0:T(8,128)S(1)} %copy-done.3), custom_call_target="tpu_custom_call" | custom-call | flops 25165824 | bytes 884736 | tf_op jit(solution)/shard_map/pallas_call | solution.py:439
  47.4 12.0 %shard_map.68 = (f32[3,15,16,128]{3,2,1,0:T(8,128)S(1)}, f32[64,128]{1,0:T(8,128)S(1)}) custom-call(f32[15,16,128]{2,1,0:T(8,128)S(1)} %get-tuple-element.50.extended, f32[16,128]{1,0:T(8,128)S(1)} %collective-permute-done.8.rims_l, f32[16,128]{1,0:T(8,128)S(1)} %collective-permute-done.9.rims_r, f32[1,8,8,128]{3,2,1,0:T(8,128)S(1)} %bitcast.2, ...), custom_call_target="tpu_custom_call" | custom-call | flops 46137344 | bytes 1359872 | tf_op jit(solution)/shard_map/pallas_call | solution.py:439
  59.4 1.9 %collective-permute-start.11 = (f32[64,128]{1,0:T(8,128)S(1)}, f32[64,128]{1,0:T(8,128)S(1)}, u32[]{:S(2)}, u32[]{:S(2)}) collective-permute-start(f32[64,128]{1,0:T(8,128)S(1)} %get-tuple-element.56), channel_id=1, source_target_pairs={{0,3},{1,0},{2,1},{3,2},{4,7},{5,4},{6,5},{7,6},{8,11},{9,8},{10,9... | collective-permute-start | bytes 98312 | tf_op jit(solution)/shard_map/ppermute | solution.py:452
  61.5 1.9 %collective-permute-done.11.rims_r = f32[64,128]{1,0:T(8,128)S(1)} collective-permute-done((f32[64,128]{1,0:T(8,128)S(1)}, f32[64,128]{1,0:T(8,128)S(1)}, u32[]{:S(2)}, u32[]{:S(2)}) %collective-permute-start.11) | collective-permute-done | bytes 32800 | tf_op jit(solution)/shard_map/ppermute | solution.py:452
  63.4 3.7 %collective-permute-done.10.rims_l = f32[64,128]{1,0:T(8,128)S(1)} collective-permute-done((f32[64,128]{1,0:T(8,128)S(1)}, f32[64,128]{1,0:T(8,128)S(1)}, u32[]{:S(2)}, u32[]{:S(2)}) %collective-permute-start.10) | collective-permute-done | bytes 32800 | tf_op jit(solution)/shard_map/ppermute | solution.py:452
  67.3 1.7 %collective-permute-start.12 = (f32[192,128]{1,0:T(8,128)S(1)}, f32[192,128]{1,0:T(8,128)S(1)}, u32[]{:S(2)}, u32[]{:S(2)}) collective-permute-start(f32[192,128]{1,0:T(8,128)S(1)} %get-tuple-element.58), channel_id=1, source_target_pairs={{0,24},{8,0},{16,8},{24,16},{1,25},{9,1},{17,9},{25,17},{2,26},{10... | collective-permute-start | bytes 294920 | tf_op jit(solution)/shard_map/ppermute | solution.py:452
  69.0 2.2 %collective-permute-done.12.from_right = f32[192,128]{1,0:T(8,128)S(1)} collective-permute-done((f32[192,128]{1,0:T(8,128)S(1)}, f32[192,128]{1,0:T(8,128)S(1)}, u32[]{:S(2)}, u32[]{:S(2)}) %collective-permute-start.12) | collective-permute-done | bytes 98336 | tf_op jit(solution)/shard_map/ppermute | solution.py:452
  71.8 1.5 %collective-permute-start.14 = (f32[32,8,128]{2,1,0:T(8,128)S(1)}, f32[32,8,128]{2,1,0:T(8,128)S(1)}, u32[]{:S(2)}, u32[]{:S(2)}) collective-permute-start(f32[32,8,128]{2,1,0:T(8,128)S(1)} %get-tuple-element.61), channel_id=1, source_target_pairs={{0,4},{4,0},{1,5},{5,1},{2,6},{6,2},{3,7},{7,3},{8,12},{12,8},{9,1... | collective-permute-start | bytes 393224 | tf_op jit(solution)/shard_map/ppermute | solution.py:452
  73.3 4.8 %collective-permute-done.14.from_y = f32[32,8,128]{2,1,0:T(8,128)S(1)} collective-permute-done((f32[32,8,128]{2,1,0:T(8,128)S(1)}, f32[32,8,128]{2,1,0:T(8,128)S(1)}, u32[]{:S(2)}, u32[]{:S(2)}) %collective-permute-start.14) | collective-permute-done | bytes 131104 | tf_op jit(solution)/shard_map/ppermute | solution.py:452
  (33 shorter events, 3.8 us)
Async XLA Ops:
  0.6 1.0 %copy-start = (s32[2,2,3,8,8,128]{5,4,3,2,1,0:T(8,128)S(1)}, s32[2,2,3,8,8,128]{5,4,3,2,1,0:T(8,128)}, u32[]{:S(2)}) copy-start(s32[2,2,3,8,8,128]{5,4,3,2,1,0:T(8,128)} %cells.11) | copy-start | bytes 1179652
  1.6 1.0 %copy-start.2 = (f32[2,2,3,8,8,128]{5,4,3,2,1,0:T(8,128)S(1)}, f32[2,2,3,8,8,128]{5,4,3,2,1,0:T(8,128)}, u32[]{:S(2)}) copy-start(f32[2,2,3,8,8,128]{5,4,3,2,1,0:T(8,128)} %fracs.11) | copy-start | bytes 1179652
  2.6 0.8 copy-start.4
  3.4 0.8 copy-start.6
  4.1 22.3 %copy-start.3 = (f32[2,2,3,8,8,128]{5,4,3,2,1,0:T(8,128)S(1)}, f32[2,2,3,8,8,128]{5,4,3,2,1,0:T(8,128)}, u32[]{:S(2)}) copy-start(f32[2,2,3,8,8,128]{5,4,3,2,1,0:T(8,128)} %fracs.11) | copy-start | bytes 1179652
  6.9 19.5 %copy-start.1 = (s32[2,2,3,8,8,128]{5,4,3,2,1,0:T(8,128)S(1)}, s32[2,2,3,8,8,128]{5,4,3,2,1,0:T(8,128)}, u32[]{:S(2)}) copy-start(s32[2,2,3,8,8,128]{5,4,3,2,1,0:T(8,128)} %cells.11) | copy-start | bytes 1179652
  7.0 5.8 %collective-permute-start = (f32[24,8,128]{2,1,0:T(8,128)S(1)}, f32[24,8,128]{2,1,0:T(8,128)S(1)}, u32[]{:S(2)}, u32[]{:S(2)}) collective-permute-start(f32[24,8,128]{2,1,0:T(8,128)S(1)} %get-tuple-element.34), channel_id=1, source_target_pairs={{0,4},{4,0},{1,5},{5,1},{2,6},{6,2},{3,7},{7,3},{8,12},{12,8},{9,1... | collective-permute-start | bytes 294920 | tf_op jit(solution)/shard_map/ppermute | solution.py:452
  12.8 4.0 %collective-permute-start.1 = (f32[96,128]{1,0:T(8,128)S(1)}, f32[96,128]{1,0:T(8,128)S(1)}, u32[]{:S(2)}, u32[]{:S(2)}) collective-permute-start(f32[96,128]{1,0:T(8,128)S(1)} %get-tuple-element.37), channel_id=1, source_target_pairs={{0,24},{8,0},{16,8},{24,16},{1,25},{9,1},{17,9},{25,17},{2,26},{10... | collective-permute-start | bytes 147464 | tf_op jit(solution)/shard_map/ppermute | solution.py:452
  12.9 3.8 %collective-permute-start.2 = (f32[88,128]{1,0:T(8,128)S(1)}, f32[88,128]{1,0:T(8,128)S(1)}, u32[]{:S(2)}, u32[]{:S(2)}) collective-permute-start(f32[88,128]{1,0:T(8,128)S(1)} %get-tuple-element.38), channel_id=1, source_target_pairs={{0,8},{8,16},{16,24},{24,0},{1,9},{9,17},{17,25},{25,1},{2,10},{10... | collective-permute-start | bytes 135176 | tf_op jit(solution)/shard_map/ppermute | solution.py:452
  16.9 5.4 %collective-permute-start.4 = (f32[24,128]{1,0:T(8,128)S(1)}, f32[24,128]{1,0:T(8,128)S(1)}, u32[]{:S(2)}, u32[]{:S(2)}) collective-permute-start(f32[24,128]{1,0:T(8,128)S(1)} %get-tuple-element.40), channel_id=1, source_target_pairs={{0,3},{1,0},{2,1},{3,2},{4,7},{5,4},{6,5},{7,6},{8,11},{9,8},{10,9... | collective-permute-start | bytes 36872 | tf_op jit(solution)/shard_map/ppermute | solution.py:452
  20.9 5.5 %collective-permute-start.3 = (f32[24,128]{1,0:T(8,128)S(1)}, f32[24,128]{1,0:T(8,128)S(1)}, u32[]{:S(2)}, u32[]{:S(2)}) collective-permute-start(f32[24,128]{1,0:T(8,128)S(1)} %get-tuple-element.40), channel_id=1, source_target_pairs={{0,1},{1,2},{2,3},{3,0},{4,5},{5,6},{6,7},{7,4},{8,9},{9,10},{10,1... | collective-permute-start | bytes 36872 | tf_op jit(solution)/shard_map/ppermute | solution.py:452
  29.5 4.0 %collective-permute-start.5 = (f32[8,8,128]{2,1,0:T(8,128)S(1)}, f32[8,8,128]{2,1,0:T(8,128)S(1)}, u32[]{:S(2)}, u32[]{:S(2)}) collective-permute-start(f32[8,8,128]{2,1,0:T(8,128)S(1)} %get-tuple-element.43), channel_id=1, source_target_pairs={{0,4},{4,0},{1,5},{5,1},{2,6},{6,2},{3,7},{7,3},{8,12},{12,8},{9,1... | collective-permute-start | bytes 98312 | tf_op jit(solution)/shard_map/ppermute | solution.py:452
  33.5 3.9 %collective-permute-start.6 = (f32[64,128]{1,0:T(8,128)S(1)}, f32[64,128]{1,0:T(8,128)S(1)}, u32[]{:S(2)}, u32[]{:S(2)}) collective-permute-start(f32[64,128]{1,0:T(8,128)S(1)} %get-tuple-element.47), channel_id=1, source_target_pairs={{0,24},{8,0},{16,8},{24,16},{1,25},{9,1},{17,9},{25,17},{2,26},{10... | collective-permute-start | bytes 98312 | tf_op jit(solution)/shard_map/ppermute | solution.py:452
  33.6 3.8 %collective-permute-start.7 = (f32[48,128]{1,0:T(8,128)S(1)}, f32[48,128]{1,0:T(8,128)S(1)}, u32[]{:S(2)}, u32[]{:S(2)}) collective-permute-start(f32[48,128]{1,0:T(8,128)S(1)} %get-tuple-element.48), channel_id=1, source_target_pairs={{0,8},{8,16},{16,24},{24,0},{1,9},{9,17},{17,25},{25,1},{2,10},{10... | collective-permute-start | bytes 73736 | tf_op jit(solution)/shard_map/ppermute | solution.py:452
  37.5 9.9 %copy-start.5 = (f32[8,8,128]{2,1,0:T(8,128)S(1)}, f32[8,8,128]{2,1,0:T(8,128)}, u32[]{:S(2)}) copy-start(f32[8,8,128]{2,1,0:T(8,128)} %param.5) | copy-start | bytes 98308
  37.5 9.9 %collective-permute-start.9 = (f32[16,128]{1,0:T(8,128)S(1)}, f32[16,128]{1,0:T(8,128)S(1)}, u32[]{:S(2)}, u32[]{:S(2)}) collective-permute-start(f32[16,128]{1,0:T(8,128)S(1)} %get-tuple-element.51), channel_id=1, source_target_pairs={{0,3},{1,0},{2,1},{3,2},{4,7},{5,4},{6,5},{7,6},{8,11},{9,8},{10,9... | collective-permute-start | bytes 24584 | tf_op jit(solution)/shard_map/ppermute | solution.py:452
  37.6 9.8 %collective-permute-start.8 = (f32[16,128]{1,0:T(8,128)S(1)}, f32[16,128]{1,0:T(8,128)S(1)}, u32[]{:S(2)}, u32[]{:S(2)}) collective-permute-start(f32[16,128]{1,0:T(8,128)S(1)} %get-tuple-element.51), channel_id=1, source_target_pairs={{0,1},{1,2},{2,3},{3,0},{4,5},{5,6},{6,7},{7,4},{8,9},{9,10},{10,1... | collective-permute-start | bytes 24584 | tf_op jit(solution)/shard_map/ppermute | solution.py:452
  59.4 4.0 %collective-permute-start.11 = (f32[64,128]{1,0:T(8,128)S(1)}, f32[64,128]{1,0:T(8,128)S(1)}, u32[]{:S(2)}, u32[]{:S(2)}) collective-permute-start(f32[64,128]{1,0:T(8,128)S(1)} %get-tuple-element.56), channel_id=1, source_target_pairs={{0,3},{1,0},{2,1},{3,2},{4,7},{5,4},{6,5},{7,6},{8,11},{9,8},{10,9... | collective-permute-start | bytes 98312 | tf_op jit(solution)/shard_map/ppermute | solution.py:452
  61.3 5.7 %collective-permute-start.10 = (f32[64,128]{1,0:T(8,128)S(1)}, f32[64,128]{1,0:T(8,128)S(1)}, u32[]{:S(2)}, u32[]{:S(2)}) collective-permute-start(f32[64,128]{1,0:T(8,128)S(1)} %get-tuple-element.56), channel_id=1, source_target_pairs={{0,1},{1,2},{2,3},{3,0},{4,5},{5,6},{6,7},{7,4},{8,9},{9,10},{10,1... | collective-permute-start | bytes 98312 | tf_op jit(solution)/shard_map/ppermute | solution.py:452
  67.2 4.5 %collective-permute-start.13 = (f32[256,128]{1,0:T(8,128)S(1)}, f32[256,128]{1,0:T(8,128)S(1)}, u32[]{:S(2)}, u32[]{:S(2)}) collective-permute-start(f32[256,128]{1,0:T(8,128)S(1)} %get-tuple-element.59), channel_id=1, source_target_pairs={{0,8},{8,16},{16,24},{24,0},{1,9},{9,17},{17,25},{25,1},{2,10},{10... | collective-permute-start | bytes 393224 | tf_op jit(solution)/shard_map/ppermute | solution.py:452
  67.3 4.0 %collective-permute-start.12 = (f32[192,128]{1,0:T(8,128)S(1)}, f32[192,128]{1,0:T(8,128)S(1)}, u32[]{:S(2)}, u32[]{:S(2)}) collective-permute-start(f32[192,128]{1,0:T(8,128)S(1)} %get-tuple-element.58), channel_id=1, source_target_pairs={{0,24},{8,0},{16,8},{24,16},{1,25},{9,1},{17,9},{25,17},{2,26},{10... | collective-permute-start | bytes 294920 | tf_op jit(solution)/shard_map/ppermute | solution.py:452
  71.8 6.3 %collective-permute-start.14 = (f32[32,8,128]{2,1,0:T(8,128)S(1)}, f32[32,8,128]{2,1,0:T(8,128)S(1)}, u32[]{:S(2)}, u32[]{:S(2)}) collective-permute-start(f32[32,8,128]{2,1,0:T(8,128)S(1)} %get-tuple-element.61), channel_id=1, source_target_pairs={{0,4},{4,0},{1,5},{5,1},{2,6},{6,2},{3,7},{7,3},{8,12},{12,8},{9,1... | collective-permute-start | bytes 393224 | tf_op jit(solution)/shard_map/ppermute | solution.py:452

commit v2 on v1

--- a/solution.py
+++ b/solution.py
@@ -12,7 +12,7 @@
 ROWS = 4
 SHIFTS = 8
 LANES = 128
-PILES = 4
+PILES = 1
 F32 = jnp.float32
 
 
@@ -71,19 +71,38 @@
     lax.fori_loop(0, cells.shape[1], plane, 0)
 
 
-def shift_planes(extended, rim, shifted):
+def gather_planes(blocks, rims, extended, shifted):
     planes, rows, _ = extended.shape
+    ny, nx = rows - 2 * ROWS, planes - LO - HI
     lane = lane_of(rows)
-    for X in range(planes):
-        core = extended[X]
-        ends = pltpu.roll(rim, (-8 * X) % LANES, 1)
-        for j in range(SHIFTS):
-            d = j - LO
-            if d == 0:
-                shifted[j, X] = core
-            else:
-                wraps = lane >= LANES + d if d < 0 else lane < d
-                shifted[j, X] = pltpu.roll(jnp.where(wraps, ends, core), (-d) % LANES, 1)
+    gx, gy, gz = [lax.axis_index(axis) for axis in ("gx", "gy", "gz")]
+    sx, sy, sz = [lax.axis_size(axis) for axis in ("gx", "gy", "gz")]
+    below, above = lax.rem(gy + sy - 1, sy), lax.rem(gy + 1, sy)
+    before, after = lax.rem(gz + sz - 1, sz), lax.rem(gz + 1, sz)
+    low = low_lanes(ny)
+    for column, first, count, start in ((sx - 1, nx - LO, LO, 0), (0, 0, nx, LO), (1, 0, HI, LO + nx)):
+        row = lax.rem(gx + column, sx) * sy
+        ends = []
+        for y in (below, gy, above):
+            at = (row + y) * sz
+            ends.append(jnp.where(low, rims[at + after], rims[at + before]))
+        ends = jnp.concatenate([ends[0][ny - ROWS :], ends[1], ends[2][:ROWS]], axis=0)
+        for i in range(count):
+            x, X = first + i, start + i
+            extended[X, 0:ROWS] = blocks[row + below, x, ny - ROWS : ny]
+            extended[X, ROWS : ROWS + ny] = blocks[row + gy, x]
+            extended[X, ROWS + ny : rows] = blocks[row + above, x, 0:ROWS]
+            shift_plane(extended[X], pltpu.roll(ends, (-8 * x) % LANES, 1), shifted, X, lane)
+
+
+def shift_plane(core, ends, shifted, X, lane):
+    for j in range(SHIFTS):
+        d = j - LO
+        if d == 0:
+            shifted[j, X] = core
+        else:
+            wraps = lane >= LANES + d if d < 0 else lane < d
+            shifted[j, X] = pltpu.roll(jnp.where(wraps, ends, core), (-d) % LANES, 1)
 
 
 def interpolate(shifted, weights, slopes, nx, ny, emit):
@@ -203,46 +222,18 @@
     return jnp.concatenate([above, jnp.zeros((ny - 2 * ROWS, LANES), F32), below], axis=0)
 
 
-def put_edges(out, at, plane, ny):
-    if ny == 2 * ROWS:
-        out[at] = plane
-    else:
-        out[at, 0:ROWS] = plane[0:ROWS]
-        out[at, ROWS : 2 * ROWS] = plane[ny - ROWS : ny]
-
-
 def put_rims(out, at, plane, ny):
     out[at, 0:ROWS] = plane[0:ROWS]
     out[at, ROWS : 2 * ROWS] = plane[ROWS + ny : 2 * ROWS + ny]
 
 
-def place_edges(extended, X, core, edges, ny):
-    extended[X, 0:ROWS] = edges[ROWS : 2 * ROWS]
-    extended[X, ROWS : ROWS + ny] = core
-    extended[X, ROWS + ny : 2 * ROWS + ny] = edges[0:ROWS]
-
-
-def fill_planes(extended, middle, from_right, from_left, nx):
-    rows = middle.shape[1]
-    for x in range(nx):
-        extended[LO + x] = middle[x]
-    for i in range(HI):
-        extended[LO + nx + i] = from_right[i * rows : (i + 1) * rows]
-    for i in range(LO):
-        extended[i] = from_left[i * rows : (i + 1) * rows]
-
-
-def edge_planes(middle, to_left, to_right, nx):
-    rows = middle.shape[1]
-    for i in range(HI):
-        to_left[i * rows : (i + 1) * rows] = middle[i]
-    for i in range(LO):
-        to_right[i * rows : (i + 1) * rows] = middle[nx - LO + i]
+def start_kernel(nx, ny, intensity, rim):
+    rim[...] = pack_rim(intensity)
 
 
 def first_kernel(
-    nx, ny, intensity, cotangent, cells, fracs,
-    image, to_y, own,
+    nx, ny, cotangent, cells, fracs,
+    to_y, own,
     cells_here, fracs_here, cotangent_here, sems, weights, scaled, piled, rims, *piles,
 ):
     copies = [
@@ -252,7 +243,6 @@
                 (cells.at[1, 1], cells_here),
                 (fracs.at[1, 1], fracs_here),
                 (cotangent, cotangent_here),
-                (intensity, image),
             )
         )
     ]
@@ -264,79 +254,61 @@
     deposit(cotangent_here, weights, scaled, piles)
     settle(piles, piled, rims)
     planes = nx + LO + HI
-    for x in range(nx):
-        put_edges(to_y, x, image[x], ny)
     for X in range(planes + 1):
         plane = piled[0, X] if X < planes else rims[0]
-        put_rims(to_y, nx + X, plane, ny)
+        put_rims(to_y, X, plane, ny)
         own[X] = plane[ROWS : ROWS + ny]
 
 
-def first_y_kernel(nx, ny, image, own, from_y, middle, part, to_left, to_right):
+def first_y_kernel(nx, ny, own, from_y, part, to_left, to_right):
     planes = nx + LO + HI
-    rows = ny + 2 * ROWS
-    for x in range(nx):
-        place_edges(middle, x, image[x], from_y[x], ny)
     for X in range(planes + 1):
-        part[X] = own[X] + fold_rows(from_y[nx + X], ny)
-    edge_planes(middle, to_left, to_right, nx)
+        part[X] = own[X] + fold_rows(from_y[X], ny)
     for i, X in enumerate(list(range(LO)) + [planes]):
-        to_left[HI * rows + i * ny : HI * rows + (i + 1) * ny] = part[X]
+        to_left[i] = part[X]
     for i, X in enumerate(list(range(LO + nx, planes)) + [planes]):
-        to_right[LO * rows + i * ny : LO * rows + (i + 1) * ny] = part[X]
-
-
-def first_x_kernel(nx, ny, middle, part, from_right, from_left, extended, folded, rims):
-    rows = ny + 2 * ROWS
-    fill_planes(extended, middle, from_right, from_left, nx)
-    rims[0:rows] = pack_rim(extended)
-
-    def right(i):
-        return from_right[HI * rows + i * ny : HI * rows + (i + 1) * ny]
-
-    def left(i):
-        return from_left[LO * rows + i * ny : LO * rows + (i + 1) * ny]
-
+        to_right[i] = part[X]
+
+
+def first_x_kernel(nx, ny, part, from_right, from_left, folded, rim_out):
     for x in range(nx):
         plane = part[LO + x]
         if x >= nx - LO:
-            plane = plane + right(x - (nx - LO))
+            plane = plane + from_right[x - (nx - LO)]
         if x < HI:
-            plane = plane + left(x)
+            plane = plane + from_left[x]
         folded[x] = plane
     group = group_of(ny)
     turn = 8 * nx
-    high = pltpu.roll(right(LO), turn % LANES, 1)
-    low = pltpu.roll(left(HI), (-turn) % LANES, 1)
+    high = pltpu.roll(from_right[LO], turn % LANES, 1)
+    low = pltpu.roll(from_left[HI], (-turn) % LANES, 1)
     rim = part[nx + LO + HI]
     rim = rim + jnp.where((group >= nx) & (group < nx + LO), high, 0.0)
-    rims[rows : rows + ny] = rim + jnp.where((group >= LO) & (group < LO + HI), low, 0.0)
-
-
-def middle_kernel(nx, ny, extended, rims_l, rims_r, folded, cells, fracs, image, to_y, shifted, adjoint, weights):
-    rows = ny + 2 * ROWS
-    rim = jnp.where(low_lanes(rows), rims_r[0:rows], rims_l[0:rows])
-    shift_planes(extended, rim, shifted)
+    rim_out[...] = rim + jnp.where((group >= LO) & (group < LO + HI), low, 0.0)
+
+
+def middle_kernel(nx, ny, blocks, gathered, cells, fracs, image, rim, shifted, extended, weights):
+    gather_planes(blocks, gathered, extended, shifted)
     write_tables(cells.at[0, 1], fracs.at[0, 1], weights)
 
     def emit(x, sums):
         image[x] = sums[0]
 
     interpolate(shifted, weights, None, nx, ny, emit)
-    for x in range(nx):
-        put_edges(to_y, x, image[x], ny)
-    back = jnp.where(low_lanes(ny), rims_l[rows : rows + ny], rims_r[rows : rows + ny])
+    rim[...] = pack_rim(image)
+
+
+def early_kernel(
+    nx, ny, shifted, folded, gathered, cells, fracs,
+    piled_adjoint, adjoint_rims, piled, rims,
+    adjoint, grad, weights, slopes, scaled, scaled_one, *piles,
+):
+    size = lax.axis_size("gz")
+    gz = lax.axis_index("gz")
+    before, after = lax.rem(gz + size - 1, size), lax.rem(gz + 1, size)
+    back = jnp.where(low_lanes(ny), gathered[before], gathered[after])
     for x in range(nx):
         adjoint[0, x] = folded[x] + unpack_rim(back, LO + x)
-
-
-def adjoint_kernel(nx, ny, adjoint, cells, fracs, piled, rims, weights, scaled, *piles):
-    write_tables(cells.at[0, 1], fracs.at[0, 1], weights)
-    deposit(adjoint, weights, scaled, piles)
-    settle(piles, piled, rims)
-
-
-def early_grad_kernel(nx, ny, shifted, adjoint, cells, fracs, grad, weights, slopes):
     write_tables(cells.at[0, 1], fracs.at[0, 1], weights, slopes)
 
     def emit(x, sums):
@@ -344,32 +316,21 @@
             grad[c, x] = adjoint[0, x] * sums[c]
 
     interpolate(shifted, weights, slopes, nx, ny, emit)
-
-
-def early_spread_kernel(nx, ny, grad, cells, fracs, piled, rims, weights, scaled, *piles):
+    ones = [pile.at[0:1] for pile in piles]
+    deposit(adjoint, weights, scaled_one, ones)
+    settle(ones, piled_adjoint, adjoint_rims)
     write_tables(cells.at[0, 0], fracs.at[0, 0], weights)
     deposit(grad, weights, scaled, piles)
     settle(piles, piled, rims)
 
 
-def second_y_kernel(nx, ny, image, from_y, earlier, middle, to_left, to_right):
-    for x in range(nx):
-        place_edges(middle, x, image[x], from_y[x], ny)
-    edge_planes(middle, to_left, to_right, nx)
-
-
-def second_x_kernel(nx, ny, middle, from_right, from_left, earlier, extended, rims):
-    fill_planes(extended, middle, from_right, from_left, nx)
-    rims[...] = pack_rim(extended)
-
-
 def late_kernel(
-    nx, ny, extended, rims_l, rims_r, cotangent, cells, fracs, early, early_rims, adjoint_rims,
+    nx, ny, blocks, gathered, cotangent, cells, fracs, early, early_rims, adjoint_rims,
     piled, rims,
-    shifted, weights, slopes, grad, scaled, rims_here, *piles,
+    shifted, extended, weights, slopes, grad, scaled, rims_here, *piles,
 ):
     rows = ny + 2 * ROWS
-    shift_planes(extended, jnp.where(low_lanes(rows), rims_r[...], rims_l[...]), shifted)
+    gather_planes(blocks, gathered, extended, shifted)
     write_tables(cells.at[1, 1], fracs.at[1, 1], weights, slopes)
 
     def emit(x, sums):
@@ -427,7 +388,7 @@
                 velocity_adjoint[c, x] = plane
 
 
-def call(kernel, args, outs, scratch, flops, spaces=None):
+def call(kernel, args, outs, scratch, flops, spaces=None, limit=24):
     def struct(shape):
         return jax.ShapeDtypeStruct(shape, F32)
 
@@ -442,7 +403,7 @@
         in_specs=in_specs,
         out_specs=[in_vmem] * len(outs),
         scratch_shapes=[pltpu.VMEM(s, F32) if isinstance(s, tuple) else s for s in scratch],
-        compiler_params=pltpu.CompilerParams(vmem_limit_bytes=24 * 1024 * 1024),
+        compiler_params=pltpu.CompilerParams(vmem_limit_bytes=limit * 1024 * 1024),
         cost_estimate=pl.CostEstimate(flops=flops, bytes_accessed=moved, transcendentals=0),
     )(*args)
 
@@ -489,97 +450,74 @@
     def piled(channels):
         return [(channels, planes, rows, nz), (channels, rows, nz)]
 
+    def gather(block, rim):
+        return (
+            lax.all_gather(block, ("gx", "gy")),
+            lax.all_gather(rim, ("gx", "gy", "gz")),
+        )
+
+    field = (nx, ny, nz)
+    (rim,) = run(start_kernel, (intensity,), [(ny, nz)], [], unit // 64)
+    blocks, rims = gather(intensity, rim)
+
     part = (3, nx, ny, nz)
-    image, to_y, own = run(
+    to_y, own = run(
         first_kernel,
-        (intensity, cotangent, cells, fracs),
-        [(nx, ny, nz), (nx + planes + 1, ring, nz), (planes + 1, ny, nz)],
+        (cotangent, cells, fracs),
+        [(planes + 1, ring, nz), (planes + 1, ny, nz)],
         [
             pltpu.VMEM(part, jnp.int32),
             part,
             (1, nx, ny, nz),
-            pltpu.SemaphoreType.DMA((4,)),
+            pltpu.SemaphoreType.DMA((3,)),
             table,
             scaled(1),
         ]
         + piled(1)
         + piles(1),
         2 * unit,
-        spaces=dict.fromkeys(range(4), pltpu.HBM),
-    )
-    middle, part, *to_x = run(
+        spaces=dict.fromkeys(range(3), pltpu.HBM),
+        limit=61,
+    )
+    part, *to_x = run(
         first_y_kernel,
-        (image, own, send_y(to_y)),
-        [
-            (nx, rows, nz),
-            (planes + 1, ny, nz),
-            (HI * rows + (LO + 1) * ny, nz),
-            (LO * rows + (HI + 1) * ny, nz),
-        ],
+        (own, send_y(to_y)),
+        [(planes + 1, ny, nz), (LO + 1, ny, nz), (HI + 1, ny, nz)],
         [],
         unit // 32,
     )
-    extended, folded, rims = run(
+    folded, adjoint_rim = run(
         first_x_kernel,
-        (middle, part) + send_x(*to_x),
-        [(planes, rows, nz), (nx, ny, nz), (rows + ny, nz)],
+        (part,) + send_x(*to_x),
+        [field, (ny, nz)],
         [],
         unit // 32,
     )
-    image, to_y, shifted, adjoint = run(
+    adjoint_rims = lax.all_gather(adjoint_rim, "gz")
+
+    image, rim, shifted = run(
         middle_kernel,
-        (extended,) + send_z(rims) + (folded, cells, fracs),
-        [(nx, ny, nz), (nx, ring, nz), (SHIFTS, planes, rows, nz), (1, nx, ny, nz)],
-        [table],
+        (blocks, rims, cells, fracs),
+        [field, (ny, nz), (SHIFTS, planes, rows, nz)],
+        [(planes, rows, nz), table],
         2 * unit,
     )
-
-    from_y = send_y(to_y)
-    piled_adjoint, adjoint_rims = run(
-        adjoint_kernel,
-        (adjoint, cells, fracs),
-        piled(1),
-        [table, scaled(1)] + piles(1),
-        2 * unit,
-    )
-    middle, *to_x = run(
-        second_y_kernel,
-        (image, from_y, piled_adjoint),
-        [(nx, rows, nz), (HI * rows, nz), (LO * rows, nz)],
-        [],
-        unit // 32,
-        spaces={2: pl.ANY},
-    )
-    from_right, from_left = send_x(*to_x)
-    (grad,) = run(
-        early_grad_kernel,
-        (shifted, adjoint, cells, fracs),
-        [(3, nx, ny, nz)],
-        [table, table],
-        5 * unit,
-    )
-    extended, rims = run(
-        second_x_kernel,
-        (middle, from_right, from_left, grad),
-        [(planes, rows, nz), (rows, nz)],
-        [],
-        unit // 32,
-        spaces={3: pl.ANY},
-    )
-    rims_l, rims_r = send_z(rims)
-    early, early_rims = run(
-        early_spread_kernel,
-        (grad, cells, fracs),
-        piled(3),
-        [table, scaled(3)] + piles(3),
-        6 * unit,
+    blocks, rims = gather(image, rim)
+
+    piled_adjoint, adjoint_rims, early, early_rims = run(
+        early_kernel,
+        (shifted, folded, adjoint_rims, cells, fracs),
+        piled(1) + piled(3),
+        [(1,) + field, (3,) + field, table, table, scaled(3), scaled(1)] + piles(3),
+        13 * unit,
     )
 
     velocity, rims = run(
         late_kernel,
-        (extended, rims_l, rims_r, cotangent, cells, fracs, early, early_rims, adjoint_rims),
+        (blocks, rims, cotangent, cells, fracs, early, early_rims, adjoint_rims),
         [(3, planes, rows, nz), (4 * rows, nz)],
-        [(SHIFTS, planes, rows, nz), table, table, (3, nx, ny, nz), scaled(3), (3, rows, nz)] + piles(3),
+        [(SHIFTS, planes, rows, nz), (planes, rows, nz), table, table, (3, nx, ny, nz), scaled(3), (3, rows, nz)]
+        + piles(3),
         11 * unit,
     )
     *to_x, own = run(

time: 79 us -> 232 us (2.94)
  blocking collectives: 0 us -> 177 us
  waiting for transfers between devices: 24.7 us -> 8.95 us
  starting transfers between devices: 17.2 us -> 12.5 us
  local copies, waits for them, and re-layouts: 3.52 us -> 0.02 us
    all_gather x0 -> x5, blocking collectives: none -> 177 us  [the longest x2 133 us: gather(): lax.all_gather(rim, ('gx', 'gy', 'gz'))]
    ppermute x15 -> x8, waiting for transfers between devices: 24.7 us -> 8.95 us  [send(): lax.ppermute(message, axis, [(i, (i + move) % size) for i in range(size)])]
    ppermute x15 -> x8, starting transfers between devices: 17.2 us -> 12.5 us  [send(): lax.ppermute(message, axis, [(i, (i + move) % size) for i in range(size)])]
    unnamed x14 -> x10, local copies, waits for them, and re-layouts: 3.52 us -> 0.02 us
    pallas_call x13 -> x10, Pallas kernels: 32.5 us -> 32.7 us  [call(): pl.pallas_call(kernel, out_shape=[struct(s) for s in outs], in_specs=in_s...]
  transfers between devices with their start and end apart: 15 -> 8, of which waited for: 9 -> 3; matrix products, arithmetic and copies ran while one was open for 0% -> 0% of each run, Pallas kernels for 17% -> 1%
where the time goes in v2:
time: 232 us
  blocking collectives  177 us (76%)
  Pallas kernels  32.7 us (14%)
  starting transfers between devices  12.5 us (5%)
  waiting for transfers between devices  8.95 us (4%)
    all_gather x2, blocking collectives, gather(): lax.all_gather(rim, ('gx', 'gy', 'gz'))  133 us
    pallas_call x10, Pallas kernels, call(): pl.pallas_call(kernel, out_shape=[struct(s) for s in outs], in_specs=in_s...  32.7 us
    all_gather x2, blocking collectives, gather(): lax.all_gather(block, ('gx', 'gy'))  31.2 us
    all_gather x1, blocking collectives, body(): adjoint_rims = lax.all_gather(adjoint_rim, 'gz')  13.1 us
    ppermute x8, starting transfers between devices, send(): lax.ppermute(message, axis, [(i, (i + move) % size) for i in range(size)])  12.5 us
    ppermute x8, waiting for transfers between devices, send(): lax.ppermute(message, axis, [(i, (i + move) % size) for i in range(size)])  8.95 us
  transfers between devices with their start and end apart: 8, of which 3 were waited for; matrix products, arithmetic and copies ran while one was open for 0% of the time, Pallas kernels for 1%

profile of v2, /device:TPU:0, one launch (start us, length us, event | category | flops | bytes accessed | tf_op | source)
XLA Modules:
  0.0 231.8 jit_solution(12379561458722754614)
XLA Ops:
  0.6 4.0 %shard_map.61 = (f32[16,8,128]{2,1,0:T(8,128)}, f32[16,8,128]{2,1,0:T(8,128)}) custom-call(f32[1,8,8,128]{3,2,1,0:T(8,128)} %bitcast.10, s32[2,2,3,8,8,128]{5,4,3,2,1,0:T(8,128)} %cells.7, f32[2,2,3,8,8,128]{5,4,3,2,1,0:T(8,128)} %fracs.7), custom_call_target="tpu_custom_call" | custom-call | flops 8388608 | bytes 819200 | tf_op jit(solution)/shard_map/pallas_call | solution.py:400
  4.7 3.0 %collective-permute-start = (f32[16,8,128]{2,1,0:T(8,128)}, f32[16,8,128]{2,1,0:T(8,128)S(1)}, u32[]{:S(2)}, u32[]{:S(2)}) collective-permute-start(f32[16,8,128]{2,1,0:T(8,128)} %get-tuple-element.27), channel_id=1, source_target_pairs={{0,4},{4,0},{1,5},{5,1},{2,6},{6,2},{3,7},{7,3},{8,12},{12,8},{9,1... | collective-permute-start | bytes 196616 | tf_op jit(solution)/shard_map/ppermute | solution.py:413
  7.7 0.1 shard_map.59
  7.8 68.0 %all-gather.1 = f32[256,128]{1,0:T(8,128)S(1)} all-gather(f32[8,128]{1,0:T(8,128)S(1)} %shard_map.59), channel_id=3, replica_groups=mesh['gx'=4,'gy'=2,'gz'=4] {'gx','gy','gz'}, dimensions={0}, use_global_device_ids=true | all-gather | bytes 135168 | tf_op jit(solution)/shard_map/all_gather | solution.py:456
  75.7 15.6 %all-gather = f32[64,8,128]{2,1,0:T(8,128)S(1)} all-gather(f32[8,8,128]{2,1,0:T(8,128)S(1)} %copy-done.3), channel_id=2, replica_groups=mesh['gx'=4,'gy'=2,'gz'=4] {'gx','gy'}, dimensions={0}, use_global_device_ids=true | all-gather | bytes 294912 | tf_op jit(solution)/shard_map/all_gather | solution.py:455
  91.4 3.1 %shard_map.60 = (f32[8,8,128]{2,1,0:T(8,128)S(1)}, f32[8,128]{1,0:T(8,128)S(1)}, f32[8,15,16,128]{3,2,1,0:T(8,128)S(1)}) custom-call(f32[8,8,8,128]{3,2,1,0:T(8,128)S(1)} %bitcast.7, f32[32,8,128]{2,1,0:T(8,128)S(1)} %bitcast.9, s32[2,2,3,8,8,128]{5,4,3,2,1,0:T(8,128)S(1)} %copy-done, f32[2,2,3,8,8,128]{5,4,3,2,1,0:T(8,128)S(1)} %copy-done.1), custom_call_target="tpu_custom_call" | custom-call | flops 8388608 | bytes 1179648 | tf_op jit(solution)/shard_map/pallas_call | solution.py:400
  94.5 64.5 %all-gather.3 = f32[256,128]{1,0:T(8,128)S(1)} all-gather(f32[8,128]{1,0:T(8,128)S(1)} %get-tuple-element.24), channel_id=5, replica_groups=mesh['gx'=4,'gy'=2,'gz'=4] {'gx','gy','gz'}, dimensions={0}, use_global_device_ids=true | all-gather | bytes 135168 | tf_op jit(solution)/shard_map/all_gather | solution.py:456
  159.0 0.1 collective-permute-start.2
  159.1 1.7 collective-permute-start.1
  160.8 15.6 %all-gather.2 = f32[64,8,128]{2,1,0:T(8,128)S(1)} all-gather(f32[8,8,128]{2,1,0:T(8,128)S(1)} %get-tuple-element.23), channel_id=4, replica_groups=mesh['gx'=4,'gy'=2,'gz'=4] {'gx','gy'}, dimensions={0}, use_global_device_ids=true | all-gather | bytes 294912 | tf_op jit(solution)/shard_map/all_gather | solution.py:455
  176.4 0.1 shard_map.63
  176.5 13.1 %all-gather.4 = f32[32,128]{1,0:T(8,128)S(1)} all-gather(f32[8,128]{1,0:T(8,128)S(1)} %get-tuple-element.32), channel_id=6, replica_groups=mesh['gx'=4,'gy'=2,'gz'=4] {'gz'}, dimensions={0}, use_global_device_ids=true | all-gather | bytes 20480 | tf_op jit(solution)/shard_map/all_gather | solution.py:496
  189.6 12.7 %shard_map.64 = (f32[1,15,16,128]{3,2,1,0:T(8,128)S(1)}, f32[1,16,128]{2,1,0:T(8,128)S(1)}, f32[3,15,16,128]{3,2,1,0:T(8,128)S(1)}, f32[3,16,128]{2,1,0:T(8,128)S(1)}) custom-call(f32[8,15,16,128]{3,2,1,0:T(8,128)S(1)} %get-tuple-element.25.shifted, f32[8,8,128]{2,1,0:T(8,128)S(1)} %get-tuple-element.31.folded, f32[4,8,128]{2,1,0:T(8,128)S(1)} %bitcast.12, ...), custom_call_target="tpu_custom_call" | custom-call | flops 54525952 | bytes 1818624 | tf_op jit(solution)/shard_map/pallas_call | solution.py:400
  202.3 11.9 %shard_map.65 = (f32[3,15,16,128]{3,2,1,0:T(8,128)S(1)}, f32[64,128]{1,0:T(8,128)S(1)}) custom-call(f32[8,8,8,128]{3,2,1,0:T(8,128)S(1)} %bitcast.6, f32[32,8,128]{2,1,0:T(8,128)S(1)} %bitcast.8, f32[1,8,8,128]{3,2,1,0:T(8,128)S(1)} %bitcast.11, s32[2,2,3,8,8,128]{5,4,3,2,1,0:T(8,128)S(1)} %copy-done, f32[2,2,3,8,8,128]{5,4,3,2,1,0:T(8,128)S(1)} %copy-done.1, ...), custom_call_target="tpu_custom_call" | custom-call | flops 46137344 | bytes 1613824 | tf_op jit(solution)/shard_map/pallas_call | solution.py:400
  214.2 0.3 collective-permute-start.3
  214.5 3.5 %collective-permute-start.4 = (f32[64,128]{1,0:T(8,128)S(1)}, f32[64,128]{1,0:T(8,128)S(1)}, u32[]{:S(2)}, u32[]{:S(2)}) collective-permute-start(f32[64,128]{1,0:T(8,128)S(1)} %get-tuple-element.38), channel_id=1, source_target_pairs={{0,3},{1,0},{2,1},{3,2},{4,7},{5,4},{6,5},{7,6},{8,11},{9,8},{10,9... | collective-permute-start | bytes 98312 | tf_op jit(solution)/shard_map/ppermute | solution.py:413
  218.0 1.9 collective-permute-done.3.rims_l
  219.9 0.2 shard_map.66
  220.1 0.1 collective-permute-start.6
  220.2 1.7 collective-permute-start.5
  221.9 2.9 %collective-permute-done.5.from_right = f32[192,128]{1,0:T(8,128)S(1)} collective-permute-done((f32[192,128]{1,0:T(8,128)S(1)}, f32[192,128]{1,0:T(8,128)S(1)}, u32[]{:S(2)}, u32[]{:S(2)}) %collective-permute-start.5) | collective-permute-done | bytes 98336 | tf_op jit(solution)/shard_map/ppermute | solution.py:413
  224.9 2.1 collective-permute-start.7
  227.0 4.1 %collective-permute-done.7.from_y = f32[32,8,128]{2,1,0:T(8,128)S(1)} collective-permute-done((f32[32,8,128]{2,1,0:T(8,128)S(1)}, f32[32,8,128]{2,1,0:T(8,128)S(1)}, u32[]{:S(2)}, u32[]{:S(2)}) %collective-permute-start.7) | collective-permute-done | bytes 131104 | tf_op jit(solution)/shard_map/ppermute | solution.py:413
  231.1 0.7 shard_map.68
  (17 shorter events, 0.1 us)
Async XLA Ops:
  0.6 7.1 %copy-start.3 = (f32[8,8,128]{2,1,0:T(8,128)S(1)}, f32[8,8,128]{2,1,0:T(8,128)}, u32[]{:S(2)}) copy-start(f32[8,8,128]{2,1,0:T(8,128)} %intensity.1) | copy-start | bytes 98308
  0.6 90.7 %copy-start.1 = (f32[2,2,3,8,8,128]{5,4,3,2,1,0:T(8,128)S(1)}, f32[2,2,3,8,8,128]{5,4,3,2,1,0:T(8,128)}, u32[]{:S(2)}) copy-start(f32[2,2,3,8,8,128]{5,4,3,2,1,0:T(8,128)} %fracs.7) | copy-start | bytes 1179652
  4.6 86.7 %copy-start = (s32[2,2,3,8,8,128]{5,4,3,2,1,0:T(8,128)S(1)}, s32[2,2,3,8,8,128]{5,4,3,2,1,0:T(8,128)}, u32[]{:S(2)}) copy-start(s32[2,2,3,8,8,128]{5,4,3,2,1,0:T(8,128)} %cells.7) | copy-start | bytes 1179652
  4.7 154.3 %collective-permute-start = (f32[16,8,128]{2,1,0:T(8,128)}, f32[16,8,128]{2,1,0:T(8,128)S(1)}, u32[]{:S(2)}, u32[]{:S(2)}) collective-permute-start(f32[16,8,128]{2,1,0:T(8,128)} %get-tuple-element.27), channel_id=1, source_target_pairs={{0,4},{4,0},{1,5},{5,1},{2,6},{6,2},{3,7},{7,3},{8,12},{12,8},{9,1... | collective-permute-start | bytes 196616 | tf_op jit(solution)/shard_map/ppermute | solution.py:413
  94.4 64.6 %copy-start.4 = (f32[16,8,128]{2,1,0:T(8,128)S(1)}, f32[16,8,128]{2,1,0:T(8,128)}, u32[]{:S(2)}) copy-start(f32[16,8,128]{2,1,0:T(8,128)} %get-tuple-element.26.own) | copy-start | bytes 196612
  159.0 17.4 %collective-permute-start.2 = (f32[5,8,128]{2,1,0:T(8,128)S(1)}, f32[5,8,128]{2,1,0:T(8,128)S(1)}, u32[]{:S(2)}, u32[]{:S(2)}) collective-permute-start(f32[5,8,128]{2,1,0:T(8,128)S(1)} %get-tuple-element.30), channel_id=1, source_target_pairs={{0,8},{8,16},{16,24},{24,0},{1,9},{9,17},{17,25},{25,1},{2,10},{10... | collective-permute-start | bytes 61448 | tf_op jit(solution)/shard_map/ppermute | solution.py:413
  159.1 17.3 %collective-permute-start.1 = (f32[4,8,128]{2,1,0:T(8,128)S(1)}, f32[4,8,128]{2,1,0:T(8,128)S(1)}, u32[]{:S(2)}, u32[]{:S(2)}) collective-permute-start(f32[4,8,128]{2,1,0:T(8,128)S(1)} %get-tuple-element.29), channel_id=1, source_target_pairs={{0,24},{8,0},{16,8},{24,16},{1,25},{9,1},{17,9},{25,17},{2,26},{10... | collective-permute-start | bytes 49160 | tf_op jit(solution)/shard_map/ppermute | solution.py:413
  189.6 12.7 %copy-start.2 = (f32[8,8,128]{2,1,0:T(8,128)S(1)}, f32[8,8,128]{2,1,0:T(8,128)}, u32[]{:S(2)}) copy-start(f32[8,8,128]{2,1,0:T(8,128)} %param.5) | copy-start | bytes 98308
  214.2 5.7 %collective-permute-start.3 = (f32[64,128]{1,0:T(8,128)S(1)}, f32[64,128]{1,0:T(8,128)S(1)}, u32[]{:S(2)}, u32[]{:S(2)}) collective-permute-start(f32[64,128]{1,0:T(8,128)S(1)} %get-tuple-element.38), channel_id=1, source_target_pairs={{0,1},{1,2},{2,3},{3,0},{4,5},{5,6},{6,7},{7,4},{8,9},{9,10},{10,1... | collective-permute-start | bytes 98312 | tf_op jit(solution)/shard_map/ppermute | solution.py:413
  214.5 5.4 %collective-permute-start.4 = (f32[64,128]{1,0:T(8,128)S(1)}, f32[64,128]{1,0:T(8,128)S(1)}, u32[]{:S(2)}, u32[]{:S(2)}) collective-permute-start(f32[64,128]{1,0:T(8,128)S(1)} %get-tuple-element.38), channel_id=1, source_target_pairs={{0,3},{1,0},{2,1},{3,2},{4,7},{5,4},{6,5},{7,6},{8,11},{9,8},{10,9... | collective-permute-start | bytes 98312 | tf_op jit(solution)/shard_map/ppermute | solution.py:413
  220.1 4.7 %collective-permute-start.6 = (f32[256,128]{1,0:T(8,128)S(1)}, f32[256,128]{1,0:T(8,128)S(1)}, u32[]{:S(2)}, u32[]{:S(2)}) collective-permute-start(f32[256,128]{1,0:T(8,128)S(1)} %get-tuple-element.41), channel_id=1, source_target_pairs={{0,8},{8,16},{16,24},{24,0},{1,9},{9,17},{17,25},{25,1},{2,10},{10... | collective-permute-start | bytes 393224 | tf_op jit(solution)/shard_map/ppermute | solution.py:413
  220.2 4.7 %collective-permute-start.5 = (f32[192,128]{1,0:T(8,128)S(1)}, f32[192,128]{1,0:T(8,128)S(1)}, u32[]{:S(2)}, u32[]{:S(2)}) collective-permute-start(f32[192,128]{1,0:T(8,128)S(1)} %get-tuple-element.40), channel_id=1, source_target_pairs={{0,24},{8,0},{16,8},{24,16},{1,25},{9,1},{17,9},{25,17},{2,26},{10... | collective-permute-start | bytes 294920 | tf_op jit(solution)/shard_map/ppermute | solution.py:413
  224.9 6.2 %collective-permute-start.7 = (f32[32,8,128]{2,1,0:T(8,128)S(1)}, f32[32,8,128]{2,1,0:T(8,128)S(1)}, u32[]{:S(2)}, u32[]{:S(2)}) collective-permute-start(f32[32,8,128]{2,1,0:T(8,128)S(1)} %get-tuple-element.43), channel_id=1, source_target_pairs={{0,4},{4,0},{1,5},{5,1},{2,6},{6,2},{3,7},{7,3},{8,12},{12,8},{9,1... | collective-permute-start | bytes 393224 | tf_op jit(solution)/shard_map/ppermute | solution.py:413

commit v3 on v2

--- a/solution.py
+++ b/solution.py
@@ -429,6 +429,14 @@
     return send(rims, "gz", 1), send(rims, "gz", -1)
 
 
+def spread(block, axes):
+    size = 1
+    for axis in axes:
+        size *= lax.axis_size(axis)
+    slots = jnp.broadcast_to(block, (size,) + block.shape)
+    return lax.all_to_all(slots, axes, 0, 0)
+
+
 def body(intensity, cotangent, cells, fracs):
     nx, ny, nz = intensity.shape
     rows = ny + 2 * ROWS
@@ -452,8 +460,8 @@
 
     def gather(block, rim):
         return (
-            lax.all_gather(block, ("gx", "gy")),
-            lax.all_gather(rim, ("gx", "gy", "gz")),
+            spread(block, ("gx", "gy")),
+            spread(rim, ("gx", "gy", "gz")),
         )
 
     field = (nx, ny, nz)
@@ -493,7 +501,7 @@
         [],
         unit // 32,
     )
-    adjoint_rims = lax.all_gather(adjoint_rim, "gz")
+    adjoint_rims = spread(adjoint_rim, ("gz",))
 
     image, rim, shifted = run(
         middle_kernel,

time: 232 us -> 98.6 us (0.42)
  blocking collectives: 177 us -> 9.52 us
  starting transfers between devices: 12.5 us -> 28.2 us
  waiting for transfers between devices: 8.95 us -> 22.4 us
  local copies, waits for them, and re-layouts: 0.02 us -> 4.33 us
    all_gather x5 -> x0, blocking collectives: 177 us -> none  [the longest x2 133 us: gather(): lax.all_gather(rim, ('gx', 'gy', 'gz'))]
    all_to_all x0 -> x4, starting transfers between devices: none -> 17.5 us  [spread(): return lax.all_to_all(slots, axes, 0, 0)]
    all_to_all x0 -> x1, blocking collectives: none -> 9.52 us  [spread(): return lax.all_to_all(slots, axes, 0, 0)]
    all_to_all x0 -> x4, waiting for transfers between devices: none -> 8.52 us  [spread(): return lax.all_to_all(slots, axes, 0, 0)]
    ppermute x8, waiting for transfers between devices: 8.95 us -> 13.9 us  [send(): lax.ppermute(message, axis, [(i, (i + move) % size) for i in range(size)])]
    broadcast_in_dim x0 -> x5, local copies, waits for them, and re-layouts: none -> 3.47 us  [spread(): slots = jnp.broadcast_to(block, (size,) + block.shape)]
  transfers between devices with their start and end apart: 8 -> 12, of which waited for: 3 -> 8; matrix products, arithmetic and copies ran while one was open for 0% -> 0% of each run, Pallas kernels for 1% -> 20%
where the time goes in v3:
time: 98.6 us; the launch traced here: 98 us
  Pallas kernels  32.8 us (33%)
  starting transfers between devices  28.2 us (29%)
  waiting for transfers between devices  22.4 us (23%)
  blocking collectives  9.52 us (10%)
  local copies, waits for them, and re-layouts  4.33 us (4%)
    pallas_call x10, Pallas kernels, call(): pl.pallas_call(kernel, out_shape=[struct(s) for s in outs], in_specs=in_s...  32.8 us
    all_to_all x4, starting transfers between devices, spread(): return lax.all_to_all(slots, axes, 0, 0)  17.5 us
    ppermute x8, waiting for transfers between devices, send(): lax.ppermute(message, axis, [(i, (i + move) % size) for i in range(size)])  13.9 us
    ppermute x8, starting transfers between devices, send(): lax.ppermute(message, axis, [(i, (i + move) % size) for i in range(size)])  10.8 us
    all_to_all x1, blocking collectives, spread(): return lax.all_to_all(slots, axes, 0, 0)  9.52 us
    all_to_all x4, waiting for transfers between devices, spread(): return lax.all_to_all(slots, axes, 0, 0)  8.52 us
    broadcast_in_dim x5, local copies, waits for them, and re-layouts, spread(): slots = jnp.broadcast_to(block, (size,) + block.shape)  3.47 us
  transfers between devices with their start and end apart: 12, of which 8 were waited for; matrix products, arithmetic and copies ran while one was open for 0% of the time, Pallas kernels for 20%

profile of v3, /device:TPU:0, one launch (start us, length us, event | category | flops | bytes accessed | tf_op | source)
XLA Modules:
  0.0 98.0 jit_solution(6303564905060901261)
XLA Ops:
  0.6 1.5 %broadcast_in_dim.18 = f32[8,8,8,128]{3,2,1,0:T(8,128)} broadcast(f32[8,8,128]{2,1,0:T(8,128)} %intensity.1), dimensions={1,2,3} | broadcast | bytes 294912 | tf_op jit(solution)/shard_map/broadcast_in_dim | solution.py:436
  2.1 5.3 %all-to-all-start = ((f32[8,8,8,128]{3,2,1,0:T(8,128)}), f32[8,8,8,128]{3,2,1,0:T(8,128)S(1)}, u32[]{:S(2)}, u32[]{:S(2)}) async-start(f32[8,8,8,128]{3,2,1,0:T(8,128)} %broadcast_in_dim.18), calls=%async_computation | async-start | bytes 524288 | tf_op jit(solution)/shard_map/all_to_all | solution.py:437
  7.5 6.0 %all-to-all-done.blocks = f32[8,8,8,128]{3,2,1,0:T(8,128)S(1)} async-done(((f32[8,8,8,128]{3,2,1,0:T(8,128)}), f32[8,8,8,128]{3,2,1,0:T(8,128)S(1)}, u32[]{:S(2)}, u32[]{:S(2)}) %all-to-all-start) | async-done | bytes 262176 | tf_op jit(solution)/shard_map/all_to_all | solution.py:437
  14.1 4.9 %all-to-all-start.1 = ((f32[32,8,128]{2,1,0:T(8,128)}), f32[32,8,128]{2,1,0:T(8,128)S(1)}, u32[]{:S(2)}, u32[]{:S(2)}) async-start(f32[32,8,128]{2,1,0:T(8,128)} %broadcast_in_dim.19), calls=%async_computation.1 | async-start | bytes 262144 | tf_op jit(solution)/shard_map/all_to_all | solution.py:437
  19.0 4.0 %shard_map.61 = (f32[16,8,128]{2,1,0:T(8,128)}, f32[16,8,128]{2,1,0:T(8,128)}) custom-call(f32[1,8,8,128]{3,2,1,0:T(8,128)} %bitcast.1, s32[2,2,3,8,8,128]{5,4,3,2,1,0:T(8,128)} %cells.7, f32[2,2,3,8,8,128]{5,4,3,2,1,0:T(8,128)} %fracs.7), custom_call_target="tpu_custom_call" | custom-call | flops 8388608 | bytes 819200 | tf_op jit(solution)/shard_map/pallas_call | solution.py:400
  23.1 1.8 %collective-permute-start = (f32[16,8,128]{2,1,0:T(8,128)}, f32[16,8,128]{2,1,0:T(8,128)S(1)}, u32[]{:S(2)}, u32[]{:S(2)}) collective-permute-start(f32[16,8,128]{2,1,0:T(8,128)} %get-tuple-element.27), channel_id=1, source_target_pairs={{0,4},{4,0},{1,5},{5,1},{2,6},{6,2},{3,7},{7,3},{8,12},{12,8},{9,1... | collective-permute-start | bytes 196616 | tf_op jit(solution)/shard_map/ppermute | solution.py:413
  24.9 2.9 %collective-permute-done.from_y = f32[16,8,128]{2,1,0:T(8,128)S(1)} collective-permute-done((f32[16,8,128]{2,1,0:T(8,128)}, f32[16,8,128]{2,1,0:T(8,128)S(1)}, u32[]{:S(2)}, u32[]{:S(2)}) %collective-permute-start) | collective-permute-done | bytes 65568 | tf_op jit(solution)/shard_map/ppermute | solution.py:413
  27.8 0.8 copy-done.4
  28.7 1.7 %collective-permute-start.1 = (f32[4,8,128]{2,1,0:T(8,128)S(1)}, f32[4,8,128]{2,1,0:T(8,128)S(1)}, u32[]{:S(2)}, u32[]{:S(2)}) collective-permute-start(f32[4,8,128]{2,1,0:T(8,128)S(1)} %get-tuple-element.29), channel_id=1, source_target_pairs={{0,24},{8,0},{16,8},{24,16},{1,25},{9,1},{17,9},{25,17},{2,26},{10... | collective-permute-start | bytes 49160 | tf_op jit(solution)/shard_map/ppermute | solution.py:413
  30.4 1.4 %collective-permute-done.1.from_right = f32[4,8,128]{2,1,0:T(8,128)S(1)} collective-permute-done((f32[4,8,128]{2,1,0:T(8,128)S(1)}, f32[4,8,128]{2,1,0:T(8,128)S(1)}, u32[]{:S(2)}, u32[]{:S(2)}) %collective-permute-start.1) | collective-permute-done | bytes 16416 | tf_op jit(solution)/shard_map/ppermute | solution.py:413
  32.6 4.7 %all-to-all-start.4 = ((f32[4,8,128]{2,1,0:T(8,128)}), f32[4,8,128]{2,1,0:T(8,128)S(1)}, u32[]{:S(2)}, u32[]{:S(2)}) async-start(f32[4,8,128]{2,1,0:T(8,128)} %broadcast_in_dim.23), calls=%async_computation.4 | async-start | bytes 32768 | tf_op jit(solution)/shard_map/all_to_all | solution.py:437
  37.3 3.0 %shard_map.60 = (f32[8,8,128]{2,1,0:T(8,128)S(1)}, f32[8,128]{1,0:T(8,128)S(1)}, f32[8,15,16,128]{3,2,1,0:T(8,128)S(1)}) custom-call(f32[8,8,8,128]{3,2,1,0:T(8,128)S(1)} %all-to-all-done.blocks, f32[32,8,128]{2,1,0:T(8,128)S(1)} %all-to-all-done.1.gathered, s32[2,2,3,8,8,128]{5,4,3,2,1,0:T(8,128)S(1)} %copy-done, f32[2,2,3,8,8,128]{5,4,3,2,1,0:T(8,128)S(1)} %copy-done.1), custom_call_target="tpu_custom_call" | custom-call | flops 8388608 | bytes 1179648 | tf_op jit(solution)/shard_map/pallas_call | solution.py:400
  40.4 2.6 %all-to-all-done.4.gathered = f32[4,8,128]{2,1,0:T(8,128)S(1)} async-done(((f32[4,8,128]{2,1,0:T(8,128)}), f32[4,8,128]{2,1,0:T(8,128)S(1)}, u32[]{:S(2)}, u32[]{:S(2)}) %all-to-all-start.4) | async-done | bytes 16416 | tf_op jit(solution)/shard_map/all_to_all | solution.py:437
  42.9 9.5 %all_to_all.25.blocks = f32[8,8,8,128]{3,2,1,0:T(8,128)S(1)} all-to-all(f32[8,8,8,128]{3,2,1,0:T(8,128)S(1)} %broadcast_in_dim.20), channel_id=1, replica_groups=mesh['gx'=4,'gy'=2,'gz'=4] {'gx','gy'}, dimensions={0} | all-to-all | bytes 524288 | tf_op jit(solution)/shard_map/all_to_all | solution.py:437
  53.1 2.6 %all-to-all-start.3 = ((f32[32,8,128]{2,1,0:T(8,128)}), f32[32,8,128]{2,1,0:T(8,128)S(1)}, u32[]{:S(2)}, u32[]{:S(2)}) async-start(f32[32,8,128]{2,1,0:T(8,128)} %broadcast_in_dim.21), calls=%async_computation.3 | async-start | bytes 262144 | tf_op jit(solution)/shard_map/all_to_all | solution.py:437
  55.7 12.7 %shard_map.64 = (f32[1,15,16,128]{3,2,1,0:T(8,128)S(1)}, f32[1,16,128]{2,1,0:T(8,128)S(1)}, f32[3,15,16,128]{3,2,1,0:T(8,128)S(1)}, f32[3,16,128]{2,1,0:T(8,128)S(1)}) custom-call(f32[8,15,16,128]{3,2,1,0:T(8,128)S(1)} %get-tuple-element.25.shifted, f32[8,8,128]{2,1,0:T(8,128)S(1)} %get-tuple-element.31.folded, f32[4,8,128]{2,1,0:T(8,128)S(1)} %all-to-all-done.4.gathered, ...), custom_call_target="tpu_custom_call" | custom-call | flops 54525952 | bytes 1818624 | tf_op jit(solution)/shard_map/pallas_call | solution.py:400
  68.5 11.9 %shard_map.65 = (f32[3,15,16,128]{3,2,1,0:T(8,128)S(1)}, f32[64,128]{1,0:T(8,128)S(1)}) custom-call(f32[8,8,8,128]{3,2,1,0:T(8,128)S(1)} %all_to_all.25.blocks, f32[32,8,128]{2,1,0:T(8,128)S(1)} %all-to-all-done.3.gathered, f32[1,8,8,128]{3,2,1,0:T(8,128)S(1)} %bitcast.2, s32[2,2,3,8,8,128]{5,4,3,2,1,0:T(8,128)S(1)} %copy-done, ...), custom_call_target="tpu_custom_call" | custom-call | flops 46137344 | bytes 1613824 | tf_op jit(solution)/shard_map/pallas_call | solution.py:400
  80.4 1.7 %collective-permute-start.3 = (f32[64,128]{1,0:T(8,128)S(1)}, f32[64,128]{1,0:T(8,128)S(1)}, u32[]{:S(2)}, u32[]{:S(2)}) collective-permute-start(f32[64,128]{1,0:T(8,128)S(1)} %get-tuple-element.38), channel_id=1, source_target_pairs={{0,1},{1,2},{2,3},{3,0},{4,5},{5,6},{6,7},{7,4},{8,9},{9,10},{10,1... | collective-permute-start | bytes 98312 | tf_op jit(solution)/shard_map/ppermute | solution.py:413
  82.1 2.1 %collective-permute-start.4 = (f32[64,128]{1,0:T(8,128)S(1)}, f32[64,128]{1,0:T(8,128)S(1)}, u32[]{:S(2)}, u32[]{:S(2)}) collective-permute-start(f32[64,128]{1,0:T(8,128)S(1)} %get-tuple-element.38), channel_id=1, source_target_pairs={{0,3},{1,0},{2,1},{3,2},{4,7},{5,4},{6,5},{7,6},{8,11},{9,8},{10,9... | collective-permute-start | bytes 98312 | tf_op jit(solution)/shard_map/ppermute | solution.py:413
  84.2 2.0 %collective-permute-done.3.rims_l = f32[64,128]{1,0:T(8,128)S(1)} collective-permute-done((f32[64,128]{1,0:T(8,128)S(1)}, f32[64,128]{1,0:T(8,128)S(1)}, u32[]{:S(2)}, u32[]{:S(2)}) %collective-permute-start.3) | collective-permute-done | bytes 32800 | tf_op jit(solution)/shard_map/ppermute | solution.py:413
  86.6 1.7 %collective-permute-start.5 = (f32[192,128]{1,0:T(8,128)S(1)}, f32[192,128]{1,0:T(8,128)S(1)}, u32[]{:S(2)}, u32[]{:S(2)}) collective-permute-start(f32[192,128]{1,0:T(8,128)S(1)} %get-tuple-element.40), channel_id=1, source_target_pairs={{0,24},{8,0},{16,8},{24,16},{1,25},{9,1},{17,9},{25,17},{2,26},{10... | collective-permute-start | bytes 294920 | tf_op jit(solution)/shard_map/ppermute | solution.py:413
  88.4 2.7 %collective-permute-done.5.from_right = f32[192,128]{1,0:T(8,128)S(1)} collective-permute-done((f32[192,128]{1,0:T(8,128)S(1)}, f32[192,128]{1,0:T(8,128)S(1)}, u32[]{:S(2)}, u32[]{:S(2)}) %collective-permute-start.5) | collective-permute-done | bytes 98336 | tf_op jit(solution)/shard_map/ppermute | solution.py:413
  91.1 1.5 %collective-permute-start.7 = (f32[32,8,128]{2,1,0:T(8,128)S(1)}, f32[32,8,128]{2,1,0:T(8,128)S(1)}, u32[]{:S(2)}, u32[]{:S(2)}) collective-permute-start(f32[32,8,128]{2,1,0:T(8,128)S(1)} %get-tuple-element.43), channel_id=1, source_target_pairs={{0,4},{4,0},{1,5},{5,1},{2,6},{6,2},{3,7},{7,3},{8,12},{12,8},{9,1... | collective-permute-start | bytes 393224 | tf_op jit(solution)/shard_map/ppermute | solution.py:413
  92.6 4.7 %collective-permute-done.7.from_y = f32[32,8,128]{2,1,0:T(8,128)S(1)} collective-permute-done((f32[32,8,128]{2,1,0:T(8,128)S(1)}, f32[32,8,128]{2,1,0:T(8,128)S(1)}, u32[]{:S(2)}, u32[]{:S(2)}) %collective-permute-start.7) | collective-permute-done | bytes 131104 | tf_op jit(solution)/shard_map/ppermute | solution.py:413
  (26 shorter events, 3.3 us)
Async XLA Ops:
  2.1 5.3 %copy-start.3 = (f32[8,8,128]{2,1,0:T(8,128)S(1)}, f32[8,8,128]{2,1,0:T(8,128)}, u32[]{:S(2)}) copy-start(f32[8,8,128]{2,1,0:T(8,128)} %intensity.1) | copy-start | bytes 98308
  2.1 11.3 %all-to-all-start = ((f32[8,8,8,128]{3,2,1,0:T(8,128)}), f32[8,8,8,128]{3,2,1,0:T(8,128)S(1)}, u32[]{:S(2)}, u32[]{:S(2)}) async-start(f32[8,8,8,128]{3,2,1,0:T(8,128)} %broadcast_in_dim.18), calls=%async_computation | async-start | bytes 524288 | tf_op jit(solution)/shard_map/all_to_all | solution.py:437
  14.1 17.8 %all-to-all-start.1 = ((f32[32,8,128]{2,1,0:T(8,128)}), f32[32,8,128]{2,1,0:T(8,128)S(1)}, u32[]{:S(2)}, u32[]{:S(2)}) async-start(f32[32,8,128]{2,1,0:T(8,128)} %broadcast_in_dim.19), calls=%async_computation.1 | async-start | bytes 262144 | tf_op jit(solution)/shard_map/all_to_all | solution.py:437
  19.0 18.3 %copy-start = (s32[2,2,3,8,8,128]{5,4,3,2,1,0:T(8,128)S(1)}, s32[2,2,3,8,8,128]{5,4,3,2,1,0:T(8,128)}, u32[]{:S(2)}) copy-start(s32[2,2,3,8,8,128]{5,4,3,2,1,0:T(8,128)} %cells.7) | copy-start | bytes 1179652
  19.0 18.3 %copy-start.1 = (f32[2,2,3,8,8,128]{5,4,3,2,1,0:T(8,128)S(1)}, f32[2,2,3,8,8,128]{5,4,3,2,1,0:T(8,128)}, u32[]{:S(2)}) copy-start(f32[2,2,3,8,8,128]{5,4,3,2,1,0:T(8,128)} %fracs.7) | copy-start | bytes 1179652
  23.1 4.7 %collective-permute-start = (f32[16,8,128]{2,1,0:T(8,128)}, f32[16,8,128]{2,1,0:T(8,128)S(1)}, u32[]{:S(2)}, u32[]{:S(2)}) collective-permute-start(f32[16,8,128]{2,1,0:T(8,128)} %get-tuple-element.27), channel_id=1, source_target_pairs={{0,4},{4,0},{1,5},{5,1},{2,6},{6,2},{3,7},{7,3},{8,12},{12,8},{9,1... | collective-permute-start | bytes 196616 | tf_op jit(solution)/shard_map/ppermute | solution.py:413
  27.8 0.8 copy-start.4
  28.6 3.3 %collective-permute-start.2 = (f32[5,8,128]{2,1,0:T(8,128)S(1)}, f32[5,8,128]{2,1,0:T(8,128)S(1)}, u32[]{:S(2)}, u32[]{:S(2)}) collective-permute-start(f32[5,8,128]{2,1,0:T(8,128)S(1)} %get-tuple-element.30), channel_id=1, source_target_pairs={{0,8},{8,16},{16,24},{24,0},{1,9},{9,17},{17,25},{25,1},{2,10},{10... | collective-permute-start | bytes 61448 | tf_op jit(solution)/shard_map/ppermute | solution.py:413
  28.7 3.2 %collective-permute-start.1 = (f32[4,8,128]{2,1,0:T(8,128)S(1)}, f32[4,8,128]{2,1,0:T(8,128)S(1)}, u32[]{:S(2)}, u32[]{:S(2)}) collective-permute-start(f32[4,8,128]{2,1,0:T(8,128)S(1)} %get-tuple-element.29), channel_id=1, source_target_pairs={{0,24},{8,0},{16,8},{24,16},{1,25},{9,1},{17,9},{25,17},{2,26},{10... | collective-permute-start | bytes 49160 | tf_op jit(solution)/shard_map/ppermute | solution.py:413
  32.6 10.3 %all-to-all-start.4 = ((f32[4,8,128]{2,1,0:T(8,128)}), f32[4,8,128]{2,1,0:T(8,128)S(1)}, u32[]{:S(2)}, u32[]{:S(2)}) async-start(f32[4,8,128]{2,1,0:T(8,128)} %broadcast_in_dim.23), calls=%async_computation.4 | async-start | bytes 32768 | tf_op jit(solution)/shard_map/all_to_all | solution.py:437
  53.1 15.3 %all-to-all-start.3 = ((f32[32,8,128]{2,1,0:T(8,128)}), f32[32,8,128]{2,1,0:T(8,128)S(1)}, u32[]{:S(2)}, u32[]{:S(2)}) async-start(f32[32,8,128]{2,1,0:T(8,128)} %broadcast_in_dim.21), calls=%async_computation.3 | async-start | bytes 262144 | tf_op jit(solution)/shard_map/all_to_all | solution.py:437
  55.7 12.8 %copy-start.2 = (f32[8,8,128]{2,1,0:T(8,128)S(1)}, f32[8,8,128]{2,1,0:T(8,128)}, u32[]{:S(2)}) copy-start(f32[8,8,128]{2,1,0:T(8,128)} %param.5) | copy-start | bytes 98308
  80.4 5.9 %collective-permute-start.3 = (f32[64,128]{1,0:T(8,128)S(1)}, f32[64,128]{1,0:T(8,128)S(1)}, u32[]{:S(2)}, u32[]{:S(2)}) collective-permute-start(f32[64,128]{1,0:T(8,128)S(1)} %get-tuple-element.38), channel_id=1, source_target_pairs={{0,1},{1,2},{2,3},{3,0},{4,5},{5,6},{6,7},{7,4},{8,9},{9,10},{10,1... | collective-permute-start | bytes 98312 | tf_op jit(solution)/shard_map/ppermute | solution.py:413
  82.1 4.3 %collective-permute-start.4 = (f32[64,128]{1,0:T(8,128)S(1)}, f32[64,128]{1,0:T(8,128)S(1)}, u32[]{:S(2)}, u32[]{:S(2)}) collective-permute-start(f32[64,128]{1,0:T(8,128)S(1)} %get-tuple-element.38), channel_id=1, source_target_pairs={{0,3},{1,0},{2,1},{3,2},{4,7},{5,4},{6,5},{7,6},{8,11},{9,8},{10,9... | collective-permute-start | bytes 98312 | tf_op jit(solution)/shard_map/ppermute | solution.py:413
  86.6 4.5 %collective-permute-start.6 = (f32[256,128]{1,0:T(8,128)S(1)}, f32[256,128]{1,0:T(8,128)S(1)}, u32[]{:S(2)}, u32[]{:S(2)}) collective-permute-start(f32[256,128]{1,0:T(8,128)S(1)} %get-tuple-element.41), channel_id=1, source_target_pairs={{0,8},{8,16},{16,24},{24,0},{1,9},{9,17},{17,25},{25,1},{2,10},{10... | collective-permute-start | bytes 393224 | tf_op jit(solution)/shard_map/ppermute | solution.py:413
  86.6 4.4 %collective-permute-start.5 = (f32[192,128]{1,0:T(8,128)S(1)}, f32[192,128]{1,0:T(8,128)S(1)}, u32[]{:S(2)}, u32[]{:S(2)}) collective-permute-start(f32[192,128]{1,0:T(8,128)S(1)} %get-tuple-element.40), channel_id=1, source_target_pairs={{0,24},{8,0},{16,8},{24,16},{1,25},{9,1},{17,9},{25,17},{2,26},{10... | collective-permute-start | bytes 294920 | tf_op jit(solution)/shard_map/ppermute | solution.py:413
  91.1 6.2 %collective-permute-start.7 = (f32[32,8,128]{2,1,0:T(8,128)S(1)}, f32[32,8,128]{2,1,0:T(8,128)S(1)}, u32[]{:S(2)}, u32[]{:S(2)}) collective-permute-start(f32[32,8,128]{2,1,0:T(8,128)S(1)} %get-tuple-element.43), channel_id=1, source_target_pairs={{0,4},{4,0},{1,5},{5,1},{2,6},{6,2},{3,7},{7,3},{8,12},{12,8},{9,1... | collective-permute-start | bytes 393224 | tf_op jit(solution)/shard_map/ppermute | solution.py:413

commit v4 on v0

--- a/solution.py
+++ b/solution.py
@@ -48,11 +48,11 @@
     )
 
 
-def write_tables(cells, fracs, step, section, weights, slopes=None):
+def write_tables(cells, fracs, weights, slopes=None):
     def plane(x, carry):
         for c in range(3):
-            k = cells[step, section, c, x]
-            t = fracs[step, section, c, x]
+            k = cells[c, x]
+            t = fracs[c, x]
             hits = {s: k == s for s in range(-2, 3)}
             for ref, taps in ((weights, cubic_weights), (slopes, cubic_slopes)):
                 if ref is None:
@@ -67,7 +67,7 @@
                     ref[c, j, x] = entry
         return carry
 
-    lax.fori_loop(0, cells.shape[3], plane, 0)
+    lax.fori_loop(0, cells.shape[1], plane, 0)
 
 
 def shift_planes(extended, rim, shifted):
@@ -86,31 +86,46 @@
 
 
 def interpolate(shifted, weights, slopes, nx, ny, emit):
-    def plane(x, carry):
-        tz = [weights[2, j, x] for j in range(SHIFTS)]
-        sz = None if slopes is None else [slopes[2, j, x] for j in range(SHIFTS)]
+    pair = 2 if nx % 2 == 0 else 1
+
+    def plane(step, carry):
+        x0 = step * pair
+        tz = [[weights[2, j, x0 + p] for j in range(SHIFTS)] for p in range(pair)]
+        if slopes is not None:
+            sz = [[slopes[2, j, x0 + p] for j in range(SHIFTS)] for p in range(pair)]
 
         def row(sy, sums):
-            ty = weights[1, sy, x]
-            a = b = c = None
-            for sx in range(SHIFTS):
-                window = [shifted[j, x + sx, pl.ds(sy + 1, ny), :] for j in range(SHIFTS)]
-                column = total([tz[j] * window[j] for j in range(SHIFTS)])
-                tx = weights[0, sx, x]
-                a = plus(a, tx * column)
-                if slopes is not None:
-                    b = plus(b, slopes[0, sx, x] * column)
-                    c = plus(c, tx * total([sz[j] * window[j] for j in range(SHIFTS)]))
-            if slopes is None:
-                return (sums[0] + ty * a,)
-            return (sums[0] + ty * b, sums[1] + slopes[1, sy, x] * a, sums[2] + ty * c)
+            a, b, c = [None] * pair, [None] * pair, [None] * pair
+            for q in range(SHIFTS + pair - 1):
+                window = [shifted[j, x0 + q, pl.ds(sy + 1, ny), :] for j in range(SHIFTS)]
+                for p in range(pair):
+                    sx = q - p
+                    if not 0 <= sx < SHIFTS:
+                        continue
+                    x = x0 + p
+                    column = total([tz[p][j] * window[j] for j in range(SHIFTS)])
+                    tx = weights[0, sx, x]
+                    a[p] = plus(a[p], tx * column)
+                    if slopes is not None:
+                        b[p] = plus(b[p], slopes[0, sx, x] * column)
+                        c[p] = plus(c[p], tx * total([sz[p][j] * window[j] for j in range(SHIFTS)]))
+            out = []
+            for p in range(pair):
+                ty = weights[1, sy, x0 + p]
+                if slopes is None:
+                    out.append((sums[p][0] + ty * a[p],))
+                else:
+                    steep = slopes[1, sy, x0 + p] * a[p]
+                    out.append((sums[p][0] + ty * b[p], sums[p][1] + steep, sums[p][2] + ty * c[p]))
+            return tuple(out)
 
         zero = jnp.zeros((ny, LANES), F32)
-        sums = lax.fori_loop(0, SHIFTS, row, (zero,) * (1 if slopes is None else 3))
-        emit(x, sums)
+        sums = lax.fori_loop(0, SHIFTS, row, ((zero,) * (1 if slopes is None else 3),) * pair)
+        for p in range(pair):
+            emit(x0 + p, sums[p])
         return carry
 
-    lax.fori_loop(0, nx, plane, 0)
+    lax.fori_loop(0, nx // pair, plane, 0)
 
 
 def total(terms):
@@ -123,35 +138,52 @@
     return b if a is None else a + b
 
 
-def deposit(sources, weights, scaled, piles):
+def deposit(sources, weights, scaled, piles, ys, js):
     channels, nx, ny, _ = sources.shape
-    planes = piles.shape[2]
+    planes = nx + LO + HI
     piles[...] = jnp.zeros(piles.shape, F32)
 
-    def row(sy, carry):
+    def scale(sy, carry):
         for x in range(nx):
             ty = weights[1, sy, x]
             for c in range(channels):
-                scaled[c, x] = sources[c, x] * ty
+                scaled[c, sy, x] = sources[c, x] * ty
+        return carry
+
+    lax.fori_loop(0, SHIFTS, scale, 0)
+
+    def row(step, carry):
+        first = step * ys
+        pending = []
+
+        def flush(count):
+            for _ in range(min(count, len(pending))):
+                c, y, j, X, value = pending.pop(0)
+                piles[c, j, X, pl.ds(first + y + 1, ny), :] += value
+
         for X in range(planes):
-            sums = [[None] * SHIFTS for _ in range(channels)]
-            for x in range(max(0, X - SHIFTS + 1), min(nx - 1, X) + 1):
-                tx = weights[0, X - x, x]
-                parts = [scaled[c, x] * tx for c in range(channels)]
-                for j in range(SHIFTS):
-                    tz = weights[2, j, x]
-                    for c in range(channels):
-                        sums[c][j] = plus(sums[c][j], parts[c] * tz)
-            for c in range(channels):
-                for j in range(SHIFTS):
-                    piles[c, j, X, pl.ds(sy + 1, ny), :] += sums[c][j]
+            xs = range(max(0, X - SHIFTS + 1), min(nx - 1, X) + 1)
+            for j0 in range(0, SHIFTS, js):
+                pace = -(-len(pending) // len(xs))
+                sums = {}
+                for x in xs:
+                    tx = weights[0, X - x, x]
+                    parts = {(c, y): scaled[c, first + y, x] * tx for c in range(channels) for y in range(ys)}
+                    for j in range(j0, j0 + js):
+                        tz = weights[2, j, x]
+                        for at, part in parts.items():
+                            sums[at + (j,)] = plus(sums.get(at + (j,)), part * tz)
+                    flush(pace)
+                flush(len(pending))
+                pending.extend(at + (X, value) for at, value in sums.items())
+        flush(len(pending))
         return carry
 
-    lax.fori_loop(0, SHIFTS, row, 0)
-
-
-def settle(piles, out, base=None):
-    channels, _, planes, rows, _ = piles.shape
+    lax.fori_loop(0, SHIFTS // ys, row, 0)
+
+
+def settle(piles, out, rims, base=None, base_rims=None):
+    channels, planes, rows, _ = out.shape
     lane = lane_of(rows)
     group = group_of(rows)
     for c in range(channels):
@@ -169,7 +201,7 @@
                 ends = ends + jnp.where(wraps, moved, 0.0)
             out[c, X] = core if base is None else core + base[c, X]
             rim = jnp.where(group == X, pltpu.roll(ends, (8 * X) % LANES, 1), rim)
-        out[c, planes] = rim if base is None else rim + base[c, planes]
+        rims[c] = rim if base_rims is None else rim + base_rims[c]
 
 
 def pack_rim(extended):
@@ -278,11 +310,31 @@
         put_edges(to_right_y, i, field[nx - LO + i], ny)
 
 
-def first_kernel(nx, ny, intensity, cotangent, cells, fracs, to_y, to_l, to_r, to_ly, to_ry, own, weights, scaled, piles, piled):
-    write_tables(cells, fracs, 1, 1, weights)
-    deposit(cotangent, weights, scaled, piles)
-    settle(piles, piled)
-    split_halo(intensity, (to_y, to_l, to_r, to_ly, to_ry), nx, ny)
+def first_kernel(
+    nx, ny, intensity, cotangent, cells, fracs,
+    to_y, to_l, to_r, to_ly, to_ry, own,
+    cells_here, fracs_here, cotangent_here, image, sems, weights, scaled, piles, piled, rims,
+):
+    copies = [
+        pltpu.make_async_copy(source, target, sems.at[i])
+        for i, (source, target) in enumerate(
+            (
+                (cells.at[1, 1], cells_here),
+                (fracs.at[1, 1], fracs_here),
+                (cotangent, cotangent_here),
+                (intensity, image),
+            )
+        )
+    ]
+    for copy in copies:
+        copy.start()
+    for copy in copies:
+        copy.wait()
+    write_tables(cells_here, fracs_here, weights)
+    deposit(cotangent_here, weights, scaled, piles, 2, SHIFTS)
+    settle(piles, piled.at[:, 0 : nx + LO + HI], rims)
+    piled[0, nx + LO + HI] = rims[0]
+    split_halo(image, (to_y, to_l, to_r, to_ly, to_ry), nx, ny)
     split_deposits(piled.at[0], (to_y, to_l, to_r, to_ly, to_ry, own), (nx, HI, LO, 0), nx, ny)
 
 
@@ -301,7 +353,7 @@
     rows = ny + 2 * ROWS
     rim = jnp.where(low_lanes(rows), rims_r[0:rows], rims_l[0:rows])
     shift_planes(extended, rim, shifted)
-    write_tables(cells, fracs, 0, 1, weights)
+    write_tables(cells.at[0, 1], fracs.at[0, 1], weights)
 
     def emit(x, sums):
         image[x] = sums[0]
@@ -313,90 +365,103 @@
         adjoint[0, x] = part[x] + unpack_rim(back, LO + x)
 
 
-def early_kernel(nx, ny, shifted, adjoint, cells, fracs, grad, piled, weights, slopes, scaled, piles):
-    write_tables(cells, fracs, 0, 1, weights, slopes)
+def early_kernel(nx, ny, shifted, adjoint, cells, fracs, grad, piled, rims, weights, slopes, scaled, piles):
+    write_tables(cells.at[0, 1], fracs.at[0, 1], weights, slopes)
 
     def emit(x, sums):
         for c in range(3):
             grad[c, x] = adjoint[0, x] * sums[c]
 
     interpolate(shifted, weights, slopes, nx, ny, emit)
-    deposit(adjoint, weights, scaled, piles)
-    settle(piles, piled)
-
-
-def early_spread_kernel(nx, ny, grad, cells, fracs, piled, weights, scaled, piles):
-    write_tables(cells, fracs, 0, 0, weights)
-    deposit(grad, weights, scaled, piles)
-    settle(piles, piled)
-
-
-def second_join_kernel(nx, ny, image, from_y, from_r, from_l, from_ry, from_ly, extended, rims):
+    deposit(adjoint, weights, scaled, piles, 2, SHIFTS)
+    settle(piles, piled, rims)
+
+
+def early_spread_kernel(nx, ny, grad, cells, fracs, piled, rims, weights, scaled, piles):
+    write_tables(cells.at[0, 0], fracs.at[0, 0], weights)
+    deposit(grad, weights, scaled, piles, 1, SHIFTS // 2)
+    settle(piles, piled, rims)
+
+
+def second_join_kernel(nx, ny, image, from_y, from_r, from_l, from_ry, from_ly, earlier, extended, rims):
     join_halo(image, (from_y, from_r, from_l, from_ry, from_ly), extended, nx, ny)
     rims[...] = pack_rim(extended)
 
 
 def late_kernel(
-    nx, ny, extended, rims_l, rims_r, cotangent, cells, fracs, piled_adjoint, piled_early,
-    to_y, to_l, to_r, to_ly, to_ry, own,
-    shifted, weights, slopes, grad, scaled, piles, piled,
+    nx, ny, extended, rims_l, rims_r, cotangent, cells, fracs, early, early_rims, adjoint_rims,
+    piled, rims,
+    shifted, weights, slopes, grad, scaled, rims_here, piles,
 ):
     rows = ny + 2 * ROWS
     shift_planes(extended, jnp.where(low_lanes(rows), rims_r[...], rims_l[...]), shifted)
-    write_tables(cells, fracs, 1, 1, weights, slopes)
+    write_tables(cells.at[1, 1], fracs.at[1, 1], weights, slopes)
 
     def emit(x, sums):
         for c in range(3):
             grad[c, x] = cotangent[0, x] * sums[c]
 
     interpolate(shifted, weights, slopes, nx, ny, emit)
-    write_tables(cells, fracs, 1, 0, weights)
-    deposit(grad, weights, scaled, piles)
-    settle(piles, piled, piled_early)
-    outs = (to_y, to_l, to_r, to_ly, to_ry, own)
+    write_tables(cells.at[1, 0], fracs.at[1, 0], weights)
+    deposit(grad, weights, scaled, piles, 1, SHIFTS // 2)
+    settle(piles, piled, rims_here, early, early_rims)
+    for c in range(3):
+        rims[c * rows : (c + 1) * rows] = rims_here[c]
+    rims[3 * rows : 4 * rows] = adjoint_rims[0]
+
+
+def last_z_kernel(nx, ny, velocity, adjoint, rims_l, rims_r, to_y, to_l, to_r, to_ly, to_ry, own):
+    rows = ny + 2 * ROWS
+    low = low_lanes(rows)
+    core = slice(ROWS, ROWS + ny)
     for c in range(4):
-        source = piled_adjoint.at[0] if c == 0 else piled.at[c - 1]
-        at = (c * (nx + 1), c * (LO + 1), c * (HI + 1), c * (nx + 1))
-        split_deposits(source, outs, at, nx, ny)
-
-
-def last_join_kernel(nx, ny, from_y, from_r, from_l, from_ry, from_ly, own, part, rims):
-    ins = (from_y, from_r, from_l, from_ry, from_ly, own)
+        here = slice(c * rows, (c + 1) * rows)
+        back = jnp.where(low, rims_l[here], rims_r[here])
+        for X in range(nx + LO + HI):
+            plane = (velocity[c, X] if c < 3 else adjoint[0, X]) + unpack_rim(back, X)
+            if X < LO:
+                straight, corner, at = to_l, to_ly, c * LO + X
+            elif X < LO + nx:
+                straight, corner, at = own, to_y, c * nx + X - LO
+            else:
+                straight, corner, at = to_r, to_ry, c * HI + X - LO - nx
+            straight[at] = plane[core]
+            put_rims(corner, at, plane, ny)
+
+
+def last_kernel(nx, ny, own, from_y, from_r, from_l, from_ry, from_ly, intensity_adjoint, velocity_adjoint):
     for c in range(4):
-
-        def put(x, plane, c=c):
-            part[c, x] = plane
-
-        at = (c * (nx + 1), c * (LO + 1), c * (HI + 1), c * (nx + 1))
-        rims[c * ny : (c + 1) * ny] = join_deposits(ins, at, nx, ny, put)
-
-
-def last_kernel(nx, ny, part, rims_l, rims_r, intensity_adjoint, velocity_adjoint):
-    low = low_lanes(ny)
-    for c in range(4):
-        rows = slice(c * ny, (c + 1) * ny)
-        back = jnp.where(low, rims_l[rows], rims_r[rows])
         for x in range(nx):
-            plane = part[c, x] + unpack_rim(back, LO + x)
-            if c == 0:
+            at = c * nx + x
+            plane = own[at] + fold_rows(from_y[at], ny)
+            if x >= nx - LO:
+                at = c * LO + x - (nx - LO)
+                plane = plane + from_r[at] + fold_rows(from_ry[at], ny)
+            if x < HI:
+                at = c * HI + x
+                plane = plane + from_l[at] + fold_rows(from_ly[at], ny)
+            if c == 3:
                 intensity_adjoint[x] = plane
             else:
-                velocity_adjoint[c - 1, x] = plane
-
-
-def call(kernel, args, outs, scratch, flops):
+                velocity_adjoint[c, x] = plane
+
+
+def call(kernel, args, outs, scratch, flops, spaces=None, limit=24):
     def struct(shape):
         return jax.ShapeDtypeStruct(shape, F32)
 
     in_vmem = pl.BlockSpec(memory_space=pltpu.VMEM)
+    in_specs = [in_vmem] * len(args)
+    for i, space in (spaces or {}).items():
+        in_specs[i] = pl.BlockSpec(memory_space=space)
     moved = 4 * sum(a.size for a in args)
     return pl.pallas_call(
         kernel,
         out_shape=[struct(s) for s in outs],
-        in_specs=[in_vmem] * len(args),
+        in_specs=in_specs,
         out_specs=[in_vmem] * len(outs),
-        scratch_shapes=[pltpu.VMEM(s, F32) for s in scratch],
-        compiler_params=pltpu.CompilerParams(vmem_limit_bytes=24 * 1024 * 1024),
+        scratch_shapes=[pltpu.VMEM(s, F32) if isinstance(s, tuple) else s for s in scratch],
+        compiler_params=pltpu.CompilerParams(vmem_limit_bytes=limit * 1024 * 1024),
         cost_estimate=pl.CostEstimate(flops=flops, bytes_accessed=moved, transcendentals=0),
     )(*args)
 
@@ -438,114 +503,102 @@
     return send(rims, (("gz", 1),)), send(rims, (("gz", -1),))
 
 
+FIRST_LIMIT = 56
+
+
 def body(intensity, cotangent, cells, fracs):
     nx, ny, nz = intensity.shape
     rows = ny + 2 * ROWS
     planes = nx + LO + HI
-    table = (3, SHIFTS, nx, ny, nz)
-    bound = functools.partial
     ring = 2 * ROWS
-
-    def pile(channels):
-        return [(channels, nx, ny, nz), (channels, SHIFTS, planes, rows, nz)]
-
-    def piled(channels):
-        return (channels, planes + 1, rows, nz)
-
+    field = (nx, ny, nz)
+    table = (3, SHIFTS) + field
     cotangent = cotangent[None]
     unit = nx * ny * nz * 512
 
-    y_planes, l_planes, r_planes = nx, HI, LO
-    *outs, own = call(
-        bound(first_kernel, nx, ny),
+    def run(kernel, *rest, **more):
+        return call(functools.partial(kernel, nx, ny), *rest, **more)
+
+    def pile(channels):
+        return [(channels, SHIFTS) + field, (channels, SHIFTS, planes, rows, nz)]
+
+    def piled(channels):
+        return [(channels, planes, rows, nz), (channels, rows, nz)]
+
+    def messages(y, l, r):
+        return [(y, ring, nz), (l, ny, nz), (r, ny, nz), (l, ring, nz), (r, ring, nz)]
+
+    part = (3,) + field
+    *outs, own = run(
+        first_kernel,
         (intensity, cotangent, cells, fracs),
-        [
-            (2 * nx + 1, ring, nz),
-            (HI + LO + 1, ny, nz),
-            (LO + HI + 1, ny, nz),
-            (HI + LO + 1, ring, nz),
-            (LO + HI + 1, ring, nz),
-            (nx + 1, ny, nz),
-        ],
-        [table] + pile(1) + [piled(1)],
+        messages(2 * nx + 1, HI + LO + 1, LO + HI + 1) + [(nx + 1, ny, nz)],
+        [pltpu.VMEM(part, jnp.int32), part, (1,) + field, field, pltpu.SemaphoreType.DMA((4,)), table]
+        + pile(1)
+        + [(1, planes + 1, rows, nz), (1, rows, nz)],
         2 * unit,
-    )
-    sides = send_sides(*outs)
-    extended, part, rims = call(
-        bound(first_join_kernel, nx, ny),
-        (intensity,) + sides + (own,),
-        [(planes, rows, nz), (nx, ny, nz), (rows + ny, nz)],
+        spaces=dict.fromkeys(range(4), pltpu.HBM),
+        limit=FIRST_LIMIT,
+    )
+    extended, folded, rims = run(
+        first_join_kernel,
+        (intensity,) + send_sides(*outs) + (own,),
+        [(planes, rows, nz), field, (rows + ny, nz)],
         [],
         unit // 16,
     )
-    rims_l, rims_r = send_z(rims)
-    image, *outs, shifted, adjoint = call(
-        bound(middle_kernel, nx, ny),
-        (extended, rims_l, rims_r, part, cells, fracs),
-        [
-            (nx, ny, nz),
-            (nx, ring, nz),
-            (HI, ny, nz),
-            (LO, ny, nz),
-            (HI, ring, nz),
-            (LO, ring, nz),
-            (SHIFTS, planes, rows, nz),
-            (1, nx, ny, nz),
-        ],
+    image, *outs, shifted, adjoint = run(
+        middle_kernel,
+        (extended,) + send_z(rims) + (folded, cells, fracs),
+        [field] + messages(nx, HI, LO) + [(SHIFTS, planes, rows, nz), (1,) + field],
         [table],
         2 * unit,
     )
+
     sides = send_sides(*outs)
-    grad, piled_adjoint = call(
-        bound(early_kernel, nx, ny),
+    grad, piled_adjoint, adjoint_rims = run(
+        early_kernel,
         (shifted, adjoint, cells, fracs),
-        [(3, nx, ny, nz), piled(1)],
+        [(3,) + field] + piled(1),
         [table, table] + pile(1),
         7 * unit,
     )
-    extended, rims = call(
-        bound(second_join_kernel, nx, ny),
-        (image,) + sides,
+    extended, rims = run(
+        second_join_kernel,
+        (image,) + sides + (grad,),
         [(planes, rows, nz), (rows, nz)],
         [],
         unit // 16,
+        spaces={6: pl.ANY},
     )
     rims_l, rims_r = send_z(rims)
-    (piled_early,) = call(
-        bound(early_spread_kernel, nx, ny),
+    early, early_rims = run(
+        early_spread_kernel,
         (grad, cells, fracs),
-        [piled(3)],
+        piled(3),
         [table] + pile(3),
         6 * unit,
     )
-    *outs, own = call(
-        bound(late_kernel, nx, ny),
-        (extended, rims_l, rims_r, cotangent, cells, fracs, piled_adjoint, piled_early),
-        [
-            (4 * (nx + 1), ring, nz),
-            (4 * (LO + 1), ny, nz),
-            (4 * (HI + 1), ny, nz),
-            (4 * (LO + 1), ring, nz),
-            (4 * (HI + 1), ring, nz),
-            (4 * (nx + 1), ny, nz),
-        ],
-        [(SHIFTS, planes, rows, nz), table, table, (3, nx, ny, nz)] + pile(3) + [piled(3)],
+
+    velocity, rims = run(
+        late_kernel,
+        (extended, rims_l, rims_r, cotangent, cells, fracs, early, early_rims, adjoint_rims),
+        [(3, planes, rows, nz), (4 * rows, nz)],
+        [(SHIFTS, planes, rows, nz), table, table, (3,) + field, pile(3)[0], (3, rows, nz), pile(3)[1]],
         11 * unit,
     )
-    sides = send_sides(*outs)
-    part, rims = call(
-        bound(last_join_kernel, nx, ny),
-        sides + (own,),
-        [(4, nx, ny, nz), (4 * ny, nz)],
+    *outs, own = run(
+        last_z_kernel,
+        (velocity, piled_adjoint) + send_z(rims),
+        messages(4 * nx, 4 * LO, 4 * HI) + [(4 * nx, ny, nz)],
         [],
         unit // 16,
     )
-    rims_l, rims_r = send_z(rims)
     return tuple(
-        call(
-            bound(last_kernel, nx, ny),
-            (part, rims_l, rims_r),
-            [(nx, ny, nz), (3, nx, ny, nz)],
+        run(
+            last_kernel,
+            (own,) + send_sides(*outs),
+            [field, (3,) + field],
             [],
             unit // 16,
         )

time: 74.8 us -> 74.7 us (level)
  waiting for transfers between devices: 13.3 us -> 18.5 us
  starting transfers between devices: 26.6 us -> 21.9 us
  local copies, waits for them, and re-layouts: 3.51 us -> 0.79 us
  Pallas kernels: 30.4 us -> 32.3 us
    ppermute x15, waiting for transfers between devices: 5.9 us -> 14 us  [send(): return lax.ppermute(message, axes[0], pairs)]
    ppermute x15, starting transfers between devices: 21.3 us -> 14.2 us  [send(): return lax.ppermute(message, axes[0], pairs)]
    ppermute x6, waiting for transfers between devices: 7.35 us -> 4.53 us  [send(): return lax.ppermute(message, axes, pairs)]
    unnamed x14 -> x10, local copies, waits for them, and re-layouts: 3.51 us -> 0.79 us
    ppermute x6, starting transfers between devices: 5.32 us -> 7.76 us  [send(): return lax.ppermute(message, axes, pairs)]
    pallas_call x9, Pallas kernels: 30.4 us -> 32.3 us  [call(): pl.pallas_call(kernel, out_shape=[struct(s) for s in outs], in_specs=in_s...]
  transfers between devices with their start and end apart: 21 -> 21, of which waited for: 7 -> 10; matrix products, arithmetic and copies ran while one was open for 0% -> 0% of each run, Pallas kernels for 17% -> 17%
where the time goes in v4:
time: 74.7 us; the launch traced here: 74.3 us
  Pallas kernels  32.3 us (43%)
  starting transfers between devices  21.9 us (29%)
  waiting for transfers between devices  18.5 us (25%)
  local copies, waits for them, and re-layouts  0.79 us (1%)
  between operations  0.77 us (1%)
    pallas_call x9, Pallas kernels, call(): pl.pallas_call(kernel, out_shape=[struct(s) for s in outs], in_specs=in_s...  32.3 us
    ppermute x15, starting transfers between devices, send(): return lax.ppermute(message, axes[0], pairs)  14.2 us
    ppermute x15, waiting for transfers between devices, send(): return lax.ppermute(message, axes[0], pairs)  14 us
    ppermute x6, starting transfers between devices, send(): return lax.ppermute(message, axes, pairs)  7.76 us
    ppermute x6, waiting for transfers between devices, send(): return lax.ppermute(message, axes, pairs)  4.53 us
  transfers between devices with their start and end apart: 21, of which 10 were waited for; matrix products, arithmetic and copies ran while one was open for 0% of the time, Pallas kernels for 17%

profile of v4, /device:TPU:0, one launch (start us, length us, event | category | flops | bytes accessed | tf_op | source)
XLA Modules:
  0.0 74.3 jit_solution(6109006553754496204)
XLA Ops:
  0.7 4.4 %shard_map.59 = (f32[17,8,128]{2,1,0:T(8,128)}, f32[8,8,128]{2,1,0:T(8,128)}, f32[8,8,128]{2,1,0:T(8,128)}, f32[8,8,128]{2,1,0:T(8,128)}, f32[8,8,128]{2,1,0:T(8,128)}, /*index=5*/f32[9,8,128]{2,1,0:T(8,128)}) custom-call(f32[8,8,128]{2,1,0:T(8,128)} %intensity.3, f32[1,8,8,128]{3,2,1,0:T(8,128)} %bitcast.1, s32[2,2,3,8,8,128]{5,4,3,2,1,0:T(8,128)} %cells.9, ...), custom_call_target="tpu_custom_call" | custom-call | flops 8388608 | bytes 851968 | tf_op jit(solution)/shard_map/pallas_call | solution.py:458
  5.0 3.0 %collective-permute-start = (f32[17,8,128]{2,1,0:T(8,128)}, f32[17,8,128]{2,1,0:T(8,128)S(1)}, u32[]{:S(2)}, u32[]{:S(2)}) collective-permute-start(f32[17,8,128]{2,1,0:T(8,128)} %get-tuple-element.34), channel_id=1, source_target_pairs={{0,4},{4,0},{1,5},{5,1},{2,6},{6,2},{3,7},{7,3},{8,12},{12,8},{9,1... | collective-permute-start | bytes 208904 | tf_op jit(solution)/shard_map/ppermute | solution.py:474
  8.7 1.7 %collective-permute-start.3 = (f32[8,8,128]{2,1,0:T(8,128)}, f32[8,8,128]{2,1,0:T(8,128)S(1)}, u32[]{:S(2)}, u32[]{:S(2)}) collective-permute-start(f32[8,8,128]{2,1,0:T(8,128)} %get-tuple-element.37), channel_id=1, source_target_pairs={{0,28},{4,24},{8,4},{12,0},{16,12},{20,8},{24,20},{28,16},{1,29},{... | collective-permute-start | bytes 98312 | tf_op jit(solution)/shard_map/ppermute | solution.py:480
  10.6 1.6 %collective-permute-done.2.from_l = f32[8,8,128]{2,1,0:T(8,128)S(1)} collective-permute-done((f32[8,8,128]{2,1,0:T(8,128)}, f32[8,8,128]{2,1,0:T(8,128)S(1)}, u32[]{:S(2)}, u32[]{:S(2)}) %collective-permute-start.2) | collective-permute-done | bytes 32800 | tf_op jit(solution)/shard_map/ppermute | solution.py:474
  12.3 2.5 %collective-permute-done.4.from_ly = f32[8,8,128]{2,1,0:T(8,128)S(1)} collective-permute-done((f32[8,8,128]{2,1,0:T(8,128)}, f32[8,8,128]{2,1,0:T(8,128)S(1)}, u32[]{:S(2)}, u32[]{:S(2)}) %collective-permute-start.4) | collective-permute-done | bytes 32800 | tf_op jit(solution)/shard_map/ppermute | solution.py:480
  14.9 0.8 %copy-done.4 = f32[9,8,128]{2,1,0:T(8,128)S(1)} copy-done((f32[9,8,128]{2,1,0:T(8,128)S(1)}, f32[9,8,128]{2,1,0:T(8,128)}, u32[]{:S(2)}) %copy-start.4) | copy-done | bytes 36888
  15.7 3.7 %collective-permute-start.6 = (f32[24,128]{1,0:T(8,128)S(1)}, f32[24,128]{1,0:T(8,128)S(1)}, u32[]{:S(2)}, u32[]{:S(2)}) collective-permute-start(f32[24,128]{1,0:T(8,128)S(1)} %get-tuple-element.41), channel_id=1, source_target_pairs={{0,3},{1,0},{2,1},{3,2},{4,7},{5,4},{6,5},{7,6},{8,11},{9,8},{10,9... | collective-permute-start | bytes 36872 | tf_op jit(solution)/shard_map/ppermute | solution.py:474
  19.4 1.4 %collective-permute-done.6.rims_r = f32[24,128]{1,0:T(8,128)S(1)} collective-permute-done((f32[24,128]{1,0:T(8,128)S(1)}, f32[24,128]{1,0:T(8,128)S(1)}, u32[]{:S(2)}, u32[]{:S(2)}) %collective-permute-start.6) | collective-permute-done | bytes 12320 | tf_op jit(solution)/shard_map/ppermute | solution.py:474
  20.8 4.1 %collective-permute-done.5.rims_l = f32[24,128]{1,0:T(8,128)S(1)} collective-permute-done((f32[24,128]{1,0:T(8,128)S(1)}, f32[24,128]{1,0:T(8,128)S(1)}, u32[]{:S(2)}, u32[]{:S(2)}) %collective-permute-start.5) | collective-permute-done | bytes 12320 | tf_op jit(solution)/shard_map/ppermute | solution.py:474
  24.9 2.6 %shard_map.61 = (f32[8,8,128]{2,1,0:T(8,128)S(1)}, f32[8,8,128]{2,1,0:T(8,128)S(1)}, f32[4,8,128]{2,1,0:T(8,128)S(1)}, f32[3,8,128]{2,1,0:T(8,128)S(1)}, f32[4,8...) custom-call(f32[15,16,128]{2,1,0:T(8,128)S(1)} %get-tuple-element.40, ...), custom_call_target="tpu_custom_call" | custom-call | flops 8388608 | bytes 966656 | tf_op jit(solution)/shard_map/pallas_call | solution.py:458
  27.5 1.5 %collective-permute-start.7 = (f32[8,8,128]{2,1,0:T(8,128)S(1)}, f32[8,8,128]{2,1,0:T(8,128)S(1)}, u32[]{:S(2)}, u32[]{:S(2)}) collective-permute-start(f32[8,8,128]{2,1,0:T(8,128)S(1)} %get-tuple-element.44), channel_id=1, source_target_pairs={{0,4},{4,0},{1,5},{5,1},{2,6},{6,2},{3,7},{7,3},{8,12},{12,8},{9,1... | collective-permute-start | bytes 98312 | tf_op jit(solution)/shard_map/ppermute | solution.py:474
  29.0 1.0 %collective-permute-start.10 = (f32[4,8,128]{2,1,0:T(8,128)S(1)}, f32[4,8,128]{2,1,0:T(8,128)S(1)}, u32[]{:S(2)}, u32[]{:S(2)}) collective-permute-start(f32[4,8,128]{2,1,0:T(8,128)S(1)} %get-tuple-element.47), channel_id=1, source_target_pairs={{0,28},{4,24},{8,4},{12,0},{16,12},{20,8},{24,20},{28,16},{1,29},{... | collective-permute-start | bytes 49160 | tf_op jit(solution)/shard_map/ppermute | solution.py:480
  30.1 2.3 %collective-permute-start.11 = (f32[3,8,128]{2,1,0:T(8,128)S(1)}, f32[3,8,128]{2,1,0:T(8,128)S(1)}, u32[]{:S(2)}, u32[]{:S(2)}) collective-permute-start(f32[3,8,128]{2,1,0:T(8,128)S(1)} %get-tuple-element.48), channel_id=1, source_target_pairs={{0,12},{4,8},{8,20},{12,16},{16,28},{20,24},{24,4},{28,0},{1,13},{... | collective-permute-start | bytes 36872 | tf_op jit(solution)/shard_map/ppermute | solution.py:480
  32.3 5.6 %shard_map.62 = (f32[3,8,8,128]{3,2,1,0:T(8,128)S(1)}, f32[1,15,16,128]{3,2,1,0:T(8,128)S(1)}, f32[1,16,128]{2,1,0:T(8,128)S(1)}) custom-call(f32[8,15,16,128]{3,2,1,0:T(8,128)S(1)} %get-tuple-element.49.shifted, f32[1,8,8,128]{3,2,1,0:T(8,128)S(1)} %get-tuple-element.50.adjoint, s32[2,2,3,8,8,128]{5,4,3,2,1,0:T(8,128)S(1)} %copy-done, ...), custom_call_target="tpu_custom_call" | custom-call | flops 29360128 | bytes 1802240 | tf_op jit(solution)/shard_map/pallas_call | solution.py:458
  38.2 2.0 %collective-permute-start.12 = (f32[16,128]{1,0:T(8,128)S(1)}, f32[16,128]{1,0:T(8,128)S(1)}, u32[]{:S(2)}, u32[]{:S(2)}) collective-permute-start(f32[16,128]{1,0:T(8,128)S(1)} %get-tuple-element.53), channel_id=1, source_target_pairs={{0,1},{1,2},{2,3},{3,0},{4,5},{5,6},{6,7},{7,4},{8,9},{9,10},{10,1... | collective-permute-start | bytes 24584 | tf_op jit(solution)/shard_map/ppermute | solution.py:474
  40.2 7.3 %shard_map.64 = (f32[3,15,16,128]{3,2,1,0:T(8,128)S(1)}, f32[3,16,128]{2,1,0:T(8,128)S(1)}) custom-call(f32[3,8,8,128]{3,2,1,0:T(8,128)S(1)} %get-tuple-element.51.earlier.grad, s32[2,2,3,8,8,128]{5,4,3,2,1,0:T(8,128)S(1)} %copy-done, f32[2,2,3,8,8,128]{5,4,3,2,1,0:T(8,128)S(1)} %copy-done.1), custom_call_target="tpu_custom_call" | custom-call | flops 25165824 | bytes 884736 | tf_op jit(solution)/shard_map/pallas_call | solution.py:458
  47.6 11.3 %shard_map.65 = (f32[3,15,16,128]{3,2,1,0:T(8,128)S(1)}, f32[64,128]{1,0:T(8,128)S(1)}) custom-call(f32[15,16,128]{2,1,0:T(8,128)S(1)} %get-tuple-element.52.extended, f32[16,128]{1,0:T(8,128)S(1)} %collective-permute-done.12.rims_l, f32[16,128]{1,0:T(8,128)S(1)} %collective-permute-done.13.rims_r, f32[1,8,8,128]{3,2,1,0:T(8,128)S(1)} %bitcast.2, ...), custom_call_target="tpu_custom_call" | custom-call | flops 46137344 | bytes 1359872 | tf_op jit(solution)/shard_map/pallas_call | solution.py:458
  58.9 1.9 %collective-permute-start.15 = (f32[64,128]{1,0:T(8,128)S(1)}, f32[64,128]{1,0:T(8,128)S(1)}, u32[]{:S(2)}, u32[]{:S(2)}) collective-permute-start(f32[64,128]{1,0:T(8,128)S(1)} %get-tuple-element.59), channel_id=1, source_target_pairs={{0,3},{1,0},{2,1},{3,2},{4,7},{5,4},{6,5},{7,6},{8,11},{9,8},{10,9... | collective-permute-start | bytes 98312 | tf_op jit(solution)/shard_map/ppermute | solution.py:474
  61.0 1.9 %collective-permute-done.15.rims_r = f32[64,128]{1,0:T(8,128)S(1)} collective-permute-done((f32[64,128]{1,0:T(8,128)S(1)}, f32[64,128]{1,0:T(8,128)S(1)}, u32[]{:S(2)}, u32[]{:S(2)}) %collective-permute-start.15) | collective-permute-done | bytes 32800 | tf_op jit(solution)/shard_map/ppermute | solution.py:474
  62.8 3.7 %collective-permute-done.14.rims_l = f32[64,128]{1,0:T(8,128)S(1)} collective-permute-done((f32[64,128]{1,0:T(8,128)S(1)}, f32[64,128]{1,0:T(8,128)S(1)}, u32[]{:S(2)}, u32[]{:S(2)}) %collective-permute-start.14) | collective-permute-done | bytes 32800 | tf_op jit(solution)/shard_map/ppermute | solution.py:474
  67.3 2.1 %collective-permute-start.20 = (f32[16,8,128]{2,1,0:T(8,128)S(1)}, f32[16,8,128]{2,1,0:T(8,128)S(1)}, u32[]{:S(2)}, u32[]{:S(2)}) collective-permute-start(f32[16,8,128]{2,1,0:T(8,128)S(1)} %get-tuple-element.65), channel_id=1, source_target_pairs={{0,12},{4,8},{8,20},{12,16},{16,28},{20,24},{24,4},{28,0},{1,13},{... | collective-permute-start | bytes 196616 | tf_op jit(solution)/shard_map/ppermute | solution.py:480
  70.6 1.1 %collective-permute-done.17.from_r = f32[12,8,128]{2,1,0:T(8,128)S(1)} collective-permute-done((f32[12,8,128]{2,1,0:T(8,128)S(1)}, f32[12,8,128]{2,1,0:T(8,128)S(1)}, u32[]{:S(2)}, u32[]{:S(2)}) %collective-permute-start.17) | collective-permute-done | bytes 49184 | tf_op jit(solution)/shard_map/ppermute | solution.py:474
  71.7 1.9 %collective-permute-done.19.from_ry = f32[12,8,128]{2,1,0:T(8,128)S(1)} collective-permute-done((f32[12,8,128]{2,1,0:T(8,128)S(1)}, f32[12,8,128]{2,1,0:T(8,128)S(1)}, u32[]{:S(2)}, u32[]{:S(2)}) %collective-permute-start.19) | collective-permute-done | bytes 49184 | tf_op jit(solution)/shard_map/ppermute | solution.py:480
  73.7 0.7 shard_map.67
  (37 shorter events, 3.4 us)
Async XLA Ops:
  0.6 14.2 %copy-start.2 = (f32[8,8,128]{2,1,0:T(8,128)S(1)}, f32[8,8,128]{2,1,0:T(8,128)}, u32[]{:S(2)}) copy-start(f32[8,8,128]{2,1,0:T(8,128)} %intensity.3) | copy-start | bytes 98308
  0.6 24.2 %copy-start = (s32[2,2,3,8,8,128]{5,4,3,2,1,0:T(8,128)S(1)}, s32[2,2,3,8,8,128]{5,4,3,2,1,0:T(8,128)}, u32[]{:S(2)}) copy-start(s32[2,2,3,8,8,128]{5,4,3,2,1,0:T(8,128)} %cells.9) | copy-start | bytes 1179652
  0.6 24.2 %copy-start.1 = (f32[2,2,3,8,8,128]{5,4,3,2,1,0:T(8,128)S(1)}, f32[2,2,3,8,8,128]{5,4,3,2,1,0:T(8,128)}, u32[]{:S(2)}) copy-start(f32[2,2,3,8,8,128]{5,4,3,2,1,0:T(8,128)} %fracs.9) | copy-start | bytes 1179652
  5.0 9.8 %collective-permute-start = (f32[17,8,128]{2,1,0:T(8,128)}, f32[17,8,128]{2,1,0:T(8,128)S(1)}, u32[]{:S(2)}, u32[]{:S(2)}) collective-permute-start(f32[17,8,128]{2,1,0:T(8,128)} %get-tuple-element.34), channel_id=1, source_target_pairs={{0,4},{4,0},{1,5},{5,1},{2,6},{6,2},{3,7},{7,3},{8,12},{12,8},{9,1... | collective-permute-start | bytes 208904 | tf_op jit(solution)/shard_map/ppermute | solution.py:474
  8.1 2.6 %collective-permute-start.1 = (f32[8,8,128]{2,1,0:T(8,128)}, f32[8,8,128]{2,1,0:T(8,128)S(1)}, u32[]{:S(2)}, u32[]{:S(2)}) collective-permute-start(f32[8,8,128]{2,1,0:T(8,128)} %get-tuple-element.35), channel_id=1, source_target_pairs={{0,24},{8,0},{16,8},{24,16},{1,25},{9,1},{17,9},{25,17},{2,26},{10... | collective-permute-start | bytes 98312 | tf_op jit(solution)/shard_map/ppermute | solution.py:474
  8.7 3.6 %collective-permute-start.2 = (f32[8,8,128]{2,1,0:T(8,128)}, f32[8,8,128]{2,1,0:T(8,128)S(1)}, u32[]{:S(2)}, u32[]{:S(2)}) collective-permute-start(f32[8,8,128]{2,1,0:T(8,128)} %get-tuple-element.36), channel_id=1, source_target_pairs={{0,8},{8,16},{16,24},{24,0},{1,9},{9,17},{17,25},{25,1},{2,10},{10... | collective-permute-start | bytes 98312 | tf_op jit(solution)/shard_map/ppermute | solution.py:474
  8.7 3.6 %collective-permute-start.3 = (f32[8,8,128]{2,1,0:T(8,128)}, f32[8,8,128]{2,1,0:T(8,128)S(1)}, u32[]{:S(2)}, u32[]{:S(2)}) collective-permute-start(f32[8,8,128]{2,1,0:T(8,128)} %get-tuple-element.37), channel_id=1, source_target_pairs={{0,28},{4,24},{8,4},{12,0},{16,12},{20,8},{24,20},{28,16},{1,29},{... | collective-permute-start | bytes 98312 | tf_op jit(solution)/shard_map/ppermute | solution.py:480
  10.4 4.4 %collective-permute-start.4 = (f32[8,8,128]{2,1,0:T(8,128)}, f32[8,8,128]{2,1,0:T(8,128)S(1)}, u32[]{:S(2)}, u32[]{:S(2)}) collective-permute-start(f32[8,8,128]{2,1,0:T(8,128)} %get-tuple-element.38), channel_id=1, source_target_pairs={{0,12},{4,8},{8,20},{12,16},{16,28},{20,24},{24,4},{28,0},{1,13},{... | collective-permute-start | bytes 98312 | tf_op jit(solution)/shard_map/ppermute | solution.py:480
  15.7 5.1 %collective-permute-start.6 = (f32[24,128]{1,0:T(8,128)S(1)}, f32[24,128]{1,0:T(8,128)S(1)}, u32[]{:S(2)}, u32[]{:S(2)}) collective-permute-start(f32[24,128]{1,0:T(8,128)S(1)} %get-tuple-element.41), channel_id=1, source_target_pairs={{0,3},{1,0},{2,1},{3,2},{4,7},{5,4},{6,5},{7,6},{8,11},{9,8},{10,9... | collective-permute-start | bytes 36872 | tf_op jit(solution)/shard_map/ppermute | solution.py:474
  19.4 5.5 %collective-permute-start.5 = (f32[24,128]{1,0:T(8,128)S(1)}, f32[24,128]{1,0:T(8,128)S(1)}, u32[]{:S(2)}, u32[]{:S(2)}) collective-permute-start(f32[24,128]{1,0:T(8,128)S(1)} %get-tuple-element.41), channel_id=1, source_target_pairs={{0,1},{1,2},{2,3},{3,0},{4,5},{5,6},{6,7},{7,4},{8,9},{9,10},{10,1... | collective-permute-start | bytes 36872 | tf_op jit(solution)/shard_map/ppermute | solution.py:474
  27.5 10.5 %collective-permute-start.7 = (f32[8,8,128]{2,1,0:T(8,128)S(1)}, f32[8,8,128]{2,1,0:T(8,128)S(1)}, u32[]{:S(2)}, u32[]{:S(2)}) collective-permute-start(f32[8,8,128]{2,1,0:T(8,128)S(1)} %get-tuple-element.44), channel_id=1, source_target_pairs={{0,4},{4,0},{1,5},{5,1},{2,6},{6,2},{3,7},{7,3},{8,12},{12,8},{9,1... | collective-permute-start | bytes 98312 | tf_op jit(solution)/shard_map/ppermute | solution.py:474
  29.0 9.0 %collective-permute-start.8 = (f32[4,8,128]{2,1,0:T(8,128)S(1)}, f32[4,8,128]{2,1,0:T(8,128)S(1)}, u32[]{:S(2)}, u32[]{:S(2)}) collective-permute-start(f32[4,8,128]{2,1,0:T(8,128)S(1)} %get-tuple-element.45), channel_id=1, source_target_pairs={{0,24},{8,0},{16,8},{24,16},{1,25},{9,1},{17,9},{25,17},{2,26},{10... | collective-permute-start | bytes 49160 | tf_op jit(solution)/shard_map/ppermute | solution.py:474
  29.0 9.0 %collective-permute-start.10 = (f32[4,8,128]{2,1,0:T(8,128)S(1)}, f32[4,8,128]{2,1,0:T(8,128)S(1)}, u32[]{:S(2)}, u32[]{:S(2)}) collective-permute-start(f32[4,8,128]{2,1,0:T(8,128)S(1)} %get-tuple-element.47), channel_id=1, source_target_pairs={{0,28},{4,24},{8,4},{12,0},{16,12},{20,8},{24,20},{28,16},{1,29},{... | collective-permute-start | bytes 49160 | tf_op jit(solution)/shard_map/ppermute | solution.py:480
  30.1 7.9 %collective-permute-start.9 = (f32[3,8,128]{2,1,0:T(8,128)S(1)}, f32[3,8,128]{2,1,0:T(8,128)S(1)}, u32[]{:S(2)}, u32[]{:S(2)}) collective-permute-start(f32[3,8,128]{2,1,0:T(8,128)S(1)} %get-tuple-element.46), channel_id=1, source_target_pairs={{0,8},{8,16},{16,24},{24,0},{1,9},{9,17},{17,25},{25,1},{2,10},{10... | collective-permute-start | bytes 36872 | tf_op jit(solution)/shard_map/ppermute | solution.py:474
  30.1 7.9 %collective-permute-start.11 = (f32[3,8,128]{2,1,0:T(8,128)S(1)}, f32[3,8,128]{2,1,0:T(8,128)S(1)}, u32[]{:S(2)}, u32[]{:S(2)}) collective-permute-start(f32[3,8,128]{2,1,0:T(8,128)S(1)} %get-tuple-element.48), channel_id=1, source_target_pairs={{0,12},{4,8},{8,20},{12,16},{16,28},{20,24},{24,4},{28,0},{1,13},{... | collective-permute-start | bytes 36872 | tf_op jit(solution)/shard_map/ppermute | solution.py:480
  38.1 9.4 %collective-permute-start.13 = (f32[16,128]{1,0:T(8,128)S(1)}, f32[16,128]{1,0:T(8,128)S(1)}, u32[]{:S(2)}, u32[]{:S(2)}) collective-permute-start(f32[16,128]{1,0:T(8,128)S(1)} %get-tuple-element.53), channel_id=1, source_target_pairs={{0,3},{1,0},{2,1},{3,2},{4,7},{5,4},{6,5},{7,6},{8,11},{9,8},{10,9... | collective-permute-start | bytes 24584 | tf_op jit(solution)/shard_map/ppermute | solution.py:474
  38.2 9.4 %collective-permute-start.12 = (f32[16,128]{1,0:T(8,128)S(1)}, f32[16,128]{1,0:T(8,128)S(1)}, u32[]{:S(2)}, u32[]{:S(2)}) collective-permute-start(f32[16,128]{1,0:T(8,128)S(1)} %get-tuple-element.53), channel_id=1, source_target_pairs={{0,1},{1,2},{2,3},{3,0},{4,5},{5,6},{6,7},{7,4},{8,9},{9,10},{10,1... | collective-permute-start | bytes 24584 | tf_op jit(solution)/shard_map/ppermute | solution.py:474
  58.9 3.9 %collective-permute-start.15 = (f32[64,128]{1,0:T(8,128)S(1)}, f32[64,128]{1,0:T(8,128)S(1)}, u32[]{:S(2)}, u32[]{:S(2)}) collective-permute-start(f32[64,128]{1,0:T(8,128)S(1)} %get-tuple-element.59), channel_id=1, source_target_pairs={{0,3},{1,0},{2,1},{3,2},{4,7},{5,4},{6,5},{7,6},{8,11},{9,8},{10,9... | collective-permute-start | bytes 98312 | tf_op jit(solution)/shard_map/ppermute | solution.py:474
  60.8 5.7 %collective-permute-start.14 = (f32[64,128]{1,0:T(8,128)S(1)}, f32[64,128]{1,0:T(8,128)S(1)}, u32[]{:S(2)}, u32[]{:S(2)}) collective-permute-start(f32[64,128]{1,0:T(8,128)S(1)} %get-tuple-element.59), channel_id=1, source_target_pairs={{0,1},{1,2},{2,3},{3,0},{4,5},{5,6},{6,7},{7,4},{8,9},{9,10},{10,1... | collective-permute-start | bytes 98312 | tf_op jit(solution)/shard_map/ppermute | solution.py:474
  66.7 7.0 %collective-permute-start.16 = (f32[32,8,128]{2,1,0:T(8,128)S(1)}, f32[32,8,128]{2,1,0:T(8,128)S(1)}, u32[]{:S(2)}, u32[]{:S(2)}) collective-permute-start(f32[32,8,128]{2,1,0:T(8,128)S(1)} %get-tuple-element.61), channel_id=1, source_target_pairs={{0,4},{4,0},{1,5},{5,1},{2,6},{6,2},{3,7},{7,3},{8,12},{12,8},{9,1... | collective-permute-start | bytes 393224 | tf_op jit(solution)/shard_map/ppermute | solution.py:474
  67.3 6.4 %collective-permute-start.18 = (f32[16,8,128]{2,1,0:T(8,128)S(1)}, f32[16,8,128]{2,1,0:T(8,128)S(1)}, u32[]{:S(2)}, u32[]{:S(2)}) collective-permute-start(f32[16,8,128]{2,1,0:T(8,128)S(1)} %get-tuple-element.63), channel_id=1, source_target_pairs={{0,8},{8,16},{16,24},{24,0},{1,9},{9,17},{17,25},{25,1},{2,10},{10... | collective-permute-start | bytes 196616 | tf_op jit(solution)/shard_map/ppermute | solution.py:474
  67.3 6.4 %collective-permute-start.20 = (f32[16,8,128]{2,1,0:T(8,128)S(1)}, f32[16,8,128]{2,1,0:T(8,128)S(1)}, u32[]{:S(2)}, u32[]{:S(2)}) collective-permute-start(f32[16,8,128]{2,1,0:T(8,128)S(1)} %get-tuple-element.65), channel_id=1, source_target_pairs={{0,12},{4,8},{8,20},{12,16},{16,28},{20,24},{24,4},{28,0},{1,13},{... | collective-permute-start | bytes 196616 | tf_op jit(solution)/shard_map/ppermute | solution.py:480
  69.4 2.4 %collective-permute-start.17 = (f32[12,8,128]{2,1,0:T(8,128)S(1)}, f32[12,8,128]{2,1,0:T(8,128)S(1)}, u32[]{:S(2)}, u32[]{:S(2)}) collective-permute-start(f32[12,8,128]{2,1,0:T(8,128)S(1)} %get-tuple-element.62), channel_id=1, source_target_pairs={{0,24},{8,0},{16,8},{24,16},{1,25},{9,1},{17,9},{25,17},{2,26},{10... | collective-permute-start | bytes 147464 | tf_op jit(solution)/shard_map/ppermute | solution.py:474
  70.0 3.7 %collective-permute-start.19 = (f32[12,8,128]{2,1,0:T(8,128)S(1)}, f32[12,8,128]{2,1,0:T(8,128)S(1)}, u32[]{:S(2)}, u32[]{:S(2)}) collective-permute-start(f32[12,8,128]{2,1,0:T(8,128)S(1)} %get-tuple-element.64), channel_id=1, source_target_pairs={{0,28},{4,24},{8,4},{12,0},{16,12},{20,8},{24,20},{28,16},{1,29},{... | collective-permute-start | bytes 147464 | tf_op jit(solution)/shard_map/ppermute | solution.py:480
  (2 other events, 10.2 us)

commit v5 on v4

--- a/solution.py
+++ b/solution.py
@@ -85,14 +85,13 @@
                 shifted[j, X] = pltpu.roll(jnp.where(wraps, ends, core), (-d) % LANES, 1)
 
 
-def interpolate(shifted, weights, slopes, nx, ny, emit):
+def interpolate(shifted, weights, slopes, nx, ny, emit, with_value):
     pair = 2 if nx % 2 == 0 else 1
 
     def plane(step, carry):
         x0 = step * pair
         tz = [[weights[2, j, x0 + p] for j in range(SHIFTS)] for p in range(pair)]
-        if slopes is not None:
-            sz = [[slopes[2, j, x0 + p] for j in range(SHIFTS)] for p in range(pair)]
+        sz = [[slopes[2, j, x0 + p] for j in range(SHIFTS)] for p in range(pair)]
 
         def row(sy, sums):
             a, b, c = [None] * pair, [None] * pair, [None] * pair
@@ -106,21 +105,19 @@
                     column = total([tz[p][j] * window[j] for j in range(SHIFTS)])
                     tx = weights[0, sx, x]
                     a[p] = plus(a[p], tx * column)
-                    if slopes is not None:
-                        b[p] = plus(b[p], slopes[0, sx, x] * column)
-                        c[p] = plus(c[p], tx * total([sz[p][j] * window[j] for j in range(SHIFTS)]))
+                    b[p] = plus(b[p], slopes[0, sx, x] * column)
+                    c[p] = plus(c[p], tx * total([sz[p][j] * window[j] for j in range(SHIFTS)]))
             out = []
             for p in range(pair):
                 ty = weights[1, sy, x0 + p]
-                if slopes is None:
-                    out.append((sums[p][0] + ty * a[p],))
-                else:
-                    steep = slopes[1, sy, x0 + p] * a[p]
-                    out.append((sums[p][0] + ty * b[p], sums[p][1] + steep, sums[p][2] + ty * c[p]))
+                terms = [ty * b[p], slopes[1, sy, x0 + p] * a[p], ty * c[p]]
+                if with_value:
+                    terms.append(ty * a[p])
+                out.append(tuple(old + new for old, new in zip(sums[p], terms)))
             return tuple(out)
 
         zero = jnp.zeros((ny, LANES), F32)
-        sums = lax.fori_loop(0, SHIFTS, row, ((zero,) * (1 if slopes is None else 3),) * pair)
+        sums = lax.fori_loop(0, SHIFTS, row, ((zero,) * (4 if with_value else 3),) * pair)
         for p in range(pair):
             emit(x0 + p, sums[p])
         return carry
@@ -138,10 +135,11 @@
     return b if a is None else a + b
 
 
-def deposit(sources, weights, scaled, piles, ys, js):
+def deposit(sources, weights, scaled, piles, ys, js, fresh=True):
     channels, nx, ny, _ = sources.shape
     planes = nx + LO + HI
-    piles[...] = jnp.zeros(piles.shape, F32)
+    if fresh:
+        piles[...] = jnp.zeros(piles.shape, F32)
 
     def scale(sy, carry):
         for x in range(nx):
@@ -182,7 +180,7 @@
     lax.fori_loop(0, SHIFTS // ys, row, 0)
 
 
-def settle(piles, out, rims, base=None, base_rims=None):
+def settle(piles, out, rims):
     channels, planes, rows, _ = out.shape
     lane = lane_of(rows)
     group = group_of(rows)
@@ -199,9 +197,9 @@
                 wraps = lane >= LANES + d if d < 0 else lane < d
                 core = core + jnp.where(wraps, 0.0, moved)
                 ends = ends + jnp.where(wraps, moved, 0.0)
-            out[c, X] = core if base is None else core + base[c, X]
+            out[c, X] = core
             rim = jnp.where(group == X, pltpu.roll(ends, (8 * X) % LANES, 1), rim)
-        rims[c] = rim if base_rims is None else rim + base_rims[c]
+        rims[c] = rim
 
 
 def pack_rim(extended):
@@ -312,8 +310,8 @@
 
 def first_kernel(
     nx, ny, intensity, cotangent, cells, fracs,
-    to_y, to_l, to_r, to_ly, to_ry, own,
-    cells_here, fracs_here, cotangent_here, image, sems, weights, scaled, piles, piled, rims,
+    to_y, to_l, to_r, to_ly, to_ry, own, image,
+    cells_here, fracs_here, cotangent_here, sems, weights, scaled, piles, piled, rims,
 ):
     copies = [
         pltpu.make_async_copy(source, target, sems.at[i])
@@ -349,38 +347,39 @@
     rims[rows : rows + ny] = join_deposits((from_y, from_r, from_l, from_ry, from_ly, own), (nx, HI, LO, 0), nx, ny, put)
 
 
-def middle_kernel(nx, ny, extended, rims_l, rims_r, part, cells, fracs, image, to_y, to_l, to_r, to_ly, to_ry, shifted, adjoint, weights):
+def middle_kernel(
+    nx, ny, extended, rims_l, rims_r, part, cells, fracs,
+    image, to_y, to_l, to_r, to_ly, to_ry, adjoint, gradient, weights,
+    shifted, slopes,
+):
     rows = ny + 2 * ROWS
     rim = jnp.where(low_lanes(rows), rims_r[0:rows], rims_l[0:rows])
     shift_planes(extended, rim, shifted)
-    write_tables(cells.at[0, 1], fracs.at[0, 1], weights)
+    write_tables(cells.at[0, 1], fracs.at[0, 1], weights, slopes)
 
     def emit(x, sums):
-        image[x] = sums[0]
-
-    interpolate(shifted, weights, None, nx, ny, emit)
+        image[x] = sums[3]
+        for c in range(3):
+            gradient[c, x] = sums[c]
+
+    interpolate(shifted, weights, slopes, nx, ny, emit, True)
     split_halo(image, (to_y, to_l, to_r, to_ly, to_ry), nx, ny)
     back = jnp.where(low_lanes(ny), rims_l[rows : rows + ny], rims_r[rows : rows + ny])
     for x in range(nx):
         adjoint[0, x] = part[x] + unpack_rim(back, LO + x)
 
 
-def early_kernel(nx, ny, shifted, adjoint, cells, fracs, grad, piled, rims, weights, slopes, scaled, piles):
-    write_tables(cells.at[0, 1], fracs.at[0, 1], weights, slopes)
-
-    def emit(x, sums):
-        for c in range(3):
-            grad[c, x] = adjoint[0, x] * sums[c]
-
-    interpolate(shifted, weights, slopes, nx, ny, emit)
+def adjoint_kernel(nx, ny, adjoint, weights, piled, rims, scaled, piles):
     deposit(adjoint, weights, scaled, piles, 2, SHIFTS)
     settle(piles, piled, rims)
 
 
-def early_spread_kernel(nx, ny, grad, cells, fracs, piled, rims, weights, scaled, piles):
+def early_kernel(nx, ny, gradient, adjoint, cells, fracs, piles, product, weights, scaled):
     write_tables(cells.at[0, 0], fracs.at[0, 0], weights)
-    deposit(grad, weights, scaled, piles, 1, SHIFTS // 2)
-    settle(piles, piled, rims)
+    for c in range(3):
+        for x in range(nx):
+            product[c, x] = adjoint[0, x] * gradient[c, x]
+    deposit(product, weights, scaled, piles, 1, SHIFTS // 2)
 
 
 def second_join_kernel(nx, ny, image, from_y, from_r, from_l, from_ry, from_ly, earlier, extended, rims):
@@ -389,9 +388,9 @@
 
 
 def late_kernel(
-    nx, ny, extended, rims_l, rims_r, cotangent, cells, fracs, early, early_rims, adjoint_rims,
-    piled, rims,
-    shifted, weights, slopes, grad, scaled, rims_here, piles,
+    nx, ny, extended, rims_l, rims_r, cotangent, cells, fracs, adjoint_rims, early_piles,
+    piled, rims, piles,
+    shifted, weights, slopes, product, scaled, rims_here,
 ):
     rows = ny + 2 * ROWS
     shift_planes(extended, jnp.where(low_lanes(rows), rims_r[...], rims_l[...]), shifted)
@@ -399,12 +398,12 @@
 
     def emit(x, sums):
         for c in range(3):
-            grad[c, x] = cotangent[0, x] * sums[c]
-
-    interpolate(shifted, weights, slopes, nx, ny, emit)
+            product[c, x] = cotangent[0, x] * sums[c]
+
+    interpolate(shifted, weights, slopes, nx, ny, emit, False)
     write_tables(cells.at[1, 0], fracs.at[1, 0], weights)
-    deposit(grad, weights, scaled, piles, 1, SHIFTS // 2)
-    settle(piles, piled, rims_here, early, early_rims)
+    deposit(product, weights, scaled, piles, 1, SHIFTS // 2, fresh=False)
+    settle(piles, piled, rims_here)
     for c in range(3):
         rims[c * rows : (c + 1) * rows] = rims_here[c]
     rims[3 * rows : 4 * rows] = adjoint_rims[0]
@@ -446,7 +445,7 @@
                 velocity_adjoint[c, x] = plane
 
 
-def call(kernel, args, outs, scratch, flops, spaces=None, limit=24):
+def call(kernel, args, outs, scratch, flops, spaces=None, limit=24 * 1024, aliases=None):
     def struct(shape):
         return jax.ShapeDtypeStruct(shape, F32)
 
@@ -461,7 +460,8 @@
         in_specs=in_specs,
         out_specs=[in_vmem] * len(outs),
         scratch_shapes=[pltpu.VMEM(s, F32) if isinstance(s, tuple) else s for s in scratch],
-        compiler_params=pltpu.CompilerParams(vmem_limit_bytes=limit * 1024 * 1024),
+        input_output_aliases=aliases or {},
+        compiler_params=pltpu.CompilerParams(vmem_limit_bytes=limit * 1024),
         cost_estimate=pl.CostEstimate(flops=flops, bytes_accessed=moved, transcendentals=0),
     )(*args)
 
@@ -503,7 +503,7 @@
     return send(rims, (("gz", 1),)), send(rims, (("gz", -1),))
 
 
-FIRST_LIMIT = 56
+FIRST_LIMIT = 55150
 
 
 def body(intensity, cotangent, cells, fracs):
@@ -529,11 +529,11 @@
         return [(y, ring, nz), (l, ny, nz), (r, ny, nz), (l, ring, nz), (r, ring, nz)]
 
     part = (3,) + field
-    *outs, own = run(
+    *outs, own, image = run(
         first_kernel,
         (intensity, cotangent, cells, fracs),
-        messages(2 * nx + 1, HI + LO + 1, LO + HI + 1) + [(nx + 1, ny, nz)],
-        [pltpu.VMEM(part, jnp.int32), part, (1,) + field, field, pltpu.SemaphoreType.DMA((4,)), table]
+        messages(2 * nx + 1, HI + LO + 1, LO + HI + 1) + [(nx + 1, ny, nz), field],
+        [pltpu.VMEM(part, jnp.int32), part, (1,) + field, pltpu.SemaphoreType.DMA((4,)), table]
         + pile(1)
         + [(1, planes + 1, rows, nz), (1, rows, nz)],
         2 * unit,
@@ -542,50 +542,52 @@
     )
     extended, folded, rims = run(
         first_join_kernel,
-        (intensity,) + send_sides(*outs) + (own,),
+        (image,) + send_sides(*outs) + (own,),
         [(planes, rows, nz), field, (rows + ny, nz)],
         [],
         unit // 16,
     )
-    image, *outs, shifted, adjoint = run(
+    image, *outs, adjoint, gradient, weights = run(
         middle_kernel,
         (extended,) + send_z(rims) + (folded, cells, fracs),
-        [field] + messages(nx, HI, LO) + [(SHIFTS, planes, rows, nz), (1,) + field],
-        [table],
+        [field] + messages(nx, HI, LO) + [(1,) + field, (3,) + field, table],
+        [(SHIFTS, planes, rows, nz), table],
+        5 * unit,
+    )
+
+    sides = send_sides(*outs)
+    piled_adjoint, adjoint_rims = run(
+        adjoint_kernel,
+        (adjoint, weights),
+        piled(1),
+        pile(1),
         2 * unit,
-    )
-
-    sides = send_sides(*outs)
-    grad, piled_adjoint, adjoint_rims = run(
-        early_kernel,
-        (shifted, adjoint, cells, fracs),
-        [(3,) + field] + piled(1),
-        [table, table] + pile(1),
-        7 * unit,
     )
     extended, rims = run(
         second_join_kernel,
-        (image,) + sides + (grad,),
+        (image,) + sides + (piled_adjoint,),
         [(planes, rows, nz), (rows, nz)],
         [],
         unit // 16,
         spaces={6: pl.ANY},
     )
     rims_l, rims_r = send_z(rims)
-    early, early_rims = run(
-        early_spread_kernel,
-        (grad, cells, fracs),
-        piled(3),
-        [table] + pile(3),
+    scaled_3, piles_3 = pile(3)
+    (piles,) = run(
+        early_kernel,
+        (gradient, adjoint, cells, fracs),
+        [piles_3],
+        [(3,) + field, table, scaled_3],
         6 * unit,
     )
 
-    velocity, rims = run(
+    velocity, rims, _ = run(
         late_kernel,
-        (extended, rims_l, rims_r, cotangent, cells, fracs, early, early_rims, adjoint_rims),
-        [(3, planes, rows, nz), (4 * rows, nz)],
-        [(SHIFTS, planes, rows, nz), table, table, (3,) + field, pile(3)[0], (3, rows, nz), pile(3)[1]],
+        (extended, rims_l, rims_r, cotangent, cells, fracs, adjoint_rims, piles),
+        [(3, planes, rows, nz), (4 * rows, nz), piles_3],
+        [(SHIFTS, planes, rows, nz), table, table, (3,) + field, scaled_3, (3, rows, nz)],
         11 * unit,
+        aliases={7: 2},
     )
     *outs, own = run(
         last_z_kernel,

time: 74.7 us -> 72.3 us (0.968)
  Pallas kernels: 32.3 us -> 27 us
  local copies, waits for them, and re-layouts: 0.79 us -> 3.53 us
    pallas_call x9, Pallas kernels: 32.3 us -> 27 us  [call(): pl.pallas_call(kernel, out_shape=[struct(s) for s in outs], in_specs=in_s...]
    unnamed x10 -> x14, local copies, waits for them, and re-layouts: 0.79 us -> 3.53 us
  transfers between devices with their start and end apart: 21 -> 21, of which waited for: 10 -> 9; matrix products, arithmetic and copies ran while one was open for 0% -> 0% of each run, Pallas kernels for 17% -> 9%
where the time goes in v5:
time: 72.3 us; the launch traced here: 71.9 us
  Pallas kernels  27 us (37%)
  starting transfers between devices  22 us (30%)
  waiting for transfers between devices  18.5 us (26%)
  local copies, waits for them, and re-layouts  3.53 us (5%)
  between operations  0.77 us (1%)
    pallas_call x9, Pallas kernels, call(): pl.pallas_call(kernel, out_shape=[struct(s) for s in outs], in_specs=in_s...  27 us
    ppermute x15, starting transfers between devices, send(): return lax.ppermute(message, axes[0], pairs)  14.3 us
    ppermute x15, waiting for transfers between devices, send(): return lax.ppermute(message, axes[0], pairs)  13.7 us
    ppermute x6, starting transfers between devices, send(): return lax.ppermute(message, axes, pairs)  7.76 us
    ppermute x6, waiting for transfers between devices, send(): return lax.ppermute(message, axes, pairs)  4.86 us
    unnamed x14, local copies, waits for them, and re-layouts  3.53 us
  transfers between devices with their start and end apart: 21, of which 9 were waited for; matrix products, arithmetic and copies ran while one was open for 0% of the time, Pallas kernels for 9%

profile of v5, /device:TPU:0, one launch (start us, length us, event | category | flops | bytes accessed | tf_op | source)
XLA Modules:
  0.0 71.9 jit_solution(2935020815455953115)
XLA Ops:
  0.7 4.3 %shard_map.59 = (f32[17,8,128]{2,1,0:T(8,128)}, f32[8,8,128]{2,1,0:T(8,128)S(1)}, f32[8,8,128]{2,1,0:T(8,128)S(1)}, f32[8,8,128]{2,1,0:T(8,128)}, f32[8,8,128]{2...) custom-call(f32[8,8,128]{2,1,0:T(8,128)} %intensity.1, f32[1,8,8,128]{3,2,1,0:T(8,128)} %bitcast.1, ...), custom_call_target="tpu_custom_call" | custom-call | flops 8388608 | bytes 851968 | tf_op jit(solution)/shard_map/pallas_call | solution.py:457
  5.0 3.0 %collective-permute-start = (f32[17,8,128]{2,1,0:T(8,128)}, f32[17,8,128]{2,1,0:T(8,128)S(1)}, u32[]{:S(2)}, u32[]{:S(2)}) collective-permute-start(f32[17,8,128]{2,1,0:T(8,128)} %get-tuple-element.34), channel_id=1, source_target_pairs={{0,4},{4,0},{1,5},{5,1},{2,6},{6,2},{3,7},{7,3},{8,12},{12,8},{9,1... | collective-permute-start | bytes 208904 | tf_op jit(solution)/shard_map/ppermute | solution.py:474
  8.7 1.7 %collective-permute-start.3 = (f32[8,8,128]{2,1,0:T(8,128)}, f32[8,8,128]{2,1,0:T(8,128)S(1)}, u32[]{:S(2)}, u32[]{:S(2)}) collective-permute-start(f32[8,8,128]{2,1,0:T(8,128)} %get-tuple-element.37), channel_id=1, source_target_pairs={{0,28},{4,24},{8,4},{12,0},{16,12},{20,8},{24,20},{28,16},{1,29},{... | collective-permute-start | bytes 98312 | tf_op jit(solution)/shard_map/ppermute | solution.py:480
  10.4 1.6 %collective-permute-done.2.from_l = f32[8,8,128]{2,1,0:T(8,128)S(1)} collective-permute-done((f32[8,8,128]{2,1,0:T(8,128)S(1)}, f32[8,8,128]{2,1,0:T(8,128)S(1)}, u32[]{:S(2)}, u32[]{:S(2)}) %collective-permute-start.2) | collective-permute-done | bytes 32800 | tf_op jit(solution)/shard_map/ppermute | solution.py:474
  12.3 2.5 %collective-permute-done.4.from_ly = f32[8,8,128]{2,1,0:T(8,128)S(1)} collective-permute-done((f32[8,8,128]{2,1,0:T(8,128)}, f32[8,8,128]{2,1,0:T(8,128)S(1)}, u32[]{:S(2)}, u32[]{:S(2)}) %collective-permute-start.4) | collective-permute-done | bytes 32800 | tf_op jit(solution)/shard_map/ppermute | solution.py:480
  16.4 3.7 %collective-permute-start.6 = (f32[24,128]{1,0:T(8,128)S(1)}, f32[24,128]{1,0:T(8,128)S(1)}, u32[]{:S(2)}, u32[]{:S(2)}) collective-permute-start(f32[24,128]{1,0:T(8,128)S(1)} %get-tuple-element.41), channel_id=1, source_target_pairs={{0,3},{1,0},{2,1},{3,2},{4,7},{5,4},{6,5},{7,6},{8,11},{9,8},{10,9... | collective-permute-start | bytes 36872 | tf_op jit(solution)/shard_map/ppermute | solution.py:474
  20.1 1.4 %collective-permute-done.6.rims_r = f32[24,128]{1,0:T(8,128)S(1)} collective-permute-done((f32[24,128]{1,0:T(8,128)S(1)}, f32[24,128]{1,0:T(8,128)S(1)}, u32[]{:S(2)}, u32[]{:S(2)}) %collective-permute-start.6) | collective-permute-done | bytes 12320 | tf_op jit(solution)/shard_map/ppermute | solution.py:474
  21.5 4.1 %collective-permute-done.5.rims_l = f32[24,128]{1,0:T(8,128)S(1)} collective-permute-done((f32[24,128]{1,0:T(8,128)S(1)}, f32[24,128]{1,0:T(8,128)S(1)}, u32[]{:S(2)}, u32[]{:S(2)}) %collective-permute-start.5) | collective-permute-done | bytes 12320 | tf_op jit(solution)/shard_map/ppermute | solution.py:474
  25.6 1.0 %copy-done = s32[2,2,3,8,8,128]{5,4,3,2,1,0:T(8,128)S(1)} copy-done((s32[2,2,3,8,8,128]{5,4,3,2,1,0:T(8,128)S(1)}, s32[2,2,3,8,8,128]{5,4,3,2,1,0:T(8,128)}, u32[]{:S(2)}) %copy-start) | copy-done | bytes 393240
  26.6 1.0 %copy-done.2 = f32[2,2,3,8,8,128]{5,4,3,2,1,0:T(8,128)S(1)} copy-done((f32[2,2,3,8,8,128]{5,4,3,2,1,0:T(8,128)S(1)}, f32[2,2,3,8,8,128]{5,4,3,2,1,0:T(8,128)}, u32[]{:S(2)}) %copy-start.2) | copy-done | bytes 393240
  27.6 4.0 %shard_map.61 = (f32[8,8,128]{2,1,0:T(8,128)S(1)}, f32[8,8,128]{2,1,0:T(8,128)S(1)}, f32[4,8,128]{2,1,0:T(8,128)S(1)}, f32[3,8,128]{2,1,0:T(8,128)S(1)}, f32[4,8...) custom-call(f32[15,16,128]{2,1,0:T(8,128)S(1)} %get-tuple-element.40, ...), custom_call_target="tpu_custom_call" | custom-call | flops 20971520 | bytes 966656 | tf_op jit(solution)/shard_map/pallas_call | solution.py:457
  31.6 1.5 %collective-permute-start.7 = (f32[8,8,128]{2,1,0:T(8,128)S(1)}, f32[8,8,128]{2,1,0:T(8,128)S(1)}, u32[]{:S(2)}, u32[]{:S(2)}) collective-permute-start(f32[8,8,128]{2,1,0:T(8,128)S(1)} %get-tuple-element.44), channel_id=1, source_target_pairs={{0,4},{4,0},{1,5},{5,1},{2,6},{6,2},{3,7},{7,3},{8,12},{12,8},{9,1... | collective-permute-start | bytes 98312 | tf_op jit(solution)/shard_map/ppermute | solution.py:474
  33.2 1.0 %collective-permute-start.10 = (f32[4,8,128]{2,1,0:T(8,128)S(1)}, f32[4,8,128]{2,1,0:T(8,128)S(1)}, u32[]{:S(2)}, u32[]{:S(2)}) collective-permute-start(f32[4,8,128]{2,1,0:T(8,128)S(1)} %get-tuple-element.47), channel_id=1, source_target_pairs={{0,28},{4,24},{8,4},{12,0},{16,12},{20,8},{24,20},{28,16},{1,29},{... | collective-permute-start | bytes 49160 | tf_op jit(solution)/shard_map/ppermute | solution.py:480
  34.2 2.3 %collective-permute-start.11 = (f32[3,8,128]{2,1,0:T(8,128)S(1)}, f32[3,8,128]{2,1,0:T(8,128)S(1)}, u32[]{:S(2)}, u32[]{:S(2)}) collective-permute-start(f32[3,8,128]{2,1,0:T(8,128)S(1)} %get-tuple-element.48), channel_id=1, source_target_pairs={{0,12},{4,8},{8,20},{12,16},{16,28},{20,24},{24,4},{28,0},{1,13},{... | collective-permute-start | bytes 36872 | tf_op jit(solution)/shard_map/ppermute | solution.py:480
  36.5 2.5 %shard_map.62 = (f32[1,15,16,128]{3,2,1,0:T(8,128)S(1)}, f32[1,16,128]{2,1,0:T(8,128)S(1)}) custom-call(f32[1,8,8,128]{3,2,1,0:T(8,128)S(1)} %get-tuple-element.49.adjoint, f32[3,8,8,8,128]{4,3,2,1,0:T(8,128)S(1)} %get-tuple-element.50.weights), custom_call_target="tpu_custom_call" | custom-call | flops 8388608 | bytes 819200 | tf_op jit(solution)/shard_map/pallas_call | solution.py:457
  39.2 2.0 %collective-permute-start.12 = (f32[16,128]{1,0:T(8,128)S(1)}, f32[16,128]{1,0:T(8,128)S(1)}, u32[]{:S(2)}, u32[]{:S(2)}) collective-permute-start(f32[16,128]{1,0:T(8,128)S(1)} %get-tuple-element.53), channel_id=1, source_target_pairs={{0,1},{1,2},{2,3},{3,0},{4,5},{5,6},{6,7},{7,4},{8,9},{9,10},{10,1... | collective-permute-start | bytes 24584 | tf_op jit(solution)/shard_map/ppermute | solution.py:474
  41.2 4.0 %shard_map.64.early_piles = f32[3,8,15,16,128]{4,3,2,1,0:T(8,128)S(1)} custom-call(f32[3,8,8,128]{3,2,1,0:T(8,128)S(1)} %get-tuple-element.55.gradient, f32[1,8,8,128]{3,2,1,0:T(8,128)S(1)} %get-tuple-element.49.adjoint, s32[2,2,3,8,8,128]{5,4,3,2,1,0:T(8,128)S(1)} %copy-done.1, f32[2,2,3,8,8,128]{5,4,3,2,1,0:T(8,128)S(1)} %copy-done.3), custom_call_target="tpu_custom_call" | custom-call | flops 25165824 | bytes 917504 | tf_op jit(solution)/shard_map/pallas_call | solution.py:457
  45.3 11.1 %shard_map.65 = (f32[3,15,16,128]{3,2,1,0:T(8,128)S(1)}, f32[64,128]{1,0:T(8,128)S(1)}, f32[3,8,15,16,128]{4,3,2,1,0:T(8,128)S(1)}) custom-call(f32[15,16,128]{2,1,0:T(8,128)S(1)} %get-tuple-element.52.extended, f32[16,128]{1,0:T(8,128)S(1)} %collective-permute-done.12.rims_l, ...), custom_call_target="tpu_custom_call", output_to_operand_aliasing={{2}: (7, {})} | custom-call | flops 46137344 | bytes 3915776 | tf_op jit(solution)/shard_map/pallas_call | solution.py:457
  56.3 1.9 %collective-permute-start.15 = (f32[64,128]{1,0:T(8,128)S(1)}, f32[64,128]{1,0:T(8,128)S(1)}, u32[]{:S(2)}, u32[]{:S(2)}) collective-permute-start(f32[64,128]{1,0:T(8,128)S(1)} %get-tuple-element.57), channel_id=1, source_target_pairs={{0,3},{1,0},{2,1},{3,2},{4,7},{5,4},{6,5},{7,6},{8,11},{9,8},{10,9... | collective-permute-start | bytes 98312 | tf_op jit(solution)/shard_map/ppermute | solution.py:474
  58.4 1.9 %collective-permute-done.15.rims_r = f32[64,128]{1,0:T(8,128)S(1)} collective-permute-done((f32[64,128]{1,0:T(8,128)S(1)}, f32[64,128]{1,0:T(8,128)S(1)}, u32[]{:S(2)}, u32[]{:S(2)}) %collective-permute-start.15) | collective-permute-done | bytes 32800 | tf_op jit(solution)/shard_map/ppermute | solution.py:474
  60.3 3.7 %collective-permute-done.14.rims_l = f32[64,128]{1,0:T(8,128)S(1)} collective-permute-done((f32[64,128]{1,0:T(8,128)S(1)}, f32[64,128]{1,0:T(8,128)S(1)}, u32[]{:S(2)}, u32[]{:S(2)}) %collective-permute-start.14) | collective-permute-done | bytes 32800 | tf_op jit(solution)/shard_map/ppermute | solution.py:474
  64.8 2.0 %collective-permute-start.20 = (f32[16,8,128]{2,1,0:T(8,128)S(1)}, f32[16,8,128]{2,1,0:T(8,128)S(1)}, u32[]{:S(2)}, u32[]{:S(2)}) collective-permute-start(f32[16,8,128]{2,1,0:T(8,128)S(1)} %get-tuple-element.63), channel_id=1, source_target_pairs={{0,12},{4,8},{8,20},{12,16},{16,28},{20,24},{24,4},{28,0},{1,13},{... | collective-permute-start | bytes 196616 | tf_op jit(solution)/shard_map/ppermute | solution.py:480
  68.1 1.0 %collective-permute-done.17.from_r = f32[12,8,128]{2,1,0:T(8,128)S(1)} collective-permute-done((f32[12,8,128]{2,1,0:T(8,128)S(1)}, f32[12,8,128]{2,1,0:T(8,128)S(1)}, u32[]{:S(2)}, u32[]{:S(2)}) %collective-permute-start.17) | collective-permute-done | bytes 49184 | tf_op jit(solution)/shard_map/ppermute | solution.py:474
  69.1 2.1 %collective-permute-done.19.from_ry = f32[12,8,128]{2,1,0:T(8,128)S(1)} collective-permute-done((f32[12,8,128]{2,1,0:T(8,128)S(1)}, f32[12,8,128]{2,1,0:T(8,128)S(1)}, u32[]{:S(2)}, u32[]{:S(2)}) %collective-permute-start.19) | collective-permute-done | bytes 49184 | tf_op jit(solution)/shard_map/ppermute | solution.py:480
  (41 shorter events, 5.9 us)
Async XLA Ops:
  0.6 40.6 %copy-start.3 = (f32[2,2,3,8,8,128]{5,4,3,2,1,0:T(8,128)S(1)}, f32[2,2,3,8,8,128]{5,4,3,2,1,0:T(8,128)}, u32[]{:S(2)}) copy-start(f32[2,2,3,8,8,128]{5,4,3,2,1,0:T(8,128)} %fracs.7) | copy-start | bytes 1179652
  0.6 40.5 %copy-start.1 = (s32[2,2,3,8,8,128]{5,4,3,2,1,0:T(8,128)S(1)}, s32[2,2,3,8,8,128]{5,4,3,2,1,0:T(8,128)}, u32[]{:S(2)}) copy-start(s32[2,2,3,8,8,128]{5,4,3,2,1,0:T(8,128)} %cells.7) | copy-start | bytes 1179652
  5.0 9.8 %collective-permute-start = (f32[17,8,128]{2,1,0:T(8,128)}, f32[17,8,128]{2,1,0:T(8,128)S(1)}, u32[]{:S(2)}, u32[]{:S(2)}) collective-permute-start(f32[17,8,128]{2,1,0:T(8,128)} %get-tuple-element.34), channel_id=1, source_target_pairs={{0,4},{4,0},{1,5},{5,1},{2,6},{6,2},{3,7},{7,3},{8,12},{12,8},{9,1... | collective-permute-start | bytes 208904 | tf_op jit(solution)/shard_map/ppermute | solution.py:474
  8.0 2.4 %collective-permute-start.1 = (f32[8,8,128]{2,1,0:T(8,128)S(1)}, f32[8,8,128]{2,1,0:T(8,128)S(1)}, u32[]{:S(2)}, u32[]{:S(2)}) collective-permute-start(f32[8,8,128]{2,1,0:T(8,128)S(1)} %get-tuple-element.35), channel_id=1, source_target_pairs={{0,24},{8,0},{16,8},{24,16},{1,25},{9,1},{17,9},{25,17},{2,26},{10... | collective-permute-start | bytes 98312 | tf_op jit(solution)/shard_map/ppermute | solution.py:474
  8.7 3.3 %collective-permute-start.2 = (f32[8,8,128]{2,1,0:T(8,128)S(1)}, f32[8,8,128]{2,1,0:T(8,128)S(1)}, u32[]{:S(2)}, u32[]{:S(2)}) collective-permute-start(f32[8,8,128]{2,1,0:T(8,128)S(1)} %get-tuple-element.36), channel_id=1, source_target_pairs={{0,8},{8,16},{16,24},{24,0},{1,9},{9,17},{17,25},{25,1},{2,10},{10... | collective-permute-start | bytes 98312 | tf_op jit(solution)/shard_map/ppermute | solution.py:474
  8.7 3.6 %collective-permute-start.3 = (f32[8,8,128]{2,1,0:T(8,128)}, f32[8,8,128]{2,1,0:T(8,128)S(1)}, u32[]{:S(2)}, u32[]{:S(2)}) collective-permute-start(f32[8,8,128]{2,1,0:T(8,128)} %get-tuple-element.37), channel_id=1, source_target_pairs={{0,28},{4,24},{8,4},{12,0},{16,12},{20,8},{24,20},{28,16},{1,29},{... | collective-permute-start | bytes 98312 | tf_op jit(solution)/shard_map/ppermute | solution.py:480
  10.4 4.4 %collective-permute-start.4 = (f32[8,8,128]{2,1,0:T(8,128)}, f32[8,8,128]{2,1,0:T(8,128)S(1)}, u32[]{:S(2)}, u32[]{:S(2)}) collective-permute-start(f32[8,8,128]{2,1,0:T(8,128)} %get-tuple-element.38), channel_id=1, source_target_pairs={{0,12},{4,8},{8,20},{12,16},{16,28},{20,24},{24,4},{28,0},{1,13},{... | collective-permute-start | bytes 98312 | tf_op jit(solution)/shard_map/ppermute | solution.py:480
  16.4 5.1 %collective-permute-start.6 = (f32[24,128]{1,0:T(8,128)S(1)}, f32[24,128]{1,0:T(8,128)S(1)}, u32[]{:S(2)}, u32[]{:S(2)}) collective-permute-start(f32[24,128]{1,0:T(8,128)S(1)} %get-tuple-element.41), channel_id=1, source_target_pairs={{0,3},{1,0},{2,1},{3,2},{4,7},{5,4},{6,5},{7,6},{8,11},{9,8},{10,9... | collective-permute-start | bytes 36872 | tf_op jit(solution)/shard_map/ppermute | solution.py:474
  20.1 5.5 %collective-permute-start.5 = (f32[24,128]{1,0:T(8,128)S(1)}, f32[24,128]{1,0:T(8,128)S(1)}, u32[]{:S(2)}, u32[]{:S(2)}) collective-permute-start(f32[24,128]{1,0:T(8,128)S(1)} %get-tuple-element.41), channel_id=1, source_target_pairs={{0,1},{1,2},{2,3},{3,0},{4,5},{5,6},{6,7},{7,4},{8,9},{9,10},{10,1... | collective-permute-start | bytes 36872 | tf_op jit(solution)/shard_map/ppermute | solution.py:474
  27.6 17.7 %copy-start.4 = (f32[8,8,128]{2,1,0:T(8,128)S(1)}, f32[8,8,128]{2,1,0:T(8,128)}, u32[]{:S(2)}) copy-start(f32[8,8,128]{2,1,0:T(8,128)} %param.5) | copy-start | bytes 98308
  31.6 7.4 %collective-permute-start.7 = (f32[8,8,128]{2,1,0:T(8,128)S(1)}, f32[8,8,128]{2,1,0:T(8,128)S(1)}, u32[]{:S(2)}, u32[]{:S(2)}) collective-permute-start(f32[8,8,128]{2,1,0:T(8,128)S(1)} %get-tuple-element.44), channel_id=1, source_target_pairs={{0,4},{4,0},{1,5},{5,1},{2,6},{6,2},{3,7},{7,3},{8,12},{12,8},{9,1... | collective-permute-start | bytes 98312 | tf_op jit(solution)/shard_map/ppermute | solution.py:474
  33.2 5.8 %collective-permute-start.8 = (f32[4,8,128]{2,1,0:T(8,128)S(1)}, f32[4,8,128]{2,1,0:T(8,128)S(1)}, u32[]{:S(2)}, u32[]{:S(2)}) collective-permute-start(f32[4,8,128]{2,1,0:T(8,128)S(1)} %get-tuple-element.45), channel_id=1, source_target_pairs={{0,24},{8,0},{16,8},{24,16},{1,25},{9,1},{17,9},{25,17},{2,26},{10... | collective-permute-start | bytes 49160 | tf_op jit(solution)/shard_map/ppermute | solution.py:474
  33.2 5.8 %collective-permute-start.10 = (f32[4,8,128]{2,1,0:T(8,128)S(1)}, f32[4,8,128]{2,1,0:T(8,128)S(1)}, u32[]{:S(2)}, u32[]{:S(2)}) collective-permute-start(f32[4,8,128]{2,1,0:T(8,128)S(1)} %get-tuple-element.47), channel_id=1, source_target_pairs={{0,28},{4,24},{8,4},{12,0},{16,12},{20,8},{24,20},{28,16},{1,29},{... | collective-permute-start | bytes 49160 | tf_op jit(solution)/shard_map/ppermute | solution.py:480
  34.2 4.8 %collective-permute-start.9 = (f32[3,8,128]{2,1,0:T(8,128)S(1)}, f32[3,8,128]{2,1,0:T(8,128)S(1)}, u32[]{:S(2)}, u32[]{:S(2)}) collective-permute-start(f32[3,8,128]{2,1,0:T(8,128)S(1)} %get-tuple-element.46), channel_id=1, source_target_pairs={{0,8},{8,16},{16,24},{24,0},{1,9},{9,17},{17,25},{25,1},{2,10},{10... | collective-permute-start | bytes 36872 | tf_op jit(solution)/shard_map/ppermute | solution.py:474
  34.2 4.8 %collective-permute-start.11 = (f32[3,8,128]{2,1,0:T(8,128)S(1)}, f32[3,8,128]{2,1,0:T(8,128)S(1)}, u32[]{:S(2)}, u32[]{:S(2)}) collective-permute-start(f32[3,8,128]{2,1,0:T(8,128)S(1)} %get-tuple-element.48), channel_id=1, source_target_pairs={{0,12},{4,8},{8,20},{12,16},{16,28},{20,24},{24,4},{28,0},{1,13},{... | collective-permute-start | bytes 36872 | tf_op jit(solution)/shard_map/ppermute | solution.py:480
  39.1 6.1 %collective-permute-start.13 = (f32[16,128]{1,0:T(8,128)S(1)}, f32[16,128]{1,0:T(8,128)S(1)}, u32[]{:S(2)}, u32[]{:S(2)}) collective-permute-start(f32[16,128]{1,0:T(8,128)S(1)} %get-tuple-element.53), channel_id=1, source_target_pairs={{0,3},{1,0},{2,1},{3,2},{4,7},{5,4},{6,5},{7,6},{8,11},{9,8},{10,9... | collective-permute-start | bytes 24584 | tf_op jit(solution)/shard_map/ppermute | solution.py:474
  39.2 6.1 %collective-permute-start.12 = (f32[16,128]{1,0:T(8,128)S(1)}, f32[16,128]{1,0:T(8,128)S(1)}, u32[]{:S(2)}, u32[]{:S(2)}) collective-permute-start(f32[16,128]{1,0:T(8,128)S(1)} %get-tuple-element.53), channel_id=1, source_target_pairs={{0,1},{1,2},{2,3},{3,0},{4,5},{5,6},{6,7},{7,4},{8,9},{9,10},{10,1... | collective-permute-start | bytes 24584 | tf_op jit(solution)/shard_map/ppermute | solution.py:474
  56.3 3.9 %collective-permute-start.15 = (f32[64,128]{1,0:T(8,128)S(1)}, f32[64,128]{1,0:T(8,128)S(1)}, u32[]{:S(2)}, u32[]{:S(2)}) collective-permute-start(f32[64,128]{1,0:T(8,128)S(1)} %get-tuple-element.57), channel_id=1, source_target_pairs={{0,3},{1,0},{2,1},{3,2},{4,7},{5,4},{6,5},{7,6},{8,11},{9,8},{10,9... | collective-permute-start | bytes 98312 | tf_op jit(solution)/shard_map/ppermute | solution.py:474
  58.2 5.7 %collective-permute-start.14 = (f32[64,128]{1,0:T(8,128)S(1)}, f32[64,128]{1,0:T(8,128)S(1)}, u32[]{:S(2)}, u32[]{:S(2)}) collective-permute-start(f32[64,128]{1,0:T(8,128)S(1)} %get-tuple-element.57), channel_id=1, source_target_pairs={{0,1},{1,2},{2,3},{3,0},{4,5},{5,6},{6,7},{7,4},{8,9},{9,10},{10,1... | collective-permute-start | bytes 98312 | tf_op jit(solution)/shard_map/ppermute | solution.py:474
  64.1 7.1 %collective-permute-start.16 = (f32[32,8,128]{2,1,0:T(8,128)S(1)}, f32[32,8,128]{2,1,0:T(8,128)S(1)}, u32[]{:S(2)}, u32[]{:S(2)}) collective-permute-start(f32[32,8,128]{2,1,0:T(8,128)S(1)} %get-tuple-element.59), channel_id=1, source_target_pairs={{0,4},{4,0},{1,5},{5,1},{2,6},{6,2},{3,7},{7,3},{8,12},{12,8},{9,1... | collective-permute-start | bytes 393224 | tf_op jit(solution)/shard_map/ppermute | solution.py:474
  64.8 6.4 %collective-permute-start.18 = (f32[16,8,128]{2,1,0:T(8,128)S(1)}, f32[16,8,128]{2,1,0:T(8,128)S(1)}, u32[]{:S(2)}, u32[]{:S(2)}) collective-permute-start(f32[16,8,128]{2,1,0:T(8,128)S(1)} %get-tuple-element.61), channel_id=1, source_target_pairs={{0,8},{8,16},{16,24},{24,0},{1,9},{9,17},{17,25},{25,1},{2,10},{10... | collective-permute-start | bytes 196616 | tf_op jit(solution)/shard_map/ppermute | solution.py:474
  64.8 6.4 %collective-permute-start.20 = (f32[16,8,128]{2,1,0:T(8,128)S(1)}, f32[16,8,128]{2,1,0:T(8,128)S(1)}, u32[]{:S(2)}, u32[]{:S(2)}) collective-permute-start(f32[16,8,128]{2,1,0:T(8,128)S(1)} %get-tuple-element.63), channel_id=1, source_target_pairs={{0,12},{4,8},{8,20},{12,16},{16,28},{20,24},{24,4},{28,0},{1,13},{... | collective-permute-start | bytes 196616 | tf_op jit(solution)/shard_map/ppermute | solution.py:480
  66.8 2.4 %collective-permute-start.17 = (f32[12,8,128]{2,1,0:T(8,128)S(1)}, f32[12,8,128]{2,1,0:T(8,128)S(1)}, u32[]{:S(2)}, u32[]{:S(2)}) collective-permute-start(f32[12,8,128]{2,1,0:T(8,128)S(1)} %get-tuple-element.60), channel_id=1, source_target_pairs={{0,24},{8,0},{16,8},{24,16},{1,25},{9,1},{17,9},{25,17},{2,26},{10... | collective-permute-start | bytes 147464 | tf_op jit(solution)/shard_map/ppermute | solution.py:474
  67.4 3.8 %collective-permute-start.19 = (f32[12,8,128]{2,1,0:T(8,128)S(1)}, f32[12,8,128]{2,1,0:T(8,128)S(1)}, u32[]{:S(2)}, u32[]{:S(2)}) collective-permute-start(f32[12,8,128]{2,1,0:T(8,128)S(1)} %get-tuple-element.62), channel_id=1, source_target_pairs={{0,28},{4,24},{8,4},{12,0},{16,12},{20,8},{24,20},{28,16},{1,29},{... | collective-permute-start | bytes 147464 | tf_op jit(solution)/shard_map/ppermute | solution.py:480
  (4 other events, 3.5 us)

commit v6 on v5

--- a/solution.py
+++ b/solution.py
@@ -12,6 +12,7 @@
 ROWS = 4
 SHIFTS = 8
 LANES = 128
+BATCH = 5
 F32 = jnp.float32
 
 
@@ -50,6 +51,7 @@
 
 def write_tables(cells, fracs, weights, slopes=None):
     def plane(x, carry):
+        entries = []
         for c in range(3):
             k = cells[c, x]
             t = fracs[c, x]
@@ -64,7 +66,9 @@
                         s = j - 3 - (a - 1)
                         if -2 <= s <= 2:
                             entry = jnp.where(hits[s], values[a], entry)
-                    ref[c, j, x] = entry
+                    entries.append((ref, c, j, entry))
+        for ref, c, j, entry in entries:
+            ref[c, j, x] = entry
         return carry
 
     lax.fori_loop(0, cells.shape[1], plane, 0)
@@ -73,16 +77,21 @@
 def shift_planes(extended, rim, shifted):
     planes, rows, _ = extended.shape
     lane = lane_of(rows)
-    for X in range(planes):
-        core = extended[X]
-        ends = pltpu.roll(rim, (-8 * X) % LANES, 1)
-        for j in range(SHIFTS):
-            d = j - LO
-            if d == 0:
-                shifted[j, X] = core
-            else:
-                wraps = lane >= LANES + d if d < 0 else lane < d
-                shifted[j, X] = pltpu.roll(jnp.where(wraps, ends, core), (-d) % LANES, 1)
+    for first in range(0, planes, BATCH):
+        batch = range(first, min(first + BATCH, planes))
+        cores = {X: extended[X] for X in batch}
+        moved = []
+        for X in batch:
+            ends = pltpu.roll(rim, (-8 * X) % LANES, 1)
+            for j in range(SHIFTS):
+                d = j - LO
+                if d == 0:
+                    moved.append((j, X, cores[X]))
+                else:
+                    wraps = lane >= LANES + d if d < 0 else lane < d
+                    moved.append((j, X, pltpu.roll(jnp.where(wraps, ends, cores[X]), (-d) % LANES, 1)))
+        for j, X, value in moved:
+            shifted[j, X] = value
 
 
 def interpolate(shifted, weights, slopes, nx, ny, emit, with_value):
@@ -127,7 +136,8 @@
 
 def total(terms):
     while len(terms) > 1:
-        terms = [terms[i] + terms[i + 1] for i in range(0, len(terms), 2)]
+        odd = terms[len(terms) & ~1 :]
+        terms = [terms[i] + terms[i + 1] for i in range(0, len(terms) - 1, 2)] + odd
     return terms[0]
 
 
@@ -142,10 +152,10 @@
         piles[...] = jnp.zeros(piles.shape, F32)
 
     def scale(sy, carry):
-        for x in range(nx):
-            ty = weights[1, sy, x]
-            for c in range(channels):
-                scaled[c, sy, x] = sources[c, x] * ty
+        tys = [weights[1, sy, x] for x in range(nx)]
+        products = [(c, x, sources[c, x] * tys[x]) for c in range(channels) for x in range(nx)]
+        for c, x, product in products:
+            scaled[c, sy, x] = product
         return carry
 
     lax.fori_loop(0, SHIFTS, scale, 0)
@@ -186,19 +196,22 @@
     group = group_of(rows)
     for c in range(channels):
         rim = jnp.zeros((rows, LANES), F32)
-        for X in range(planes):
-            core = piles[c, LO, X]
-            ends = jnp.zeros((rows, LANES), F32)
-            for j in range(SHIFTS):
-                d = j - LO
-                if d == 0:
-                    continue
-                moved = pltpu.roll(piles[c, j, X], d % LANES, 1)
-                wraps = lane >= LANES + d if d < 0 else lane < d
-                core = core + jnp.where(wraps, 0.0, moved)
-                ends = ends + jnp.where(wraps, moved, 0.0)
-            out[c, X] = core
-            rim = jnp.where(group == X, pltpu.roll(ends, (8 * X) % LANES, 1), rim)
+        for first in range(0, planes, BATCH):
+            cores = []
+            for X in range(first, min(first + BATCH, planes)):
+                inside, ends = [piles[c, LO, X]], []
+                for j in range(SHIFTS):
+                    d = j - LO
+                    if d == 0:
+                        continue
+                    moved = pltpu.roll(piles[c, j, X], d % LANES, 1)
+                    wraps = lane >= LANES + d if d < 0 else lane < d
+                    inside.append(jnp.where(wraps, 0.0, moved))
+                    ends.append(jnp.where(wraps, moved, 0.0))
+                cores.append((X, total(inside)))
+                rim = jnp.where(group == X, pltpu.roll(total(ends), (8 * X) % LANES, 1), rim)
+            for X, core in cores:
+                out[c, X] = core
         rims[c] = rim
 
 
@@ -310,8 +323,8 @@
 
 def first_kernel(
     nx, ny, intensity, cotangent, cells, fracs,
-    to_y, to_l, to_r, to_ly, to_ry, own, image,
-    cells_here, fracs_here, cotangent_here, sems, weights, scaled, piles, piled, rims,
+    to_y, to_l, to_r, to_ly, to_ry, own,
+    cells_here, fracs_here, cotangent_here, image, sems, weights, scaled, piles, piled, rims,
 ):
     copies = [
         pltpu.make_async_copy(source, target, sems.at[i])
@@ -503,7 +516,7 @@
     return send(rims, (("gz", 1),)), send(rims, (("gz", -1),))
 
 
-FIRST_LIMIT = 55150
+FIRST_LIMIT = 56 * 1024
 
 
 def body(intensity, cotangent, cells, fracs):
@@ -529,11 +542,11 @@
         return [(y, ring, nz), (l, ny, nz), (r, ny, nz), (l, ring, nz), (r, ring, nz)]
 
     part = (3,) + field
-    *outs, own, image = run(
+    *outs, own = run(
         first_kernel,
         (intensity, cotangent, cells, fracs),
-        messages(2 * nx + 1, HI + LO + 1, LO + HI + 1) + [(nx + 1, ny, nz), field],
-        [pltpu.VMEM(part, jnp.int32), part, (1,) + field, pltpu.SemaphoreType.DMA((4,)), table]
+        messages(2 * nx + 1, HI + LO + 1, LO + HI + 1) + [(nx + 1, ny, nz)],
+        [pltpu.VMEM(part, jnp.int32), part, (1,) + field, field, pltpu.SemaphoreType.DMA((4,)), table]
         + pile(1)
         + [(1, planes + 1, rows, nz), (1, rows, nz)],
         2 * unit,
@@ -542,7 +555,7 @@
     )
     extended, folded, rims = run(
         first_join_kernel,
-        (image,) + send_sides(*outs) + (own,),
+        (intensity,) + send_sides(*outs) + (own,),
         [(planes, rows, nz), field, (rows + ny, nz)],
         [],
         unit // 16,

time: 72.3 us -> 72.4 us (level)
  transfers between devices with their start and end apart: 21 -> 21, of which waited for: 9 -> 10; matrix products, arithmetic and copies ran while one was open for 0% -> 0% of each run, Pallas kernels for 9% -> 9%
where the time goes in v6:
time: 72.4 us; the launch traced here: 72 us
  Pallas kernels  27.1 us (37%)
  starting transfers between devices  22 us (30%)
  waiting for transfers between devices  18.5 us (26%)
  local copies, waits for them, and re-layouts  3.53 us (5%)
  between operations  0.77 us (1%)
    pallas_call x9, Pallas kernels, call(): pl.pallas_call(kernel, out_shape=[struct(s) for s in outs], in_specs=in_s...  27.1 us
    ppermute x15, starting transfers between devices, send(): return lax.ppermute(message, axes[0], pairs)  14.3 us
    ppermute x15, waiting for transfers between devices, send(): return lax.ppermute(message, axes[0], pairs)  13.9 us
    ppermute x6, starting transfers between devices, send(): return lax.ppermute(message, axes, pairs)  7.76 us
    ppermute x6, waiting for transfers between devices, send(): return lax.ppermute(message, axes, pairs)  4.64 us
    unnamed x14, local copies, waits for them, and re-layouts  3.53 us
  transfers between devices with their start and end apart: 21, of which 10 were waited for; matrix products, arithmetic and copies ran while one was open for 0% of the time, Pallas kernels for 9%

profile of v6, /device:TPU:0, one launch (start us, length us, event | category | flops | bytes accessed | tf_op | source)
XLA Modules:
  0.0 72.0 jit_solution(9500305424037841629)
XLA Ops:
  0.7 4.3 %shard_map.59 = (f32[17,8,128]{2,1,0:T(8,128)}, f32[8,8,128]{2,1,0:T(8,128)}, f32[8,8,128]{2,1,0:T(8,128)}, f32[8,8,128]{2,1,0:T(8,128)}, f32[8,8,128]{2,1,0:T(8,128)}, /*index=5*/f32[9,8,128]{2,1,0:T(8,128)}) custom-call(f32[8,8,128]{2,1,0:T(8,128)} %intensity.3, f32[1,8,8,128]{3,2,1,0:T(8,128)} %bitcast.1, s32[2,2,3,8,8,128]{5,4,3,2,1,0:T(8,128)} %cells.7, ...), custom_call_target="tpu_custom_call" | custom-call | flops 8388608 | bytes 851968 | tf_op jit(solution)/shard_map/pallas_call | solution.py:470
  5.0 3.0 %collective-permute-start = (f32[17,8,128]{2,1,0:T(8,128)}, f32[17,8,128]{2,1,0:T(8,128)S(1)}, u32[]{:S(2)}, u32[]{:S(2)}) collective-permute-start(f32[17,8,128]{2,1,0:T(8,128)} %get-tuple-element.32), channel_id=1, source_target_pairs={{0,4},{4,0},{1,5},{5,1},{2,6},{6,2},{3,7},{7,3},{8,12},{12,8},{9,1... | collective-permute-start | bytes 208904 | tf_op jit(solution)/shard_map/ppermute | solution.py:487
  8.7 1.7 %collective-permute-start.3 = (f32[8,8,128]{2,1,0:T(8,128)}, f32[8,8,128]{2,1,0:T(8,128)S(1)}, u32[]{:S(2)}, u32[]{:S(2)}) collective-permute-start(f32[8,8,128]{2,1,0:T(8,128)} %get-tuple-element.35), channel_id=1, source_target_pairs={{0,28},{4,24},{8,4},{12,0},{16,12},{20,8},{24,20},{28,16},{1,29},{... | collective-permute-start | bytes 98312 | tf_op jit(solution)/shard_map/ppermute | solution.py:493
  10.6 1.6 %collective-permute-done.2.from_l = f32[8,8,128]{2,1,0:T(8,128)S(1)} collective-permute-done((f32[8,8,128]{2,1,0:T(8,128)}, f32[8,8,128]{2,1,0:T(8,128)S(1)}, u32[]{:S(2)}, u32[]{:S(2)}) %collective-permute-start.2) | collective-permute-done | bytes 32800 | tf_op jit(solution)/shard_map/ppermute | solution.py:487
  12.3 2.5 %collective-permute-done.4.from_ly = f32[8,8,128]{2,1,0:T(8,128)S(1)} collective-permute-done((f32[8,8,128]{2,1,0:T(8,128)}, f32[8,8,128]{2,1,0:T(8,128)S(1)}, u32[]{:S(2)}, u32[]{:S(2)}) %collective-permute-start.4) | collective-permute-done | bytes 32800 | tf_op jit(solution)/shard_map/ppermute | solution.py:493
  16.5 3.7 %collective-permute-start.6 = (f32[24,128]{1,0:T(8,128)S(1)}, f32[24,128]{1,0:T(8,128)S(1)}, u32[]{:S(2)}, u32[]{:S(2)}) collective-permute-start(f32[24,128]{1,0:T(8,128)S(1)} %get-tuple-element.39), channel_id=1, source_target_pairs={{0,3},{1,0},{2,1},{3,2},{4,7},{5,4},{6,5},{7,6},{8,11},{9,8},{10,9... | collective-permute-start | bytes 36872 | tf_op jit(solution)/shard_map/ppermute | solution.py:487
  20.1 1.4 %collective-permute-done.6.rims_r = f32[24,128]{1,0:T(8,128)S(1)} collective-permute-done((f32[24,128]{1,0:T(8,128)S(1)}, f32[24,128]{1,0:T(8,128)S(1)}, u32[]{:S(2)}, u32[]{:S(2)}) %collective-permute-start.6) | collective-permute-done | bytes 12320 | tf_op jit(solution)/shard_map/ppermute | solution.py:487
  21.5 4.1 %collective-permute-done.5.rims_l = f32[24,128]{1,0:T(8,128)S(1)} collective-permute-done((f32[24,128]{1,0:T(8,128)S(1)}, f32[24,128]{1,0:T(8,128)S(1)}, u32[]{:S(2)}, u32[]{:S(2)}) %collective-permute-start.5) | collective-permute-done | bytes 12320 | tf_op jit(solution)/shard_map/ppermute | solution.py:487
  25.6 1.0 %copy-done = s32[2,2,3,8,8,128]{5,4,3,2,1,0:T(8,128)S(1)} copy-done((s32[2,2,3,8,8,128]{5,4,3,2,1,0:T(8,128)S(1)}, s32[2,2,3,8,8,128]{5,4,3,2,1,0:T(8,128)}, u32[]{:S(2)}) %copy-start) | copy-done | bytes 393240
  26.6 1.0 %copy-done.2 = f32[2,2,3,8,8,128]{5,4,3,2,1,0:T(8,128)S(1)} copy-done((f32[2,2,3,8,8,128]{5,4,3,2,1,0:T(8,128)S(1)}, f32[2,2,3,8,8,128]{5,4,3,2,1,0:T(8,128)}, u32[]{:S(2)}) %copy-start.2) | copy-done | bytes 393240
  27.6 4.0 %shard_map.61 = (f32[8,8,128]{2,1,0:T(8,128)S(1)}, f32[8,8,128]{2,1,0:T(8,128)S(1)}, f32[4,8,128]{2,1,0:T(8,128)S(1)}, f32[3,8,128]{2,1,0:T(8,128)S(1)}, f32[4,8...) custom-call(f32[15,16,128]{2,1,0:T(8,128)S(1)} %get-tuple-element.38, ...), custom_call_target="tpu_custom_call" | custom-call | flops 20971520 | bytes 966656 | tf_op jit(solution)/shard_map/pallas_call | solution.py:470
  31.7 1.5 %collective-permute-start.7 = (f32[8,8,128]{2,1,0:T(8,128)S(1)}, f32[8,8,128]{2,1,0:T(8,128)S(1)}, u32[]{:S(2)}, u32[]{:S(2)}) collective-permute-start(f32[8,8,128]{2,1,0:T(8,128)S(1)} %get-tuple-element.42), channel_id=1, source_target_pairs={{0,4},{4,0},{1,5},{5,1},{2,6},{6,2},{3,7},{7,3},{8,12},{12,8},{9,1... | collective-permute-start | bytes 98312 | tf_op jit(solution)/shard_map/ppermute | solution.py:487
  33.2 1.0 %collective-permute-start.10 = (f32[4,8,128]{2,1,0:T(8,128)S(1)}, f32[4,8,128]{2,1,0:T(8,128)S(1)}, u32[]{:S(2)}, u32[]{:S(2)}) collective-permute-start(f32[4,8,128]{2,1,0:T(8,128)S(1)} %get-tuple-element.45), channel_id=1, source_target_pairs={{0,28},{4,24},{8,4},{12,0},{16,12},{20,8},{24,20},{28,16},{1,29},{... | collective-permute-start | bytes 49160 | tf_op jit(solution)/shard_map/ppermute | solution.py:493
  34.2 2.3 %collective-permute-start.11 = (f32[3,8,128]{2,1,0:T(8,128)S(1)}, f32[3,8,128]{2,1,0:T(8,128)S(1)}, u32[]{:S(2)}, u32[]{:S(2)}) collective-permute-start(f32[3,8,128]{2,1,0:T(8,128)S(1)} %get-tuple-element.46), channel_id=1, source_target_pairs={{0,12},{4,8},{8,20},{12,16},{16,28},{20,24},{24,4},{28,0},{1,13},{... | collective-permute-start | bytes 36872 | tf_op jit(solution)/shard_map/ppermute | solution.py:493
  36.5 2.5 %shard_map.62 = (f32[1,15,16,128]{3,2,1,0:T(8,128)S(1)}, f32[1,16,128]{2,1,0:T(8,128)S(1)}) custom-call(f32[1,8,8,128]{3,2,1,0:T(8,128)S(1)} %get-tuple-element.47.adjoint, f32[3,8,8,8,128]{4,3,2,1,0:T(8,128)S(1)} %get-tuple-element.48.weights), custom_call_target="tpu_custom_call" | custom-call | flops 8388608 | bytes 819200 | tf_op jit(solution)/shard_map/pallas_call | solution.py:470
  39.2 2.0 %collective-permute-start.12 = (f32[16,128]{1,0:T(8,128)S(1)}, f32[16,128]{1,0:T(8,128)S(1)}, u32[]{:S(2)}, u32[]{:S(2)}) collective-permute-start(f32[16,128]{1,0:T(8,128)S(1)} %get-tuple-element.51), channel_id=1, source_target_pairs={{0,1},{1,2},{2,3},{3,0},{4,5},{5,6},{6,7},{7,4},{8,9},{9,10},{10,1... | collective-permute-start | bytes 24584 | tf_op jit(solution)/shard_map/ppermute | solution.py:487
  41.2 4.1 %shard_map.64.early_piles = f32[3,8,15,16,128]{4,3,2,1,0:T(8,128)S(1)} custom-call(f32[3,8,8,128]{3,2,1,0:T(8,128)S(1)} %get-tuple-element.53.gradient, f32[1,8,8,128]{3,2,1,0:T(8,128)S(1)} %get-tuple-element.47.adjoint, s32[2,2,3,8,8,128]{5,4,3,2,1,0:T(8,128)S(1)} %copy-done.1, f32[2,2,3,8,8,128]{5,4,3,2,1,0:T(8,128)S(1)} %copy-done.3), custom_call_target="tpu_custom_call" | custom-call | flops 25165824 | bytes 917504 | tf_op jit(solution)/shard_map/pallas_call | solution.py:470
  45.3 11.1 %shard_map.65 = (f32[3,15,16,128]{3,2,1,0:T(8,128)S(1)}, f32[64,128]{1,0:T(8,128)S(1)}, f32[3,8,15,16,128]{4,3,2,1,0:T(8,128)S(1)}) custom-call(f32[15,16,128]{2,1,0:T(8,128)S(1)} %get-tuple-element.50.extended, f32[16,128]{1,0:T(8,128)S(1)} %collective-permute-done.12.rims_l, ...), custom_call_target="tpu_custom_call", output_to_operand_aliasing={{2}: (7, {})} | custom-call | flops 46137344 | bytes 3915776 | tf_op jit(solution)/shard_map/pallas_call | solution.py:470
  56.4 1.9 %collective-permute-start.15 = (f32[64,128]{1,0:T(8,128)S(1)}, f32[64,128]{1,0:T(8,128)S(1)}, u32[]{:S(2)}, u32[]{:S(2)}) collective-permute-start(f32[64,128]{1,0:T(8,128)S(1)} %get-tuple-element.55), channel_id=1, source_target_pairs={{0,3},{1,0},{2,1},{3,2},{4,7},{5,4},{6,5},{7,6},{8,11},{9,8},{10,9... | collective-permute-start | bytes 98312 | tf_op jit(solution)/shard_map/ppermute | solution.py:487
  58.4 1.9 %collective-permute-done.15.rims_r = f32[64,128]{1,0:T(8,128)S(1)} collective-permute-done((f32[64,128]{1,0:T(8,128)S(1)}, f32[64,128]{1,0:T(8,128)S(1)}, u32[]{:S(2)}, u32[]{:S(2)}) %collective-permute-start.15) | collective-permute-done | bytes 32800 | tf_op jit(solution)/shard_map/ppermute | solution.py:487
  60.3 3.7 %collective-permute-done.14.rims_l = f32[64,128]{1,0:T(8,128)S(1)} collective-permute-done((f32[64,128]{1,0:T(8,128)S(1)}, f32[64,128]{1,0:T(8,128)S(1)}, u32[]{:S(2)}, u32[]{:S(2)}) %collective-permute-start.14) | collective-permute-done | bytes 32800 | tf_op jit(solution)/shard_map/ppermute | solution.py:487
  64.9 2.0 %collective-permute-start.20 = (f32[16,8,128]{2,1,0:T(8,128)S(1)}, f32[16,8,128]{2,1,0:T(8,128)S(1)}, u32[]{:S(2)}, u32[]{:S(2)}) collective-permute-start(f32[16,8,128]{2,1,0:T(8,128)S(1)} %get-tuple-element.61), channel_id=1, source_target_pairs={{0,12},{4,8},{8,20},{12,16},{16,28},{20,24},{24,4},{28,0},{1,13},{... | collective-permute-start | bytes 196616 | tf_op jit(solution)/shard_map/ppermute | solution.py:493
  68.2 1.0 %collective-permute-done.17.from_r = f32[12,8,128]{2,1,0:T(8,128)S(1)} collective-permute-done((f32[12,8,128]{2,1,0:T(8,128)S(1)}, f32[12,8,128]{2,1,0:T(8,128)S(1)}, u32[]{:S(2)}, u32[]{:S(2)}) %collective-permute-start.17) | collective-permute-done | bytes 49184 | tf_op jit(solution)/shard_map/ppermute | solution.py:487
  69.2 2.0 %collective-permute-done.19.from_ry = f32[12,8,128]{2,1,0:T(8,128)S(1)} collective-permute-done((f32[12,8,128]{2,1,0:T(8,128)S(1)}, f32[12,8,128]{2,1,0:T(8,128)S(1)}, u32[]{:S(2)}, u32[]{:S(2)}) %collective-permute-start.19) | collective-permute-done | bytes 49184 | tf_op jit(solution)/shard_map/ppermute | solution.py:493
  (41 shorter events, 5.8 us)
Async XLA Ops:
  0.6 40.6 %copy-start.3 = (f32[2,2,3,8,8,128]{5,4,3,2,1,0:T(8,128)S(1)}, f32[2,2,3,8,8,128]{5,4,3,2,1,0:T(8,128)}, u32[]{:S(2)}) copy-start(f32[2,2,3,8,8,128]{5,4,3,2,1,0:T(8,128)} %fracs.7) | copy-start | bytes 1179652
  0.6 40.6 %copy-start.1 = (s32[2,2,3,8,8,128]{5,4,3,2,1,0:T(8,128)S(1)}, s32[2,2,3,8,8,128]{5,4,3,2,1,0:T(8,128)}, u32[]{:S(2)}) copy-start(s32[2,2,3,8,8,128]{5,4,3,2,1,0:T(8,128)} %cells.7) | copy-start | bytes 1179652
  5.0 9.8 %collective-permute-start = (f32[17,8,128]{2,1,0:T(8,128)}, f32[17,8,128]{2,1,0:T(8,128)S(1)}, u32[]{:S(2)}, u32[]{:S(2)}) collective-permute-start(f32[17,8,128]{2,1,0:T(8,128)} %get-tuple-element.32), channel_id=1, source_target_pairs={{0,4},{4,0},{1,5},{5,1},{2,6},{6,2},{3,7},{7,3},{8,12},{12,8},{9,1... | collective-permute-start | bytes 208904 | tf_op jit(solution)/shard_map/ppermute | solution.py:487
  8.0 2.6 %collective-permute-start.1 = (f32[8,8,128]{2,1,0:T(8,128)}, f32[8,8,128]{2,1,0:T(8,128)S(1)}, u32[]{:S(2)}, u32[]{:S(2)}) collective-permute-start(f32[8,8,128]{2,1,0:T(8,128)} %get-tuple-element.33), channel_id=1, source_target_pairs={{0,24},{8,0},{16,8},{24,16},{1,25},{9,1},{17,9},{25,17},{2,26},{10... | collective-permute-start | bytes 98312 | tf_op jit(solution)/shard_map/ppermute | solution.py:487
  8.7 3.6 %collective-permute-start.2 = (f32[8,8,128]{2,1,0:T(8,128)}, f32[8,8,128]{2,1,0:T(8,128)S(1)}, u32[]{:S(2)}, u32[]{:S(2)}) collective-permute-start(f32[8,8,128]{2,1,0:T(8,128)} %get-tuple-element.34), channel_id=1, source_target_pairs={{0,8},{8,16},{16,24},{24,0},{1,9},{9,17},{17,25},{25,1},{2,10},{10... | collective-permute-start | bytes 98312 | tf_op jit(solution)/shard_map/ppermute | solution.py:487
  8.7 3.6 %collective-permute-start.3 = (f32[8,8,128]{2,1,0:T(8,128)}, f32[8,8,128]{2,1,0:T(8,128)S(1)}, u32[]{:S(2)}, u32[]{:S(2)}) collective-permute-start(f32[8,8,128]{2,1,0:T(8,128)} %get-tuple-element.35), channel_id=1, source_target_pairs={{0,28},{4,24},{8,4},{12,0},{16,12},{20,8},{24,20},{28,16},{1,29},{... | collective-permute-start | bytes 98312 | tf_op jit(solution)/shard_map/ppermute | solution.py:493
  10.4 4.4 %collective-permute-start.4 = (f32[8,8,128]{2,1,0:T(8,128)}, f32[8,8,128]{2,1,0:T(8,128)S(1)}, u32[]{:S(2)}, u32[]{:S(2)}) collective-permute-start(f32[8,8,128]{2,1,0:T(8,128)} %get-tuple-element.36), channel_id=1, source_target_pairs={{0,12},{4,8},{8,20},{12,16},{16,28},{20,24},{24,4},{28,0},{1,13},{... | collective-permute-start | bytes 98312 | tf_op jit(solution)/shard_map/ppermute | solution.py:493
  16.5 5.1 %collective-permute-start.6 = (f32[24,128]{1,0:T(8,128)S(1)}, f32[24,128]{1,0:T(8,128)S(1)}, u32[]{:S(2)}, u32[]{:S(2)}) collective-permute-start(f32[24,128]{1,0:T(8,128)S(1)} %get-tuple-element.39), channel_id=1, source_target_pairs={{0,3},{1,0},{2,1},{3,2},{4,7},{5,4},{6,5},{7,6},{8,11},{9,8},{10,9... | collective-permute-start | bytes 36872 | tf_op jit(solution)/shard_map/ppermute | solution.py:487
  20.1 5.5 %collective-permute-start.5 = (f32[24,128]{1,0:T(8,128)S(1)}, f32[24,128]{1,0:T(8,128)S(1)}, u32[]{:S(2)}, u32[]{:S(2)}) collective-permute-start(f32[24,128]{1,0:T(8,128)S(1)} %get-tuple-element.39), channel_id=1, source_target_pairs={{0,1},{1,2},{2,3},{3,0},{4,5},{5,6},{6,7},{7,4},{8,9},{9,10},{10,1... | collective-permute-start | bytes 36872 | tf_op jit(solution)/shard_map/ppermute | solution.py:487
  27.6 17.7 %copy-start.4 = (f32[8,8,128]{2,1,0:T(8,128)S(1)}, f32[8,8,128]{2,1,0:T(8,128)}, u32[]{:S(2)}) copy-start(f32[8,8,128]{2,1,0:T(8,128)} %param.5) | copy-start | bytes 98308
  31.7 7.4 %collective-permute-start.7 = (f32[8,8,128]{2,1,0:T(8,128)S(1)}, f32[8,8,128]{2,1,0:T(8,128)S(1)}, u32[]{:S(2)}, u32[]{:S(2)}) collective-permute-start(f32[8,8,128]{2,1,0:T(8,128)S(1)} %get-tuple-element.42), channel_id=1, source_target_pairs={{0,4},{4,0},{1,5},{5,1},{2,6},{6,2},{3,7},{7,3},{8,12},{12,8},{9,1... | collective-permute-start | bytes 98312 | tf_op jit(solution)/shard_map/ppermute | solution.py:487
  33.2 5.8 %collective-permute-start.8 = (f32[4,8,128]{2,1,0:T(8,128)S(1)}, f32[4,8,128]{2,1,0:T(8,128)S(1)}, u32[]{:S(2)}, u32[]{:S(2)}) collective-permute-start(f32[4,8,128]{2,1,0:T(8,128)S(1)} %get-tuple-element.43), channel_id=1, source_target_pairs={{0,24},{8,0},{16,8},{24,16},{1,25},{9,1},{17,9},{25,17},{2,26},{10... | collective-permute-start | bytes 49160 | tf_op jit(solution)/shard_map/ppermute | solution.py:487
  33.2 5.8 %collective-permute-start.10 = (f32[4,8,128]{2,1,0:T(8,128)S(1)}, f32[4,8,128]{2,1,0:T(8,128)S(1)}, u32[]{:S(2)}, u32[]{:S(2)}) collective-permute-start(f32[4,8,128]{2,1,0:T(8,128)S(1)} %get-tuple-element.45), channel_id=1, source_target_pairs={{0,28},{4,24},{8,4},{12,0},{16,12},{20,8},{24,20},{28,16},{1,29},{... | collective-permute-start | bytes 49160 | tf_op jit(solution)/shard_map/ppermute | solution.py:493
  34.2 4.8 %collective-permute-start.9 = (f32[3,8,128]{2,1,0:T(8,128)S(1)}, f32[3,8,128]{2,1,0:T(8,128)S(1)}, u32[]{:S(2)}, u32[]{:S(2)}) collective-permute-start(f32[3,8,128]{2,1,0:T(8,128)S(1)} %get-tuple-element.44), channel_id=1, source_target_pairs={{0,8},{8,16},{16,24},{24,0},{1,9},{9,17},{17,25},{25,1},{2,10},{10... | collective-permute-start | bytes 36872 | tf_op jit(solution)/shard_map/ppermute | solution.py:487
  34.2 4.8 %collective-permute-start.11 = (f32[3,8,128]{2,1,0:T(8,128)S(1)}, f32[3,8,128]{2,1,0:T(8,128)S(1)}, u32[]{:S(2)}, u32[]{:S(2)}) collective-permute-start(f32[3,8,128]{2,1,0:T(8,128)S(1)} %get-tuple-element.46), channel_id=1, source_target_pairs={{0,12},{4,8},{8,20},{12,16},{16,28},{20,24},{24,4},{28,0},{1,13},{... | collective-permute-start | bytes 36872 | tf_op jit(solution)/shard_map/ppermute | solution.py:493
  39.1 6.1 %collective-permute-start.13 = (f32[16,128]{1,0:T(8,128)S(1)}, f32[16,128]{1,0:T(8,128)S(1)}, u32[]{:S(2)}, u32[]{:S(2)}) collective-permute-start(f32[16,128]{1,0:T(8,128)S(1)} %get-tuple-element.51), channel_id=1, source_target_pairs={{0,3},{1,0},{2,1},{3,2},{4,7},{5,4},{6,5},{7,6},{8,11},{9,8},{10,9... | collective-permute-start | bytes 24584 | tf_op jit(solution)/shard_map/ppermute | solution.py:487
  39.2 6.1 %collective-permute-start.12 = (f32[16,128]{1,0:T(8,128)S(1)}, f32[16,128]{1,0:T(8,128)S(1)}, u32[]{:S(2)}, u32[]{:S(2)}) collective-permute-start(f32[16,128]{1,0:T(8,128)S(1)} %get-tuple-element.51), channel_id=1, source_target_pairs={{0,1},{1,2},{2,3},{3,0},{4,5},{5,6},{6,7},{7,4},{8,9},{9,10},{10,1... | collective-permute-start | bytes 24584 | tf_op jit(solution)/shard_map/ppermute | solution.py:487
  56.4 3.9 %collective-permute-start.15 = (f32[64,128]{1,0:T(8,128)S(1)}, f32[64,128]{1,0:T(8,128)S(1)}, u32[]{:S(2)}, u32[]{:S(2)}) collective-permute-start(f32[64,128]{1,0:T(8,128)S(1)} %get-tuple-element.55), channel_id=1, source_target_pairs={{0,3},{1,0},{2,1},{3,2},{4,7},{5,4},{6,5},{7,6},{8,11},{9,8},{10,9... | collective-permute-start | bytes 98312 | tf_op jit(solution)/shard_map/ppermute | solution.py:487
  58.3 5.7 %collective-permute-start.14 = (f32[64,128]{1,0:T(8,128)S(1)}, f32[64,128]{1,0:T(8,128)S(1)}, u32[]{:S(2)}, u32[]{:S(2)}) collective-permute-start(f32[64,128]{1,0:T(8,128)S(1)} %get-tuple-element.55), channel_id=1, source_target_pairs={{0,1},{1,2},{2,3},{3,0},{4,5},{5,6},{6,7},{7,4},{8,9},{9,10},{10,1... | collective-permute-start | bytes 98312 | tf_op jit(solution)/shard_map/ppermute | solution.py:487
  64.2 7.1 %collective-permute-start.16 = (f32[32,8,128]{2,1,0:T(8,128)S(1)}, f32[32,8,128]{2,1,0:T(8,128)S(1)}, u32[]{:S(2)}, u32[]{:S(2)}) collective-permute-start(f32[32,8,128]{2,1,0:T(8,128)S(1)} %get-tuple-element.57), channel_id=1, source_target_pairs={{0,4},{4,0},{1,5},{5,1},{2,6},{6,2},{3,7},{7,3},{8,12},{12,8},{9,1... | collective-permute-start | bytes 393224 | tf_op jit(solution)/shard_map/ppermute | solution.py:487
  64.9 6.4 %collective-permute-start.18 = (f32[16,8,128]{2,1,0:T(8,128)S(1)}, f32[16,8,128]{2,1,0:T(8,128)S(1)}, u32[]{:S(2)}, u32[]{:S(2)}) collective-permute-start(f32[16,8,128]{2,1,0:T(8,128)S(1)} %get-tuple-element.59), channel_id=1, source_target_pairs={{0,8},{8,16},{16,24},{24,0},{1,9},{9,17},{17,25},{25,1},{2,10},{10... | collective-permute-start | bytes 196616 | tf_op jit(solution)/shard_map/ppermute | solution.py:487
  64.9 6.4 %collective-permute-start.20 = (f32[16,8,128]{2,1,0:T(8,128)S(1)}, f32[16,8,128]{2,1,0:T(8,128)S(1)}, u32[]{:S(2)}, u32[]{:S(2)}) collective-permute-start(f32[16,8,128]{2,1,0:T(8,128)S(1)} %get-tuple-element.61), channel_id=1, source_target_pairs={{0,12},{4,8},{8,20},{12,16},{16,28},{20,24},{24,4},{28,0},{1,13},{... | collective-permute-start | bytes 196616 | tf_op jit(solution)/shard_map/ppermute | solution.py:493
  66.8 2.4 %collective-permute-start.17 = (f32[12,8,128]{2,1,0:T(8,128)S(1)}, f32[12,8,128]{2,1,0:T(8,128)S(1)}, u32[]{:S(2)}, u32[]{:S(2)}) collective-permute-start(f32[12,8,128]{2,1,0:T(8,128)S(1)} %get-tuple-element.58), channel_id=1, source_target_pairs={{0,24},{8,0},{16,8},{24,16},{1,25},{9,1},{17,9},{25,17},{2,26},{10... | collective-permute-start | bytes 147464 | tf_op jit(solution)/shard_map/ppermute | solution.py:487
  67.5 3.8 %collective-permute-start.19 = (f32[12,8,128]{2,1,0:T(8,128)S(1)}, f32[12,8,128]{2,1,0:T(8,128)S(1)}, u32[]{:S(2)}, u32[]{:S(2)}) collective-permute-start(f32[12,8,128]{2,1,0:T(8,128)S(1)} %get-tuple-element.60), channel_id=1, source_target_pairs={{0,28},{4,24},{8,4},{12,0},{16,12},{20,8},{24,20},{28,16},{1,29},{... | collective-permute-start | bytes 147464 | tf_op jit(solution)/shard_map/ppermute | solution.py:493
  (4 other events, 3.5 us)

commit v7 on v5

--- a/solution.py
+++ b/solution.py
@@ -50,6 +50,7 @@
 
 def write_tables(cells, fracs, weights, slopes=None):
     def plane(x, carry):
+        entries = []
         for c in range(3):
             k = cells[c, x]
             t = fracs[c, x]
@@ -64,25 +65,28 @@
                         s = j - 3 - (a - 1)
                         if -2 <= s <= 2:
                             entry = jnp.where(hits[s], values[a], entry)
-                    ref[c, j, x] = entry
+                    entries.append((ref, c, j, entry))
+        for ref, c, j, entry in entries:
+            ref[c, j, x] = entry
         return carry
 
     lax.fori_loop(0, cells.shape[1], plane, 0)
 
 
-def shift_planes(extended, rim, shifted):
+def shift_planes(extended, rim, ends, shifted):
     planes, rows, _ = extended.shape
     lane = lane_of(rows)
     for X in range(planes):
-        core = extended[X]
-        ends = pltpu.roll(rim, (-8 * X) % LANES, 1)
+        ends[X] = pltpu.roll(rim, (-8 * X) % LANES, 1)
+    for X in range(planes):
+        core, end = extended[X], ends[X]
         for j in range(SHIFTS):
             d = j - LO
             if d == 0:
                 shifted[j, X] = core
             else:
                 wraps = lane >= LANES + d if d < 0 else lane < d
-                shifted[j, X] = pltpu.roll(jnp.where(wraps, ends, core), (-d) % LANES, 1)
+                shifted[j, X] = pltpu.roll(jnp.where(wraps, end, core), (-d) % LANES, 1)
 
 
 def interpolate(shifted, weights, slopes, nx, ny, emit, with_value):
@@ -127,7 +131,8 @@
 
 def total(terms):
     while len(terms) > 1:
-        terms = [terms[i] + terms[i + 1] for i in range(0, len(terms), 2)]
+        odd = terms[len(terms) & ~1 :]
+        terms = [terms[i] + terms[i + 1] for i in range(0, len(terms) - 1, 2)] + odd
     return terms[0]
 
 
@@ -142,10 +147,10 @@
         piles[...] = jnp.zeros(piles.shape, F32)
 
     def scale(sy, carry):
-        for x in range(nx):
-            ty = weights[1, sy, x]
-            for c in range(channels):
-                scaled[c, sy, x] = sources[c, x] * ty
+        tys = [weights[1, sy, x] for x in range(nx)]
+        products = [(c, x, sources[c, x] * tys[x]) for c in range(channels) for x in range(nx)]
+        for c, x, product in products:
+            scaled[c, sy, x] = product
         return carry
 
     lax.fori_loop(0, SHIFTS, scale, 0)
@@ -180,26 +185,24 @@
     lax.fori_loop(0, SHIFTS // ys, row, 0)
 
 
-def settle(piles, out, rims):
+def settle(piles, ends, out, rims):
     channels, planes, rows, _ = out.shape
     lane = lane_of(rows)
-    group = group_of(rows)
     for c in range(channels):
-        rim = jnp.zeros((rows, LANES), F32)
         for X in range(planes):
-            core = piles[c, LO, X]
-            ends = jnp.zeros((rows, LANES), F32)
+            inside, outside = [piles[c, LO, X]], []
             for j in range(SHIFTS):
                 d = j - LO
                 if d == 0:
                     continue
                 moved = pltpu.roll(piles[c, j, X], d % LANES, 1)
                 wraps = lane >= LANES + d if d < 0 else lane < d
-                core = core + jnp.where(wraps, 0.0, moved)
-                ends = ends + jnp.where(wraps, moved, 0.0)
-            out[c, X] = core
-            rim = jnp.where(group == X, pltpu.roll(ends, (8 * X) % LANES, 1), rim)
-        rims[c] = rim
+                inside.append(jnp.where(wraps, 0.0, moved))
+                outside.append(jnp.where(wraps, moved, 0.0))
+            out[c, X] = total(inside)
+            ends[c, X] = total(outside)
+    for c in range(channels):
+        rims[c] = pack_rim(ends.at[c])
 
 
 def pack_rim(extended):
@@ -310,29 +313,14 @@
 
 def first_kernel(
     nx, ny, intensity, cotangent, cells, fracs,
-    to_y, to_l, to_r, to_ly, to_ry, own, image,
-    cells_here, fracs_here, cotangent_here, sems, weights, scaled, piles, piled, rims,
+    to_y, to_l, to_r, to_ly, to_ry, own,
+    weights, scaled, piles, ends, piled, rims,
 ):
-    copies = [
-        pltpu.make_async_copy(source, target, sems.at[i])
-        for i, (source, target) in enumerate(
-            (
-                (cells.at[1, 1], cells_here),
-                (fracs.at[1, 1], fracs_here),
-                (cotangent, cotangent_here),
-                (intensity, image),
-            )
-        )
-    ]
-    for copy in copies:
-        copy.start()
-    for copy in copies:
-        copy.wait()
-    write_tables(cells_here, fracs_here, weights)
-    deposit(cotangent_here, weights, scaled, piles, 2, SHIFTS)
-    settle(piles, piled.at[:, 0 : nx + LO + HI], rims)
+    write_tables(cells.at[1, 1], fracs.at[1, 1], weights)
+    deposit(cotangent, weights, scaled, piles, 2, SHIFTS)
+    settle(piles, ends, piled.at[:, 0 : nx + LO + HI], rims)
     piled[0, nx + LO + HI] = rims[0]
-    split_halo(image, (to_y, to_l, to_r, to_ly, to_ry), nx, ny)
+    split_halo(intensity, (to_y, to_l, to_r, to_ly, to_ry), nx, ny)
     split_deposits(piled.at[0], (to_y, to_l, to_r, to_ly, to_ry, own), (nx, HI, LO, 0), nx, ny)
 
 
@@ -350,11 +338,11 @@
 def middle_kernel(
     nx, ny, extended, rims_l, rims_r, part, cells, fracs,
     image, to_y, to_l, to_r, to_ly, to_ry, adjoint, gradient, weights,
-    shifted, slopes,
+    shifted, ends, slopes,
 ):
     rows = ny + 2 * ROWS
     rim = jnp.where(low_lanes(rows), rims_r[0:rows], rims_l[0:rows])
-    shift_planes(extended, rim, shifted)
+    shift_planes(extended, rim, ends, shifted)
     write_tables(cells.at[0, 1], fracs.at[0, 1], weights, slopes)
 
     def emit(x, sums):
@@ -369,9 +357,9 @@
         adjoint[0, x] = part[x] + unpack_rim(back, LO + x)
 
 
-def adjoint_kernel(nx, ny, adjoint, weights, piled, rims, scaled, piles):
+def adjoint_kernel(nx, ny, adjoint, weights, piled, rims, scaled, piles, ends):
     deposit(adjoint, weights, scaled, piles, 2, SHIFTS)
-    settle(piles, piled, rims)
+    settle(piles, ends, piled, rims)
 
 
 def early_kernel(nx, ny, gradient, adjoint, cells, fracs, piles, product, weights, scaled):
@@ -390,10 +378,10 @@
 def late_kernel(
     nx, ny, extended, rims_l, rims_r, cotangent, cells, fracs, adjoint_rims, early_piles,
     piled, rims, piles,
-    shifted, weights, slopes, product, scaled, rims_here,
+    shifted, ends, weights, slopes, product, scaled, rims_here,
 ):
     rows = ny + 2 * ROWS
-    shift_planes(extended, jnp.where(low_lanes(rows), rims_r[...], rims_l[...]), shifted)
+    shift_planes(extended, jnp.where(low_lanes(rows), rims_r[...], rims_l[...]), ends.at[0], shifted)
     write_tables(cells.at[1, 1], fracs.at[1, 1], weights, slopes)
 
     def emit(x, sums):
@@ -403,7 +391,7 @@
     interpolate(shifted, weights, slopes, nx, ny, emit, False)
     write_tables(cells.at[1, 0], fracs.at[1, 0], weights)
     deposit(product, weights, scaled, piles, 1, SHIFTS // 2, fresh=False)
-    settle(piles, piled, rims_here)
+    settle(piles, ends, piled, rims_here)
     for c in range(3):
         rims[c * rows : (c + 1) * rows] = rims_here[c]
     rims[3 * rows : 4 * rows] = adjoint_rims[0]
@@ -445,7 +433,7 @@
                 velocity_adjoint[c, x] = plane
 
 
-def call(kernel, args, outs, scratch, flops, spaces=None, limit=24 * 1024, aliases=None):
+def call(kernel, args, outs, scratch, flops, spaces=None, aliases=None):
     def struct(shape):
         return jax.ShapeDtypeStruct(shape, F32)
 
@@ -461,7 +449,7 @@
         out_specs=[in_vmem] * len(outs),
         scratch_shapes=[pltpu.VMEM(s, F32) if isinstance(s, tuple) else s for s in scratch],
         input_output_aliases=aliases or {},
-        compiler_params=pltpu.CompilerParams(vmem_limit_bytes=limit * 1024),
+        compiler_params=pltpu.CompilerParams(vmem_limit_bytes=24 * 1024 * 1024),
         cost_estimate=pl.CostEstimate(flops=flops, bytes_accessed=moved, transcendentals=0),
     )(*args)
 
@@ -503,9 +491,6 @@
     return send(rims, (("gz", 1),)), send(rims, (("gz", -1),))
 
 
-FIRST_LIMIT = 55150
-
-
 def body(intensity, cotangent, cells, fracs):
     nx, ny, nz = intensity.shape
     rows = ny + 2 * ROWS
@@ -528,21 +513,16 @@
     def messages(y, l, r):
         return [(y, ring, nz), (l, ny, nz), (r, ny, nz), (l, ring, nz), (r, ring, nz)]
 
-    part = (3,) + field
-    *outs, own, image = run(
+    *outs, own = run(
         first_kernel,
         (intensity, cotangent, cells, fracs),
-        messages(2 * nx + 1, HI + LO + 1, LO + HI + 1) + [(nx + 1, ny, nz), field],
-        [pltpu.VMEM(part, jnp.int32), part, (1,) + field, pltpu.SemaphoreType.DMA((4,)), table]
-        + pile(1)
-        + [(1, planes + 1, rows, nz), (1, rows, nz)],
+        messages(2 * nx + 1, HI + LO + 1, LO + HI + 1) + [(nx + 1, ny, nz)],
+        [table] + pile(1) + [(1, planes, rows, nz), (1, planes + 1, rows, nz), (1, rows, nz)],
         2 * unit,
-        spaces=dict.fromkeys(range(4), pltpu.HBM),
-        limit=FIRST_LIMIT,
     )
     extended, folded, rims = run(
         first_join_kernel,
-        (image,) + send_sides(*outs) + (own,),
+        (intensity,) + send_sides(*outs) + (own,),
         [(planes, rows, nz), field, (rows + ny, nz)],
         [],
         unit // 16,
@@ -551,7 +531,7 @@
         middle_kernel,
         (extended,) + send_z(rims) + (folded, cells, fracs),
         [field] + messages(nx, HI, LO) + [(1,) + field, (3,) + field, table],
-        [(SHIFTS, planes, rows, nz), table],
+        [(SHIFTS, planes, rows, nz), (planes, rows, nz), table],
         5 * unit,
     )
 
@@ -560,7 +540,7 @@
         adjoint_kernel,
         (adjoint, weights),
         piled(1),
-        pile(1),
+        pile(1) + [(1, planes, rows, nz)],
         2 * unit,
     )
     extended, rims = run(
@@ -585,7 +565,7 @@
         late_kernel,
         (extended, rims_l, rims_r, cotangent, cells, fracs, adjoint_rims, piles),
         [(3, planes, rows, nz), (4 * rows, nz), piles_3],
-        [(SHIFTS, planes, rows, nz), table, table, (3,) + field, scaled_3, (3, rows, nz)],
+        [(SHIFTS, planes, rows, nz), (3, planes, rows, nz), table, table, (3,) + field, scaled_3, (3, rows, nz)],
         11 * unit,
         aliases={7: 2},
     )

time: 72.3 us -> 68.4 us (0.946)
  Pallas kernels: 27 us -> 21.2 us
  local copies, waits for them, and re-layouts: 3.53 us -> 5.5 us
    pallas_call x9, Pallas kernels: 27 us -> 21.2 us  [call(): pl.pallas_call(kernel, out_shape=[struct(s) for s in outs], in_specs=in_s...]
    unnamed x14 -> x18, local copies, waits for them, and re-layouts: 3.53 us -> 5.5 us
  transfers between devices with their start and end apart: 21 -> 21, of which waited for: 9 -> 8; matrix products, arithmetic and copies ran while one was open for 0% -> 0% of each run, Pallas kernels for 9% -> 9%
where the time goes in v7:
time: 68.4 us; the launch traced here: 67.9 us
  starting transfers between devices  22.5 us (33%)
  Pallas kernels  21.2 us (31%)
  waiting for transfers between devices  17.9 us (26%)
  local copies, waits for them, and re-layouts  5.5 us (8%)
  between operations  0.76 us (1%)
    pallas_call x9, Pallas kernels, call(): pl.pallas_call(kernel, out_shape=[struct(s) for s in outs], in_specs=in_s...  21.2 us
    ppermute x15, starting transfers between devices, send(): return lax.ppermute(message, axes[0], pairs)  14.7 us
    ppermute x15, waiting for transfers between devices, send(): return lax.ppermute(message, axes[0], pairs)  13.2 us
    ppermute x6, starting transfers between devices, send(): return lax.ppermute(message, axes, pairs)  7.84 us
    unnamed x18, local copies, waits for them, and re-layouts  5.5 us
    ppermute x6, waiting for transfers between devices, send(): return lax.ppermute(message, axes, pairs)  4.71 us
  transfers between devices with their start and end apart: 21, of which 8 were waited for; matrix products, arithmetic and copies ran while one was open for 0% of the time, Pallas kernels for 9%

profile of v7, /device:TPU:0, one launch (start us, length us, event | category | flops | bytes accessed | tf_op | source)
XLA Modules:
  0.0 67.9 jit_solution(13173235809450385030)
XLA Ops:
  4.1 2.1 %shard_map.59 = (f32[17,8,128]{2,1,0:T(8,128)S(1)}, f32[8,8,128]{2,1,0:T(8,128)S(1)}, f32[8,8,128]{2,1,0:T(8,128)S(1)}, f32[8,8,128]{2,1,0:T(8,128)S(1)}, f32[8,...) custom-call(f32[8,8,128]{2,1,0:T(8,128)S(1)} %copy-done.8, f32[1,8,8,128]{3,2,1,0:T(8,128)S(1)} %bitcast.1, ...), custom_call_target="tpu_custom_call" | custom-call | flops 8388608 | bytes 851968 | tf_op jit(solution)/shard_map/pallas_call | solution.py:445
  6.3 3.0 %collective-permute-start = (f32[17,8,128]{2,1,0:T(8,128)S(1)}, f32[17,8,128]{2,1,0:T(8,128)S(1)}, u32[]{:S(2)}, u32[]{:S(2)}) collective-permute-start(f32[17,8,128]{2,1,0:T(8,128)S(1)} %get-tuple-element.32), channel_id=1, source_target_pairs={{0,4},{4,0},{1,5},{5,1},{2,6},{6,2},{3,7},{7,3},{8,12},{12,8},{9,1... | collective-permute-start | bytes 208904 | tf_op jit(solution)/shard_map/ppermute | solution.py:462
  9.9 1.7 %collective-permute-start.3 = (f32[8,8,128]{2,1,0:T(8,128)S(1)}, f32[8,8,128]{2,1,0:T(8,128)S(1)}, u32[]{:S(2)}, u32[]{:S(2)}) collective-permute-start(f32[8,8,128]{2,1,0:T(8,128)S(1)} %get-tuple-element.35), channel_id=1, source_target_pairs={{0,28},{4,24},{8,4},{12,0},{16,12},{20,8},{24,20},{28,16},{1,29},{... | collective-permute-start | bytes 98312 | tf_op jit(solution)/shard_map/ppermute | solution.py:468
  11.7 1.6 %collective-permute-done.2.from_l = f32[8,8,128]{2,1,0:T(8,128)S(1)} collective-permute-done((f32[8,8,128]{2,1,0:T(8,128)S(1)}, f32[8,8,128]{2,1,0:T(8,128)S(1)}, u32[]{:S(2)}, u32[]{:S(2)}) %collective-permute-start.2) | collective-permute-done | bytes 32800 | tf_op jit(solution)/shard_map/ppermute | solution.py:462
  13.3 2.6 %collective-permute-done.4.from_ly = f32[8,8,128]{2,1,0:T(8,128)S(1)} collective-permute-done((f32[8,8,128]{2,1,0:T(8,128)S(1)}, f32[8,8,128]{2,1,0:T(8,128)S(1)}, u32[]{:S(2)}, u32[]{:S(2)}) %collective-permute-start.4) | collective-permute-done | bytes 32800 | tf_op jit(solution)/shard_map/ppermute | solution.py:468
  16.0 3.7 %collective-permute-start.6 = (f32[24,128]{1,0:T(8,128)S(1)}, f32[24,128]{1,0:T(8,128)S(1)}, u32[]{:S(2)}, u32[]{:S(2)}) collective-permute-start(f32[24,128]{1,0:T(8,128)S(1)} %get-tuple-element.39), channel_id=1, source_target_pairs={{0,3},{1,0},{2,1},{3,2},{4,7},{5,4},{6,5},{7,6},{8,11},{9,8},{10,9... | collective-permute-start | bytes 36872 | tf_op jit(solution)/shard_map/ppermute | solution.py:462
  19.6 1.4 %collective-permute-done.6.rims_r = f32[24,128]{1,0:T(8,128)S(1)} collective-permute-done((f32[24,128]{1,0:T(8,128)S(1)}, f32[24,128]{1,0:T(8,128)S(1)}, u32[]{:S(2)}, u32[]{:S(2)}) %collective-permute-start.6) | collective-permute-done | bytes 12320 | tf_op jit(solution)/shard_map/ppermute | solution.py:462
  21.0 4.1 %collective-permute-done.5.rims_l = f32[24,128]{1,0:T(8,128)S(1)} collective-permute-done((f32[24,128]{1,0:T(8,128)S(1)}, f32[24,128]{1,0:T(8,128)S(1)}, u32[]{:S(2)}, u32[]{:S(2)}) %collective-permute-start.5) | collective-permute-done | bytes 12320 | tf_op jit(solution)/shard_map/ppermute | solution.py:462
  25.1 1.0 %copy-done.1 = s32[2,2,3,8,8,128]{5,4,3,2,1,0:T(8,128)S(1)} copy-done((s32[2,2,3,8,8,128]{5,4,3,2,1,0:T(8,128)S(1)}, s32[2,2,3,8,8,128]{5,4,3,2,1,0:T(8,128)}, u32[]{:S(2)}) %copy-start.1) | copy-done | bytes 393240
  27.1 3.5 %shard_map.61 = (f32[8,8,128]{2,1,0:T(8,128)S(1)}, f32[8,8,128]{2,1,0:T(8,128)S(1)}, f32[4,8,128]{2,1,0:T(8,128)S(1)}, f32[3,8,128]{2,1,0:T(8,128)S(1)}, f32[4,8...) custom-call(f32[15,16,128]{2,1,0:T(8,128)S(1)} %get-tuple-element.38, ...), custom_call_target="tpu_custom_call" | custom-call | flops 20971520 | bytes 966656 | tf_op jit(solution)/shard_map/pallas_call | solution.py:445
  30.7 1.5 %collective-permute-start.7 = (f32[8,8,128]{2,1,0:T(8,128)S(1)}, f32[8,8,128]{2,1,0:T(8,128)S(1)}, u32[]{:S(2)}, u32[]{:S(2)}) collective-permute-start(f32[8,8,128]{2,1,0:T(8,128)S(1)} %get-tuple-element.42), channel_id=1, source_target_pairs={{0,4},{4,0},{1,5},{5,1},{2,6},{6,2},{3,7},{7,3},{8,12},{12,8},{9,1... | collective-permute-start | bytes 98312 | tf_op jit(solution)/shard_map/ppermute | solution.py:462
  32.2 1.0 %collective-permute-start.10 = (f32[4,8,128]{2,1,0:T(8,128)S(1)}, f32[4,8,128]{2,1,0:T(8,128)S(1)}, u32[]{:S(2)}, u32[]{:S(2)}) collective-permute-start(f32[4,8,128]{2,1,0:T(8,128)S(1)} %get-tuple-element.45), channel_id=1, source_target_pairs={{0,28},{4,24},{8,4},{12,0},{16,12},{20,8},{24,20},{28,16},{1,29},{... | collective-permute-start | bytes 49160 | tf_op jit(solution)/shard_map/ppermute | solution.py:468
  33.2 2.3 %collective-permute-start.11 = (f32[3,8,128]{2,1,0:T(8,128)S(1)}, f32[3,8,128]{2,1,0:T(8,128)S(1)}, u32[]{:S(2)}, u32[]{:S(2)}) collective-permute-start(f32[3,8,128]{2,1,0:T(8,128)S(1)} %get-tuple-element.46), channel_id=1, source_target_pairs={{0,12},{4,8},{8,20},{12,16},{16,28},{20,24},{24,4},{28,0},{1,13},{... | collective-permute-start | bytes 36872 | tf_op jit(solution)/shard_map/ppermute | solution.py:468
  35.5 2.0 %shard_map.62 = (f32[1,15,16,128]{3,2,1,0:T(8,128)S(1)}, f32[1,16,128]{2,1,0:T(8,128)S(1)}) custom-call(f32[1,8,8,128]{3,2,1,0:T(8,128)S(1)} %get-tuple-element.47.adjoint, f32[3,8,8,8,128]{4,3,2,1,0:T(8,128)S(1)} %get-tuple-element.48.weights), custom_call_target="tpu_custom_call" | custom-call | flops 8388608 | bytes 819200 | tf_op jit(solution)/shard_map/pallas_call | solution.py:445
  37.8 2.0 %collective-permute-start.12 = (f32[16,128]{1,0:T(8,128)S(1)}, f32[16,128]{1,0:T(8,128)S(1)}, u32[]{:S(2)}, u32[]{:S(2)}) collective-permute-start(f32[16,128]{1,0:T(8,128)S(1)} %get-tuple-element.51), channel_id=1, source_target_pairs={{0,1},{1,2},{2,3},{3,0},{4,5},{5,6},{6,7},{7,4},{8,9},{9,10},{10,1... | collective-permute-start | bytes 24584 | tf_op jit(solution)/shard_map/ppermute | solution.py:462
  39.8 4.1 %shard_map.64.early_piles = f32[3,8,15,16,128]{4,3,2,1,0:T(8,128)S(1)} custom-call(f32[3,8,8,128]{3,2,1,0:T(8,128)S(1)} %get-tuple-element.53.gradient, f32[1,8,8,128]{3,2,1,0:T(8,128)S(1)} %get-tuple-element.47.adjoint, s32[2,2,3,8,8,128]{5,4,3,2,1,0:T(8,128)S(1)} %copy-done.2, f32[2,2,3,8,8,128]{5,4,3,2,1,0:T(8,128)S(1)} %copy-done.5), custom_call_target="tpu_custom_call" | custom-call | flops 25165824 | bytes 917504 | tf_op jit(solution)/shard_map/pallas_call | solution.py:445
  43.9 8.4 %shard_map.65 = (f32[3,15,16,128]{3,2,1,0:T(8,128)S(1)}, f32[64,128]{1,0:T(8,128)S(1)}, f32[3,8,15,16,128]{4,3,2,1,0:T(8,128)S(1)}) custom-call(f32[15,16,128]{2,1,0:T(8,128)S(1)} %get-tuple-element.50.extended, f32[16,128]{1,0:T(8,128)S(1)} %collective-permute-done.12.rims_l, ...), custom_call_target="tpu_custom_call", output_to_operand_aliasing={{2}: (7, {})} | custom-call | flops 46137344 | bytes 3915776 | tf_op jit(solution)/shard_map/pallas_call | solution.py:445
  52.2 1.9 %collective-permute-start.15 = (f32[64,128]{1,0:T(8,128)S(1)}, f32[64,128]{1,0:T(8,128)S(1)}, u32[]{:S(2)}, u32[]{:S(2)}) collective-permute-start(f32[64,128]{1,0:T(8,128)S(1)} %get-tuple-element.55), channel_id=1, source_target_pairs={{0,3},{1,0},{2,1},{3,2},{4,7},{5,4},{6,5},{7,6},{8,11},{9,8},{10,9... | collective-permute-start | bytes 98312 | tf_op jit(solution)/shard_map/ppermute | solution.py:462
  54.3 1.9 %collective-permute-done.15.rims_r = f32[64,128]{1,0:T(8,128)S(1)} collective-permute-done((f32[64,128]{1,0:T(8,128)S(1)}, f32[64,128]{1,0:T(8,128)S(1)}, u32[]{:S(2)}, u32[]{:S(2)}) %collective-permute-start.15) | collective-permute-done | bytes 32800 | tf_op jit(solution)/shard_map/ppermute | solution.py:462
  56.2 3.7 %collective-permute-done.14.rims_l = f32[64,128]{1,0:T(8,128)S(1)} collective-permute-done((f32[64,128]{1,0:T(8,128)S(1)}, f32[64,128]{1,0:T(8,128)S(1)}, u32[]{:S(2)}, u32[]{:S(2)}) %collective-permute-start.14) | collective-permute-done | bytes 32800 | tf_op jit(solution)/shard_map/ppermute | solution.py:462
  60.1 1.1 %collective-permute-start.16 = (f32[32,8,128]{2,1,0:T(8,128)S(1)}, f32[32,8,128]{2,1,0:T(8,128)S(1)}, u32[]{:S(2)}, u32[]{:S(2)}) collective-permute-start(f32[32,8,128]{2,1,0:T(8,128)S(1)} %get-tuple-element.57), channel_id=1, source_target_pairs={{0,4},{4,0},{1,5},{5,1},{2,6},{6,2},{3,7},{7,3},{8,12},{12,8},{9,1... | collective-permute-start | bytes 393224 | tf_op jit(solution)/shard_map/ppermute | solution.py:462
  61.2 1.6 %collective-permute-start.20 = (f32[16,8,128]{2,1,0:T(8,128)S(1)}, f32[16,8,128]{2,1,0:T(8,128)S(1)}, u32[]{:S(2)}, u32[]{:S(2)}) collective-permute-start(f32[16,8,128]{2,1,0:T(8,128)S(1)} %get-tuple-element.61), channel_id=1, source_target_pairs={{0,12},{4,8},{8,20},{12,16},{16,28},{20,24},{24,4},{28,0},{1,13},{... | collective-permute-start | bytes 196616 | tf_op jit(solution)/shard_map/ppermute | solution.py:468
  63.3 1.2 %collective-permute-start.19 = (f32[12,8,128]{2,1,0:T(8,128)S(1)}, f32[12,8,128]{2,1,0:T(8,128)S(1)}, u32[]{:S(2)}, u32[]{:S(2)}) collective-permute-start(f32[12,8,128]{2,1,0:T(8,128)S(1)} %get-tuple-element.60), channel_id=1, source_target_pairs={{0,28},{4,24},{8,4},{12,0},{16,12},{20,8},{24,20},{28,16},{1,29},{... | collective-permute-start | bytes 147464 | tf_op jit(solution)/shard_map/ppermute | solution.py:468
  65.1 2.1 %collective-permute-done.19.from_ry = f32[12,8,128]{2,1,0:T(8,128)S(1)} collective-permute-done((f32[12,8,128]{2,1,0:T(8,128)S(1)}, f32[12,8,128]{2,1,0:T(8,128)S(1)}, u32[]{:S(2)}, u32[]{:S(2)}) %collective-permute-start.19) | collective-permute-done | bytes 49184 | tf_op jit(solution)/shard_map/ppermute | solution.py:468
  (45 shorter events, 7.7 us)
Async XLA Ops:
  4.1 35.6 %copy-start.2 = (s32[2,2,3,8,8,128]{5,4,3,2,1,0:T(8,128)S(1)}, s32[2,2,3,8,8,128]{5,4,3,2,1,0:T(8,128)}, u32[]{:S(2)}) copy-start(s32[2,2,3,8,8,128]{5,4,3,2,1,0:T(8,128)} %cells.7) | copy-start | bytes 1179652
  4.1 35.6 %copy-start.5 = (f32[2,2,3,8,8,128]{5,4,3,2,1,0:T(8,128)S(1)}, f32[2,2,3,8,8,128]{5,4,3,2,1,0:T(8,128)}, u32[]{:S(2)}) copy-start(f32[2,2,3,8,8,128]{5,4,3,2,1,0:T(8,128)} %fracs.7) | copy-start | bytes 1179652
  6.3 9.6 %collective-permute-start = (f32[17,8,128]{2,1,0:T(8,128)S(1)}, f32[17,8,128]{2,1,0:T(8,128)S(1)}, u32[]{:S(2)}, u32[]{:S(2)}) collective-permute-start(f32[17,8,128]{2,1,0:T(8,128)S(1)} %get-tuple-element.32), channel_id=1, source_target_pairs={{0,4},{4,0},{1,5},{5,1},{2,6},{6,2},{3,7},{7,3},{8,12},{12,8},{9,1... | collective-permute-start | bytes 208904 | tf_op jit(solution)/shard_map/ppermute | solution.py:462
  9.3 2.4 %collective-permute-start.1 = (f32[8,8,128]{2,1,0:T(8,128)S(1)}, f32[8,8,128]{2,1,0:T(8,128)S(1)}, u32[]{:S(2)}, u32[]{:S(2)}) collective-permute-start(f32[8,8,128]{2,1,0:T(8,128)S(1)} %get-tuple-element.33), channel_id=1, source_target_pairs={{0,24},{8,0},{16,8},{24,16},{1,25},{9,1},{17,9},{25,17},{2,26},{10... | collective-permute-start | bytes 98312 | tf_op jit(solution)/shard_map/ppermute | solution.py:462
  9.9 3.3 %collective-permute-start.2 = (f32[8,8,128]{2,1,0:T(8,128)S(1)}, f32[8,8,128]{2,1,0:T(8,128)S(1)}, u32[]{:S(2)}, u32[]{:S(2)}) collective-permute-start(f32[8,8,128]{2,1,0:T(8,128)S(1)} %get-tuple-element.34), channel_id=1, source_target_pairs={{0,8},{8,16},{16,24},{24,0},{1,9},{9,17},{17,25},{25,1},{2,10},{10... | collective-permute-start | bytes 98312 | tf_op jit(solution)/shard_map/ppermute | solution.py:462
  9.9 3.3 %collective-permute-start.3 = (f32[8,8,128]{2,1,0:T(8,128)S(1)}, f32[8,8,128]{2,1,0:T(8,128)S(1)}, u32[]{:S(2)}, u32[]{:S(2)}) collective-permute-start(f32[8,8,128]{2,1,0:T(8,128)S(1)} %get-tuple-element.35), channel_id=1, source_target_pairs={{0,28},{4,24},{8,4},{12,0},{16,12},{20,8},{24,20},{28,16},{1,29},{... | collective-permute-start | bytes 98312 | tf_op jit(solution)/shard_map/ppermute | solution.py:468
  11.6 4.2 %collective-permute-start.4 = (f32[8,8,128]{2,1,0:T(8,128)S(1)}, f32[8,8,128]{2,1,0:T(8,128)S(1)}, u32[]{:S(2)}, u32[]{:S(2)}) collective-permute-start(f32[8,8,128]{2,1,0:T(8,128)S(1)} %get-tuple-element.36), channel_id=1, source_target_pairs={{0,12},{4,8},{8,20},{12,16},{16,28},{20,24},{24,4},{28,0},{1,13},{... | collective-permute-start | bytes 98312 | tf_op jit(solution)/shard_map/ppermute | solution.py:468
  16.0 5.1 %collective-permute-start.6 = (f32[24,128]{1,0:T(8,128)S(1)}, f32[24,128]{1,0:T(8,128)S(1)}, u32[]{:S(2)}, u32[]{:S(2)}) collective-permute-start(f32[24,128]{1,0:T(8,128)S(1)} %get-tuple-element.39), channel_id=1, source_target_pairs={{0,3},{1,0},{2,1},{3,2},{4,7},{5,4},{6,5},{7,6},{8,11},{9,8},{10,9... | collective-permute-start | bytes 36872 | tf_op jit(solution)/shard_map/ppermute | solution.py:462
  19.6 5.5 %collective-permute-start.5 = (f32[24,128]{1,0:T(8,128)S(1)}, f32[24,128]{1,0:T(8,128)S(1)}, u32[]{:S(2)}, u32[]{:S(2)}) collective-permute-start(f32[24,128]{1,0:T(8,128)S(1)} %get-tuple-element.39), channel_id=1, source_target_pairs={{0,1},{1,2},{2,3},{3,0},{4,5},{5,6},{6,7},{7,4},{8,9},{9,10},{10,1... | collective-permute-start | bytes 36872 | tf_op jit(solution)/shard_map/ppermute | solution.py:462
  27.1 16.7 %copy-start.7 = (f32[8,8,128]{2,1,0:T(8,128)S(1)}, f32[8,8,128]{2,1,0:T(8,128)}, u32[]{:S(2)}) copy-start(f32[8,8,128]{2,1,0:T(8,128)} %param.5) | copy-start | bytes 98308
  30.7 6.9 %collective-permute-start.7 = (f32[8,8,128]{2,1,0:T(8,128)S(1)}, f32[8,8,128]{2,1,0:T(8,128)S(1)}, u32[]{:S(2)}, u32[]{:S(2)}) collective-permute-start(f32[8,8,128]{2,1,0:T(8,128)S(1)} %get-tuple-element.42), channel_id=1, source_target_pairs={{0,4},{4,0},{1,5},{5,1},{2,6},{6,2},{3,7},{7,3},{8,12},{12,8},{9,1... | collective-permute-start | bytes 98312 | tf_op jit(solution)/shard_map/ppermute | solution.py:462
  32.2 5.4 %collective-permute-start.8 = (f32[4,8,128]{2,1,0:T(8,128)S(1)}, f32[4,8,128]{2,1,0:T(8,128)S(1)}, u32[]{:S(2)}, u32[]{:S(2)}) collective-permute-start(f32[4,8,128]{2,1,0:T(8,128)S(1)} %get-tuple-element.43), channel_id=1, source_target_pairs={{0,24},{8,0},{16,8},{24,16},{1,25},{9,1},{17,9},{25,17},{2,26},{10... | collective-permute-start | bytes 49160 | tf_op jit(solution)/shard_map/ppermute | solution.py:462
  32.2 5.4 %collective-permute-start.10 = (f32[4,8,128]{2,1,0:T(8,128)S(1)}, f32[4,8,128]{2,1,0:T(8,128)S(1)}, u32[]{:S(2)}, u32[]{:S(2)}) collective-permute-start(f32[4,8,128]{2,1,0:T(8,128)S(1)} %get-tuple-element.45), channel_id=1, source_target_pairs={{0,28},{4,24},{8,4},{12,0},{16,12},{20,8},{24,20},{28,16},{1,29},{... | collective-permute-start | bytes 49160 | tf_op jit(solution)/shard_map/ppermute | solution.py:468
  33.2 4.3 %collective-permute-start.9 = (f32[3,8,128]{2,1,0:T(8,128)S(1)}, f32[3,8,128]{2,1,0:T(8,128)S(1)}, u32[]{:S(2)}, u32[]{:S(2)}) collective-permute-start(f32[3,8,128]{2,1,0:T(8,128)S(1)} %get-tuple-element.44), channel_id=1, source_target_pairs={{0,8},{8,16},{16,24},{24,0},{1,9},{9,17},{17,25},{25,1},{2,10},{10... | collective-permute-start | bytes 36872 | tf_op jit(solution)/shard_map/ppermute | solution.py:462
  33.2 4.3 %collective-permute-start.11 = (f32[3,8,128]{2,1,0:T(8,128)S(1)}, f32[3,8,128]{2,1,0:T(8,128)S(1)}, u32[]{:S(2)}, u32[]{:S(2)}) collective-permute-start(f32[3,8,128]{2,1,0:T(8,128)S(1)} %get-tuple-element.46), channel_id=1, source_target_pairs={{0,12},{4,8},{8,20},{12,16},{16,28},{20,24},{24,4},{28,0},{1,13},{... | collective-permute-start | bytes 36872 | tf_op jit(solution)/shard_map/ppermute | solution.py:468
  37.7 6.1 %collective-permute-start.13 = (f32[16,128]{1,0:T(8,128)S(1)}, f32[16,128]{1,0:T(8,128)S(1)}, u32[]{:S(2)}, u32[]{:S(2)}) collective-permute-start(f32[16,128]{1,0:T(8,128)S(1)} %get-tuple-element.51), channel_id=1, source_target_pairs={{0,3},{1,0},{2,1},{3,2},{4,7},{5,4},{6,5},{7,6},{8,11},{9,8},{10,9... | collective-permute-start | bytes 24584 | tf_op jit(solution)/shard_map/ppermute | solution.py:462
  37.8 6.1 %collective-permute-start.12 = (f32[16,128]{1,0:T(8,128)S(1)}, f32[16,128]{1,0:T(8,128)S(1)}, u32[]{:S(2)}, u32[]{:S(2)}) collective-permute-start(f32[16,128]{1,0:T(8,128)S(1)} %get-tuple-element.51), channel_id=1, source_target_pairs={{0,1},{1,2},{2,3},{3,0},{4,5},{5,6},{6,7},{7,4},{8,9},{9,10},{10,1... | collective-permute-start | bytes 24584 | tf_op jit(solution)/shard_map/ppermute | solution.py:462
  52.2 4.0 %collective-permute-start.15 = (f32[64,128]{1,0:T(8,128)S(1)}, f32[64,128]{1,0:T(8,128)S(1)}, u32[]{:S(2)}, u32[]{:S(2)}) collective-permute-start(f32[64,128]{1,0:T(8,128)S(1)} %get-tuple-element.55), channel_id=1, source_target_pairs={{0,3},{1,0},{2,1},{3,2},{4,7},{5,4},{6,5},{7,6},{8,11},{9,8},{10,9... | collective-permute-start | bytes 98312 | tf_op jit(solution)/shard_map/ppermute | solution.py:462
  54.2 5.7 %collective-permute-start.14 = (f32[64,128]{1,0:T(8,128)S(1)}, f32[64,128]{1,0:T(8,128)S(1)}, u32[]{:S(2)}, u32[]{:S(2)}) collective-permute-start(f32[64,128]{1,0:T(8,128)S(1)} %get-tuple-element.55), channel_id=1, source_target_pairs={{0,1},{1,2},{2,3},{3,0},{4,5},{5,6},{6,7},{7,4},{8,9},{9,10},{10,1... | collective-permute-start | bytes 98312 | tf_op jit(solution)/shard_map/ppermute | solution.py:462
  60.1 7.2 %collective-permute-start.16 = (f32[32,8,128]{2,1,0:T(8,128)S(1)}, f32[32,8,128]{2,1,0:T(8,128)S(1)}, u32[]{:S(2)}, u32[]{:S(2)}) collective-permute-start(f32[32,8,128]{2,1,0:T(8,128)S(1)} %get-tuple-element.57), channel_id=1, source_target_pairs={{0,4},{4,0},{1,5},{5,1},{2,6},{6,2},{3,7},{7,3},{8,12},{12,8},{9,1... | collective-permute-start | bytes 393224 | tf_op jit(solution)/shard_map/ppermute | solution.py:462
  61.2 6.0 %collective-permute-start.18 = (f32[16,8,128]{2,1,0:T(8,128)S(1)}, f32[16,8,128]{2,1,0:T(8,128)S(1)}, u32[]{:S(2)}, u32[]{:S(2)}) collective-permute-start(f32[16,8,128]{2,1,0:T(8,128)S(1)} %get-tuple-element.59), channel_id=1, source_target_pairs={{0,8},{8,16},{16,24},{24,0},{1,9},{9,17},{17,25},{25,1},{2,10},{10... | collective-permute-start | bytes 196616 | tf_op jit(solution)/shard_map/ppermute | solution.py:462
  61.2 6.0 %collective-permute-start.20 = (f32[16,8,128]{2,1,0:T(8,128)S(1)}, f32[16,8,128]{2,1,0:T(8,128)S(1)}, u32[]{:S(2)}, u32[]{:S(2)}) collective-permute-start(f32[16,8,128]{2,1,0:T(8,128)S(1)} %get-tuple-element.61), channel_id=1, source_target_pairs={{0,12},{4,8},{8,20},{12,16},{16,28},{20,24},{24,4},{28,0},{1,13},{... | collective-permute-start | bytes 196616 | tf_op jit(solution)/shard_map/ppermute | solution.py:468
  62.8 2.3 %collective-permute-start.17 = (f32[12,8,128]{2,1,0:T(8,128)S(1)}, f32[12,8,128]{2,1,0:T(8,128)S(1)}, u32[]{:S(2)}, u32[]{:S(2)}) collective-permute-start(f32[12,8,128]{2,1,0:T(8,128)S(1)} %get-tuple-element.58), channel_id=1, source_target_pairs={{0,24},{8,0},{16,8},{24,16},{1,25},{9,1},{17,9},{25,17},{2,26},{10... | collective-permute-start | bytes 147464 | tf_op jit(solution)/shard_map/ppermute | solution.py:462
  63.3 3.9 %collective-permute-start.19 = (f32[12,8,128]{2,1,0:T(8,128)S(1)}, f32[12,8,128]{2,1,0:T(8,128)S(1)}, u32[]{:S(2)}, u32[]{:S(2)}) collective-permute-start(f32[12,8,128]{2,1,0:T(8,128)S(1)} %get-tuple-element.60), channel_id=1, source_target_pairs={{0,28},{4,24},{8,4},{12,0},{16,12},{20,8},{24,20},{28,16},{1,29},{... | collective-permute-start | bytes 147464 | tf_op jit(solution)/shard_map/ppermute | solution.py:468
  (6 other events, 5.5 us)

commit v8 on v7

--- a/solution.py
+++ b/solution.py
@@ -48,7 +48,7 @@
     )
 
 
-def write_tables(cells, fracs, weights, slopes=None):
+def write_tables(cells, fracs, weights=None, slopes=None):
     def plane(x, carry):
         entries = []
         for c in range(3):
@@ -311,12 +311,16 @@
         put_edges(to_right_y, i, field[nx - LO + i], ny)
 
 
+def table_kernel(nx, ny, cells, fracs, late, early, early_slopes):
+    write_tables(cells.at[1, 1], fracs.at[1, 1], late)
+    write_tables(cells.at[0, 1], fracs.at[0, 1], early, early_slopes)
+
+
 def first_kernel(
-    nx, ny, intensity, cotangent, cells, fracs,
+    nx, ny, intensity, cotangent, weights,
     to_y, to_l, to_r, to_ly, to_ry, own,
-    weights, scaled, piles, ends, piled, rims,
+    scaled, piles, ends, piled, rims,
 ):
-    write_tables(cells.at[1, 1], fracs.at[1, 1], weights)
     deposit(cotangent, weights, scaled, piles, 2, SHIFTS)
     settle(piles, ends, piled.at[:, 0 : nx + LO + HI], rims)
     piled[0, nx + LO + HI] = rims[0]
@@ -336,14 +340,13 @@
 
 
 def middle_kernel(
-    nx, ny, extended, rims_l, rims_r, part, cells, fracs,
-    image, to_y, to_l, to_r, to_ly, to_ry, adjoint, gradient, weights,
-    shifted, ends, slopes,
+    nx, ny, extended, rims_l, rims_r, part, weights, slopes,
+    image, to_y, to_l, to_r, to_ly, to_ry, adjoint, gradient,
+    shifted, ends,
 ):
     rows = ny + 2 * ROWS
     rim = jnp.where(low_lanes(rows), rims_r[0:rows], rims_l[0:rows])
     shift_planes(extended, rim, ends, shifted)
-    write_tables(cells.at[0, 1], fracs.at[0, 1], weights, slopes)
 
     def emit(x, sums):
         image[x] = sums[3]
@@ -357,13 +360,19 @@
         adjoint[0, x] = part[x] + unpack_rim(back, LO + x)
 
 
-def adjoint_kernel(nx, ny, adjoint, weights, piled, rims, scaled, piles, ends):
+def adjoint_kernel(
+    nx, ny, adjoint, weights, cells, fracs,
+    piled, rims, early_mid, late_slopes, late_mid,
+    scaled, piles, ends,
+):
     deposit(adjoint, weights, scaled, piles, 2, SHIFTS)
     settle(piles, ends, piled, rims)
-
-
-def early_kernel(nx, ny, gradient, adjoint, cells, fracs, piles, product, weights, scaled):
-    write_tables(cells.at[0, 0], fracs.at[0, 0], weights)
+    write_tables(cells.at[0, 0], fracs.at[0, 0], early_mid)
+    write_tables(cells.at[1, 1], fracs.at[1, 1], None, late_slopes)
+    write_tables(cells.at[1, 0], fracs.at[1, 0], late_mid)
+
+
+def early_kernel(nx, ny, gradient, adjoint, weights, piles, product, scaled):
     for c in range(3):
         for x in range(nx):
             product[c, x] = adjoint[0, x] * gradient[c, x]
@@ -376,21 +385,19 @@
 
 
 def late_kernel(
-    nx, ny, extended, rims_l, rims_r, cotangent, cells, fracs, adjoint_rims, early_piles,
+    nx, ny, extended, rims_l, rims_r, cotangent, weights, slopes, mid_weights, adjoint_rims, early_piles,
     piled, rims, piles,
-    shifted, ends, weights, slopes, product, scaled, rims_here,
+    shifted, ends, product, scaled, rims_here,
 ):
     rows = ny + 2 * ROWS
     shift_planes(extended, jnp.where(low_lanes(rows), rims_r[...], rims_l[...]), ends.at[0], shifted)
-    write_tables(cells.at[1, 1], fracs.at[1, 1], weights, slopes)
 
     def emit(x, sums):
         for c in range(3):
             product[c, x] = cotangent[0, x] * sums[c]
 
     interpolate(shifted, weights, slopes, nx, ny, emit, False)
-    write_tables(cells.at[1, 0], fracs.at[1, 0], weights)
-    deposit(product, weights, scaled, piles, 1, SHIFTS // 2, fresh=False)
+    deposit(product, mid_weights, scaled, piles, 1, SHIFTS // 2, fresh=False)
     settle(piles, ends, piled, rims_here)
     for c in range(3):
         rims[c * rows : (c + 1) * rows] = rims_here[c]
@@ -513,11 +520,18 @@
     def messages(y, l, r):
         return [(y, ring, nz), (l, ny, nz), (r, ny, nz), (l, ring, nz), (r, ring, nz)]
 
+    late, early, early_slopes = run(
+        table_kernel,
+        (cells, fracs),
+        [table, table, table],
+        [],
+        unit // 16,
+    )
     *outs, own = run(
         first_kernel,
-        (intensity, cotangent, cells, fracs),
+        (intensity, cotangent, late),
         messages(2 * nx + 1, HI + LO + 1, LO + HI + 1) + [(nx + 1, ny, nz)],
-        [table] + pile(1) + [(1, planes, rows, nz), (1, planes + 1, rows, nz), (1, rows, nz)],
+        pile(1) + [(1, planes, rows, nz), (1, planes + 1, rows, nz), (1, rows, nz)],
         2 * unit,
     )
     extended, folded, rims = run(
@@ -527,19 +541,19 @@
         [],
         unit // 16,
     )
-    image, *outs, adjoint, gradient, weights = run(
+    image, *outs, adjoint, gradient = run(
         middle_kernel,
-        (extended,) + send_z(rims) + (folded, cells, fracs),
-        [field] + messages(nx, HI, LO) + [(1,) + field, (3,) + field, table],
-        [(SHIFTS, planes, rows, nz), (planes, rows, nz), table],
+        (extended,) + send_z(rims) + (folded, early, early_slopes),
+        [field] + messages(nx, HI, LO) + [(1,) + field, (3,) + field],
+        [(SHIFTS, planes, rows, nz), (planes, rows, nz)],
         5 * unit,
     )
 
     sides = send_sides(*outs)
-    piled_adjoint, adjoint_rims = run(
+    piled_adjoint, adjoint_rims, early_mid, late_slopes, late_mid = run(
         adjoint_kernel,
-        (adjoint, weights),
-        piled(1),
+        (adjoint, early, cells, fracs),
+        piled(1) + [table, table, table],
         pile(1) + [(1, planes, rows, nz)],
         2 * unit,
     )
@@ -555,19 +569,19 @@
     scaled_3, piles_3 = pile(3)
     (piles,) = run(
         early_kernel,
-        (gradient, adjoint, cells, fracs),
+        (gradient, adjoint, early_mid),
         [piles_3],
-        [(3,) + field, table, scaled_3],
+        [(3,) + field, scaled_3],
         6 * unit,
     )
 
     velocity, rims, _ = run(
         late_kernel,
-        (extended, rims_l, rims_r, cotangent, cells, fracs, adjoint_rims, piles),
+        (extended, rims_l, rims_r, cotangent, late, late_slopes, late_mid, adjoint_rims, piles),
         [(3, planes, rows, nz), (4 * rows, nz), piles_3],
-        [(SHIFTS, planes, rows, nz), (3, planes, rows, nz), table, table, (3,) + field, scaled_3, (3, rows, nz)],
+        [(SHIFTS, planes, rows, nz), (3, planes, rows, nz), (3,) + field, scaled_3, (3, rows, nz)],
         11 * unit,
-        aliases={7: 2},
+        aliases={8: 2},
     )
     *outs, own = run(
         last_z_kernel,

time: 68.4 us -> 66.3 us (0.969)
  local copies, waits for them, and re-layouts: 5.5 us -> 3.5 us
    unnamed x18 -> x12, local copies, waits for them, and re-layouts: 5.5 us -> 3.5 us
    pallas_call x9 -> x10, Pallas kernels: 21.2 us -> 21.2 us  [call(): pl.pallas_call(kernel, out_shape=[struct(s) for s in outs], in_specs=in_s...]
  transfers between devices with their start and end apart: 21 -> 21, of which waited for: 8 -> 8; matrix products, arithmetic and copies ran while one was open for 0% -> 0% of each run, Pallas kernels for 9% -> 10%
where the time goes in v8:
time: 66.3 us; the launch traced here: 66 us
  starting transfers between devices  22.1 us (33%)
  Pallas kernels  21.2 us (32%)
  waiting for transfers between devices  18.3 us (28%)
  local copies, waits for them, and re-layouts  3.5 us (5%)
  between operations  0.79 us (1%)
    pallas_call x10, Pallas kernels, call(): pl.pallas_call(kernel, out_shape=[struct(s) for s in outs], in_specs=in_s...  21.2 us
    ppermute x15, starting transfers between devices, send(): return lax.ppermute(message, axes[0], pairs)  14.4 us
    ppermute x15, waiting for transfers between devices, send(): return lax.ppermute(message, axes[0], pairs)  13.6 us
    ppermute x6, starting transfers between devices, send(): return lax.ppermute(message, axes, pairs)  7.76 us
    ppermute x6, waiting for transfers between devices, send(): return lax.ppermute(message, axes, pairs)  4.68 us
    unnamed x12, local copies, waits for them, and re-layouts  3.5 us
  transfers between devices with their start and end apart: 21, of which 8 were waited for; matrix products, arithmetic and copies ran while one was open for 0% of the time, Pallas kernels for 10%

profile of v8, /device:TPU:0, one launch (start us, length us, event | category | flops | bytes accessed | tf_op | source)
XLA Modules:
  0.0 66.0 jit_solution(1139652042069245778)
XLA Ops:
  0.6 1.0 %copy-done = s32[2,2,3,8,8,128]{5,4,3,2,1,0:T(8,128)S(1)} copy-done((s32[2,2,3,8,8,128]{5,4,3,2,1,0:T(8,128)S(1)}, s32[2,2,3,8,8,128]{5,4,3,2,1,0:T(8,128)}, u32[]{:S(2)}) %copy-start) | copy-done | bytes 393240
  1.6 1.0 %copy-done.2 = f32[2,2,3,8,8,128]{5,4,3,2,1,0:T(8,128)S(1)} copy-done((f32[2,2,3,8,8,128]{5,4,3,2,1,0:T(8,128)S(1)}, f32[2,2,3,8,8,128]{5,4,3,2,1,0:T(8,128)}, u32[]{:S(2)}) %copy-start.2) | copy-done | bytes 393240
  4.6 2.0 %shard_map.60 = (f32[17,8,128]{2,1,0:T(8,128)S(1)}, f32[8,8,128]{2,1,0:T(8,128)S(1)}, f32[8,8,128]{2,1,0:T(8,128)S(1)}, f32[8,8,128]{2,1,0:T(8,128)S(1)}, f32[8,...) custom-call(f32[8,8,128]{2,1,0:T(8,128)S(1)} %copy-done.5, f32[1,8,8,128]{3,2,1,0:T(8,128)S(1)} %bitcast.1, ...), custom_call_target="tpu_custom_call" | custom-call | flops 8388608 | bytes 851968 | tf_op jit(solution)/shard_map/pallas_call | solution.py:452
  6.6 3.0 %collective-permute-start = (f32[17,8,128]{2,1,0:T(8,128)S(1)}, f32[17,8,128]{2,1,0:T(8,128)S(1)}, u32[]{:S(2)}, u32[]{:S(2)}) collective-permute-start(f32[17,8,128]{2,1,0:T(8,128)S(1)} %get-tuple-element.38), channel_id=1, source_target_pairs={{0,4},{4,0},{1,5},{5,1},{2,6},{6,2},{3,7},{7,3},{8,12},{12,8},{9,1... | collective-permute-start | bytes 208904 | tf_op jit(solution)/shard_map/ppermute | solution.py:469
  10.3 1.7 %collective-permute-start.3 = (f32[8,8,128]{2,1,0:T(8,128)S(1)}, f32[8,8,128]{2,1,0:T(8,128)S(1)}, u32[]{:S(2)}, u32[]{:S(2)}) collective-permute-start(f32[8,8,128]{2,1,0:T(8,128)S(1)} %get-tuple-element.41), channel_id=1, source_target_pairs={{0,28},{4,24},{8,4},{12,0},{16,12},{20,8},{24,20},{28,16},{1,29},{... | collective-permute-start | bytes 98312 | tf_op jit(solution)/shard_map/ppermute | solution.py:475
  12.0 1.6 %collective-permute-done.2.from_l = f32[8,8,128]{2,1,0:T(8,128)S(1)} collective-permute-done((f32[8,8,128]{2,1,0:T(8,128)S(1)}, f32[8,8,128]{2,1,0:T(8,128)S(1)}, u32[]{:S(2)}, u32[]{:S(2)}) %collective-permute-start.2) | collective-permute-done | bytes 32800 | tf_op jit(solution)/shard_map/ppermute | solution.py:469
  13.6 2.6 %collective-permute-done.4.from_ly = f32[8,8,128]{2,1,0:T(8,128)S(1)} collective-permute-done((f32[8,8,128]{2,1,0:T(8,128)S(1)}, f32[8,8,128]{2,1,0:T(8,128)S(1)}, u32[]{:S(2)}, u32[]{:S(2)}) %collective-permute-start.4) | collective-permute-done | bytes 32800 | tf_op jit(solution)/shard_map/ppermute | solution.py:475
  16.3 3.7 %collective-permute-start.6 = (f32[24,128]{1,0:T(8,128)S(1)}, f32[24,128]{1,0:T(8,128)S(1)}, u32[]{:S(2)}, u32[]{:S(2)}) collective-permute-start(f32[24,128]{1,0:T(8,128)S(1)} %get-tuple-element.45), channel_id=1, source_target_pairs={{0,3},{1,0},{2,1},{3,2},{4,7},{5,4},{6,5},{7,6},{8,11},{9,8},{10,9... | collective-permute-start | bytes 36872 | tf_op jit(solution)/shard_map/ppermute | solution.py:469
  20.0 1.4 %collective-permute-done.6.rims_r = f32[24,128]{1,0:T(8,128)S(1)} collective-permute-done((f32[24,128]{1,0:T(8,128)S(1)}, f32[24,128]{1,0:T(8,128)S(1)}, u32[]{:S(2)}, u32[]{:S(2)}) %collective-permute-start.6) | collective-permute-done | bytes 12320 | tf_op jit(solution)/shard_map/ppermute | solution.py:469
  21.4 4.1 %collective-permute-done.5.rims_l = f32[24,128]{1,0:T(8,128)S(1)} collective-permute-done((f32[24,128]{1,0:T(8,128)S(1)}, f32[24,128]{1,0:T(8,128)S(1)}, u32[]{:S(2)}, u32[]{:S(2)}) %collective-permute-start.5) | collective-permute-done | bytes 12320 | tf_op jit(solution)/shard_map/ppermute | solution.py:469
  25.5 3.3 %shard_map.62 = (f32[8,8,128]{2,1,0:T(8,128)S(1)}, f32[8,8,128]{2,1,0:T(8,128)S(1)}, f32[4,8,128]{2,1,0:T(8,128)S(1)}, f32[3,8,128]{2,1,0:T(8,128)S(1)}, f32[4,8...) custom-call(f32[15,16,128]{2,1,0:T(8,128)S(1)} %get-tuple-element.44., ...), custom_call_target="tpu_custom_call" | custom-call | flops 20971520 | bytes 1753088 | tf_op jit(solution)/shard_map/pallas_call | solution.py:452
  28.8 1.6 %collective-permute-start.7 = (f32[8,8,128]{2,1,0:T(8,128)S(1)}, f32[8,8,128]{2,1,0:T(8,128)S(1)}, u32[]{:S(2)}, u32[]{:S(2)}) collective-permute-start(f32[8,8,128]{2,1,0:T(8,128)S(1)} %get-tuple-element.50), channel_id=1, source_target_pairs={{0,4},{4,0},{1,5},{5,1},{2,6},{6,2},{3,7},{7,3},{8,12},{12,8},{9,1... | collective-permute-start | bytes 98312 | tf_op jit(solution)/shard_map/ppermute | solution.py:469
  30.3 1.0 %collective-permute-start.10 = (f32[4,8,128]{2,1,0:T(8,128)S(1)}, f32[4,8,128]{2,1,0:T(8,128)S(1)}, u32[]{:S(2)}, u32[]{:S(2)}) collective-permute-start(f32[4,8,128]{2,1,0:T(8,128)S(1)} %get-tuple-element.53), channel_id=1, source_target_pairs={{0,28},{4,24},{8,4},{12,0},{16,12},{20,8},{24,20},{28,16},{1,29},{... | collective-permute-start | bytes 49160 | tf_op jit(solution)/shard_map/ppermute | solution.py:475
  31.4 2.3 %collective-permute-start.11 = (f32[3,8,128]{2,1,0:T(8,128)S(1)}, f32[3,8,128]{2,1,0:T(8,128)S(1)}, u32[]{:S(2)}, u32[]{:S(2)}) collective-permute-start(f32[3,8,128]{2,1,0:T(8,128)S(1)} %get-tuple-element.54), channel_id=1, source_target_pairs={{0,12},{4,8},{8,20},{12,16},{16,28},{20,24},{24,4},{28,0},{1,13},{... | collective-permute-start | bytes 36872 | tf_op jit(solution)/shard_map/ppermute | solution.py:475
  33.7 2.4 %shard_map.63 = (f32[1,15,16,128]{3,2,1,0:T(8,128)S(1)}, f32[1,16,128]{2,1,0:T(8,128)S(1)}, f32[3,8,8,8,128]{4,3,2,1,0:T(8,128)S(1)}, f32[3,8,8,8,128]{4,3,2,1,0:T(8,128)S(1)}, f32[3,8,8,8,128]{4,3,2,1,0:T(8,128)S(1)}) custom-call(f32[1,8,8,128]{3,2,1,0:T(8,128)S(1)} %get-tuple-element.55.adjoint, f32[3,8,8,8,128]{4,3,2,1,0:T(8,128)S(1)} %get-tuple-element.47.weights, ...), custom_call_target="tpu_custom_call" | custom-call | flops 8388608 | bytes 1605632 | tf_op jit(solution)/shard_map/pallas_call | solution.py:452
  36.3 2.0 %collective-permute-start.12 = (f32[16,128]{1,0:T(8,128)S(1)}, f32[16,128]{1,0:T(8,128)S(1)}, u32[]{:S(2)}, u32[]{:S(2)}) collective-permute-start(f32[16,128]{1,0:T(8,128)S(1)} %get-tuple-element.58), channel_id=1, source_target_pairs={{0,1},{1,2},{2,3},{3,0},{4,5},{5,6},{6,7},{7,4},{8,9},{9,10},{10,1... | collective-permute-start | bytes 24584 | tf_op jit(solution)/shard_map/ppermute | solution.py:469
  38.3 3.9 %shard_map.65.early_piles = f32[3,8,15,16,128]{4,3,2,1,0:T(8,128)S(1)} custom-call(f32[3,8,8,128]{3,2,1,0:T(8,128)S(1)} %get-tuple-element.62.gradient, f32[1,8,8,128]{3,2,1,0:T(8,128)S(1)} %get-tuple-element.55.adjoint, f32[3,8,8,8,128]{4,3,2,1,0:T(8,128)S(1)} %get-tuple-element.63.weights), custom_call_target="tpu_custom_call" | custom-call | flops 25165824 | bytes 917504 | tf_op jit(solution)/shard_map/pallas_call | solution.py:452
  42.2 8.1 %shard_map.66 = (f32[3,15,16,128]{3,2,1,0:T(8,128)S(1)}, f32[64,128]{1,0:T(8,128)S(1)}, f32[3,8,15,16,128]{4,3,2,1,0:T(8,128)S(1)}) custom-call(f32[15,16,128]{2,1,0:T(8,128)S(1)} %get-tuple-element.57.extended, f32[16,128]{1,0:T(8,128)S(1)} %collective-permute-done.12.rims_l, ...), custom_call_target="tpu_custom_call", output_to_operand_aliasing={{2}: (8, {})} | custom-call | flops 46137344 | bytes 5488640 | tf_op jit(solution)/shard_map/pallas_call | solution.py:452
  50.3 1.9 %collective-permute-start.15 = (f32[64,128]{1,0:T(8,128)S(1)}, f32[64,128]{1,0:T(8,128)S(1)}, u32[]{:S(2)}, u32[]{:S(2)}) collective-permute-start(f32[64,128]{1,0:T(8,128)S(1)} %get-tuple-element.65), channel_id=1, source_target_pairs={{0,3},{1,0},{2,1},{3,2},{4,7},{5,4},{6,5},{7,6},{8,11},{9,8},{10,9... | collective-permute-start | bytes 98312 | tf_op jit(solution)/shard_map/ppermute | solution.py:469
  52.4 1.9 %collective-permute-done.15.rims_r = f32[64,128]{1,0:T(8,128)S(1)} collective-permute-done((f32[64,128]{1,0:T(8,128)S(1)}, f32[64,128]{1,0:T(8,128)S(1)}, u32[]{:S(2)}, u32[]{:S(2)}) %collective-permute-start.15) | collective-permute-done | bytes 32800 | tf_op jit(solution)/shard_map/ppermute | solution.py:469
  54.3 3.7 %collective-permute-done.14.rims_l = f32[64,128]{1,0:T(8,128)S(1)} collective-permute-done((f32[64,128]{1,0:T(8,128)S(1)}, f32[64,128]{1,0:T(8,128)S(1)}, u32[]{:S(2)}, u32[]{:S(2)}) %collective-permute-start.14) | collective-permute-done | bytes 32800 | tf_op jit(solution)/shard_map/ppermute | solution.py:469
  58.9 1.9 %collective-permute-start.20 = (f32[16,8,128]{2,1,0:T(8,128)S(1)}, f32[16,8,128]{2,1,0:T(8,128)S(1)}, u32[]{:S(2)}, u32[]{:S(2)}) collective-permute-start(f32[16,8,128]{2,1,0:T(8,128)S(1)} %get-tuple-element.71), channel_id=1, source_target_pairs={{0,12},{4,8},{8,20},{12,16},{16,28},{20,24},{24,4},{28,0},{1,13},{... | collective-permute-start | bytes 196616 | tf_op jit(solution)/shard_map/ppermute | solution.py:475
  62.2 1.0 %collective-permute-done.17.from_r = f32[12,8,128]{2,1,0:T(8,128)S(1)} collective-permute-done((f32[12,8,128]{2,1,0:T(8,128)S(1)}, f32[12,8,128]{2,1,0:T(8,128)S(1)}, u32[]{:S(2)}, u32[]{:S(2)}) %collective-permute-start.17) | collective-permute-done | bytes 49184 | tf_op jit(solution)/shard_map/ppermute | solution.py:469
  63.2 2.1 %collective-permute-done.19.from_ry = f32[12,8,128]{2,1,0:T(8,128)S(1)} collective-permute-done((f32[12,8,128]{2,1,0:T(8,128)S(1)}, f32[12,8,128]{2,1,0:T(8,128)S(1)}, u32[]{:S(2)}, u32[]{:S(2)}) %collective-permute-start.19) | collective-permute-done | bytes 49184 | tf_op jit(solution)/shard_map/ppermute | solution.py:475
  (40 shorter events, 6.1 us)
Async XLA Ops:
  0.6 1.0 %copy-start = (s32[2,2,3,8,8,128]{5,4,3,2,1,0:T(8,128)S(1)}, s32[2,2,3,8,8,128]{5,4,3,2,1,0:T(8,128)}, u32[]{:S(2)}) copy-start(s32[2,2,3,8,8,128]{5,4,3,2,1,0:T(8,128)} %cells.3) | copy-start | bytes 1179652
  2.6 31.0 %copy-start.1 = (s32[2,2,3,8,8,128]{5,4,3,2,1,0:T(8,128)S(1)}, s32[2,2,3,8,8,128]{5,4,3,2,1,0:T(8,128)}, u32[]{:S(2)}) copy-start(s32[2,2,3,8,8,128]{5,4,3,2,1,0:T(8,128)} %cells.3) | copy-start | bytes 1179652
  6.6 9.6 %collective-permute-start = (f32[17,8,128]{2,1,0:T(8,128)S(1)}, f32[17,8,128]{2,1,0:T(8,128)S(1)}, u32[]{:S(2)}, u32[]{:S(2)}) collective-permute-start(f32[17,8,128]{2,1,0:T(8,128)S(1)} %get-tuple-element.38), channel_id=1, source_target_pairs={{0,4},{4,0},{1,5},{5,1},{2,6},{6,2},{3,7},{7,3},{8,12},{12,8},{9,1... | collective-permute-start | bytes 208904 | tf_op jit(solution)/shard_map/ppermute | solution.py:469
  9.6 2.4 %collective-permute-start.1 = (f32[8,8,128]{2,1,0:T(8,128)S(1)}, f32[8,8,128]{2,1,0:T(8,128)S(1)}, u32[]{:S(2)}, u32[]{:S(2)}) collective-permute-start(f32[8,8,128]{2,1,0:T(8,128)S(1)} %get-tuple-element.39), channel_id=1, source_target_pairs={{0,24},{8,0},{16,8},{24,16},{1,25},{9,1},{17,9},{25,17},{2,26},{10... | collective-permute-start | bytes 98312 | tf_op jit(solution)/shard_map/ppermute | solution.py:469
  10.3 3.3 %collective-permute-start.2 = (f32[8,8,128]{2,1,0:T(8,128)S(1)}, f32[8,8,128]{2,1,0:T(8,128)S(1)}, u32[]{:S(2)}, u32[]{:S(2)}) collective-permute-start(f32[8,8,128]{2,1,0:T(8,128)S(1)} %get-tuple-element.40), channel_id=1, source_target_pairs={{0,8},{8,16},{16,24},{24,0},{1,9},{9,17},{17,25},{25,1},{2,10},{10... | collective-permute-start | bytes 98312 | tf_op jit(solution)/shard_map/ppermute | solution.py:469
  10.3 3.3 %collective-permute-start.3 = (f32[8,8,128]{2,1,0:T(8,128)S(1)}, f32[8,8,128]{2,1,0:T(8,128)S(1)}, u32[]{:S(2)}, u32[]{:S(2)}) collective-permute-start(f32[8,8,128]{2,1,0:T(8,128)S(1)} %get-tuple-element.41), channel_id=1, source_target_pairs={{0,28},{4,24},{8,4},{12,0},{16,12},{20,8},{24,20},{28,16},{1,29},{... | collective-permute-start | bytes 98312 | tf_op jit(solution)/shard_map/ppermute | solution.py:475
  12.0 4.2 %collective-permute-start.4 = (f32[8,8,128]{2,1,0:T(8,128)S(1)}, f32[8,8,128]{2,1,0:T(8,128)S(1)}, u32[]{:S(2)}, u32[]{:S(2)}) collective-permute-start(f32[8,8,128]{2,1,0:T(8,128)S(1)} %get-tuple-element.42), channel_id=1, source_target_pairs={{0,12},{4,8},{8,20},{12,16},{16,28},{20,24},{24,4},{28,0},{1,13},{... | collective-permute-start | bytes 98312 | tf_op jit(solution)/shard_map/ppermute | solution.py:475
  16.3 5.1 %collective-permute-start.6 = (f32[24,128]{1,0:T(8,128)S(1)}, f32[24,128]{1,0:T(8,128)S(1)}, u32[]{:S(2)}, u32[]{:S(2)}) collective-permute-start(f32[24,128]{1,0:T(8,128)S(1)} %get-tuple-element.45), channel_id=1, source_target_pairs={{0,3},{1,0},{2,1},{3,2},{4,7},{5,4},{6,5},{7,6},{8,11},{9,8},{10,9... | collective-permute-start | bytes 36872 | tf_op jit(solution)/shard_map/ppermute | solution.py:469
  20.0 5.5 %collective-permute-start.5 = (f32[24,128]{1,0:T(8,128)S(1)}, f32[24,128]{1,0:T(8,128)S(1)}, u32[]{:S(2)}, u32[]{:S(2)}) collective-permute-start(f32[24,128]{1,0:T(8,128)S(1)} %get-tuple-element.45), channel_id=1, source_target_pairs={{0,1},{1,2},{2,3},{3,0},{4,5},{5,6},{6,7},{7,4},{8,9},{9,10},{10,1... | collective-permute-start | bytes 36872 | tf_op jit(solution)/shard_map/ppermute | solution.py:469
  28.8 13.5 %copy-start.4 = (f32[8,8,128]{2,1,0:T(8,128)S(1)}, f32[8,8,128]{2,1,0:T(8,128)}, u32[]{:S(2)}) copy-start(f32[8,8,128]{2,1,0:T(8,128)} %param.5) | copy-start | bytes 98308
  28.8 7.4 %collective-permute-start.7 = (f32[8,8,128]{2,1,0:T(8,128)S(1)}, f32[8,8,128]{2,1,0:T(8,128)S(1)}, u32[]{:S(2)}, u32[]{:S(2)}) collective-permute-start(f32[8,8,128]{2,1,0:T(8,128)S(1)} %get-tuple-element.50), channel_id=1, source_target_pairs={{0,4},{4,0},{1,5},{5,1},{2,6},{6,2},{3,7},{7,3},{8,12},{12,8},{9,1... | collective-permute-start | bytes 98312 | tf_op jit(solution)/shard_map/ppermute | solution.py:469
  30.3 5.8 %collective-permute-start.8 = (f32[4,8,128]{2,1,0:T(8,128)S(1)}, f32[4,8,128]{2,1,0:T(8,128)S(1)}, u32[]{:S(2)}, u32[]{:S(2)}) collective-permute-start(f32[4,8,128]{2,1,0:T(8,128)S(1)} %get-tuple-element.51), channel_id=1, source_target_pairs={{0,24},{8,0},{16,8},{24,16},{1,25},{9,1},{17,9},{25,17},{2,26},{10... | collective-permute-start | bytes 49160 | tf_op jit(solution)/shard_map/ppermute | solution.py:469
  30.3 5.8 %collective-permute-start.10 = (f32[4,8,128]{2,1,0:T(8,128)S(1)}, f32[4,8,128]{2,1,0:T(8,128)S(1)}, u32[]{:S(2)}, u32[]{:S(2)}) collective-permute-start(f32[4,8,128]{2,1,0:T(8,128)S(1)} %get-tuple-element.53), channel_id=1, source_target_pairs={{0,28},{4,24},{8,4},{12,0},{16,12},{20,8},{24,20},{28,16},{1,29},{... | collective-permute-start | bytes 49160 | tf_op jit(solution)/shard_map/ppermute | solution.py:475
  31.4 4.7 %collective-permute-start.9 = (f32[3,8,128]{2,1,0:T(8,128)S(1)}, f32[3,8,128]{2,1,0:T(8,128)S(1)}, u32[]{:S(2)}, u32[]{:S(2)}) collective-permute-start(f32[3,8,128]{2,1,0:T(8,128)S(1)} %get-tuple-element.52), channel_id=1, source_target_pairs={{0,8},{8,16},{16,24},{24,0},{1,9},{9,17},{17,25},{25,1},{2,10},{10... | collective-permute-start | bytes 36872 | tf_op jit(solution)/shard_map/ppermute | solution.py:469
  31.4 4.7 %collective-permute-start.11 = (f32[3,8,128]{2,1,0:T(8,128)S(1)}, f32[3,8,128]{2,1,0:T(8,128)S(1)}, u32[]{:S(2)}, u32[]{:S(2)}) collective-permute-start(f32[3,8,128]{2,1,0:T(8,128)S(1)} %get-tuple-element.54), channel_id=1, source_target_pairs={{0,12},{4,8},{8,20},{12,16},{16,28},{20,24},{24,4},{28,0},{1,13},{... | collective-permute-start | bytes 36872 | tf_op jit(solution)/shard_map/ppermute | solution.py:475
  36.2 6.0 %collective-permute-start.13 = (f32[16,128]{1,0:T(8,128)S(1)}, f32[16,128]{1,0:T(8,128)S(1)}, u32[]{:S(2)}, u32[]{:S(2)}) collective-permute-start(f32[16,128]{1,0:T(8,128)S(1)} %get-tuple-element.58), channel_id=1, source_target_pairs={{0,3},{1,0},{2,1},{3,2},{4,7},{5,4},{6,5},{7,6},{8,11},{9,8},{10,9... | collective-permute-start | bytes 24584 | tf_op jit(solution)/shard_map/ppermute | solution.py:469
  36.3 5.9 %collective-permute-start.12 = (f32[16,128]{1,0:T(8,128)S(1)}, f32[16,128]{1,0:T(8,128)S(1)}, u32[]{:S(2)}, u32[]{:S(2)}) collective-permute-start(f32[16,128]{1,0:T(8,128)S(1)} %get-tuple-element.58), channel_id=1, source_target_pairs={{0,1},{1,2},{2,3},{3,0},{4,5},{5,6},{6,7},{7,4},{8,9},{9,10},{10,1... | collective-permute-start | bytes 24584 | tf_op jit(solution)/shard_map/ppermute | solution.py:469
  50.3 4.0 %collective-permute-start.15 = (f32[64,128]{1,0:T(8,128)S(1)}, f32[64,128]{1,0:T(8,128)S(1)}, u32[]{:S(2)}, u32[]{:S(2)}) collective-permute-start(f32[64,128]{1,0:T(8,128)S(1)} %get-tuple-element.65), channel_id=1, source_target_pairs={{0,3},{1,0},{2,1},{3,2},{4,7},{5,4},{6,5},{7,6},{8,11},{9,8},{10,9... | collective-permute-start | bytes 98312 | tf_op jit(solution)/shard_map/ppermute | solution.py:469
  52.3 5.7 %collective-permute-start.14 = (f32[64,128]{1,0:T(8,128)S(1)}, f32[64,128]{1,0:T(8,128)S(1)}, u32[]{:S(2)}, u32[]{:S(2)}) collective-permute-start(f32[64,128]{1,0:T(8,128)S(1)} %get-tuple-element.65), channel_id=1, source_target_pairs={{0,1},{1,2},{2,3},{3,0},{4,5},{5,6},{6,7},{7,4},{8,9},{9,10},{10,1... | collective-permute-start | bytes 98312 | tf_op jit(solution)/shard_map/ppermute | solution.py:469
  58.2 7.1 %collective-permute-start.16 = (f32[32,8,128]{2,1,0:T(8,128)S(1)}, f32[32,8,128]{2,1,0:T(8,128)S(1)}, u32[]{:S(2)}, u32[]{:S(2)}) collective-permute-start(f32[32,8,128]{2,1,0:T(8,128)S(1)} %get-tuple-element.67), channel_id=1, source_target_pairs={{0,4},{4,0},{1,5},{5,1},{2,6},{6,2},{3,7},{7,3},{8,12},{12,8},{9,1... | collective-permute-start | bytes 393224 | tf_op jit(solution)/shard_map/ppermute | solution.py:469
  58.9 6.4 %collective-permute-start.18 = (f32[16,8,128]{2,1,0:T(8,128)S(1)}, f32[16,8,128]{2,1,0:T(8,128)S(1)}, u32[]{:S(2)}, u32[]{:S(2)}) collective-permute-start(f32[16,8,128]{2,1,0:T(8,128)S(1)} %get-tuple-element.69), channel_id=1, source_target_pairs={{0,8},{8,16},{16,24},{24,0},{1,9},{9,17},{17,25},{25,1},{2,10},{10... | collective-permute-start | bytes 196616 | tf_op jit(solution)/shard_map/ppermute | solution.py:469
  58.9 6.4 %collective-permute-start.20 = (f32[16,8,128]{2,1,0:T(8,128)S(1)}, f32[16,8,128]{2,1,0:T(8,128)S(1)}, u32[]{:S(2)}, u32[]{:S(2)}) collective-permute-start(f32[16,8,128]{2,1,0:T(8,128)S(1)} %get-tuple-element.71), channel_id=1, source_target_pairs={{0,12},{4,8},{8,20},{12,16},{16,28},{20,24},{24,4},{28,0},{1,13},{... | collective-permute-start | bytes 196616 | tf_op jit(solution)/shard_map/ppermute | solution.py:475
  60.8 2.4 %collective-permute-start.17 = (f32[12,8,128]{2,1,0:T(8,128)S(1)}, f32[12,8,128]{2,1,0:T(8,128)S(1)}, u32[]{:S(2)}, u32[]{:S(2)}) collective-permute-start(f32[12,8,128]{2,1,0:T(8,128)S(1)} %get-tuple-element.68), channel_id=1, source_target_pairs={{0,24},{8,0},{16,8},{24,16},{1,25},{9,1},{17,9},{25,17},{2,26},{10... | collective-permute-start | bytes 147464 | tf_op jit(solution)/shard_map/ppermute | solution.py:469
  61.4 3.8 %collective-permute-start.19 = (f32[12,8,128]{2,1,0:T(8,128)S(1)}, f32[12,8,128]{2,1,0:T(8,128)S(1)}, u32[]{:S(2)}, u32[]{:S(2)}) collective-permute-start(f32[12,8,128]{2,1,0:T(8,128)S(1)} %get-tuple-element.70), channel_id=1, source_target_pairs={{0,28},{4,24},{8,4},{12,0},{16,12},{20,8},{24,20},{28,16},{1,29},{... | collective-permute-start | bytes 147464 | tf_op jit(solution)/shard_map/ppermute | solution.py:475
  (3 other events, 2.5 us)

commit v9 on v8

--- a/solution.py
+++ b/solution.py
@@ -317,20 +317,20 @@
 
 
 def first_kernel(
-    nx, ny, intensity, cotangent, weights,
+    nx, ny, pair, weights,
     to_y, to_l, to_r, to_ly, to_ry, own,
     scaled, piles, ends, piled, rims,
 ):
-    deposit(cotangent, weights, scaled, piles, 2, SHIFTS)
+    deposit(pair.at[1:2], weights, scaled, piles, 2, SHIFTS)
     settle(piles, ends, piled.at[:, 0 : nx + LO + HI], rims)
     piled[0, nx + LO + HI] = rims[0]
-    split_halo(intensity, (to_y, to_l, to_r, to_ly, to_ry), nx, ny)
+    split_halo(pair.at[0], (to_y, to_l, to_r, to_ly, to_ry), nx, ny)
     split_deposits(piled.at[0], (to_y, to_l, to_r, to_ly, to_ry, own), (nx, HI, LO, 0), nx, ny)
 
 
-def first_join_kernel(nx, ny, intensity, from_y, from_r, from_l, from_ry, from_ly, own, extended, part, rims):
+def first_join_kernel(nx, ny, pair, from_y, from_r, from_l, from_ry, from_ly, own, extended, part, rims):
     rows = ny + 2 * ROWS
-    join_halo(intensity, (from_y, from_r, from_l, from_ry, from_ly), extended, nx, ny)
+    join_halo(pair.at[0], (from_y, from_r, from_l, from_ry, from_ly), extended, nx, ny)
     rims[0:rows] = pack_rim(extended)
 
     def put(x, plane):
@@ -362,7 +362,7 @@
 
 def adjoint_kernel(
     nx, ny, adjoint, weights, cells, fracs,
-    piled, rims, early_mid, late_slopes, late_mid,
+    piled, rims, early_mid, late_slopes, late_mid, cleared,
     scaled, piles, ends,
 ):
     deposit(adjoint, weights, scaled, piles, 2, SHIFTS)
@@ -370,13 +370,14 @@
     write_tables(cells.at[0, 0], fracs.at[0, 0], early_mid)
     write_tables(cells.at[1, 1], fracs.at[1, 1], None, late_slopes)
     write_tables(cells.at[1, 0], fracs.at[1, 0], late_mid)
-
-
-def early_kernel(nx, ny, gradient, adjoint, weights, piles, product, scaled):
+    cleared[...] = jnp.zeros(cleared.shape, F32)
+
+
+def early_kernel(nx, ny, gradient, adjoint, weights, cleared, piles, product, scaled):
     for c in range(3):
         for x in range(nx):
             product[c, x] = adjoint[0, x] * gradient[c, x]
-    deposit(product, weights, scaled, piles, 1, SHIFTS // 2)
+    deposit(product, weights, scaled, piles, 1, SHIFTS // 2, fresh=False)
 
 
 def second_join_kernel(nx, ny, image, from_y, from_r, from_l, from_ry, from_ly, earlier, extended, rims):
@@ -385,7 +386,7 @@
 
 
 def late_kernel(
-    nx, ny, extended, rims_l, rims_r, cotangent, weights, slopes, mid_weights, adjoint_rims, early_piles,
+    nx, ny, extended, rims_l, rims_r, pair, weights, slopes, mid_weights, adjoint_rims, early_piles,
     piled, rims, piles,
     shifted, ends, product, scaled, rims_here,
 ):
@@ -394,7 +395,7 @@
 
     def emit(x, sums):
         for c in range(3):
-            product[c, x] = cotangent[0, x] * sums[c]
+            product[c, x] = pair[1, x] * sums[c]
 
     interpolate(shifted, weights, slopes, nx, ny, emit, False)
     deposit(product, mid_weights, scaled, piles, 1, SHIFTS // 2, fresh=False)
@@ -505,7 +506,7 @@
     ring = 2 * ROWS
     field = (nx, ny, nz)
     table = (3, SHIFTS) + field
-    cotangent = cotangent[None]
+    pair = jnp.stack([intensity, cotangent])
     unit = nx * ny * nz * 512
 
     def run(kernel, *rest, **more):
@@ -529,14 +530,14 @@
     )
     *outs, own = run(
         first_kernel,
-        (intensity, cotangent, late),
+        (pair, late),
         messages(2 * nx + 1, HI + LO + 1, LO + HI + 1) + [(nx + 1, ny, nz)],
         pile(1) + [(1, planes, rows, nz), (1, planes + 1, rows, nz), (1, rows, nz)],
         2 * unit,
     )
     extended, folded, rims = run(
         first_join_kernel,
-        (intensity,) + send_sides(*outs) + (own,),
+        (pair,) + send_sides(*outs) + (own,),
         [(planes, rows, nz), field, (rows + ny, nz)],
         [],
         unit // 16,
@@ -550,10 +551,11 @@
     )
 
     sides = send_sides(*outs)
-    piled_adjoint, adjoint_rims, early_mid, late_slopes, late_mid = run(
+    scaled_3, piles_3 = pile(3)
+    piled_adjoint, adjoint_rims, early_mid, late_slopes, late_mid, cleared = run(
         adjoint_kernel,
         (adjoint, early, cells, fracs),
-        piled(1) + [table, table, table],
+        piled(1) + [table, table, table, piles_3],
         pile(1) + [(1, planes, rows, nz)],
         2 * unit,
     )
@@ -566,18 +568,18 @@
         spaces={6: pl.ANY},
     )
     rims_l, rims_r = send_z(rims)
-    scaled_3, piles_3 = pile(3)
     (piles,) = run(
         early_kernel,
-        (gradient, adjoint, early_mid),
+        (gradient, adjoint, early_mid, cleared),
         [piles_3],
         [(3,) + field, scaled_3],
         6 * unit,
+        aliases={3: 0},
     )
 
     velocity, rims, _ = run(
         late_kernel,
-        (extended, rims_l, rims_r, cotangent, late, late_slopes, late_mid, adjoint_rims, piles),
+        (extended, rims_l, rims_r, pair, late, late_slopes, late_mid, adjoint_rims, piles),
         [(3, planes, rows, nz), (4 * rows, nz), piles_3],
         [(SHIFTS, planes, rows, nz), (3, planes, rows, nz), (3,) + field, scaled_3, (3, rows, nz)],
         11 * unit,

time: 66.3 us -> 62.2 us (0.938)
  waiting for transfers between devices: 18.3 us -> 10.9 us
  starting transfers between devices: 22.1 us -> 25.9 us
  local copies, waits for them, and re-layouts: 3.5 us -> 1.99 us
  other arithmetic: 0 us -> 0.78 us
    ppermute x15, waiting for transfers between devices: 13.6 us -> 6.21 us  [send(): return lax.ppermute(message, axes[0], pairs)]
    ppermute x15, starting transfers between devices: 14.4 us -> 20.9 us  [send(): return lax.ppermute(message, axes[0], pairs)]
    ppermute x6, starting transfers between devices: 7.76 us -> 4.99 us  [send(): return lax.ppermute(message, axes, pairs)]
    unnamed x12 -> x8, local copies, waits for them, and re-layouts: 3.5 us -> 1.99 us
    another operation x0 -> x1, other arithmetic: none -> 0.78 us  [body(): pair = jnp.stack([intensity, cotangent])]
  transfers between devices with their start and end apart: 21 -> 21, of which waited for: 8 -> 6; matrix products, arithmetic and copies ran while one was open for 0% -> 0% of each run, Pallas kernels for 10% -> 11%
where the time goes in v9:
time: 62.2 us; the launch traced here: 61.9 us
  starting transfers between devices  25.9 us (42%)
  Pallas kernels  21.6 us (35%)
  waiting for transfers between devices  10.9 us (18%)
  local copies, waits for them, and re-layouts  1.99 us (3%)
  other arithmetic  0.78 us (1%)
  between operations  0.78 us (1%)
    pallas_call x10, Pallas kernels, call(): pl.pallas_call(kernel, out_shape=[struct(s) for s in outs], in_specs=in_s...  21.6 us
    ppermute x15, starting transfers between devices, send(): return lax.ppermute(message, axes[0], pairs)  20.9 us
    ppermute x15, waiting for transfers between devices, send(): return lax.ppermute(message, axes[0], pairs)  6.21 us
    ppermute x6, starting transfers between devices, send(): return lax.ppermute(message, axes, pairs)  4.99 us
    ppermute x6, waiting for transfers between devices, send(): return lax.ppermute(message, axes, pairs)  4.66 us
    unnamed x8, local copies, waits for them, and re-layouts  1.99 us
  transfers between devices with their start and end apart: 21, of which 6 were waited for; matrix products, arithmetic and copies ran while one was open for 0% of the time, Pallas kernels for 11%

profile of v9, /device:TPU:0, one launch (start us, length us, event | category | flops | bytes accessed | tf_op | source)
XLA Modules:
  0.0 61.9 jit_solution(7154201951791960996)
XLA Ops:
  0.6 1.0 %copy-done = s32[2,2,3,8,8,128]{5,4,3,2,1,0:T(8,128)S(1)} copy-done((s32[2,2,3,8,8,128]{5,4,3,2,1,0:T(8,128)S(1)}, s32[2,2,3,8,8,128]{5,4,3,2,1,0:T(8,128)}, u32[]{:S(2)}) %copy-start) | copy-done | bytes 393240
  1.6 1.0 %copy-done.2 = f32[2,2,3,8,8,128]{5,4,3,2,1,0:T(8,128)S(1)} copy-done((f32[2,2,3,8,8,128]{5,4,3,2,1,0:T(8,128)S(1)}, f32[2,2,3,8,8,128]{5,4,3,2,1,0:T(8,128)}, u32[]{:S(2)}) %copy-start.2) | copy-done | bytes 393240
  3.9 2.0 %shard_map.60 = (f32[17,8,128]{2,1,0:T(8,128)S(1)}, f32[8,8,128]{2,1,0:T(8,128)S(1)}, f32[8,8,128]{2,1,0:T(8,128)S(1)}, f32[8,8,128]{2,1,0:T(8,128)S(1)}, f32[8,...) custom-call(f32[2,8,8,128]{3,2,1,0:T(8,128)S(1)} %pad_maximum_fusion.pair, f32[3,8,8,8,128]{4,3,2,1,0:T(8,128)S(1)} %get-tuple-element.38.weights), custom_call_target="tpu_custom_call" | custom-call | flops 8388608 | bytes 851968 | tf_op jit(solution)/shard_map/pallas_call | solution.py:453
  5.9 3.0 %collective-permute-start = (f32[17,8,128]{2,1,0:T(8,128)S(1)}, f32[17,8,128]{2,1,0:T(8,128)S(1)}, u32[]{:S(2)}, u32[]{:S(2)}) collective-permute-start(f32[17,8,128]{2,1,0:T(8,128)S(1)} %get-tuple-element.39), channel_id=1, source_target_pairs={{0,4},{4,0},{1,5},{5,1},{2,6},{6,2},{3,7},{7,3},{8,12},{12,8},{9,1... | collective-permute-start | bytes 208904 | tf_op jit(solution)/shard_map/ppermute | solution.py:470
  9.6 1.7 %collective-permute-start.3 = (f32[8,8,128]{2,1,0:T(8,128)S(1)}, f32[8,8,128]{2,1,0:T(8,128)S(1)}, u32[]{:S(2)}, u32[]{:S(2)}) collective-permute-start(f32[8,8,128]{2,1,0:T(8,128)S(1)} %get-tuple-element.42), channel_id=1, source_target_pairs={{0,28},{4,24},{8,4},{12,0},{16,12},{20,8},{24,20},{28,16},{1,29},{... | collective-permute-start | bytes 98312 | tf_op jit(solution)/shard_map/ppermute | solution.py:476
  11.3 1.6 %collective-permute-done.2.from_l = f32[8,8,128]{2,1,0:T(8,128)S(1)} collective-permute-done((f32[8,8,128]{2,1,0:T(8,128)S(1)}, f32[8,8,128]{2,1,0:T(8,128)S(1)}, u32[]{:S(2)}, u32[]{:S(2)}) %collective-permute-start.2) | collective-permute-done | bytes 32800 | tf_op jit(solution)/shard_map/ppermute | solution.py:470
  12.9 2.6 %collective-permute-done.4.from_ly = f32[8,8,128]{2,1,0:T(8,128)S(1)} collective-permute-done((f32[8,8,128]{2,1,0:T(8,128)S(1)}, f32[8,8,128]{2,1,0:T(8,128)S(1)}, u32[]{:S(2)}, u32[]{:S(2)}) %collective-permute-start.4) | collective-permute-done | bytes 32800 | tf_op jit(solution)/shard_map/ppermute | solution.py:476
  15.6 1.6 %collective-permute-start.5 = (f32[24,128]{1,0:T(8,128)S(1)}, f32[24,128]{1,0:T(8,128)S(1)}, u32[]{:S(2)}, u32[]{:S(2)}) collective-permute-start(f32[24,128]{1,0:T(8,128)S(1)} %get-tuple-element.46), channel_id=1, source_target_pairs={{0,1},{1,2},{2,3},{3,0},{4,5},{5,6},{6,7},{7,4},{8,9},{9,10},{10,1... | collective-permute-start | bytes 36872 | tf_op jit(solution)/shard_map/ppermute | solution.py:470
  17.2 2.2 %collective-permute-start.6 = (f32[24,128]{1,0:T(8,128)S(1)}, f32[24,128]{1,0:T(8,128)S(1)}, u32[]{:S(2)}, u32[]{:S(2)}) collective-permute-start(f32[24,128]{1,0:T(8,128)S(1)} %get-tuple-element.46), channel_id=1, source_target_pairs={{0,3},{1,0},{2,1},{3,2},{4,7},{5,4},{6,5},{7,6},{8,11},{9,8},{10,9... | collective-permute-start | bytes 36872 | tf_op jit(solution)/shard_map/ppermute | solution.py:470
  19.5 1.7 %collective-permute-done.5.rims_l = f32[24,128]{1,0:T(8,128)S(1)} collective-permute-done((f32[24,128]{1,0:T(8,128)S(1)}, f32[24,128]{1,0:T(8,128)S(1)}, u32[]{:S(2)}, u32[]{:S(2)}) %collective-permute-start.5) | collective-permute-done | bytes 12320 | tf_op jit(solution)/shard_map/ppermute | solution.py:470
  21.2 3.3 %shard_map.62 = (f32[8,8,128]{2,1,0:T(8,128)S(1)}, f32[8,8,128]{2,1,0:T(8,128)S(1)}, f32[4,8,128]{2,1,0:T(8,128)S(1)}, f32[3,8,128]{2,1,0:T(8,128)S(1)}, f32[4,8...) custom-call(f32[15,16,128]{2,1,0:T(8,128)S(1)} %get-tuple-element.45., ...), custom_call_target="tpu_custom_call" | custom-call | flops 20971520 | bytes 1753088 | tf_op jit(solution)/shard_map/pallas_call | solution.py:453
  24.5 1.5 %collective-permute-start.7 = (f32[8,8,128]{2,1,0:T(8,128)S(1)}, f32[8,8,128]{2,1,0:T(8,128)S(1)}, u32[]{:S(2)}, u32[]{:S(2)}) collective-permute-start(f32[8,8,128]{2,1,0:T(8,128)S(1)} %get-tuple-element.51), channel_id=1, source_target_pairs={{0,4},{4,0},{1,5},{5,1},{2,6},{6,2},{3,7},{7,3},{8,12},{12,8},{9,1... | collective-permute-start | bytes 98312 | tf_op jit(solution)/shard_map/ppermute | solution.py:470
  26.0 1.2 %collective-permute-start.8 = (f32[4,8,128]{2,1,0:T(8,128)S(1)}, f32[4,8,128]{2,1,0:T(8,128)S(1)}, u32[]{:S(2)}, u32[]{:S(2)}) collective-permute-start(f32[4,8,128]{2,1,0:T(8,128)S(1)} %get-tuple-element.52), channel_id=1, source_target_pairs={{0,24},{8,0},{16,8},{24,16},{1,25},{9,1},{17,9},{25,17},{2,26},{10... | collective-permute-start | bytes 49160 | tf_op jit(solution)/shard_map/ppermute | solution.py:470
  27.7 1.6 %collective-permute-start.9 = (f32[3,8,128]{2,1,0:T(8,128)S(1)}, f32[3,8,128]{2,1,0:T(8,128)S(1)}, u32[]{:S(2)}, u32[]{:S(2)}) collective-permute-start(f32[3,8,128]{2,1,0:T(8,128)S(1)} %get-tuple-element.53), channel_id=1, source_target_pairs={{0,8},{8,16},{16,24},{24,0},{1,9},{9,17},{17,25},{25,1},{2,10},{10... | collective-permute-start | bytes 36872 | tf_op jit(solution)/shard_map/ppermute | solution.py:470
  29.3 2.6 %shard_map.63 = (f32[1,15,16,128]{3,2,1,0:T(8,128)S(1)}, f32[1,16,128]{2,1,0:T(8,128)S(1)}, f32[3,8,8,8,128]{4,3,2,1,0:T(8,128)S(1)}, f32[3,8,8,8,128]{4,3,2,1,0...) custom-call(f32[1,8,8,128]{3,2,1,0:T(8,128)S(1)} %get-tuple-element.56.adjoint, ...), custom_call_target="tpu_custom_call" | custom-call | flops 8388608 | bytes 1605632 | tf_op jit(solution)/shard_map/pallas_call | solution.py:453
  32.1 1.4 %collective-permute-start.12 = (f32[16,128]{1,0:T(8,128)S(1)}, f32[16,128]{1,0:T(8,128)S(1)}, u32[]{:S(2)}, u32[]{:S(2)}) collective-permute-start(f32[16,128]{1,0:T(8,128)S(1)} %get-tuple-element.59), channel_id=1, source_target_pairs={{0,1},{1,2},{2,3},{3,0},{4,5},{5,6},{6,7},{7,4},{8,9},{9,10},{10,1... | collective-permute-start | bytes 24584 | tf_op jit(solution)/shard_map/ppermute | solution.py:470
  33.5 2.5 %collective-permute-start.13 = (f32[16,128]{1,0:T(8,128)S(1)}, f32[16,128]{1,0:T(8,128)S(1)}, u32[]{:S(2)}, u32[]{:S(2)}) collective-permute-start(f32[16,128]{1,0:T(8,128)S(1)} %get-tuple-element.59), channel_id=1, source_target_pairs={{0,3},{1,0},{2,1},{3,2},{4,7},{5,4},{6,5},{7,6},{8,11},{9,8},{10,9... | collective-permute-start | bytes 24584 | tf_op jit(solution)/shard_map/ppermute | solution.py:470
  36.0 4.0 %shard_map.65.early_piles = f32[3,8,15,16,128]{4,3,2,1,0:T(8,128)S(1)} custom-call(f32[3,8,8,128]{3,2,1,0:T(8,128)S(1)} %get-tuple-element.63.gradient, f32[1,8,8,128]{3,2,1,0:T(8,128)S(1)} %get-tuple-element.56.adjoint, f32[3,8,8,8,128]{4,3,2,1,0:T(8,128)S(1)} %get-tuple-element.64.weights, ...), custom_call_target="tpu_custom_call", output_to_operand_aliasing={{}: (3, {})} | custom-call | flops 25165824 | bytes 3866624 | tf_op jit(solution)/shard_map/pallas_call | solution.py:453
  40.1 8.1 %shard_map.66 = (f32[3,15,16,128]{3,2,1,0:T(8,128)S(1)}, f32[64,128]{1,0:T(8,128)S(1)}, f32[3,8,15,16,128]{4,3,2,1,0:T(8,128)S(1)}) custom-call(f32[15,16,128]{2,1,0:T(8,128)S(1)} %get-tuple-element.58.extended, f32[16,128]{1,0:T(8,128)S(1)} %collective-permute-done.12.rims_l, ...), custom_call_target="tpu_custom_call", output_to_operand_aliasing={{2}: (8, {})} | custom-call | flops 46137344 | bytes 5521408 | tf_op jit(solution)/shard_map/pallas_call | solution.py:453
  48.2 3.8 %collective-permute-start.15 = (f32[64,128]{1,0:T(8,128)S(1)}, f32[64,128]{1,0:T(8,128)S(1)}, u32[]{:S(2)}, u32[]{:S(2)}) collective-permute-start(f32[64,128]{1,0:T(8,128)S(1)} %get-tuple-element.67), channel_id=1, source_target_pairs={{0,3},{1,0},{2,1},{3,2},{4,7},{5,4},{6,5},{7,6},{8,11},{9,8},{10,9... | collective-permute-start | bytes 98312 | tf_op jit(solution)/shard_map/ppermute | solution.py:470
  52.0 1.9 %collective-permute-done.14.rims_l = f32[64,128]{1,0:T(8,128)S(1)} collective-permute-done((f32[64,128]{1,0:T(8,128)S(1)}, f32[64,128]{1,0:T(8,128)S(1)}, u32[]{:S(2)}, u32[]{:S(2)}) %collective-permute-start.14) | collective-permute-done | bytes 32800 | tf_op jit(solution)/shard_map/ppermute | solution.py:470
  54.8 2.0 %collective-permute-start.20 = (f32[16,8,128]{2,1,0:T(8,128)S(1)}, f32[16,8,128]{2,1,0:T(8,128)S(1)}, u32[]{:S(2)}, u32[]{:S(2)}) collective-permute-start(f32[16,8,128]{2,1,0:T(8,128)S(1)} %get-tuple-element.73), channel_id=1, source_target_pairs={{0,12},{4,8},{8,20},{12,16},{16,28},{20,24},{24,4},{28,0},{1,13},{... | collective-permute-start | bytes 196616 | tf_op jit(solution)/shard_map/ppermute | solution.py:476
  58.2 1.0 %collective-permute-done.17.from_r = f32[12,8,128]{2,1,0:T(8,128)S(1)} collective-permute-done((f32[12,8,128]{2,1,0:T(8,128)S(1)}, f32[12,8,128]{2,1,0:T(8,128)S(1)}, u32[]{:S(2)}, u32[]{:S(2)}) %collective-permute-start.17) | collective-permute-done | bytes 49184 | tf_op jit(solution)/shard_map/ppermute | solution.py:470
  59.2 2.1 %collective-permute-done.19.from_ry = f32[12,8,128]{2,1,0:T(8,128)S(1)} collective-permute-done((f32[12,8,128]{2,1,0:T(8,128)S(1)}, f32[12,8,128]{2,1,0:T(8,128)S(1)}, u32[]{:S(2)}, u32[]{:S(2)}) %collective-permute-start.19) | collective-permute-done | bytes 49184 | tf_op jit(solution)/shard_map/ppermute | solution.py:476
  (37 shorter events, 5.7 us)
Async XLA Ops:
  0.6 1.0 %copy-start = (s32[2,2,3,8,8,128]{5,4,3,2,1,0:T(8,128)S(1)}, s32[2,2,3,8,8,128]{5,4,3,2,1,0:T(8,128)}, u32[]{:S(2)}) copy-start(s32[2,2,3,8,8,128]{5,4,3,2,1,0:T(8,128)} %cells.3) | copy-start | bytes 1179652
  2.6 26.7 %copy-start.1 = (s32[2,2,3,8,8,128]{5,4,3,2,1,0:T(8,128)S(1)}, s32[2,2,3,8,8,128]{5,4,3,2,1,0:T(8,128)}, u32[]{:S(2)}) copy-start(s32[2,2,3,8,8,128]{5,4,3,2,1,0:T(8,128)} %cells.3) | copy-start | bytes 1179652
  2.6 26.7 %copy-start.3 = (f32[2,2,3,8,8,128]{5,4,3,2,1,0:T(8,128)S(1)}, f32[2,2,3,8,8,128]{5,4,3,2,1,0:T(8,128)}, u32[]{:S(2)}) copy-start(f32[2,2,3,8,8,128]{5,4,3,2,1,0:T(8,128)} %fracs.3) | copy-start | bytes 1179652
  5.9 9.6 %collective-permute-start = (f32[17,8,128]{2,1,0:T(8,128)S(1)}, f32[17,8,128]{2,1,0:T(8,128)S(1)}, u32[]{:S(2)}, u32[]{:S(2)}) collective-permute-start(f32[17,8,128]{2,1,0:T(8,128)S(1)} %get-tuple-element.39), channel_id=1, source_target_pairs={{0,4},{4,0},{1,5},{5,1},{2,6},{6,2},{3,7},{7,3},{8,12},{12,8},{9,1... | collective-permute-start | bytes 208904 | tf_op jit(solution)/shard_map/ppermute | solution.py:470
  8.9 2.4 %collective-permute-start.1 = (f32[8,8,128]{2,1,0:T(8,128)S(1)}, f32[8,8,128]{2,1,0:T(8,128)S(1)}, u32[]{:S(2)}, u32[]{:S(2)}) collective-permute-start(f32[8,8,128]{2,1,0:T(8,128)S(1)} %get-tuple-element.40), channel_id=1, source_target_pairs={{0,24},{8,0},{16,8},{24,16},{1,25},{9,1},{17,9},{25,17},{2,26},{10... | collective-permute-start | bytes 98312 | tf_op jit(solution)/shard_map/ppermute | solution.py:470
  9.5 3.3 %collective-permute-start.2 = (f32[8,8,128]{2,1,0:T(8,128)S(1)}, f32[8,8,128]{2,1,0:T(8,128)S(1)}, u32[]{:S(2)}, u32[]{:S(2)}) collective-permute-start(f32[8,8,128]{2,1,0:T(8,128)S(1)} %get-tuple-element.41), channel_id=1, source_target_pairs={{0,8},{8,16},{16,24},{24,0},{1,9},{9,17},{17,25},{25,1},{2,10},{10... | collective-permute-start | bytes 98312 | tf_op jit(solution)/shard_map/ppermute | solution.py:470
  9.6 3.3 %collective-permute-start.3 = (f32[8,8,128]{2,1,0:T(8,128)S(1)}, f32[8,8,128]{2,1,0:T(8,128)S(1)}, u32[]{:S(2)}, u32[]{:S(2)}) collective-permute-start(f32[8,8,128]{2,1,0:T(8,128)S(1)} %get-tuple-element.42), channel_id=1, source_target_pairs={{0,28},{4,24},{8,4},{12,0},{16,12},{20,8},{24,20},{28,16},{1,29},{... | collective-permute-start | bytes 98312 | tf_op jit(solution)/shard_map/ppermute | solution.py:476
  11.2 4.2 %collective-permute-start.4 = (f32[8,8,128]{2,1,0:T(8,128)S(1)}, f32[8,8,128]{2,1,0:T(8,128)S(1)}, u32[]{:S(2)}, u32[]{:S(2)}) collective-permute-start(f32[8,8,128]{2,1,0:T(8,128)S(1)} %get-tuple-element.43), channel_id=1, source_target_pairs={{0,12},{4,8},{8,20},{12,16},{16,28},{20,24},{24,4},{28,0},{1,13},{... | collective-permute-start | bytes 98312 | tf_op jit(solution)/shard_map/ppermute | solution.py:476
  15.6 5.6 %collective-permute-start.5 = (f32[24,128]{1,0:T(8,128)S(1)}, f32[24,128]{1,0:T(8,128)S(1)}, u32[]{:S(2)}, u32[]{:S(2)}) collective-permute-start(f32[24,128]{1,0:T(8,128)S(1)} %get-tuple-element.46), channel_id=1, source_target_pairs={{0,1},{1,2},{2,3},{3,0},{4,5},{5,6},{6,7},{7,4},{8,9},{9,10},{10,1... | collective-permute-start | bytes 36872 | tf_op jit(solution)/shard_map/ppermute | solution.py:470
  17.2 4.0 %collective-permute-start.6 = (f32[24,128]{1,0:T(8,128)S(1)}, f32[24,128]{1,0:T(8,128)S(1)}, u32[]{:S(2)}, u32[]{:S(2)}) collective-permute-start(f32[24,128]{1,0:T(8,128)S(1)} %get-tuple-element.46), channel_id=1, source_target_pairs={{0,3},{1,0},{2,1},{3,2},{4,7},{5,4},{6,5},{7,6},{8,11},{9,8},{10,9... | collective-permute-start | bytes 36872 | tf_op jit(solution)/shard_map/ppermute | solution.py:470
  24.5 7.5 %collective-permute-start.7 = (f32[8,8,128]{2,1,0:T(8,128)S(1)}, f32[8,8,128]{2,1,0:T(8,128)S(1)}, u32[]{:S(2)}, u32[]{:S(2)}) collective-permute-start(f32[8,8,128]{2,1,0:T(8,128)S(1)} %get-tuple-element.51), channel_id=1, source_target_pairs={{0,4},{4,0},{1,5},{5,1},{2,6},{6,2},{3,7},{7,3},{8,12},{12,8},{9,1... | collective-permute-start | bytes 98312 | tf_op jit(solution)/shard_map/ppermute | solution.py:470
  26.0 6.0 %collective-permute-start.10 = (f32[4,8,128]{2,1,0:T(8,128)S(1)}, f32[4,8,128]{2,1,0:T(8,128)S(1)}, u32[]{:S(2)}, u32[]{:S(2)}) collective-permute-start(f32[4,8,128]{2,1,0:T(8,128)S(1)} %get-tuple-element.54), channel_id=1, source_target_pairs={{0,28},{4,24},{8,4},{12,0},{16,12},{20,8},{24,20},{28,16},{1,29},{... | collective-permute-start | bytes 49160 | tf_op jit(solution)/shard_map/ppermute | solution.py:476
  26.0 6.0 %collective-permute-start.8 = (f32[4,8,128]{2,1,0:T(8,128)S(1)}, f32[4,8,128]{2,1,0:T(8,128)S(1)}, u32[]{:S(2)}, u32[]{:S(2)}) collective-permute-start(f32[4,8,128]{2,1,0:T(8,128)S(1)} %get-tuple-element.52), channel_id=1, source_target_pairs={{0,24},{8,0},{16,8},{24,16},{1,25},{9,1},{17,9},{25,17},{2,26},{10... | collective-permute-start | bytes 49160 | tf_op jit(solution)/shard_map/ppermute | solution.py:470
  27.2 4.7 %collective-permute-start.11 = (f32[3,8,128]{2,1,0:T(8,128)S(1)}, f32[3,8,128]{2,1,0:T(8,128)S(1)}, u32[]{:S(2)}, u32[]{:S(2)}) collective-permute-start(f32[3,8,128]{2,1,0:T(8,128)S(1)} %get-tuple-element.55), channel_id=1, source_target_pairs={{0,12},{4,8},{8,20},{12,16},{16,28},{20,24},{24,4},{28,0},{1,13},{... | collective-permute-start | bytes 36872 | tf_op jit(solution)/shard_map/ppermute | solution.py:476
  27.7 4.2 %collective-permute-start.9 = (f32[3,8,128]{2,1,0:T(8,128)S(1)}, f32[3,8,128]{2,1,0:T(8,128)S(1)}, u32[]{:S(2)}, u32[]{:S(2)}) collective-permute-start(f32[3,8,128]{2,1,0:T(8,128)S(1)} %get-tuple-element.53), channel_id=1, source_target_pairs={{0,8},{8,16},{16,24},{24,0},{1,9},{9,17},{17,25},{25,1},{2,10},{10... | collective-permute-start | bytes 36872 | tf_op jit(solution)/shard_map/ppermute | solution.py:470
  32.1 8.0 %collective-permute-start.12 = (f32[16,128]{1,0:T(8,128)S(1)}, f32[16,128]{1,0:T(8,128)S(1)}, u32[]{:S(2)}, u32[]{:S(2)}) collective-permute-start(f32[16,128]{1,0:T(8,128)S(1)} %get-tuple-element.59), channel_id=1, source_target_pairs={{0,1},{1,2},{2,3},{3,0},{4,5},{5,6},{6,7},{7,4},{8,9},{9,10},{10,1... | collective-permute-start | bytes 24584 | tf_op jit(solution)/shard_map/ppermute | solution.py:470
  33.5 6.6 %collective-permute-start.13 = (f32[16,128]{1,0:T(8,128)S(1)}, f32[16,128]{1,0:T(8,128)S(1)}, u32[]{:S(2)}, u32[]{:S(2)}) collective-permute-start(f32[16,128]{1,0:T(8,128)S(1)} %get-tuple-element.59), channel_id=1, source_target_pairs={{0,3},{1,0},{2,1},{3,2},{4,7},{5,4},{6,5},{7,6},{8,11},{9,8},{10,9... | collective-permute-start | bytes 24584 | tf_op jit(solution)/shard_map/ppermute | solution.py:470
  48.2 5.8 %collective-permute-start.14 = (f32[64,128]{1,0:T(8,128)S(1)}, f32[64,128]{1,0:T(8,128)S(1)}, u32[]{:S(2)}, u32[]{:S(2)}) collective-permute-start(f32[64,128]{1,0:T(8,128)S(1)} %get-tuple-element.67), channel_id=1, source_target_pairs={{0,1},{1,2},{2,3},{3,0},{4,5},{5,6},{6,7},{7,4},{8,9},{9,10},{10,1... | collective-permute-start | bytes 98312 | tf_op jit(solution)/shard_map/ppermute | solution.py:470
  48.2 5.7 %collective-permute-start.15 = (f32[64,128]{1,0:T(8,128)S(1)}, f32[64,128]{1,0:T(8,128)S(1)}, u32[]{:S(2)}, u32[]{:S(2)}) collective-permute-start(f32[64,128]{1,0:T(8,128)S(1)} %get-tuple-element.67), channel_id=1, source_target_pairs={{0,3},{1,0},{2,1},{3,2},{4,7},{5,4},{6,5},{7,6},{8,11},{9,8},{10,9... | collective-permute-start | bytes 98312 | tf_op jit(solution)/shard_map/ppermute | solution.py:470
  54.1 7.1 %collective-permute-start.16 = (f32[32,8,128]{2,1,0:T(8,128)S(1)}, f32[32,8,128]{2,1,0:T(8,128)S(1)}, u32[]{:S(2)}, u32[]{:S(2)}) collective-permute-start(f32[32,8,128]{2,1,0:T(8,128)S(1)} %get-tuple-element.69), channel_id=1, source_target_pairs={{0,4},{4,0},{1,5},{5,1},{2,6},{6,2},{3,7},{7,3},{8,12},{12,8},{9,1... | collective-permute-start | bytes 393224 | tf_op jit(solution)/shard_map/ppermute | solution.py:470
  54.8 6.4 %collective-permute-start.18 = (f32[16,8,128]{2,1,0:T(8,128)S(1)}, f32[16,8,128]{2,1,0:T(8,128)S(1)}, u32[]{:S(2)}, u32[]{:S(2)}) collective-permute-start(f32[16,8,128]{2,1,0:T(8,128)S(1)} %get-tuple-element.71), channel_id=1, source_target_pairs={{0,8},{8,16},{16,24},{24,0},{1,9},{9,17},{17,25},{25,1},{2,10},{10... | collective-permute-start | bytes 196616 | tf_op jit(solution)/shard_map/ppermute | solution.py:470
  54.8 6.4 %collective-permute-start.20 = (f32[16,8,128]{2,1,0:T(8,128)S(1)}, f32[16,8,128]{2,1,0:T(8,128)S(1)}, u32[]{:S(2)}, u32[]{:S(2)}) collective-permute-start(f32[16,8,128]{2,1,0:T(8,128)S(1)} %get-tuple-element.73), channel_id=1, source_target_pairs={{0,12},{4,8},{8,20},{12,16},{16,28},{20,24},{24,4},{28,0},{1,13},{... | collective-permute-start | bytes 196616 | tf_op jit(solution)/shard_map/ppermute | solution.py:476
  56.8 2.4 %collective-permute-start.17 = (f32[12,8,128]{2,1,0:T(8,128)S(1)}, f32[12,8,128]{2,1,0:T(8,128)S(1)}, u32[]{:S(2)}, u32[]{:S(2)}) collective-permute-start(f32[12,8,128]{2,1,0:T(8,128)S(1)} %get-tuple-element.70), channel_id=1, source_target_pairs={{0,24},{8,0},{16,8},{24,16},{1,25},{9,1},{17,9},{25,17},{2,26},{10... | collective-permute-start | bytes 147464 | tf_op jit(solution)/shard_map/ppermute | solution.py:470
  57.4 3.8 %collective-permute-start.19 = (f32[12,8,128]{2,1,0:T(8,128)S(1)}, f32[12,8,128]{2,1,0:T(8,128)S(1)}, u32[]{:S(2)}, u32[]{:S(2)}) collective-permute-start(f32[12,8,128]{2,1,0:T(8,128)S(1)} %get-tuple-element.72), channel_id=1, source_target_pairs={{0,28},{4,24},{8,4},{12,0},{16,12},{20,8},{24,20},{28,16},{1,29},{... | collective-permute-start | bytes 147464 | tf_op jit(solution)/shard_map/ppermute | solution.py:476
  (1 other events, 1.0 us)

commit v10 on v9

--- a/solution.py
+++ b/solution.py
@@ -299,6 +299,12 @@
         place(i, from_left[i], from_left_y[i])
 
 
+def fill(size, used, *messages):
+    for message in messages:
+        for i in range(used, size):
+            message[i] = jnp.zeros(message.shape[1:], F32)
+
+
 def split_halo(field, outs, nx, ny):
     to_y, to_left, to_right, to_left_y, to_right_y = outs
     for x in range(nx):
@@ -355,6 +361,7 @@
 
     interpolate(shifted, weights, slopes, nx, ny, emit, True)
     split_halo(image, (to_y, to_l, to_r, to_ly, to_ry), nx, ny)
+    fill(HI, LO, to_r, to_ry)
     back = jnp.where(low_lanes(ny), rims_l[rows : rows + ny], rims_r[rows : rows + ny])
     for x in range(nx):
         adjoint[0, x] = part[x] + unpack_rim(back, LO + x)
@@ -422,6 +429,7 @@
                 straight, corner, at = to_r, to_ry, c * HI + X - LO - nx
             straight[at] = plane[core]
             put_rims(corner, at, plane, ny)
+    fill(4 * HI, 4 * LO, to_l, to_ly)
 
 
 def last_kernel(nx, ny, own, from_y, from_r, from_l, from_ry, from_ly, intensity_adjoint, velocity_adjoint):
@@ -545,7 +553,7 @@
     image, *outs, adjoint, gradient = run(
         middle_kernel,
         (extended,) + send_z(rims) + (folded, early, early_slopes),
-        [field] + messages(nx, HI, LO) + [(1,) + field, (3,) + field],
+        [field] + messages(nx, HI, HI) + [(1,) + field, (3,) + field],
         [(SHIFTS, planes, rows, nz), (planes, rows, nz)],
         5 * unit,
     )
@@ -588,7 +596,7 @@
     *outs, own = run(
         last_z_kernel,
         (velocity, piled_adjoint) + send_z(rims),
-        messages(4 * nx, 4 * LO, 4 * HI) + [(4 * nx, ny, nz)],
+        messages(4 * nx, 4 * HI, 4 * HI) + [(4 * nx, ny, nz)],
         [],
         unit // 16,
     )

time: 62.2 us -> 62.3 us (level)
  waiting for transfers between devices: 10.9 us -> 12.3 us
  starting transfers between devices: 25.9 us -> 24.6 us
    ppermute x15, starting transfers between devices: 20.9 us -> 19.4 us  [send(): return lax.ppermute(message, axes[0], pairs)]
    ppermute x15, waiting for transfers between devices: 6.21 us -> 6.99 us  [send(): return lax.ppermute(message, axes[0], pairs)]
    ppermute x6, waiting for transfers between devices: 4.66 us -> 5.35 us  [send(): return lax.ppermute(message, axes, pairs)]
  transfers between devices with their start and end apart: 21 -> 21, of which waited for: 6 -> 7; matrix products, arithmetic and copies ran while one was open for 0% -> 0% of each run, Pallas kernels for 11% -> 11%
where the time goes in v10:
time: 62.3 us; the launch traced here: 62.1 us
  starting transfers between devices  24.6 us (39%)
  Pallas kernels  21.6 us (35%)
  waiting for transfers between devices  12.3 us (20%)
  local copies, waits for them, and re-layouts  1.99 us (3%)
  other arithmetic  0.78 us (1%)
  between operations  0.77 us (1%)
    pallas_call x10, Pallas kernels, call(): pl.pallas_call(kernel, out_shape=[struct(s) for s in outs], in_specs=in_s...  21.6 us
    ppermute x15, starting transfers between devices, send(): return lax.ppermute(message, axes[0], pairs)  19.4 us
    ppermute x15, waiting for transfers between devices, send(): return lax.ppermute(message, axes[0], pairs)  6.99 us
    ppermute x6, waiting for transfers between devices, send(): return lax.ppermute(message, axes, pairs)  5.35 us
    ppermute x6, starting transfers between devices, send(): return lax.ppermute(message, axes, pairs)  5.24 us
    unnamed x8, local copies, waits for them, and re-layouts  1.99 us
  transfers between devices with their start and end apart: 21, of which 7 were waited for; matrix products, arithmetic and copies ran while one was open for 0% of the time, Pallas kernels for 11%

profile of v10, /device:TPU:0, one launch (start us, length us, event | category | flops | bytes accessed | tf_op | source)
XLA Modules:
  0.0 62.1 jit_solution(15512091634869102744)
XLA Ops:
  0.6 1.0 %copy-done = s32[2,2,3,8,8,128]{5,4,3,2,1,0:T(8,128)S(1)} copy-done((s32[2,2,3,8,8,128]{5,4,3,2,1,0:T(8,128)S(1)}, s32[2,2,3,8,8,128]{5,4,3,2,1,0:T(8,128)}, u32[]{:S(2)}) %copy-start) | copy-done | bytes 393240
  1.6 1.0 %copy-done.2 = f32[2,2,3,8,8,128]{5,4,3,2,1,0:T(8,128)S(1)} copy-done((f32[2,2,3,8,8,128]{5,4,3,2,1,0:T(8,128)S(1)}, f32[2,2,3,8,8,128]{5,4,3,2,1,0:T(8,128)}, u32[]{:S(2)}) %copy-start.2) | copy-done | bytes 393240
  3.9 2.0 %shard_map.60 = (f32[17,8,128]{2,1,0:T(8,128)S(1)}, f32[8,8,128]{2,1,0:T(8,128)S(1)}, f32[8,8,128]{2,1,0:T(8,128)S(1)}, f32[8,8,128]{2,1,0:T(8,128)S(1)}, f32[8,...) custom-call(f32[2,8,8,128]{3,2,1,0:T(8,128)S(1)} %pad_maximum_fusion.pair, f32[3,8,8,8,128]{4,3,2,1,0:T(8,128)S(1)} %get-tuple-element.38.weights), custom_call_target="tpu_custom_call" | custom-call | flops 8388608 | bytes 851968 | tf_op jit(solution)/shard_map/pallas_call | solution.py:461
  5.9 3.0 %collective-permute-start = (f32[17,8,128]{2,1,0:T(8,128)S(1)}, f32[17,8,128]{2,1,0:T(8,128)S(1)}, u32[]{:S(2)}, u32[]{:S(2)}) collective-permute-start(f32[17,8,128]{2,1,0:T(8,128)S(1)} %get-tuple-element.39), channel_id=1, source_target_pairs={{0,4},{4,0},{1,5},{5,1},{2,6},{6,2},{3,7},{7,3},{8,12},{12,8},{9,1... | collective-permute-start | bytes 208904 | tf_op jit(solution)/shard_map/ppermute | solution.py:478
  9.6 1.7 %collective-permute-start.3 = (f32[8,8,128]{2,1,0:T(8,128)S(1)}, f32[8,8,128]{2,1,0:T(8,128)S(1)}, u32[]{:S(2)}, u32[]{:S(2)}) collective-permute-start(f32[8,8,128]{2,1,0:T(8,128)S(1)} %get-tuple-element.42), channel_id=1, source_target_pairs={{0,28},{4,24},{8,4},{12,0},{16,12},{20,8},{24,20},{28,16},{1,29},{... | collective-permute-start | bytes 98312 | tf_op jit(solution)/shard_map/ppermute | solution.py:484
  11.3 1.6 %collective-permute-done.2.from_l = f32[8,8,128]{2,1,0:T(8,128)S(1)} collective-permute-done((f32[8,8,128]{2,1,0:T(8,128)S(1)}, f32[8,8,128]{2,1,0:T(8,128)S(1)}, u32[]{:S(2)}, u32[]{:S(2)}) %collective-permute-start.2) | collective-permute-done | bytes 32800 | tf_op jit(solution)/shard_map/ppermute | solution.py:478
  12.9 2.6 %collective-permute-done.4.from_ly = f32[8,8,128]{2,1,0:T(8,128)S(1)} collective-permute-done((f32[8,8,128]{2,1,0:T(8,128)S(1)}, f32[8,8,128]{2,1,0:T(8,128)S(1)}, u32[]{:S(2)}, u32[]{:S(2)}) %collective-permute-start.4) | collective-permute-done | bytes 32800 | tf_op jit(solution)/shard_map/ppermute | solution.py:484
  15.6 1.6 %collective-permute-start.5 = (f32[24,128]{1,0:T(8,128)S(1)}, f32[24,128]{1,0:T(8,128)S(1)}, u32[]{:S(2)}, u32[]{:S(2)}) collective-permute-start(f32[24,128]{1,0:T(8,128)S(1)} %get-tuple-element.46), channel_id=1, source_target_pairs={{0,1},{1,2},{2,3},{3,0},{4,5},{5,6},{6,7},{7,4},{8,9},{9,10},{10,1... | collective-permute-start | bytes 36872 | tf_op jit(solution)/shard_map/ppermute | solution.py:478
  17.3 2.2 %collective-permute-start.6 = (f32[24,128]{1,0:T(8,128)S(1)}, f32[24,128]{1,0:T(8,128)S(1)}, u32[]{:S(2)}, u32[]{:S(2)}) collective-permute-start(f32[24,128]{1,0:T(8,128)S(1)} %get-tuple-element.46), channel_id=1, source_target_pairs={{0,3},{1,0},{2,1},{3,2},{4,7},{5,4},{6,5},{7,6},{8,11},{9,8},{10,9... | collective-permute-start | bytes 36872 | tf_op jit(solution)/shard_map/ppermute | solution.py:478
  19.5 1.7 %collective-permute-done.5.rims_l = f32[24,128]{1,0:T(8,128)S(1)} collective-permute-done((f32[24,128]{1,0:T(8,128)S(1)}, f32[24,128]{1,0:T(8,128)S(1)}, u32[]{:S(2)}, u32[]{:S(2)}) %collective-permute-start.5) | collective-permute-done | bytes 12320 | tf_op jit(solution)/shard_map/ppermute | solution.py:478
  21.2 3.3 %shard_map.62 = (f32[8,8,128]{2,1,0:T(8,128)S(1)}, f32[8,8,128]{2,1,0:T(8,128)S(1)}, f32[4,8,128]{2,1,0:T(8,128)S(1)}, f32[4,8,128]{2,1,0:T(8,128)S(1)}, f32[4,8...) custom-call(f32[15,16,128]{2,1,0:T(8,128)S(1)} %get-tuple-element.45., ...), custom_call_target="tpu_custom_call" | custom-call | flops 20971520 | bytes 1753088 | tf_op jit(solution)/shard_map/pallas_call | solution.py:461
  24.5 1.5 %collective-permute-start.7 = (f32[8,8,128]{2,1,0:T(8,128)S(1)}, f32[8,8,128]{2,1,0:T(8,128)S(1)}, u32[]{:S(2)}, u32[]{:S(2)}) collective-permute-start(f32[8,8,128]{2,1,0:T(8,128)S(1)} %get-tuple-element.51), channel_id=1, source_target_pairs={{0,4},{4,0},{1,5},{5,1},{2,6},{6,2},{3,7},{7,3},{8,12},{12,8},{9,1... | collective-permute-start | bytes 98312 | tf_op jit(solution)/shard_map/ppermute | solution.py:478
  26.0 1.7 %collective-permute-start.11 = (f32[4,8,128]{2,1,0:T(8,128)S(1)}, f32[4,8,128]{2,1,0:T(8,128)S(1)}, u32[]{:S(2)}, u32[]{:S(2)}) collective-permute-start(f32[4,8,128]{2,1,0:T(8,128)S(1)} %get-tuple-element.55), channel_id=1, source_target_pairs={{0,12},{4,8},{8,20},{12,16},{16,28},{20,24},{24,4},{28,0},{1,13},{... | collective-permute-start | bytes 49160 | tf_op jit(solution)/shard_map/ppermute | solution.py:484
  28.3 2.6 %shard_map.63 = (f32[1,15,16,128]{3,2,1,0:T(8,128)S(1)}, f32[1,16,128]{2,1,0:T(8,128)S(1)}, f32[3,8,8,8,128]{4,3,2,1,0:T(8,128)S(1)}, f32[3,8,8,8,128]{4,3,2,1,0...) custom-call(f32[1,8,8,128]{3,2,1,0:T(8,128)S(1)} %get-tuple-element.56.adjoint, ...), custom_call_target="tpu_custom_call" | custom-call | flops 8388608 | bytes 1605632 | tf_op jit(solution)/shard_map/pallas_call | solution.py:461
  31.0 1.4 %collective-permute-start.12 = (f32[16,128]{1,0:T(8,128)S(1)}, f32[16,128]{1,0:T(8,128)S(1)}, u32[]{:S(2)}, u32[]{:S(2)}) collective-permute-start(f32[16,128]{1,0:T(8,128)S(1)} %get-tuple-element.59), channel_id=1, source_target_pairs={{0,1},{1,2},{2,3},{3,0},{4,5},{5,6},{6,7},{7,4},{8,9},{9,10},{10,1... | collective-permute-start | bytes 24584 | tf_op jit(solution)/shard_map/ppermute | solution.py:478
  32.5 2.5 %collective-permute-start.13 = (f32[16,128]{1,0:T(8,128)S(1)}, f32[16,128]{1,0:T(8,128)S(1)}, u32[]{:S(2)}, u32[]{:S(2)}) collective-permute-start(f32[16,128]{1,0:T(8,128)S(1)} %get-tuple-element.59), channel_id=1, source_target_pairs={{0,3},{1,0},{2,1},{3,2},{4,7},{5,4},{6,5},{7,6},{8,11},{9,8},{10,9... | collective-permute-start | bytes 24584 | tf_op jit(solution)/shard_map/ppermute | solution.py:478
  35.0 4.0 %shard_map.65.early_piles = f32[3,8,15,16,128]{4,3,2,1,0:T(8,128)S(1)} custom-call(f32[3,8,8,128]{3,2,1,0:T(8,128)S(1)} %get-tuple-element.63.gradient, f32[1,8,8,128]{3,2,1,0:T(8,128)S(1)} %get-tuple-element.56.adjoint, f32[3,8,8,8,128]{4,3,2,1,0:T(8,128)S(1)} %get-tuple-element.64.weights, ...), custom_call_target="tpu_custom_call", output_to_operand_aliasing={{}: (3, {})} | custom-call | flops 25165824 | bytes 3866624 | tf_op jit(solution)/shard_map/pallas_call | solution.py:461
  39.1 8.1 %shard_map.66 = (f32[3,15,16,128]{3,2,1,0:T(8,128)S(1)}, f32[64,128]{1,0:T(8,128)S(1)}, f32[3,8,15,16,128]{4,3,2,1,0:T(8,128)S(1)}) custom-call(f32[15,16,128]{2,1,0:T(8,128)S(1)} %get-tuple-element.58.extended, f32[16,128]{1,0:T(8,128)S(1)} %collective-permute-done.12.rims_l, ...), custom_call_target="tpu_custom_call", output_to_operand_aliasing={{2}: (8, {})} | custom-call | flops 46137344 | bytes 5521408 | tf_op jit(solution)/shard_map/pallas_call | solution.py:461
  47.2 3.8 %collective-permute-start.15 = (f32[64,128]{1,0:T(8,128)S(1)}, f32[64,128]{1,0:T(8,128)S(1)}, u32[]{:S(2)}, u32[]{:S(2)}) collective-permute-start(f32[64,128]{1,0:T(8,128)S(1)} %get-tuple-element.67), channel_id=1, source_target_pairs={{0,3},{1,0},{2,1},{3,2},{4,7},{5,4},{6,5},{7,6},{8,11},{9,8},{10,9... | collective-permute-start | bytes 98312 | tf_op jit(solution)/shard_map/ppermute | solution.py:478
  51.0 1.9 %collective-permute-done.14.rims_l = f32[64,128]{1,0:T(8,128)S(1)} collective-permute-done((f32[64,128]{1,0:T(8,128)S(1)}, f32[64,128]{1,0:T(8,128)S(1)}, u32[]{:S(2)}, u32[]{:S(2)}) %collective-permute-start.14) | collective-permute-done | bytes 32800 | tf_op jit(solution)/shard_map/ppermute | solution.py:478
  53.1 1.5 %collective-permute-start.16 = (f32[32,8,128]{2,1,0:T(8,128)S(1)}, f32[32,8,128]{2,1,0:T(8,128)S(1)}, u32[]{:S(2)}, u32[]{:S(2)}) collective-permute-start(f32[32,8,128]{2,1,0:T(8,128)S(1)} %get-tuple-element.69), channel_id=1, source_target_pairs={{0,4},{4,0},{1,5},{5,1},{2,6},{6,2},{3,7},{7,3},{8,12},{12,8},{9,1... | collective-permute-start | bytes 393224 | tf_op jit(solution)/shard_map/ppermute | solution.py:478
  55.1 1.3 %collective-permute-start.19 = (f32[16,8,128]{2,1,0:T(8,128)S(1)}, f32[16,8,128]{2,1,0:T(8,128)S(1)}, u32[]{:S(2)}, u32[]{:S(2)}) collective-permute-start(f32[16,8,128]{2,1,0:T(8,128)S(1)} %get-tuple-element.72), channel_id=1, source_target_pairs={{0,28},{4,24},{8,4},{12,0},{16,12},{20,8},{24,20},{28,16},{1,29},{... | collective-permute-start | bytes 196616 | tf_op jit(solution)/shard_map/ppermute | solution.py:484
  56.9 1.8 %collective-permute-done.18.from_l = f32[16,8,128]{2,1,0:T(8,128)S(1)} collective-permute-done((f32[16,8,128]{2,1,0:T(8,128)S(1)}, f32[16,8,128]{2,1,0:T(8,128)S(1)}, u32[]{:S(2)}, u32[]{:S(2)}) %collective-permute-start.18) | collective-permute-done | bytes 65568 | tf_op jit(solution)/shard_map/ppermute | solution.py:478
  58.8 2.6 %collective-permute-done.20.from_ly = f32[16,8,128]{2,1,0:T(8,128)S(1)} collective-permute-done((f32[16,8,128]{2,1,0:T(8,128)S(1)}, f32[16,8,128]{2,1,0:T(8,128)S(1)}, u32[]{:S(2)}, u32[]{:S(2)}) %collective-permute-start.20) | collective-permute-done | bytes 65568 | tf_op jit(solution)/shard_map/ppermute | solution.py:484
  (37 shorter events, 4.9 us)
Async XLA Ops:
  0.6 1.0 %copy-start = (s32[2,2,3,8,8,128]{5,4,3,2,1,0:T(8,128)S(1)}, s32[2,2,3,8,8,128]{5,4,3,2,1,0:T(8,128)}, u32[]{:S(2)}) copy-start(s32[2,2,3,8,8,128]{5,4,3,2,1,0:T(8,128)} %cells.3) | copy-start | bytes 1179652
  2.6 25.6 %copy-start.1 = (s32[2,2,3,8,8,128]{5,4,3,2,1,0:T(8,128)S(1)}, s32[2,2,3,8,8,128]{5,4,3,2,1,0:T(8,128)}, u32[]{:S(2)}) copy-start(s32[2,2,3,8,8,128]{5,4,3,2,1,0:T(8,128)} %cells.3) | copy-start | bytes 1179652
  2.6 25.6 %copy-start.3 = (f32[2,2,3,8,8,128]{5,4,3,2,1,0:T(8,128)S(1)}, f32[2,2,3,8,8,128]{5,4,3,2,1,0:T(8,128)}, u32[]{:S(2)}) copy-start(f32[2,2,3,8,8,128]{5,4,3,2,1,0:T(8,128)} %fracs.3) | copy-start | bytes 1179652
  5.9 9.6 %collective-permute-start = (f32[17,8,128]{2,1,0:T(8,128)S(1)}, f32[17,8,128]{2,1,0:T(8,128)S(1)}, u32[]{:S(2)}, u32[]{:S(2)}) collective-permute-start(f32[17,8,128]{2,1,0:T(8,128)S(1)} %get-tuple-element.39), channel_id=1, source_target_pairs={{0,4},{4,0},{1,5},{5,1},{2,6},{6,2},{3,7},{7,3},{8,12},{12,8},{9,1... | collective-permute-start | bytes 208904 | tf_op jit(solution)/shard_map/ppermute | solution.py:478
  8.9 2.4 %collective-permute-start.1 = (f32[8,8,128]{2,1,0:T(8,128)S(1)}, f32[8,8,128]{2,1,0:T(8,128)S(1)}, u32[]{:S(2)}, u32[]{:S(2)}) collective-permute-start(f32[8,8,128]{2,1,0:T(8,128)S(1)} %get-tuple-element.40), channel_id=1, source_target_pairs={{0,24},{8,0},{16,8},{24,16},{1,25},{9,1},{17,9},{25,17},{2,26},{10... | collective-permute-start | bytes 98312 | tf_op jit(solution)/shard_map/ppermute | solution.py:478
  9.6 3.3 %collective-permute-start.2 = (f32[8,8,128]{2,1,0:T(8,128)S(1)}, f32[8,8,128]{2,1,0:T(8,128)S(1)}, u32[]{:S(2)}, u32[]{:S(2)}) collective-permute-start(f32[8,8,128]{2,1,0:T(8,128)S(1)} %get-tuple-element.41), channel_id=1, source_target_pairs={{0,8},{8,16},{16,24},{24,0},{1,9},{9,17},{17,25},{25,1},{2,10},{10... | collective-permute-start | bytes 98312 | tf_op jit(solution)/shard_map/ppermute | solution.py:478
  9.6 3.3 %collective-permute-start.3 = (f32[8,8,128]{2,1,0:T(8,128)S(1)}, f32[8,8,128]{2,1,0:T(8,128)S(1)}, u32[]{:S(2)}, u32[]{:S(2)}) collective-permute-start(f32[8,8,128]{2,1,0:T(8,128)S(1)} %get-tuple-element.42), channel_id=1, source_target_pairs={{0,28},{4,24},{8,4},{12,0},{16,12},{20,8},{24,20},{28,16},{1,29},{... | collective-permute-start | bytes 98312 | tf_op jit(solution)/shard_map/ppermute | solution.py:484
  11.3 4.2 %collective-permute-start.4 = (f32[8,8,128]{2,1,0:T(8,128)S(1)}, f32[8,8,128]{2,1,0:T(8,128)S(1)}, u32[]{:S(2)}, u32[]{:S(2)}) collective-permute-start(f32[8,8,128]{2,1,0:T(8,128)S(1)} %get-tuple-element.43), channel_id=1, source_target_pairs={{0,12},{4,8},{8,20},{12,16},{16,28},{20,24},{24,4},{28,0},{1,13},{... | collective-permute-start | bytes 98312 | tf_op jit(solution)/shard_map/ppermute | solution.py:484
  15.6 5.6 %collective-permute-start.5 = (f32[24,128]{1,0:T(8,128)S(1)}, f32[24,128]{1,0:T(8,128)S(1)}, u32[]{:S(2)}, u32[]{:S(2)}) collective-permute-start(f32[24,128]{1,0:T(8,128)S(1)} %get-tuple-element.46), channel_id=1, source_target_pairs={{0,1},{1,2},{2,3},{3,0},{4,5},{5,6},{6,7},{7,4},{8,9},{9,10},{10,1... | collective-permute-start | bytes 36872 | tf_op jit(solution)/shard_map/ppermute | solution.py:478
  17.3 4.0 %collective-permute-start.6 = (f32[24,128]{1,0:T(8,128)S(1)}, f32[24,128]{1,0:T(8,128)S(1)}, u32[]{:S(2)}, u32[]{:S(2)}) collective-permute-start(f32[24,128]{1,0:T(8,128)S(1)} %get-tuple-element.46), channel_id=1, source_target_pairs={{0,3},{1,0},{2,1},{3,2},{4,7},{5,4},{6,5},{7,6},{8,11},{9,8},{10,9... | collective-permute-start | bytes 36872 | tf_op jit(solution)/shard_map/ppermute | solution.py:478
  24.5 6.4 %collective-permute-start.7 = (f32[8,8,128]{2,1,0:T(8,128)S(1)}, f32[8,8,128]{2,1,0:T(8,128)S(1)}, u32[]{:S(2)}, u32[]{:S(2)}) collective-permute-start(f32[8,8,128]{2,1,0:T(8,128)S(1)} %get-tuple-element.51), channel_id=1, source_target_pairs={{0,4},{4,0},{1,5},{5,1},{2,6},{6,2},{3,7},{7,3},{8,12},{12,8},{9,1... | collective-permute-start | bytes 98312 | tf_op jit(solution)/shard_map/ppermute | solution.py:478
  26.0 4.9 %collective-permute-start.10 = (f32[4,8,128]{2,1,0:T(8,128)S(1)}, f32[4,8,128]{2,1,0:T(8,128)S(1)}, u32[]{:S(2)}, u32[]{:S(2)}) collective-permute-start(f32[4,8,128]{2,1,0:T(8,128)S(1)} %get-tuple-element.54), channel_id=1, source_target_pairs={{0,28},{4,24},{8,4},{12,0},{16,12},{20,8},{24,20},{28,16},{1,29},{... | collective-permute-start | bytes 49160 | tf_op jit(solution)/shard_map/ppermute | solution.py:484
  26.0 4.9 %collective-permute-start.11 = (f32[4,8,128]{2,1,0:T(8,128)S(1)}, f32[4,8,128]{2,1,0:T(8,128)S(1)}, u32[]{:S(2)}, u32[]{:S(2)}) collective-permute-start(f32[4,8,128]{2,1,0:T(8,128)S(1)} %get-tuple-element.55), channel_id=1, source_target_pairs={{0,12},{4,8},{8,20},{12,16},{16,28},{20,24},{24,4},{28,0},{1,13},{... | collective-permute-start | bytes 49160 | tf_op jit(solution)/shard_map/ppermute | solution.py:484
  27.7 3.2 %collective-permute-start.8 = (f32[4,8,128]{2,1,0:T(8,128)S(1)}, f32[4,8,128]{2,1,0:T(8,128)S(1)}, u32[]{:S(2)}, u32[]{:S(2)}) collective-permute-start(f32[4,8,128]{2,1,0:T(8,128)S(1)} %get-tuple-element.52), channel_id=1, source_target_pairs={{0,24},{8,0},{16,8},{24,16},{1,25},{9,1},{17,9},{25,17},{2,26},{10... | collective-permute-start | bytes 49160 | tf_op jit(solution)/shard_map/ppermute | solution.py:478
  27.8 3.2 %collective-permute-start.9 = (f32[4,8,128]{2,1,0:T(8,128)S(1)}, f32[4,8,128]{2,1,0:T(8,128)S(1)}, u32[]{:S(2)}, u32[]{:S(2)}) collective-permute-start(f32[4,8,128]{2,1,0:T(8,128)S(1)} %get-tuple-element.53), channel_id=1, source_target_pairs={{0,8},{8,16},{16,24},{24,0},{1,9},{9,17},{17,25},{25,1},{2,10},{10... | collective-permute-start | bytes 49160 | tf_op jit(solution)/shard_map/ppermute | solution.py:478
  31.0 8.0 %collective-permute-start.12 = (f32[16,128]{1,0:T(8,128)S(1)}, f32[16,128]{1,0:T(8,128)S(1)}, u32[]{:S(2)}, u32[]{:S(2)}) collective-permute-start(f32[16,128]{1,0:T(8,128)S(1)} %get-tuple-element.59), channel_id=1, source_target_pairs={{0,1},{1,2},{2,3},{3,0},{4,5},{5,6},{6,7},{7,4},{8,9},{9,10},{10,1... | collective-permute-start | bytes 24584 | tf_op jit(solution)/shard_map/ppermute | solution.py:478
  32.5 6.6 %collective-permute-start.13 = (f32[16,128]{1,0:T(8,128)S(1)}, f32[16,128]{1,0:T(8,128)S(1)}, u32[]{:S(2)}, u32[]{:S(2)}) collective-permute-start(f32[16,128]{1,0:T(8,128)S(1)} %get-tuple-element.59), channel_id=1, source_target_pairs={{0,3},{1,0},{2,1},{3,2},{4,7},{5,4},{6,5},{7,6},{8,11},{9,8},{10,9... | collective-permute-start | bytes 24584 | tf_op jit(solution)/shard_map/ppermute | solution.py:478
  47.2 5.8 %collective-permute-start.14 = (f32[64,128]{1,0:T(8,128)S(1)}, f32[64,128]{1,0:T(8,128)S(1)}, u32[]{:S(2)}, u32[]{:S(2)}) collective-permute-start(f32[64,128]{1,0:T(8,128)S(1)} %get-tuple-element.67), channel_id=1, source_target_pairs={{0,1},{1,2},{2,3},{3,0},{4,5},{5,6},{6,7},{7,4},{8,9},{9,10},{10,1... | collective-permute-start | bytes 98312 | tf_op jit(solution)/shard_map/ppermute | solution.py:478
  47.2 5.7 %collective-permute-start.15 = (f32[64,128]{1,0:T(8,128)S(1)}, f32[64,128]{1,0:T(8,128)S(1)}, u32[]{:S(2)}, u32[]{:S(2)}) collective-permute-start(f32[64,128]{1,0:T(8,128)S(1)} %get-tuple-element.67), channel_id=1, source_target_pairs={{0,3},{1,0},{2,1},{3,2},{4,7},{5,4},{6,5},{7,6},{8,11},{9,8},{10,9... | collective-permute-start | bytes 98312 | tf_op jit(solution)/shard_map/ppermute | solution.py:478
  53.1 8.3 %collective-permute-start.16 = (f32[32,8,128]{2,1,0:T(8,128)S(1)}, f32[32,8,128]{2,1,0:T(8,128)S(1)}, u32[]{:S(2)}, u32[]{:S(2)}) collective-permute-start(f32[32,8,128]{2,1,0:T(8,128)S(1)} %get-tuple-element.69), channel_id=1, source_target_pairs={{0,4},{4,0},{1,5},{5,1},{2,6},{6,2},{3,7},{7,3},{8,12},{12,8},{9,1... | collective-permute-start | bytes 393224 | tf_op jit(solution)/shard_map/ppermute | solution.py:478
  54.6 2.3 %collective-permute-start.17 = (f32[16,8,128]{2,1,0:T(8,128)S(1)}, f32[16,8,128]{2,1,0:T(8,128)S(1)}, u32[]{:S(2)}, u32[]{:S(2)}) collective-permute-start(f32[16,8,128]{2,1,0:T(8,128)S(1)} %get-tuple-element.70), channel_id=1, source_target_pairs={{0,24},{8,0},{16,8},{24,16},{1,25},{9,1},{17,9},{25,17},{2,26},{10... | collective-permute-start | bytes 196616 | tf_op jit(solution)/shard_map/ppermute | solution.py:478
  54.6 4.0 %collective-permute-start.18 = (f32[16,8,128]{2,1,0:T(8,128)S(1)}, f32[16,8,128]{2,1,0:T(8,128)S(1)}, u32[]{:S(2)}, u32[]{:S(2)}) collective-permute-start(f32[16,8,128]{2,1,0:T(8,128)S(1)} %get-tuple-element.71), channel_id=1, source_target_pairs={{0,8},{8,16},{16,24},{24,0},{1,9},{9,17},{17,25},{25,1},{2,10},{10... | collective-permute-start | bytes 196616 | tf_op jit(solution)/shard_map/ppermute | solution.py:478
  55.1 3.7 %collective-permute-start.19 = (f32[16,8,128]{2,1,0:T(8,128)S(1)}, f32[16,8,128]{2,1,0:T(8,128)S(1)}, u32[]{:S(2)}, u32[]{:S(2)}) collective-permute-start(f32[16,8,128]{2,1,0:T(8,128)S(1)} %get-tuple-element.72), channel_id=1, source_target_pairs={{0,28},{4,24},{8,4},{12,0},{16,12},{20,8},{24,20},{28,16},{1,29},{... | collective-permute-start | bytes 196616 | tf_op jit(solution)/shard_map/ppermute | solution.py:484
  56.4 5.0 %collective-permute-start.20 = (f32[16,8,128]{2,1,0:T(8,128)S(1)}, f32[16,8,128]{2,1,0:T(8,128)S(1)}, u32[]{:S(2)}, u32[]{:S(2)}) collective-permute-start(f32[16,8,128]{2,1,0:T(8,128)S(1)} %get-tuple-element.73), channel_id=1, source_target_pairs={{0,12},{4,8},{8,20},{12,16},{16,28},{20,24},{24,4},{28,0},{1,13},{... | collective-permute-start | bytes 196616 | tf_op jit(solution)/shard_map/ppermute | solution.py:484
  (1 other events, 1.0 us)

commit v11 on v10

--- a/solution.py
+++ b/solution.py
@@ -317,7 +317,8 @@
         put_edges(to_right_y, i, field[nx - LO + i], ny)
 
 
-def table_kernel(nx, ny, cells, fracs, late, early, early_slopes):
+def table_kernel(nx, ny, departures, late, early, early_slopes):
+    cells, fracs = departures.at[0], departures.at[1]
     write_tables(cells.at[1, 1], fracs.at[1, 1], late)
     write_tables(cells.at[0, 1], fracs.at[0, 1], early, early_slopes)
 
@@ -368,10 +369,11 @@
 
 
 def adjoint_kernel(
-    nx, ny, adjoint, weights, cells, fracs,
+    nx, ny, adjoint, weights, departures,
     piled, rims, early_mid, late_slopes, late_mid, cleared,
     scaled, piles, ends,
 ):
+    cells, fracs = departures.at[0], departures.at[1]
     deposit(adjoint, weights, scaled, piles, 2, SHIFTS)
     settle(piles, ends, piled, rims)
     write_tables(cells.at[0, 0], fracs.at[0, 0], early_mid)
@@ -515,6 +517,7 @@
     field = (nx, ny, nz)
     table = (3, SHIFTS) + field
     pair = jnp.stack([intensity, cotangent])
+    departures = jnp.stack([cells.astype(F32), fracs])
     unit = nx * ny * nz * 512
 
     def run(kernel, *rest, **more):
@@ -531,7 +534,7 @@
 
     late, early, early_slopes = run(
         table_kernel,
-        (cells, fracs),
+        (departures,),
         [table, table, table],
         [],
         unit // 16,
@@ -562,7 +565,7 @@
     scaled_3, piles_3 = pile(3)
     piled_adjoint, adjoint_rims, early_mid, late_slopes, late_mid, cleared = run(
         adjoint_kernel,
-        (adjoint, early, cells, fracs),
+        (adjoint, early, departures),
         piled(1) + [table, table, table, piles_3],
         pile(1) + [(1, planes, rows, nz)],
         2 * unit,

time: 62.3 us -> 61.7 us (level)
  local copies, waits for them, and re-layouts: 1.99 us -> 0.01 us
  other arithmetic: 0.78 us -> 2.1 us
    another operation x0 -> x2, other arithmetic: none -> 2.09 us  [body(): departures = jnp.stack([cells.astype(F32), fracs])]
    unnamed x8 -> x4, local copies, waits for them, and re-layouts: 1.99 us -> 0.01 us
    another operation x1, other arithmetic: 0.78 us -> 0.01 us  [body(): pair = jnp.stack([intensity, cotangent])]
where the time goes in v11:
time: 61.7 us; the launch traced here: 61.5 us
  starting transfers between devices  24.6 us (40%)
  Pallas kernels  21.6 us (35%)
  waiting for transfers between devices  12.3 us (20%)
  other arithmetic  2.1 us (3%)
  between operations  0.81 us (1%)
    pallas_call x10, Pallas kernels, call(): pl.pallas_call(kernel, out_shape=[struct(s) for s in outs], in_specs=in_s...  21.6 us
    ppermute x15, starting transfers between devices, send(): return lax.ppermute(message, axes[0], pairs)  19.4 us
    ppermute x15, waiting for transfers between devices, send(): return lax.ppermute(message, axes[0], pairs)  6.99 us
    ppermute x6, waiting for transfers between devices, send(): return lax.ppermute(message, axes, pairs)  5.34 us
    ppermute x6, starting transfers between devices, send(): return lax.ppermute(message, axes, pairs)  5.24 us
    another operation x2, other arithmetic, body(): departures = jnp.stack([cells.astype(F32), fracs])  2.09 us
  transfers between devices with their start and end apart: 21, of which 7 were waited for; matrix products, arithmetic and copies ran while one was open for 0% of the time, Pallas kernels for 11%

profile of v11, /device:TPU:0, one launch (start us, length us, event | category | flops | bytes accessed | tf_op | source)
XLA Modules:
  0.0 61.5 jit_solution(11195198391307123441)
XLA Ops:
  0.6 1.0 %convert_bitcast_fusion = f32[1,2,2,3,8,8,128]{6,5,4,3,2,1,0:T(8,128)S(1)} fusion(s32[2,2,3,8,8,128]{5,4,3,2,1,0:T(8,128)} %param.6), kind=kLoop, calls=%fused_computation.1 | loop fusion | flops 98304 | bytes 786432 | tf_op jit(solution)/shard_map/stack | solution.py:520
  1.7 1.1 %pad_maximum_fusion.departures = f32[2,2,2,3,8,8,128]{6,5,4,3,2,1,0:T(8,128)S(1)} fusion(f32[1,2,2,3,8,8,128]{6,5,4,3,2,1,0:T(8,128)} %bitcast.5, f32[1,2,2,3,8,8,128]{6,5,4,3,2,1,0:T(8,128)S(1)} %convert_bitcast_fusion), kind=kLoop, calls=%fused_computation | loop fusion | flops 196608 | bytes 1572864 | tf_op jit(solution)/shard_map/stack | solution.py:520
  3.3 2.0 %shard_map.60 = (f32[17,8,128]{2,1,0:T(8,128)S(1)}, f32[8,8,128]{2,1,0:T(8,128)S(1)}, f32[8,8,128]{2,1,0:T(8,128)S(1)}, f32[8,8,128]{2,1,0:T(8,128)S(1)}, f32[8,...) custom-call(f32[2,8,8,128]{3,2,1,0:T(8,128)S(1)} %pad_maximum_fusion.1.pair, f32[3,8,8,8,128]{4,3,2,1,0:T(8,128)S(1)} %get-tuple-element.38.weights), custom_call_target="tpu_custom_call" | custom-call | flops 8388608 | bytes 851968 | tf_op jit(solution)/shard_map/pallas_call | solution.py:463
  5.3 3.0 %collective-permute-start = (f32[17,8,128]{2,1,0:T(8,128)S(1)}, f32[17,8,128]{2,1,0:T(8,128)S(1)}, u32[]{:S(2)}, u32[]{:S(2)}) collective-permute-start(f32[17,8,128]{2,1,0:T(8,128)S(1)} %get-tuple-element.39), channel_id=1, source_target_pairs={{0,4},{4,0},{1,5},{5,1},{2,6},{6,2},{3,7},{7,3},{8,12},{12,8},{9,1... | collective-permute-start | bytes 208904 | tf_op jit(solution)/shard_map/ppermute | solution.py:480
  9.0 1.7 %collective-permute-start.3 = (f32[8,8,128]{2,1,0:T(8,128)S(1)}, f32[8,8,128]{2,1,0:T(8,128)S(1)}, u32[]{:S(2)}, u32[]{:S(2)}) collective-permute-start(f32[8,8,128]{2,1,0:T(8,128)S(1)} %get-tuple-element.42), channel_id=1, source_target_pairs={{0,28},{4,24},{8,4},{12,0},{16,12},{20,8},{24,20},{28,16},{1,29},{... | collective-permute-start | bytes 98312 | tf_op jit(solution)/shard_map/ppermute | solution.py:486
  10.7 1.6 %collective-permute-done.2.from_l = f32[8,8,128]{2,1,0:T(8,128)S(1)} collective-permute-done((f32[8,8,128]{2,1,0:T(8,128)S(1)}, f32[8,8,128]{2,1,0:T(8,128)S(1)}, u32[]{:S(2)}, u32[]{:S(2)}) %collective-permute-start.2) | collective-permute-done | bytes 32800 | tf_op jit(solution)/shard_map/ppermute | solution.py:480
  12.3 2.6 %collective-permute-done.4.from_ly = f32[8,8,128]{2,1,0:T(8,128)S(1)} collective-permute-done((f32[8,8,128]{2,1,0:T(8,128)S(1)}, f32[8,8,128]{2,1,0:T(8,128)S(1)}, u32[]{:S(2)}, u32[]{:S(2)}) %collective-permute-start.4) | collective-permute-done | bytes 32800 | tf_op jit(solution)/shard_map/ppermute | solution.py:486
  15.0 1.6 %collective-permute-start.5 = (f32[24,128]{1,0:T(8,128)S(1)}, f32[24,128]{1,0:T(8,128)S(1)}, u32[]{:S(2)}, u32[]{:S(2)}) collective-permute-start(f32[24,128]{1,0:T(8,128)S(1)} %get-tuple-element.46), channel_id=1, source_target_pairs={{0,1},{1,2},{2,3},{3,0},{4,5},{5,6},{6,7},{7,4},{8,9},{9,10},{10,1... | collective-permute-start | bytes 36872 | tf_op jit(solution)/shard_map/ppermute | solution.py:480
  16.7 2.2 %collective-permute-start.6 = (f32[24,128]{1,0:T(8,128)S(1)}, f32[24,128]{1,0:T(8,128)S(1)}, u32[]{:S(2)}, u32[]{:S(2)}) collective-permute-start(f32[24,128]{1,0:T(8,128)S(1)} %get-tuple-element.46), channel_id=1, source_target_pairs={{0,3},{1,0},{2,1},{3,2},{4,7},{5,4},{6,5},{7,6},{8,11},{9,8},{10,9... | collective-permute-start | bytes 36872 | tf_op jit(solution)/shard_map/ppermute | solution.py:480
  18.9 1.7 %collective-permute-done.5.rims_l = f32[24,128]{1,0:T(8,128)S(1)} collective-permute-done((f32[24,128]{1,0:T(8,128)S(1)}, f32[24,128]{1,0:T(8,128)S(1)}, u32[]{:S(2)}, u32[]{:S(2)}) %collective-permute-start.5) | collective-permute-done | bytes 12320 | tf_op jit(solution)/shard_map/ppermute | solution.py:480
  20.6 3.3 %shard_map.62 = (f32[8,8,128]{2,1,0:T(8,128)S(1)}, f32[8,8,128]{2,1,0:T(8,128)S(1)}, f32[4,8,128]{2,1,0:T(8,128)S(1)}, f32[4,8,128]{2,1,0:T(8,128)S(1)}, f32[4,8...) custom-call(f32[15,16,128]{2,1,0:T(8,128)S(1)} %get-tuple-element.45., ...), custom_call_target="tpu_custom_call" | custom-call | flops 20971520 | bytes 1753088 | tf_op jit(solution)/shard_map/pallas_call | solution.py:463
  23.9 1.5 %collective-permute-start.7 = (f32[8,8,128]{2,1,0:T(8,128)S(1)}, f32[8,8,128]{2,1,0:T(8,128)S(1)}, u32[]{:S(2)}, u32[]{:S(2)}) collective-permute-start(f32[8,8,128]{2,1,0:T(8,128)S(1)} %get-tuple-element.51), channel_id=1, source_target_pairs={{0,4},{4,0},{1,5},{5,1},{2,6},{6,2},{3,7},{7,3},{8,12},{12,8},{9,1... | collective-permute-start | bytes 98312 | tf_op jit(solution)/shard_map/ppermute | solution.py:480
  25.4 1.7 %collective-permute-start.11 = (f32[4,8,128]{2,1,0:T(8,128)S(1)}, f32[4,8,128]{2,1,0:T(8,128)S(1)}, u32[]{:S(2)}, u32[]{:S(2)}) collective-permute-start(f32[4,8,128]{2,1,0:T(8,128)S(1)} %get-tuple-element.55), channel_id=1, source_target_pairs={{0,12},{4,8},{8,20},{12,16},{16,28},{20,24},{24,4},{28,0},{1,13},{... | collective-permute-start | bytes 49160 | tf_op jit(solution)/shard_map/ppermute | solution.py:486
  27.6 2.6 %shard_map.63 = (f32[1,15,16,128]{3,2,1,0:T(8,128)S(1)}, f32[1,16,128]{2,1,0:T(8,128)S(1)}, f32[3,8,8,8,128]{4,3,2,1,0:T(8,128)S(1)}, f32[3,8,8,8,128]{4,3,2,1,0...) custom-call(f32[1,8,8,128]{3,2,1,0:T(8,128)S(1)} %get-tuple-element.56.adjoint, ...), custom_call_target="tpu_custom_call" | custom-call | flops 8388608 | bytes 1605632 | tf_op jit(solution)/shard_map/pallas_call | solution.py:463
  30.4 1.4 %collective-permute-start.12 = (f32[16,128]{1,0:T(8,128)S(1)}, f32[16,128]{1,0:T(8,128)S(1)}, u32[]{:S(2)}, u32[]{:S(2)}) collective-permute-start(f32[16,128]{1,0:T(8,128)S(1)} %get-tuple-element.59), channel_id=1, source_target_pairs={{0,1},{1,2},{2,3},{3,0},{4,5},{5,6},{6,7},{7,4},{8,9},{9,10},{10,1... | collective-permute-start | bytes 24584 | tf_op jit(solution)/shard_map/ppermute | solution.py:480
  31.8 2.5 %collective-permute-start.13 = (f32[16,128]{1,0:T(8,128)S(1)}, f32[16,128]{1,0:T(8,128)S(1)}, u32[]{:S(2)}, u32[]{:S(2)}) collective-permute-start(f32[16,128]{1,0:T(8,128)S(1)} %get-tuple-element.59), channel_id=1, source_target_pairs={{0,3},{1,0},{2,1},{3,2},{4,7},{5,4},{6,5},{7,6},{8,11},{9,8},{10,9... | collective-permute-start | bytes 24584 | tf_op jit(solution)/shard_map/ppermute | solution.py:480
  34.4 4.0 %shard_map.65.early_piles = f32[3,8,15,16,128]{4,3,2,1,0:T(8,128)S(1)} custom-call(f32[3,8,8,128]{3,2,1,0:T(8,128)S(1)} %get-tuple-element.63.gradient, f32[1,8,8,128]{3,2,1,0:T(8,128)S(1)} %get-tuple-element.56.adjoint, f32[3,8,8,8,128]{4,3,2,1,0:T(8,128)S(1)} %get-tuple-element.64.weights, ...), custom_call_target="tpu_custom_call", output_to_operand_aliasing={{}: (3, {})} | custom-call | flops 25165824 | bytes 3866624 | tf_op jit(solution)/shard_map/pallas_call | solution.py:463
  38.4 8.1 %shard_map.66 = (f32[3,15,16,128]{3,2,1,0:T(8,128)S(1)}, f32[64,128]{1,0:T(8,128)S(1)}, f32[3,8,15,16,128]{4,3,2,1,0:T(8,128)S(1)}) custom-call(f32[15,16,128]{2,1,0:T(8,128)S(1)} %get-tuple-element.58.extended, f32[16,128]{1,0:T(8,128)S(1)} %collective-permute-done.12.rims_l, ...), custom_call_target="tpu_custom_call", output_to_operand_aliasing={{2}: (8, {})} | custom-call | flops 46137344 | bytes 5521408 | tf_op jit(solution)/shard_map/pallas_call | solution.py:463
  46.6 3.8 %collective-permute-start.15 = (f32[64,128]{1,0:T(8,128)S(1)}, f32[64,128]{1,0:T(8,128)S(1)}, u32[]{:S(2)}, u32[]{:S(2)}) collective-permute-start(f32[64,128]{1,0:T(8,128)S(1)} %get-tuple-element.67), channel_id=1, source_target_pairs={{0,3},{1,0},{2,1},{3,2},{4,7},{5,4},{6,5},{7,6},{8,11},{9,8},{10,9... | collective-permute-start | bytes 98312 | tf_op jit(solution)/shard_map/ppermute | solution.py:480
  50.4 1.9 %collective-permute-done.14.rims_l = f32[64,128]{1,0:T(8,128)S(1)} collective-permute-done((f32[64,128]{1,0:T(8,128)S(1)}, f32[64,128]{1,0:T(8,128)S(1)}, u32[]{:S(2)}, u32[]{:S(2)}) %collective-permute-start.14) | collective-permute-done | bytes 32800 | tf_op jit(solution)/shard_map/ppermute | solution.py:480
  52.5 1.5 %collective-permute-start.16 = (f32[32,8,128]{2,1,0:T(8,128)S(1)}, f32[32,8,128]{2,1,0:T(8,128)S(1)}, u32[]{:S(2)}, u32[]{:S(2)}) collective-permute-start(f32[32,8,128]{2,1,0:T(8,128)S(1)} %get-tuple-element.69), channel_id=1, source_target_pairs={{0,4},{4,0},{1,5},{5,1},{2,6},{6,2},{3,7},{7,3},{8,12},{12,8},{9,1... | collective-permute-start | bytes 393224 | tf_op jit(solution)/shard_map/ppermute | solution.py:480
  54.5 1.2 %collective-permute-start.19 = (f32[16,8,128]{2,1,0:T(8,128)S(1)}, f32[16,8,128]{2,1,0:T(8,128)S(1)}, u32[]{:S(2)}, u32[]{:S(2)}) collective-permute-start(f32[16,8,128]{2,1,0:T(8,128)S(1)} %get-tuple-element.72), channel_id=1, source_target_pairs={{0,28},{4,24},{8,4},{12,0},{16,12},{20,8},{24,20},{28,16},{1,29},{... | collective-permute-start | bytes 196616 | tf_op jit(solution)/shard_map/ppermute | solution.py:486
  56.3 1.8 %collective-permute-done.18.from_l = f32[16,8,128]{2,1,0:T(8,128)S(1)} collective-permute-done((f32[16,8,128]{2,1,0:T(8,128)S(1)}, f32[16,8,128]{2,1,0:T(8,128)S(1)}, u32[]{:S(2)}, u32[]{:S(2)}) %collective-permute-start.18) | collective-permute-done | bytes 65568 | tf_op jit(solution)/shard_map/ppermute | solution.py:480
  58.2 2.6 %collective-permute-done.20.from_ly = f32[16,8,128]{2,1,0:T(8,128)S(1)} collective-permute-done((f32[16,8,128]{2,1,0:T(8,128)S(1)}, f32[16,8,128]{2,1,0:T(8,128)S(1)}, u32[]{:S(2)}, u32[]{:S(2)}) %collective-permute-start.20) | collective-permute-done | bytes 65568 | tf_op jit(solution)/shard_map/ppermute | solution.py:486
  (35 shorter events, 4.1 us)
Async XLA Ops:
  0.6 2.6 %copy-start.1 = (f32[8,8,128]{2,1,0:T(8,128)S(1)}, f32[8,8,128]{2,1,0:T(8,128)}, u32[]{:S(2)}) copy-start(f32[8,8,128]{2,1,0:T(8,128)} %param.4) | copy-start | bytes 98308
  0.6 2.6 %copy-start = (f32[8,8,128]{2,1,0:T(8,128)S(1)}, f32[8,8,128]{2,1,0:T(8,128)}, u32[]{:S(2)}) copy-start(f32[8,8,128]{2,1,0:T(8,128)} %param.5) | copy-start | bytes 98308
  5.3 9.6 %collective-permute-start = (f32[17,8,128]{2,1,0:T(8,128)S(1)}, f32[17,8,128]{2,1,0:T(8,128)S(1)}, u32[]{:S(2)}, u32[]{:S(2)}) collective-permute-start(f32[17,8,128]{2,1,0:T(8,128)S(1)} %get-tuple-element.39), channel_id=1, source_target_pairs={{0,4},{4,0},{1,5},{5,1},{2,6},{6,2},{3,7},{7,3},{8,12},{12,8},{9,1... | collective-permute-start | bytes 208904 | tf_op jit(solution)/shard_map/ppermute | solution.py:480
  8.3 2.4 %collective-permute-start.1 = (f32[8,8,128]{2,1,0:T(8,128)S(1)}, f32[8,8,128]{2,1,0:T(8,128)S(1)}, u32[]{:S(2)}, u32[]{:S(2)}) collective-permute-start(f32[8,8,128]{2,1,0:T(8,128)S(1)} %get-tuple-element.40), channel_id=1, source_target_pairs={{0,24},{8,0},{16,8},{24,16},{1,25},{9,1},{17,9},{25,17},{2,26},{10... | collective-permute-start | bytes 98312 | tf_op jit(solution)/shard_map/ppermute | solution.py:480
  9.0 3.3 %collective-permute-start.2 = (f32[8,8,128]{2,1,0:T(8,128)S(1)}, f32[8,8,128]{2,1,0:T(8,128)S(1)}, u32[]{:S(2)}, u32[]{:S(2)}) collective-permute-start(f32[8,8,128]{2,1,0:T(8,128)S(1)} %get-tuple-element.41), channel_id=1, source_target_pairs={{0,8},{8,16},{16,24},{24,0},{1,9},{9,17},{17,25},{25,1},{2,10},{10... | collective-permute-start | bytes 98312 | tf_op jit(solution)/shard_map/ppermute | solution.py:480
  9.0 3.3 %collective-permute-start.3 = (f32[8,8,128]{2,1,0:T(8,128)S(1)}, f32[8,8,128]{2,1,0:T(8,128)S(1)}, u32[]{:S(2)}, u32[]{:S(2)}) collective-permute-start(f32[8,8,128]{2,1,0:T(8,128)S(1)} %get-tuple-element.42), channel_id=1, source_target_pairs={{0,28},{4,24},{8,4},{12,0},{16,12},{20,8},{24,20},{28,16},{1,29},{... | collective-permute-start | bytes 98312 | tf_op jit(solution)/shard_map/ppermute | solution.py:486
  10.7 4.2 %collective-permute-start.4 = (f32[8,8,128]{2,1,0:T(8,128)S(1)}, f32[8,8,128]{2,1,0:T(8,128)S(1)}, u32[]{:S(2)}, u32[]{:S(2)}) collective-permute-start(f32[8,8,128]{2,1,0:T(8,128)S(1)} %get-tuple-element.43), channel_id=1, source_target_pairs={{0,12},{4,8},{8,20},{12,16},{16,28},{20,24},{24,4},{28,0},{1,13},{... | collective-permute-start | bytes 98312 | tf_op jit(solution)/shard_map/ppermute | solution.py:486
  15.0 5.6 %collective-permute-start.5 = (f32[24,128]{1,0:T(8,128)S(1)}, f32[24,128]{1,0:T(8,128)S(1)}, u32[]{:S(2)}, u32[]{:S(2)}) collective-permute-start(f32[24,128]{1,0:T(8,128)S(1)} %get-tuple-element.46), channel_id=1, source_target_pairs={{0,1},{1,2},{2,3},{3,0},{4,5},{5,6},{6,7},{7,4},{8,9},{9,10},{10,1... | collective-permute-start | bytes 36872 | tf_op jit(solution)/shard_map/ppermute | solution.py:480
  16.7 4.0 %collective-permute-start.6 = (f32[24,128]{1,0:T(8,128)S(1)}, f32[24,128]{1,0:T(8,128)S(1)}, u32[]{:S(2)}, u32[]{:S(2)}) collective-permute-start(f32[24,128]{1,0:T(8,128)S(1)} %get-tuple-element.46), channel_id=1, source_target_pairs={{0,3},{1,0},{2,1},{3,2},{4,7},{5,4},{6,5},{7,6},{8,11},{9,8},{10,9... | collective-permute-start | bytes 36872 | tf_op jit(solution)/shard_map/ppermute | solution.py:480
  23.9 6.4 %collective-permute-start.7 = (f32[8,8,128]{2,1,0:T(8,128)S(1)}, f32[8,8,128]{2,1,0:T(8,128)S(1)}, u32[]{:S(2)}, u32[]{:S(2)}) collective-permute-start(f32[8,8,128]{2,1,0:T(8,128)S(1)} %get-tuple-element.51), channel_id=1, source_target_pairs={{0,4},{4,0},{1,5},{5,1},{2,6},{6,2},{3,7},{7,3},{8,12},{12,8},{9,1... | collective-permute-start | bytes 98312 | tf_op jit(solution)/shard_map/ppermute | solution.py:480
  25.4 4.9 %collective-permute-start.10 = (f32[4,8,128]{2,1,0:T(8,128)S(1)}, f32[4,8,128]{2,1,0:T(8,128)S(1)}, u32[]{:S(2)}, u32[]{:S(2)}) collective-permute-start(f32[4,8,128]{2,1,0:T(8,128)S(1)} %get-tuple-element.54), channel_id=1, source_target_pairs={{0,28},{4,24},{8,4},{12,0},{16,12},{20,8},{24,20},{28,16},{1,29},{... | collective-permute-start | bytes 49160 | tf_op jit(solution)/shard_map/ppermute | solution.py:486
  25.4 4.9 %collective-permute-start.11 = (f32[4,8,128]{2,1,0:T(8,128)S(1)}, f32[4,8,128]{2,1,0:T(8,128)S(1)}, u32[]{:S(2)}, u32[]{:S(2)}) collective-permute-start(f32[4,8,128]{2,1,0:T(8,128)S(1)} %get-tuple-element.55), channel_id=1, source_target_pairs={{0,12},{4,8},{8,20},{12,16},{16,28},{20,24},{24,4},{28,0},{1,13},{... | collective-permute-start | bytes 49160 | tf_op jit(solution)/shard_map/ppermute | solution.py:486
  27.1 3.2 %collective-permute-start.8 = (f32[4,8,128]{2,1,0:T(8,128)S(1)}, f32[4,8,128]{2,1,0:T(8,128)S(1)}, u32[]{:S(2)}, u32[]{:S(2)}) collective-permute-start(f32[4,8,128]{2,1,0:T(8,128)S(1)} %get-tuple-element.52), channel_id=1, source_target_pairs={{0,24},{8,0},{16,8},{24,16},{1,25},{9,1},{17,9},{25,17},{2,26},{10... | collective-permute-start | bytes 49160 | tf_op jit(solution)/shard_map/ppermute | solution.py:480
  27.1 3.2 %collective-permute-start.9 = (f32[4,8,128]{2,1,0:T(8,128)S(1)}, f32[4,8,128]{2,1,0:T(8,128)S(1)}, u32[]{:S(2)}, u32[]{:S(2)}) collective-permute-start(f32[4,8,128]{2,1,0:T(8,128)S(1)} %get-tuple-element.53), channel_id=1, source_target_pairs={{0,8},{8,16},{16,24},{24,0},{1,9},{9,17},{17,25},{25,1},{2,10},{10... | collective-permute-start | bytes 49160 | tf_op jit(solution)/shard_map/ppermute | solution.py:480
  30.4 8.0 %collective-permute-start.12 = (f32[16,128]{1,0:T(8,128)S(1)}, f32[16,128]{1,0:T(8,128)S(1)}, u32[]{:S(2)}, u32[]{:S(2)}) collective-permute-start(f32[16,128]{1,0:T(8,128)S(1)} %get-tuple-element.59), channel_id=1, source_target_pairs={{0,1},{1,2},{2,3},{3,0},{4,5},{5,6},{6,7},{7,4},{8,9},{9,10},{10,1... | collective-permute-start | bytes 24584 | tf_op jit(solution)/shard_map/ppermute | solution.py:480
  31.8 6.6 %collective-permute-start.13 = (f32[16,128]{1,0:T(8,128)S(1)}, f32[16,128]{1,0:T(8,128)S(1)}, u32[]{:S(2)}, u32[]{:S(2)}) collective-permute-start(f32[16,128]{1,0:T(8,128)S(1)} %get-tuple-element.59), channel_id=1, source_target_pairs={{0,3},{1,0},{2,1},{3,2},{4,7},{5,4},{6,5},{7,6},{8,11},{9,8},{10,9... | collective-permute-start | bytes 24584 | tf_op jit(solution)/shard_map/ppermute | solution.py:480
  46.5 5.8 %collective-permute-start.14 = (f32[64,128]{1,0:T(8,128)S(1)}, f32[64,128]{1,0:T(8,128)S(1)}, u32[]{:S(2)}, u32[]{:S(2)}) collective-permute-start(f32[64,128]{1,0:T(8,128)S(1)} %get-tuple-element.67), channel_id=1, source_target_pairs={{0,1},{1,2},{2,3},{3,0},{4,5},{5,6},{6,7},{7,4},{8,9},{9,10},{10,1... | collective-permute-start | bytes 98312 | tf_op jit(solution)/shard_map/ppermute | solution.py:480
  46.6 5.7 %collective-permute-start.15 = (f32[64,128]{1,0:T(8,128)S(1)}, f32[64,128]{1,0:T(8,128)S(1)}, u32[]{:S(2)}, u32[]{:S(2)}) collective-permute-start(f32[64,128]{1,0:T(8,128)S(1)} %get-tuple-element.67), channel_id=1, source_target_pairs={{0,3},{1,0},{2,1},{3,2},{4,7},{5,4},{6,5},{7,6},{8,11},{9,8},{10,9... | collective-permute-start | bytes 98312 | tf_op jit(solution)/shard_map/ppermute | solution.py:480
  52.5 8.3 %collective-permute-start.16 = (f32[32,8,128]{2,1,0:T(8,128)S(1)}, f32[32,8,128]{2,1,0:T(8,128)S(1)}, u32[]{:S(2)}, u32[]{:S(2)}) collective-permute-start(f32[32,8,128]{2,1,0:T(8,128)S(1)} %get-tuple-element.69), channel_id=1, source_target_pairs={{0,4},{4,0},{1,5},{5,1},{2,6},{6,2},{3,7},{7,3},{8,12},{12,8},{9,1... | collective-permute-start | bytes 393224 | tf_op jit(solution)/shard_map/ppermute | solution.py:480
  54.0 2.3 %collective-permute-start.17 = (f32[16,8,128]{2,1,0:T(8,128)S(1)}, f32[16,8,128]{2,1,0:T(8,128)S(1)}, u32[]{:S(2)}, u32[]{:S(2)}) collective-permute-start(f32[16,8,128]{2,1,0:T(8,128)S(1)} %get-tuple-element.70), channel_id=1, source_target_pairs={{0,24},{8,0},{16,8},{24,16},{1,25},{9,1},{17,9},{25,17},{2,26},{10... | collective-permute-start | bytes 196616 | tf_op jit(solution)/shard_map/ppermute | solution.py:480
  54.0 4.0 %collective-permute-start.18 = (f32[16,8,128]{2,1,0:T(8,128)S(1)}, f32[16,8,128]{2,1,0:T(8,128)S(1)}, u32[]{:S(2)}, u32[]{:S(2)}) collective-permute-start(f32[16,8,128]{2,1,0:T(8,128)S(1)} %get-tuple-element.71), channel_id=1, source_target_pairs={{0,8},{8,16},{16,24},{24,0},{1,9},{9,17},{17,25},{25,1},{2,10},{10... | collective-permute-start | bytes 196616 | tf_op jit(solution)/shard_map/ppermute | solution.py:480
  54.5 3.7 %collective-permute-start.19 = (f32[16,8,128]{2,1,0:T(8,128)S(1)}, f32[16,8,128]{2,1,0:T(8,128)S(1)}, u32[]{:S(2)}, u32[]{:S(2)}) collective-permute-start(f32[16,8,128]{2,1,0:T(8,128)S(1)} %get-tuple-element.72), channel_id=1, source_target_pairs={{0,28},{4,24},{8,4},{12,0},{16,12},{20,8},{24,20},{28,16},{1,29},{... | collective-permute-start | bytes 196616 | tf_op jit(solution)/shard_map/ppermute | solution.py:486
  55.8 5.0 %collective-permute-start.20 = (f32[16,8,128]{2,1,0:T(8,128)S(1)}, f32[16,8,128]{2,1,0:T(8,128)S(1)}, u32[]{:S(2)}, u32[]{:S(2)}) collective-permute-start(f32[16,8,128]{2,1,0:T(8,128)S(1)} %get-tuple-element.73), channel_id=1, source_target_pairs={{0,12},{4,8},{8,20},{12,16},{16,28},{20,24},{24,4},{28,0},{1,13},{... | collective-permute-start | bytes 196616 | tf_op jit(solution)/shard_map/ppermute | solution.py:486
